TPU v7x, 128 devices: a whole 4x4x4 slice. The times are simulated.
128 devices in a mesh: stream: 4 (over x), tile: 32 (over y, z, core).
Axes of the slice: x: 4, y: 4, z: 4, core: 2. Of those that a mesh axis runs over, the one named last changes fastest.
Arguments:
- frame_in: bfloat16 [16, 64, 128, 384], P('stream', 'tile'), may hold values from -6 to 6
- cache_first: bfloat16 [16, 2, 64, 128, 384], P('stream', None, 'tile'), may hold values from -6 to 6
- cache_second: bfloat16 [16, 2, 64, 128, 384], P('stream', None, 'tile'), may hold values from -6 to 6
- gain_first: float32 [384], replicated, may hold values from 0.1 to 1.9
- gain_second: float32 [384], replicated, may hold values from 0.1 to 1.9
- conv_first: bfloat16 [3, 3, 3, 384, 384], replicated, may hold values from -0.0625 to 0.0625
- conv_second: bfloat16 [3, 3, 3, 384, 384], replicated, may hold values from -0.0625 to 0.0625
- bias_first: float32 [384], replicated, may hold values from -0.5 to 0.5
- bias_second: float32 [384], replicated, may hold values from -0.5 to 0.5
- old_slot: int32 [16], replicated, may hold values from 0 to 15, as said below
- new_slot: int32 [16], replicated, may hold values from 0 to 15, as said below
- old_shift: int32 [16], replicated, may hold values from 0 to 31
- new_shift: int32 [16], replicated, may hold values from 0 to 31
- frame_count: int32 [16], replicated, may hold values from 0 to 2
Outputs:
- mixed_frame: bfloat16 [16, 64, 128, 384], P('stream', 'tile')
- next_first: bfloat16 [16, 2, 64, 128, 384], P('stream', None, 'tile')
- next_second: bfloat16 [16, 2, 64, 128, 384], P('stream', None, 'tile')
Inputs may be any that keep to these rules, and one draw needn't show every extreme that they name: `old_slot`: slot q is position q % 4 of group q // 4; every slot holds one stream. `new_slot`: every slot holds one stream; of the streams of one old group at most 2 go to any one new group, and from every old group exactly 2 go to one same group.
All inputs are finite; a program needn't handle non-finite values.
Results may differ from a plain program's by a relative error of at most 0.0025.
Values may be sent and summed in bfloat16 or wider, within the bound.
No kernel may reach another device: no remote copies, remote signals or barrier semaphores. Data moves between devices by JAX's collectives and lax.ppermute only.
A program may use at most 128 MiB of HBM per device.

v0:
```python
import jax
import jax.numpy as jnp
from jax import lax
from jax.sharding import PartitionSpec as P


def shifted_2(array, axis, by):
    size = lax.axis_size(axis)
    return lax.ppermute(array, axis, [(i, (i + by) % size) for i in range(size)])


def padded_2(cells, sides, width):
    for axis, dim in sides:
        count = lax.axis_size(axis)
        head = lax.slice_in_dim(cells, 0, width, axis=dim)
        tail = lax.slice_in_dim(cells, cells.shape[dim] - width, cells.shape[dim], axis=dim)
        cells = jnp.concatenate(
            [
                lax.ppermute(tail, axis, [(i, (i + 1) % count) for i in range(count)]),
                cells,
                lax.ppermute(head, axis, [((i + 1) % count, i) for i in range(count)]),
            ],
            axis=dim,
        )
    return cells


def lookup(held_table, values):
    return jnp.sum(jnp.where(held_table, values[None, :], 0), axis=1)


def activate(values, gain):
    scaled = values * lax.rsqrt(jnp.mean(values * values, axis=-1, keepdims=True) + 1e-06)
    return jax.nn.silu(scaled * gain)


def convolve(padded, weight, bias_vec):
    n_slots = padded.shape[0]
    n_rows = padded.shape[2] - 2
    n_cols = padded.shape[3]
    channels = padded.shape[4]
    widened = jnp.pad(padded, ((0, 0), (0, 0), (0, 0), (1, 1), (0, 0)))
    pieces = [
        widened[:, t_step, y_step : y_step + n_rows, x_step : x_step + n_cols, :]
        for t_step in range(3)
        for y_step in range(3)
        for x_step in range(3)
    ]
    patches = jnp.concatenate(pieces, axis=-1).reshape(-1, 27 * channels)
    result = (
        jnp.dot(
            patches, weight.reshape(27 * channels, channels), preferred_element_type=jnp.float32
        )
        + bias_vec
    )
    return result.reshape(n_slots, n_rows, n_cols, channels)


def relocate(block, send_pick, take_pick, rotation):
    n_groups = lax.axis_size("stream")
    outgoing = jnp.einsum(
        "as,sfrwc->afrwc", send_pick, block, preferred_element_type=jnp.float32
    ).astype(jnp.bfloat16)
    outgoing = outgoing.reshape((n_groups, -1) + block.shape[1:])
    arrived = lax.all_to_all(outgoing, "stream", split_axis=0, concat_axis=0, tiled=True)
    arrived = arrived.reshape((-1,) + block.shape[1:])
    placed = jnp.einsum(
        "sa,afrwc->sfrwc", take_pick, arrived, preferred_element_type=jnp.float32
    ).astype(jnp.bfloat16)
    for bit_index in range((lax.axis_size("tile") - 1).bit_length()):
        shifted = shifted_2(placed, "tile", 1 << bit_index)
        chosen = rotation >> bit_index & 1 == 1
        placed = jnp.where(chosen[:, None, None, None, None], shifted, placed)
    return placed


def local(
    frame_in,
    cache_first,
    cache_second,
    gain_first,
    gain_second,
    conv_first,
    conv_second,
    bias_first,
    bias_second,
    old_slot,
    new_slot,
    old_shift,
    new_shift,
    frame_count,
):
    n_slots, n_rows = (frame_in.shape[0], frame_in.shape[1])
    n_groups = lax.axis_size("stream")
    n_tiles = lax.axis_size("tile")
    my_group = lax.axis_index("stream")
    my_tile = lax.axis_index("tile")
    n_flight = old_slot.shape[0]
    capacity = max(2, (n_slots + n_groups - 1) // n_groups)
    slot_ids = jnp.arange(n_flight, dtype=jnp.int32)
    held_old = old_slot[None, :] == slot_ids[:, None]
    held_new = new_slot[None, :] == slot_ids[:, None]
    target_group = lookup(held_old, new_slot) // n_slots
    source_group = slot_ids // n_slots
    position = slot_ids % n_slots
    earlier = (
        (source_group[:, None] == source_group[None, :])
        & (position[None, :] < position[:, None])
        & (target_group[:, None] == target_group[None, :])
    )
    ranked = jnp.sum(earlier.astype(jnp.int32), axis=1)
    out_lane = target_group * capacity + ranked
    anchor_slot = lookup(held_new, old_slot)
    in_lane = anchor_slot // n_slots * capacity + lookup(
        anchor_slot[:, None] == slot_ids[None, :], ranked
    )
    shift_after = lookup(held_new, new_shift)
    rotation = (shift_after - lookup(held_new, old_shift)) % n_tiles
    frames_done = lookup(held_new, frame_count)
    tile_number = (my_tile - shift_after) % n_tiles
    start = my_group * n_slots
    my_out = lax.dynamic_slice_in_dim(out_lane, start, n_slots)
    my_in = lax.dynamic_slice_in_dim(in_lane, start, n_slots)
    my_rotation = lax.dynamic_slice_in_dim(rotation, start, n_slots)
    my_frames = lax.dynamic_slice_in_dim(frames_done, start, n_slots)
    my_number = lax.dynamic_slice_in_dim(tile_number, start, n_slots)
    lane_ids = jnp.arange(n_groups * capacity, dtype=jnp.int32)
    send_pick = (lane_ids[:, None] == my_out[None, :]).astype(jnp.bfloat16)
    take_pick = (my_in[:, None] == lane_ids[None, :]).astype(jnp.bfloat16)
    frame_keep = jnp.stack([my_frames >= 2, my_frames >= 1], axis=1).astype(jnp.bfloat16)[
        :, :, None, None, None
    ]
    border = jnp.ones((n_slots, n_rows + 2), jnp.bfloat16)
    border = border.at[:, 0].set((my_number != 0).astype(jnp.bfloat16))
    border = border.at[:, -1].set((my_number != n_tiles - 1).astype(jnp.bfloat16))
    border = border[:, None, :, None, None]
    kept_first = relocate(cache_first, send_pick, take_pick, my_rotation)
    kept_second = relocate(cache_second, send_pick, take_pick, my_rotation)
    kept_first = kept_first * frame_keep
    kept_second = kept_second * frame_keep

    def conv_layer(kept_cache, activation, weight, bias_vec):
        padded = padded_2(
            jnp.concatenate([kept_cache, activation[:, None]], axis=1), (("tile", 2),), 1
        )
        return convolve(padded * border, weight, bias_vec)

    act_first = activate(frame_in.astype(jnp.float32), gain_first).astype(jnp.bfloat16)
    hidden = conv_layer(kept_first, act_first, conv_first, bias_first)
    act_second = activate(hidden, gain_second).astype(jnp.bfloat16)
    second_out = conv_layer(kept_second, act_second, conv_second, bias_second)
    mixed_frame = (second_out + frame_in.astype(jnp.float32)).astype(jnp.bfloat16)
    next_first = jnp.stack([kept_first[:, 1], act_first], axis=1)
    next_second = jnp.stack([kept_second[:, 1], act_second], axis=1)
    return (mixed_frame, next_first, next_second)


def solution(mesh):
    placed = (
        P("stream", "tile", None, None),
        P("stream", None, "tile", None, None),
        P("stream", None, "tile", None, None),
        P(),
        P(),
        P(),
        P(),
        P(),
        P(),
        P(),
        P(),
        P(),
        P(),
        P(),
    )
    return jax.shard_map(
        local,
        mesh=mesh,
        in_specs=placed,
        out_specs=(
            P("stream", "tile", None, None),
            P("stream", None, "tile", None, None),
            P("stream", None, "tile", None, None),
        ),
        check_vma=False,
    )
```

profile of v0, /device:TPU:0, one launch (start us, length us, event | category | flops | bytes accessed | tf_op | source)
XLA Modules:
  0.0 566.4 jit_solution(3616751156249973611)
XLA Ops:
  2.1 2.8 convolution_convert_fusion
  4.9 6.1 %reshape.369 = bf16[4,2,2,2,128,384]{5,1,0,4,3,2:T(2,128)(2,1)S(1)} reshape(bf16[8,2,2,128,384]{4,0,3,2,1:T(8,128)(2,1)} %convolution_convert_fusion) | data formatting | bytes 6291456 | tf_op jit(solution)/shard_map/reshape | solution.py:64
  11.0 4.7 copy.238
  15.7 4.4 all-to-all-start.1
  20.1 4.4 convolution_convert_fusion.1
  24.5 7.3 %reshape.367 = bf16[4,2,2,2,128,384]{5,1,0,4,3,2:T(2,128)(2,1)} reshape(bf16[8,2,2,128,384]{4,0,3,2,1:T(8,128)(2,1)} %convolution_convert_fusion.1) | data formatting | bytes 6291456 | tf_op jit(solution)/shard_map/reshape | solution.py:64
  31.7 6.4 %copy.233 = bf16[4,2,2,2,128,384]{5,1,4,3,2,0:T(2,128)(2,1)} copy(bf16[4,2,2,2,128,384]{5,1,0,4,3,2:T(2,128)(2,1)} %reshape.367) | data formatting | bytes 6291456 | tf_op jit(solution)/shard_map/reshape | solution.py:64
  38.2 19.5 %all-to-all-done.1 = bf16[4,2,2,2,128,384]{5,1,4,3,2,0:T(2,128)(2,1)S(1)} async-done(((bf16[4,2,2,2,128,384]{5,1,4,3,2,0:T(2,128)(2,1)}), bf16[4,2,2,2,128,384]{5,1,4,3,2,0:T(2,128)(2,1)S(1)}, u32[]{:S(2)}, u32[]{:S(2)}) %all-to-all-start.1) | async-done | bytes 3145760 | tf_op jit(solution)/shard_map/all_to_all | solution.py:65
  57.6 5.1 all-to-all-start
  63.0 3.9 copy.239
  66.9 7.6 %reshape.370 = bf16[8,2,2,128,384]{4,0,3,2,1:T(8,128)(2,1)} reshape(bf16[4,2,2,2,128,384]{5,1,0,4,3,2:T(2,128)(2,1)} %copy.239) | data formatting | bytes 6291456 | tf_op jit(solution)/shard_map/reshape | solution.py:66
  74.5 2.9 fusion.20
  77.4 1.4 copy.258
  78.9 20.6 %all-to-all-done = bf16[4,2,2,2,128,384]{5,1,4,3,2,0:T(2,128)(2,1)} async-done(((bf16[4,2,2,2,128,384]{5,1,4,3,2,0:T(2,128)(2,1)}), bf16[4,2,2,2,128,384]{5,1,4,3,2,0:T(2,128)(2,1)}, u32[]{:S(2)}, u32[]{:S(2)}) %all-to-all-start) | async-done | bytes 3145760 | tf_op jit(solution)/shard_map/all_to_all | solution.py:65
  99.5 5.7 %copy.234 = bf16[4,2,2,2,128,384]{5,1,0,4,3,2:T(2,128)(2,1)} copy(bf16[4,2,2,2,128,384]{5,1,4,3,2,0:T(2,128)(2,1)} %all-to-all-done) | data formatting | bytes 6291456 | tf_op jit(solution)/shard_map/all_to_all | solution.py:65
  105.2 7.6 %reshape.368 = bf16[8,2,2,128,384]{4,0,3,2,1:T(8,128)(2,1)} reshape(bf16[4,2,2,2,128,384]{5,1,0,4,3,2:T(2,128)(2,1)} %copy.234) | data formatting | bytes 6291456 | tf_op jit(solution)/shard_map/reshape | solution.py:66
  112.7 2.9 fusion.22
  116.1 23.0 %collective-permute-done = bf16[4,2,2,128,384]{4,3,2,1,0:T(8,128)(2,1)S(1)} collective-permute-done((bf16[4,2,2,128,384]{4,3,2,1,0:T(8,128)(2,1)S(1)}, bf16[4,2,2,128,384]{4,3,2,1,0:T(8,128)(2,1)S(1)}, u32[]{:S(2)}, u32[]{:S(2)}) %collective-permute-start) | collective-permute-done | bytes 1572896 | tf_op jit(solution)/shard_map/ppermute | solution.py:9
  140.6 40.1 %collective-permute-done.1 = bf16[4,2,2,128,384]{4,3,2,1,0:T(8,128)(2,1)S(1)} collective-permute-done((bf16[4,2,2,128,384]{4,3,2,1,0:T(8,128)(2,1)S(1)}, bf16[4,2,2,128,384]{4,3,2,1,0:T(8,128)(2,1)S(1)}, u32[]{:S(2)}, u32[]{:S(2)}) %collective-permute-start.1) | collective-permute-done | bytes 1572896 | tf_op jit(solution)/shard_map/ppermute | solution.py:9
  180.8 28.9 %collective-permute-done.6 = bf16[4,2,2,128,384]{4,3,2,1,0:T(8,128)(2,1)S(1)} collective-permute-done((bf16[4,2,2,128,384]{4,3,2,1,0:T(8,128)(2,1)S(1)}, bf16[4,2,2,128,384]{4,3,2,1,0:T(8,128)(2,1)S(1)}, u32[]{:S(2)}, u32[]{:S(2)}) %collective-permute-start.6) | collective-permute-done | bytes 1572896 | tf_op jit(solution)/shard_map/ppermute | solution.py:9
  210.5 3.1 collective-permute-start.7
  213.5 37.6 %collective-permute-done.2 = bf16[4,2,2,128,384]{4,3,2,1,0:T(8,128)(2,1)S(1)} collective-permute-done((bf16[4,2,2,128,384]{4,3,2,1,0:T(8,128)(2,1)S(1)}, bf16[4,2,2,128,384]{4,3,2,1,0:T(8,128)(2,1)S(1)}, u32[]{:S(2)}, u32[]{:S(2)}) %collective-permute-start.2) | collective-permute-done | bytes 1572896 | tf_op jit(solution)/shard_map/ppermute | solution.py:9
  251.1 28.4 %collective-permute-done.7 = bf16[4,2,2,128,384]{4,3,2,1,0:T(8,128)(2,1)S(1)} collective-permute-done((bf16[4,2,2,128,384]{4,3,2,1,0:T(8,128)(2,1)S(1)}, bf16[4,2,2,128,384]{4,3,2,1,0:T(8,128)(2,1)S(1)}, u32[]{:S(2)}, u32[]{:S(2)}) %collective-permute-start.7) | collective-permute-done | bytes 1572896 | tf_op jit(solution)/shard_map/ppermute | solution.py:9
  280.0 1.5 collective-permute-start.8
  281.6 37.0 %collective-permute-done.3 = bf16[4,2,2,128,384]{4,3,2,1,0:T(8,128)(2,1)S(1)} collective-permute-done((bf16[4,2,2,128,384]{4,3,2,1,0:T(8,128)(2,1)S(1)}, bf16[4,2,2,128,384]{4,3,2,1,0:T(8,128)(2,1)S(1)}, u32[]{:S(2)}, u32[]{:S(2)}) %collective-permute-start.3) | collective-permute-done | bytes 1572896 | tf_op jit(solution)/shard_map/ppermute | solution.py:9
  318.6 27.9 %collective-permute-done.8 = bf16[4,2,2,128,384]{4,3,2,1,0:T(8,128)(2,1)S(1)} collective-permute-done((bf16[4,2,2,128,384]{4,3,2,1,0:T(8,128)(2,1)S(1)}, bf16[4,2,2,128,384]{4,3,2,1,0:T(8,128)(2,1)S(1)}, u32[]{:S(2)}, u32[]{:S(2)}) %collective-permute-start.8) | collective-permute-done | bytes 1572896 | tf_op jit(solution)/shard_map/ppermute | solution.py:9
  346.4 1.6 broadcast_select_fusion.7
  349.0 2.5 collective-permute-start.9
  352.5 34.4 %collective-permute-done.4 = bf16[4,2,2,128,384]{4,3,2,1,0:T(8,128)(2,1)} collective-permute-done((bf16[4,2,2,128,384]{4,3,2,1,0:T(8,128)(2,1)S(1)}, bf16[4,2,2,128,384]{4,3,2,1,0:T(8,128)(2,1)}, u32[]{:S(2)}, u32[]{:S(2)}) %collective-permute-start.4) | collective-permute-done | bytes 1572896 | tf_op jit(solution)/shard_map/ppermute | solution.py:9
  386.9 27.3 %collective-permute-done.9 = bf16[4,2,2,128,384]{4,3,2,1,0:T(8,128)(2,1)} collective-permute-done((bf16[4,2,2,128,384]{4,3,2,1,0:T(8,128)(2,1)}, bf16[4,2,2,128,384]{4,3,2,1,0:T(8,128)(2,1)}, u32[]{:S(2)}, u32[]{:S(2)}) %collective-permute-start.9) | collective-permute-done | bytes 1572896 | tf_op jit(solution)/shard_map/ppermute | solution.py:9
  414.2 3.3 select_multiply_fusion.1
  417.5 1.7 fusion.12
  419.2 5.1 collective-permute-start.11
  426.1 12.4 %collective-permute-done.10 = bf16[4,3,1,128,384]{4,3,2,1,0:T(8,128)(2,1)} collective-permute-done((bf16[4,3,1,128,384]{4,3,2,1,0:T(8,128)(2,1)}, bf16[4,3,1,128,384]{4,3,2,1,0:T(8,128)(2,1)}, u32[]{:S(2)}, u32[]{:S(2)}) %collective-permute-start.10) | collective-permute-done | bytes 1179680 | tf_op jit(solution)/shard_map/ppermute | solution.py:19
  438.5 2.3 maximum_multiply_fusion
  441.8 3.8 pad_slice_fusion.22
  445.6 3.6 pad_slice_fusion.23
  460.7 1.1 constant_dynamic-update-slice_fusion.15
  463.8 1.1 constant_dynamic-update-slice_fusion.12
  477.3 15.3 %multiply_reduce_fusion = (f32[1024]{0:T(1024)S(1)}, f32[1024,384]{1,0:T(8,128)S(1)}) fusion(f32[384]{0:T(512)S(1)} %copy-done.9, bf16[1024,10368]{1,0:T(8,128)(2,1)} %constant_dynamic-update-slice_fusion, bf16[10368,384]{1,0:T(8,128)(2,1)S(1)} %bitcast.160), kind=kOutput, calls=%fused_computation.27 | convolution fusion | flops 8154905600 | bytes 30774784 | tf_op jit(solution)/shard_map/dot_general | solution.py:51
  493.7 5.2 collective-permute-start.13
  499.0 1.3 pad_maximum_fusion
  500.3 1.3 pad_maximum_fusion.1
  501.7 10.7 %collective-permute-done.12 = bf16[4,3,1,128,384]{4,3,2,1,0:T(8,128)(2,1)S(1)} collective-permute-done((bf16[4,3,1,128,384]{4,3,2,1,0:T(8,128)(2,1)S(1)}, bf16[4,3,1,128,384]{4,3,2,1,0:T(8,128)(2,1)S(1)}, u32[]{:S(2)}, u32[]{:S(2)}) %collective-permute-start.12) | collective-permute-done | bytes 1179680 | tf_op jit(solution)/shard_map/ppermute | solution.py:19
  514.5 3.8 pad_slice_fusion.4
  518.3 3.6 pad_slice_fusion.5
  536.6 1.1 constant_dynamic-update-slice_fusion.39
  550.0 14.9 %convolution_add_fusion = f32[1024,384]{1,0:T(8,128)S(1)} fusion(bf16[1024,10368]{1,0:T(8,128)(2,1)} %constant_dynamic-update-slice_fusion.27, bf16[10368,384]{1,0:T(8,128)(2,1)S(1)} %bitcast.163, f32[384]{0:T(512)S(1)} %copy-done.10), kind=kOutput, calls=%fused_computation.38 | convolution fusion | flops 8154120192 | bytes 30770688 | tf_op jit(solution)/shard_map/dot_general | solution.py:51
  (132 shorter events, 66.8 us)
Async XLA Ops:
  0.6 1.5 copy-start
  15.7 41.9 %all-to-all-start.1 = ((bf16[4,2,2,2,128,384]{5,1,4,3,2,0:T(2,128)(2,1)}), bf16[4,2,2,2,128,384]{5,1,4,3,2,0:T(2,128)(2,1)S(1)}, u32[]{:S(2)}, u32[]{:S(2)}) async-start(bf16[4,2,2,2,128,384]{5,1,4,3,2,0:T(2,128)(2,1)} %copy.238), calls=%async_computation.1 | async-start | bytes 6291456 | tf_op jit(solution)/shard_map/all_to_all | solution.py:65
  57.6 41.8 %all-to-all-start = ((bf16[4,2,2,2,128,384]{5,1,4,3,2,0:T(2,128)(2,1)}), bf16[4,2,2,2,128,384]{5,1,4,3,2,0:T(2,128)(2,1)}, u32[]{:S(2)}, u32[]{:S(2)}) async-start(bf16[4,2,2,2,128,384]{5,1,4,3,2,0:T(2,128)(2,1)} %copy.233), calls=%async_computation | async-start | bytes 6291456 | tf_op jit(solution)/shard_map/all_to_all | solution.py:65
  78.8 37.2 %collective-permute-start.5 = (bf16[4,2,2,128,384]{4,3,2,1,0:T(8,128)(2,1)}, bf16[4,2,2,128,384]{4,3,2,1,0:T(8,128)(2,1)S(1)}, u32[]{:S(2)}, u32[]{:S(2)}) collective-permute-start(bf16[4,2,2,128,384]{4,3,2,1,0:T(8,128)(2,1)} %copy.258), channel_id=1, source_target_pairs={{0,1},{1,2},{2,3},{3,4},{4,5},{5,6},{6,7},{7,8},{8,9},{9,10},{10,1... | collective-permute-start | bytes 4718600 | tf_op jit(solution)/shard_map/ppermute | solution.py:9
  115.9 23.2 %collective-permute-start = (bf16[4,2,2,128,384]{4,3,2,1,0:T(8,128)(2,1)S(1)}, bf16[4,2,2,128,384]{4,3,2,1,0:T(8,128)(2,1)S(1)}, u32[]{:S(2)}, u32[]{:S(2)}) collective-permute-start(bf16[4,2,2,128,384]{4,3,2,1,0:T(8,128)(2,1)S(1)} %copy.259), channel_id=1, source_target_pairs={{0,1},{1,2},{2,3},{3,4},{4,5},{5,6},{6,7},{7,8},{8,9},{9,10},{10,1... | collective-permute-start | bytes 4718600 | tf_op jit(solution)/shard_map/ppermute | solution.py:9
  139.9 40.9 %collective-permute-start.1 = (bf16[4,2,2,128,384]{4,3,2,1,0:T(8,128)(2,1)S(1)}, bf16[4,2,2,128,384]{4,3,2,1,0:T(8,128)(2,1)S(1)}, u32[]{:S(2)}, u32[]{:S(2)}) collective-permute-start(bf16[4,2,2,128,384]{4,3,2,1,0:T(8,128)(2,1)S(1)} %get-tuple-element.112), channel_id=1, source_target_pairs={{0,2},{1,3},{2,4},{3,5},{4,6},{5,7},{6,8},{7,9},{8,10},{9,11},{10,... | collective-permute-start | bytes 4718600 | tf_op jit(solution)/shard_map/ppermute | solution.py:9
  140.1 69.5 %collective-permute-start.6 = (bf16[4,2,2,128,384]{4,3,2,1,0:T(8,128)(2,1)S(1)}, bf16[4,2,2,128,384]{4,3,2,1,0:T(8,128)(2,1)S(1)}, u32[]{:S(2)}, u32[]{:S(2)}) collective-permute-start(bf16[4,2,2,128,384]{4,3,2,1,0:T(8,128)(2,1)S(1)} %get-tuple-element.113), channel_id=1, source_target_pairs={{0,2},{1,3},{2,4},{3,5},{4,6},{5,7},{6,8},{7,9},{8,10},{9,11},{10,... | collective-permute-start | bytes 4718600 | tf_op jit(solution)/shard_map/ppermute | solution.py:9
  210.1 41.0 %collective-permute-start.2 = (bf16[4,2,2,128,384]{4,3,2,1,0:T(8,128)(2,1)S(1)}, bf16[4,2,2,128,384]{4,3,2,1,0:T(8,128)(2,1)S(1)}, u32[]{:S(2)}, u32[]{:S(2)}) collective-permute-start(bf16[4,2,2,128,384]{4,3,2,1,0:T(8,128)(2,1)S(1)} %get-tuple-element.110), channel_id=1, source_target_pairs={{0,4},{1,5},{2,6},{3,7},{4,8},{5,9},{6,10},{7,11},{8,12},{9,13},{1... | collective-permute-start | bytes 4718600 | tf_op jit(solution)/shard_map/ppermute | solution.py:9
  210.5 69.1 %collective-permute-start.7 = (bf16[4,2,2,128,384]{4,3,2,1,0:T(8,128)(2,1)S(1)}, bf16[4,2,2,128,384]{4,3,2,1,0:T(8,128)(2,1)S(1)}, u32[]{:S(2)}, u32[]{:S(2)}) collective-permute-start(bf16[4,2,2,128,384]{4,3,2,1,0:T(8,128)(2,1)S(1)} %get-tuple-element.111), channel_id=1, source_target_pairs={{0,4},{1,5},{2,6},{3,7},{4,8},{5,9},{6,10},{7,11},{8,12},{9,13},{1... | collective-permute-start | bytes 4718600 | tf_op jit(solution)/shard_map/ppermute | solution.py:9
  279.9 71.8 %copy-start.4 = (bf16[4,2,128,384]{3,2,1,0:T(8,128)(2,1)S(1)}, bf16[4,2,128,384]{3,2,1,0:T(8,128)(2,1)}, u32[]{:S(2)}) copy-start(bf16[4,2,128,384]{3,2,1,0:T(8,128)(2,1)} %param.18) | copy-start | bytes 2359300
  280.0 38.6 %collective-permute-start.3 = (bf16[4,2,2,128,384]{4,3,2,1,0:T(8,128)(2,1)S(1)}, bf16[4,2,2,128,384]{4,3,2,1,0:T(8,128)(2,1)S(1)}, u32[]{:S(2)}, u32[]{:S(2)}) collective-permute-start(bf16[4,2,2,128,384]{4,3,2,1,0:T(8,128)(2,1)S(1)} %get-tuple-element.108), channel_id=1, source_target_pairs={{0,8},{1,9},{2,10},{3,11},{4,12},{5,13},{6,14},{7,15},{8,16},{9,17... | collective-permute-start | bytes 4718600 | tf_op jit(solution)/shard_map/ppermute | solution.py:9
  280.0 66.4 %collective-permute-start.8 = (bf16[4,2,2,128,384]{4,3,2,1,0:T(8,128)(2,1)S(1)}, bf16[4,2,2,128,384]{4,3,2,1,0:T(8,128)(2,1)S(1)}, u32[]{:S(2)}, u32[]{:S(2)}) collective-permute-start(bf16[4,2,2,128,384]{4,3,2,1,0:T(8,128)(2,1)S(1)} %get-tuple-element.109), channel_id=1, source_target_pairs={{0,8},{1,9},{2,10},{3,11},{4,12},{5,13},{6,14},{7,15},{8,16},{9,17... | collective-permute-start | bytes 4718600 | tf_op jit(solution)/shard_map/ppermute | solution.py:9
  346.4 5.6 copy-start.7
  348.0 66.2 %copy-start.6 = (bf16[4,2,2,128,384]{4,3,2,1,0:T(8,128)(2,1)}, bf16[4,2,2,128,384]{4,3,2,1,0:T(8,128)(2,1)S(1)}, u32[]{:S(2)}) copy-start(bf16[4,2,2,128,384]{4,3,2,1,0:T(8,128)(2,1)S(1)} %get-tuple-element.106) | copy-start | bytes 4718596
  348.0 38.9 %collective-permute-start.4 = (bf16[4,2,2,128,384]{4,3,2,1,0:T(8,128)(2,1)S(1)}, bf16[4,2,2,128,384]{4,3,2,1,0:T(8,128)(2,1)}, u32[]{:S(2)}, u32[]{:S(2)}) collective-permute-start(bf16[4,2,2,128,384]{4,3,2,1,0:T(8,128)(2,1)S(1)} %get-tuple-element.106), channel_id=1, source_target_pairs={{0,16},{1,17},{2,18},{3,19},{4,20},{5,21},{6,22},{7,23},{8,24},{9,... | collective-permute-start | bytes 4718600 | tf_op jit(solution)/shard_map/ppermute | solution.py:9
  349.0 65.2 %collective-permute-start.9 = (bf16[4,2,2,128,384]{4,3,2,1,0:T(8,128)(2,1)}, bf16[4,2,2,128,384]{4,3,2,1,0:T(8,128)(2,1)}, u32[]{:S(2)}, u32[]{:S(2)}) collective-permute-start(bf16[4,2,2,128,384]{4,3,2,1,0:T(8,128)(2,1)} %get-tuple-element.107), channel_id=1, source_target_pairs={{0,16},{1,17},{2,18},{3,19},{4,20},{5,21},{6,22},{7,23},{8,24},{9,... | collective-permute-start | bytes 4718600 | tf_op jit(solution)/shard_map/ppermute | solution.py:9
  352.5 66.7 %copy-start.2 = (bf16[4,1,2,128,384]{4,3,2,1,0:T(8,128)(2,1)}, bf16[4,1,2,128,384]{4,3,2,1,0:T(8,128)(2,1)S(1)}, u32[]{:S(2)}) copy-start(bf16[4,1,2,128,384]{4,3,2,1,0:T(8,128)(2,1)S(1)} %fusion.13) | copy-start | bytes 2359300
  419.2 19.3 %collective-permute-start.10 = (bf16[4,3,1,128,384]{4,3,2,1,0:T(8,128)(2,1)}, bf16[4,3,1,128,384]{4,3,2,1,0:T(8,128)(2,1)}, u32[]{:S(2)}, u32[]{:S(2)}) collective-permute-start(bf16[4,3,1,128,384]{4,3,2,1,0:T(8,128)(2,1)} %get-tuple-element.102), channel_id=1, source_target_pairs={{0,1},{1,2},{2,3},{3,4},{4,5},{5,6},{6,7},{7,8},{8,9},{9,10},{10,1... | collective-permute-start | bytes 3538952 | tf_op jit(solution)/shard_map/ppermute | solution.py:19
  419.2 19.3 %collective-permute-start.11 = (bf16[4,3,1,128,384]{4,3,2,1,0:T(8,128)(2,1)}, bf16[4,3,1,128,384]{4,3,2,1,0:T(8,128)(2,1)}, u32[]{:S(2)}, u32[]{:S(2)}) collective-permute-start(bf16[4,3,1,128,384]{4,3,2,1,0:T(8,128)(2,1)} %get-tuple-element.103), channel_id=1, source_target_pairs={{1,0},{2,1},{3,2},{4,3},{5,4},{6,5},{7,6},{8,7},{9,8},{10,9},{11,1... | collective-permute-start | bytes 3538952 | tf_op jit(solution)/shard_map/ppermute | solution.py:21
  466.0 11.3 %slice-start = ((s8[7962624]{0:T(1024)(128)(4,1)}), s8[3768320]{0:T(1024)(128)(4,1)S(1)}, s32[]{:S(2)}) async-start(s8[7962624]{0:T(1024)(128)(4,1)} %bitcast.158), calls=%async_computation.2 | async-start | bytes 7536640
  471.1 6.1 %copy-start.9 = (f32[384]{0:T(512)S(1)}, f32[384]{0:T(512)}, u32[]{:S(2)}) copy-start(f32[384]{0:T(512)} %param.25) | copy-start | bytes 4612
  471.1 6.1 %slice-start.1 = ((s8[7962624]{0:T(1024)(128)(4,1)}), s8[4194304]{0:T(1024)(128)(4,1)S(1)}, s32[]{:S(2)}) async-start(s8[7962624]{0:T(1024)(128)(4,1)} %bitcast.158), calls=%async_computation.3 | async-start | bytes 8388608
  477.2 15.3 %copy-start.8 = (f32[384]{0:T(512)S(1)}, f32[384]{0:T(512)}, u32[]{:S(2)}) copy-start(f32[384]{0:T(512)} %param.22) | copy-start | bytes 4612
  492.6 6.4 %copy-start.3 = (bf16[4,1,2,128,384]{4,3,2,1,0:T(8,128)(2,1)S(1)}, bf16[4,1,2,128,384]{4,3,2,1,0:T(8,128)(2,1)}, u32[]{:S(2)}) copy-start(bf16[4,1,2,128,384]{4,3,2,1,0:T(8,128)(2,1)} %copy-done.2) | copy-start | bytes 2359300
  493.4 19.0 %collective-permute-start.12 = (bf16[4,3,1,128,384]{4,3,2,1,0:T(8,128)(2,1)S(1)}, bf16[4,3,1,128,384]{4,3,2,1,0:T(8,128)(2,1)S(1)}, u32[]{:S(2)}, u32[]{:S(2)}) collective-permute-start(bf16[4,3,1,128,384]{4,3,2,1,0:T(8,128)(2,1)S(1)} %get-tuple-element.100), channel_id=1, source_target_pairs={{0,1},{1,2},{2,3},{3,4},{4,5},{5,6},{6,7},{7,8},{8,9},{9,10},{10,1... | collective-permute-start | bytes 3538952 | tf_op jit(solution)/shard_map/ppermute | solution.py:19
  493.7 18.9 %collective-permute-start.13 = (bf16[4,3,1,128,384]{4,3,2,1,0:T(8,128)(2,1)S(1)}, bf16[4,3,1,128,384]{4,3,2,1,0:T(8,128)(2,1)S(1)}, u32[]{:S(2)}, u32[]{:S(2)}) collective-permute-start(bf16[4,3,1,128,384]{4,3,2,1,0:T(8,128)(2,1)S(1)} %get-tuple-element.101), channel_id=1, source_target_pairs={{1,0},{2,1},{3,2},{4,3},{5,4},{6,5},{7,6},{8,7},{9,8},{10,9},{11,1... | collective-permute-start | bytes 3538952 | tf_op jit(solution)/shard_map/ppermute | solution.py:21
  537.7 12.3 %slice-start.2 = ((s8[7962624]{0:T(1024)(128)(4,1)}), s8[3768320]{0:T(1024)(128)(4,1)S(1)}, s32[]{:S(2)}) async-start(s8[7962624]{0:T(1024)(128)(4,1)} %bitcast.161), calls=%async_computation.4 | async-start | bytes 7536640
  543.9 6.1 %copy-start.10 = (f32[384]{0:T(512)S(1)}, f32[384]{0:T(512)}, u32[]{:S(2)}) copy-start(f32[384]{0:T(512)} %param.26) | copy-start | bytes 4612
  543.9 6.1 %slice-start.3 = ((s8[7962624]{0:T(1024)(128)(4,1)}), s8[4194304]{0:T(1024)(128)(4,1)S(1)}, s32[]{:S(2)}) async-start(s8[7962624]{0:T(1024)(128)(4,1)} %bitcast.161), calls=%async_computation.5 | async-start | bytes 8388608
  550.0 14.9 %copy-start.5 = (bf16[4,2,128,384]{3,2,1,0:T(8,128)(2,1)S(1)}, bf16[4,2,128,384]{3,2,1,0:T(8,128)(2,1)}, u32[]{:S(2)}) copy-start(bf16[4,2,128,384]{3,2,1,0:T(8,128)(2,1)} %param.18) | copy-start | bytes 2359300
  550.0 16.0 %copy-start.1 = (bf16[4,2,2,128,384]{4,3,2,1,0:T(8,128)(2,1)S(1)}, bf16[4,2,2,128,384]{4,3,2,1,0:T(8,128)(2,1)}, u32[]{:S(2)}) copy-start(bf16[4,2,2,128,384]{4,3,2,1,0:T(8,128)(2,1)} %param.19) | copy-start | bytes 4718596
where the time goes:
time: 574 us; the launch traced here: 566 us
  waiting for transfers between devices  348 us (61%)
  local copies, waits for them, and re-layouts  125 us (22%)
  matrix products  43.1 us (8%)
  starting transfers between devices  29.4 us (5%)
  other arithmetic  19.7 us (3%)
    ppermute x10, waiting for transfers between devices, shifted_2(): lax.ppermute(array, axis, [(i, (i + by) % size) for i in range(size)])  285 us
    unnamed x82, local copies, waits for them, and re-layouts  54.2 us
    all_to_all x2, waiting for transfers between devices, relocate(): lax.all_to_all(outgoing, 'stream', split_axis=0, concat_axis=0, tiled=True)  40.1 us
    dot_general x2, matrix products, convolve(): jnp.dot(patches, weight.reshape(27 * channels, channels), preferred_eleme...  30.1 us
    reshape x4, local copies, waits for them, and re-layouts, relocate(): outgoing = outgoing.reshape((n_groups, -1) + block.shape[1:])  24.5 us
    ppermute x2, waiting for transfers between devices, padded_2(): lax.ppermute(tail, axis, [(i, (i + 1) % count) for i in range(count)])  23.1 us
    slice x6, local copies, waits for them, and re-layouts, convolve(): widened[:, t_step, y_step:y_step + n_rows, x_step:x_step + n_cols, :]  16.8 us
    reshape x2, local copies, waits for them, and re-layouts, relocate(): arrived = arrived.reshape((-1,) + block.shape[1:])  15.1 us
  transfers between devices with their start and end apart: 16, of which 14 were waited for; matrix products, arithmetic and copies ran while one was open for 10% of the time, Pallas kernels for 0%

commit v1 on v0

v1 whole, which is shorter than its diff:
```python
import jax
import jax.numpy as jnp
from jax import lax
from jax.experimental import pallas as pl
from jax.experimental.pallas import tpu as pltpu
from jax.sharding import PartitionSpec as P

BOTH = ("stream", "tile")
CB = 8


def lookup(held_table, values):
    return jnp.sum(jnp.where(held_table, values[None, :], 0), axis=1)


def activate(values, gain):
    scaled = values * lax.rsqrt(jnp.mean(values * values, axis=-1, keepdims=True) + 1e-06)
    return jax.nn.silu(scaled * gain)


def pack(first, second):
    n_slots, n_frames, n_rows, n_cols, ch = first.shape
    blocks = n_cols // CB

    def body(a_ref, b_ref, o_ref):
        for k, ref in enumerate((a_ref, b_ref)):
            for f in range(n_frames):
                for r in range(n_rows):
                    o_ref[r, k, f, :, 0] = ref[0, f, r].reshape(blocks, CB, ch)

    spec = pl.BlockSpec((1, n_frames, n_rows, n_cols, ch), lambda s: (s, 0, 0, 0, 0))
    return pl.pallas_call(
        body,
        grid=(n_slots,),
        in_specs=[spec, spec],
        out_specs=pl.BlockSpec(
            (n_rows, 2, n_frames, blocks, 1, CB, ch), lambda s: (0, 0, 0, 0, s, 0, 0)
        ),
        out_shape=jax.ShapeDtypeStruct(
            (n_rows, 2, n_frames, blocks, n_slots, CB, ch), first.dtype
        ),
        compiler_params=pltpu.CompilerParams(vmem_limit_bytes=32 << 20),
    )(first, second)


def permute(held, source, rotation, keep):
    n_groups, n_tiles, n_slots, cols, ch = held.shape

    def body(source_ref, rotation_ref, keep_ref, i_ref, o_ref):
        n = pl.program_id(0)
        by = rotation_ref[n]

        @pl.when(keep_ref[n] != 0)
        def _():
            def step(t, _):
                at = lax.rem(t + n_tiles - by, n_tiles)
                o_ref[0, t, 0] = i_ref[0, at, 0]
                return 0

            lax.fori_loop(0, n_tiles, step, 0, unroll=8)

        @pl.when(keep_ref[n] == 0)
        def _():
            o_ref[...] = jnp.zeros_like(o_ref)

    block = (1, n_tiles, 1, cols, ch)
    return pl.pallas_call(
        body,
        grid_spec=pltpu.PrefetchScalarGridSpec(
            num_scalar_prefetch=3,
            grid=(n_groups * n_slots,),
            in_specs=[
                pl.BlockSpec(
                    block,
                    lambda n, s, r, k: (lax.div(s[n], n_slots), 0, lax.rem(s[n], n_slots), 0, 0),
                )
            ],
            out_specs=pl.BlockSpec(
                block, lambda n, s, r, k: (lax.div(n, n_slots), 0, lax.rem(n, n_slots), 0, 0)
            ),
        ),
        out_shape=jax.ShapeDtypeStruct(held.shape, held.dtype),
        compiler_params=pltpu.CompilerParams(vmem_limit_bytes=32 << 20),
    )(source, rotation, keep, held)


def convolve(padded, weight, bias_vec):
    n_slots = padded.shape[0]
    n_rows = padded.shape[2] - 2
    n_cols = padded.shape[3]
    channels = padded.shape[4]
    widened = jnp.pad(padded, ((0, 0), (0, 0), (0, 0), (1, 1), (0, 0)))
    pieces = [
        widened[:, t_step, y_step : y_step + n_rows, x_step : x_step + n_cols, :]
        for t_step in range(3)
        for y_step in range(3)
        for x_step in range(3)
    ]
    patches = jnp.concatenate(pieces, axis=-1).reshape(-1, 27 * channels)
    result = (
        jnp.dot(
            patches, weight.reshape(27 * channels, channels), preferred_element_type=jnp.float32
        )
        + bias_vec
    )
    return result.reshape(n_slots, n_rows, n_cols, channels)


def local(
    frame_in,
    cache_first,
    cache_second,
    gain_first,
    gain_second,
    conv_first,
    conv_second,
    bias_first,
    bias_second,
    old_slot,
    new_slot,
    old_shift,
    new_shift,
    frame_count,
):
    n_slots, n_rows, n_cols, ch = frame_in.shape
    n_groups = lax.axis_size("stream")
    n_tiles = lax.axis_size("tile")
    my_group = lax.axis_index("stream")
    my_tile = lax.axis_index("tile")
    n_flight = old_slot.shape[0]
    blocks = n_cols // CB
    slot_ids = jnp.arange(n_flight, dtype=jnp.int32)
    held_new = new_slot[None, :] == slot_ids[:, None]
    source = lookup(held_new, old_slot)
    shift_after = lookup(held_new, new_shift)
    rotation = (shift_after - lookup(held_new, old_shift)) % n_tiles
    frames_done = lookup(held_new, frame_count)
    my_piece = my_group * n_tiles + my_tile
    my_frame = (my_piece // blocks) % 2
    keep = (frames_done >= 2 - my_frame).astype(jnp.int32)
    start = my_group * n_slots
    my_number = lax.dynamic_slice_in_dim((my_tile - shift_after) % n_tiles, start, n_slots)

    sent = pack(cache_first, cache_second).reshape(n_groups * n_tiles, n_slots, CB, ch)
    held = lax.all_to_all(sent, BOTH, 0, 0, tiled=True)
    moved = permute(held.reshape(n_groups, n_tiles, n_slots, CB, ch), source, rotation, keep)
    got = lax.all_to_all(
        moved.reshape(n_groups * n_tiles, n_slots, CB, ch), BOTH, 0, 0, tiled=True
    )
    got = got.reshape(n_rows, 2, 2, blocks, n_slots, CB, ch)

    down = [(i, (i + 1) % n_tiles) for i in range(n_tiles)]
    up = [((i + 1) % n_tiles, i) for i in range(n_tiles)]
    above = lax.ppermute(got[n_rows - 1], "tile", down)
    below = lax.ppermute(got[0], "tile", up)
    rows = jnp.concatenate([above[None], got, below[None]], axis=0)
    rows = rows.transpose(1, 4, 2, 0, 3, 5, 6).reshape(
        2, n_slots, 2, n_rows + 2, n_cols, ch
    )
    border = jnp.ones((n_slots, n_rows + 2), jnp.bfloat16)
    border = border.at[:, 0].set((my_number != 0).astype(jnp.bfloat16))
    border = border.at[:, -1].set((my_number != n_tiles - 1).astype(jnp.bfloat16))
    border = border[:, None, :, None, None]

    def conv_layer(kept, activation, weight, bias_vec):
        head = lax.ppermute(activation[:, -1:], "tile", down)
        tail = lax.ppermute(activation[:, :1], "tile", up)
        act = jnp.concatenate([head, activation, tail], axis=1)
        padded = jnp.concatenate([kept, act[:, None]], axis=1)
        return convolve(padded * border, weight, bias_vec)

    act_first = activate(frame_in.astype(jnp.float32), gain_first).astype(jnp.bfloat16)
    hidden = conv_layer(rows[0], act_first, conv_first, bias_first)
    act_second = activate(hidden, gain_second).astype(jnp.bfloat16)
    second_out = conv_layer(rows[1], act_second, conv_second, bias_second)
    mixed_frame = (second_out + frame_in.astype(jnp.float32)).astype(jnp.bfloat16)
    next_first = jnp.stack([rows[0, :, 1, 1:-1], act_first], axis=1)
    next_second = jnp.stack([rows[1, :, 1, 1:-1], act_second], axis=1)
    return (mixed_frame, next_first, next_second)


def solution(mesh):
    frame = P("stream", "tile", None, None)
    cache = P("stream", None, "tile", None, None)
    return jax.shard_map(
        local,
        mesh=mesh,
        in_specs=(frame, cache, cache) + (P(),) * 11,
        out_specs=(frame, cache, cache),
        check_vma=False,
    )
```

time: 574 us -> 262 us (0.46); the launches traced: 566 us -> 262 us
  waiting for transfers between devices: 348 us -> 52.9 us
  blocking collectives: 0 us -> 46.2 us
  local copies, waits for them, and re-layouts: 125 us -> 82.7 us
  matrix products: 43.1 us -> 30.3 us
    ppermute x14 -> x6, waiting for transfers between devices: 308 us -> 11.3 us  [the longest x2 9.95 us: conv_layer(): head = lax.ppermute(activation[:, -1:], 'tile', down)]
    all_to_all x0 -> x1, blocking collectives: none -> 46.2 us  [local(): lax.all_to_all(moved.reshape(n_groups * n_tiles, n_slots, CB, ch), BOTH,...]
    reshape x6 -> x0, local copies, waits for them, and re-layouts: 39.6 us -> none  [the longest x4 24.5 us: relocate(): outgoing = outgoing.reshape((n_groups, -1) + block.shape[1:])]
    dot_general x4 -> x0, matrix products: 13 us -> none  [the longest x2 7.16 us: relocate(): jnp.einsum('as,sfrwc->afrwc', send_pick, block, preferred_element_type=jn...]
    all_to_all x2 -> x0, local copies, waits for them, and re-layouts: 9.56 us -> none  [relocate(): lax.all_to_all(outgoing, 'stream', split_axis=0, concat_axis=0, tiled=True)]
    ppermute x14 -> x6, starting transfers between devices: 19.9 us -> 15.5 us  [the longest x2 10.4 us: conv_layer(): tail = lax.ppermute(activation[:, :1], 'tile', up)]
    unnamed x82 -> x91, local copies, waits for them, and re-layouts: 54.2 us -> 58.2 us
    all_to_all x2 -> x1, waiting for transfers between devices: 40.1 us -> 41.6 us  [local(): held = lax.all_to_all(sent, BOTH, 0, 0, tiled=True)]
  transfers between devices with their start and end apart: 16 -> 7, of which waited for: 14 -> 4; matrix products, arithmetic and copies ran while one was open for 10% -> 5% of each run, Pallas kernels for 0% -> 0%
where the time goes in v1:
time: 262 us
  local copies, waits for them, and re-layouts  82.7 us (32%)
  waiting for transfers between devices  52.9 us (20%)
  blocking collectives  46.2 us (18%)
  matrix products  30.3 us (12%)
  starting transfers between devices  26.6 us (10%)
  other arithmetic  17 us (6%)
  Pallas kernels  5.03 us (2%)
    unnamed x91, local copies, waits for them, and re-layouts  58.2 us
    all_to_all x1, blocking collectives, local(): lax.all_to_all(moved.reshape(n_groups * n_tiles, n_slots, CB, ch), BOTH,...  46.2 us
    all_to_all x1, waiting for transfers between devices, local(): held = lax.all_to_all(sent, BOTH, 0, 0, tiled=True)  41.6 us
    dot_general x2, matrix products, convolve(): jnp.dot(patches, weight.reshape(27 * channels, channels), preferred_eleme...  30.3 us
    slice x6, local copies, waits for them, and re-layouts, convolve(): widened[:, t_step, y_step:y_step + n_rows, x_step:x_step + n_cols, :]  16.4 us
    all_to_all x1, starting transfers between devices, local(): held = lax.all_to_all(sent, BOTH, 0, 0, tiled=True)  11.1 us
    ppermute x2, starting transfers between devices, conv_layer(): tail = lax.ppermute(activation[:, :1], 'tile', up)  10.4 us
    ppermute x2, waiting for transfers between devices, conv_layer(): head = lax.ppermute(activation[:, -1:], 'tile', down)  9.95 us
  transfers between devices with their start and end apart: 7, of which 4 were waited for; matrix products, arithmetic and copies ran while one was open for 5% of the time, Pallas kernels for 0%

profile of v1, /device:TPU:0, one launch (start us, length us, event | category | flops | bytes accessed | tf_op | source)
XLA Modules:
  0.0 261.9 jit_solution(7952332870753443093)
XLA Ops:
  0.6 1.4 copy-done
  2.0 1.4 copy-done.1
  3.5 2.3 shard_map.157
  5.8 11.1 %all-to-all-start = ((bf16[128,4,8,384]{3,2,1,0:T(8,128)(2,1)}), bf16[128,4,8,384]{3,2,1,0:T(8,128)(2,1)S(1)}, u32[]{:S(2)}, u32[]{:S(2)}) async-start(bf16[128,4,8,384]{3,2,1,0:T(8,128)(2,1)} %bitcast), calls=%async_computation | async-start | bytes 6291456 | tf_op jit(solution)/shard_map/all_to_all | solution.py:145
  17.2 41.6 %all-to-all-done = bf16[128,4,8,384]{3,2,1,0:T(8,128)(2,1)S(1)} async-done(((bf16[128,4,8,384]{3,2,1,0:T(8,128)(2,1)}), bf16[128,4,8,384]{3,2,1,0:T(8,128)(2,1)S(1)}, u32[]{:S(2)}, u32[]{:S(2)}) %all-to-all-start) | async-done | bytes 3145760 | tf_op jit(solution)/shard_map/all_to_all | solution.py:145
  58.8 2.7 %shard_map.158 = bf16[4,32,4,8,384]{4,3,2,1,0:T(8,128)(2,1)S(1)} custom-call(s32[16]{0:T(128)S(1)} %get-tuple-element.36.source_ref, s32[16]{0:T(128)S(1)} %get-tuple-element.104.rotation_ref, s32[16]{0:T(128)S(1)} %compare_convert_fusion.2.keep_ref, bf16[4,32,4,8,384]{4,3,2,1,0:T(8,128)(2,1)S(1)} %bitcast.97), custom_call_target="tpu_custom_call" | custom-call | tf_op jit(solution)/shard_map/pallas_call | solution.py:67
  61.5 46.2 %all_to_all.10 = bf16[128,4,8,384]{3,2,1,0:T(8,128)(2,1)S(1)} all-to-all(bf16[128,4,8,384]{3,2,1,0:T(8,128)(2,1)S(1)} %bitcast.98), channel_id=1, replica_groups=mesh['stream'=4,'tile'=32] {'stream','tile'}, dimensions={0} | all-to-all | bytes 6291456 | tf_op jit(solution)/shard_map/all_to_all | solution.py:147
  108.1 1.4 copy.23
  109.5 1.4 copy.24
  110.9 5.1 %collective-permute-start.1 = (bf16[2,2,16,4,8,384]{5,4,2,3,1,0:T(8,128)(2,1)}, bf16[2,2,16,4,8,384]{5,4,2,3,1,0:T(8,128)(2,1)}, u32[]{:S(2)}, u32[]{:S(2)}) collective-permute-start(bf16[2,2,16,4,8,384]{5,4,2,3,1,0:T(8,128)(2,1)} %copy.24), channel_id=1, source_target_pairs={{1,0},{2,1},{3,2},{4,3},{5,4},{6,5},{7,6},{8,7},{9,8},{10,9},{11,1... | collective-permute-start | bytes 4718600 | tf_op jit(solution)/shard_map/ppermute | solution.py:155
  118.6 5.1 %collective-permute-start.3 = (bf16[4,1,128,384]{3,2,1,0:T(8,128)(2,1)}, bf16[4,1,128,384]{3,2,1,0:T(8,128)(2,1)}, u32[]{:S(2)}, u32[]{:S(2)}) collective-permute-start(bf16[4,1,128,384]{3,2,1,0:T(8,128)(2,1)} %get-tuple-element.102), channel_id=1, source_target_pairs={{1,0},{2,1},{3,2},{4,3},{5,4},{6,5},{7,6},{8,7},{9,8},{10,9},{11,1... | collective-permute-start | bytes 1179656 | tf_op jit(solution)/shard_map/ppermute | solution.py:167
  126.6 2.6 fusion.24
  129.1 7.9 %collective-permute-done.2 = bf16[4,1,128,384]{3,2,1,0:T(8,128)(2,1)S(1)} collective-permute-done((bf16[4,1,128,384]{3,2,1,0:T(8,128)(2,1)}, bf16[4,1,128,384]{3,2,1,0:T(8,128)(2,1)S(1)}, u32[]{:S(2)}, u32[]{:S(2)}) %collective-permute-start.2) | collective-permute-done | bytes 393248 | tf_op jit(solution)/shard_map/ppermute | solution.py:166
  137.1 1.3 collective-permute-done.3
  138.4 1.5 maximum_bitcast_fusion
  139.9 4.8 %fusion = (bf16[2,4,2,4,128,384]{5,4,3,1,2,0:T(8,128)(2,1)S(1)}, bf16[2,4,2,4,16,8,384]{6,5,4,3,1,2,0:T(8,128)(2,1)S(1)}) fusion(bf16[1,2,2,16,4,8,384]{6,5,3,0,4,2,1:T(8,128)(2,1)} %bitcast.7, bf16[1,2,2,16,4,8,384]{6,5,3,0,4,2,1:T(8,128)(2,1)} %bitcast.4, bf16[2,2,2,16,4,8,384]{6,5,4,3,2,1,0:T(8,128)(2,1)S(1)} %bitcast.99), kind=kLoop, calls=%fused_computation.5 | loop fusion | flops 18874368 | bytes 18874368 | tf_op jit(solution)/shard_map/reshape | solution.py:157
  147.0 3.7 %pad_slice_fusion.18 = (bf16[4,1,2,128,384]{4,3,2,0,1:T(8,128)(2,1)S(1)}, bf16[4,1,2,128,384]{4,3,2,0,1:T(8,128)(2,1)S(1)}, bf16[4,1,2,128,384]{4,3,2,0,1:T(8,12...) fusion(bf16[4,3,4,128,384]{4,3,2,0,1:T(8,128)(2,1)S(1)} %maximu, ...), kind=kLoop, calls=%fused_computation.124 | loop fusion | bytes 13369344 | tf_op jit(solution)/shard_map/slice | solution.py:94
  150.8 3.6 %pad_slice_fusion.19 = (bf16[4,1,2,128,384]{4,3,2,0,1:T(8,128)(2,1)S(1)}, bf16[4,1,2,128,384]{4,3,2,0,1:T(8,128)(2,1)S(1)}, bf16[4,1,2,128,384]{4,3,2,0,1:T(8,12...) fusion(bf16[4,3,4,128,384]{4,3,2,0,1:T(8,128)(2,1)S(1)} %maximu, ...), kind=kLoop, calls=%fused_computation.125 | loop fusion | bytes 15728640 | tf_op jit(solution)/shard_map/slice | solution.py:94
  156.4 1.0 constant_dynamic-update-slice_fusion.24
  158.4 1.0 constant_dynamic-update-slice_fusion.22
  159.4 1.0 constant_dynamic-update-slice_fusion.21
  167.5 1.0 constant_dynamic-update-slice_fusion.13
  169.5 1.1 constant_dynamic-update-slice_fusion.11
  171.6 1.0 constant_dynamic-update-slice_fusion.9
  173.7 1.0 constant_dynamic-update-slice_fusion.7
  174.7 1.1 constant_dynamic-update-slice_fusion.6
  176.8 1.0 constant_dynamic-update-slice_fusion.4
  177.8 1.1 constant_dynamic-update-slice_fusion.3
  179.9 1.1 constant_dynamic-update-slice_fusion.1
  182.0 15.5 %multiply_reduce_fusion = (f32[1024]{0:T(1024)S(1)}, f32[1024,384]{1,0:T(8,128)S(1)}) fusion(f32[384]{0:T(512)S(1)} %copy-done.13, bf16[1024,10368]{1,0:T(8,128)(2,1)} %constant_dynamic-update-slice_fusion, bf16[10368,384]{1,0:T(8,128)(2,1)S(1)} %bitcast.163), kind=kOutput, calls=%fused_computation.25 | convolution fusion | flops 8154905600 | bytes 30774784 | tf_op jit(solution)/shard_map/dot_general | solution.py:101
  198.4 5.3 %collective-permute-start.5 = (bf16[4,1,128,384]{3,2,1,0:T(8,128)(2,1)S(1)}, bf16[4,1,128,384]{3,2,1,0:T(8,128)(2,1)S(1)}, u32[]{:S(2)}, u32[]{:S(2)}) collective-permute-start(bf16[4,1,128,384]{3,2,1,0:T(8,128)(2,1)S(1)} %get-tuple-element.100), channel_id=1, source_target_pairs={{1,0},{2,1},{3,2},{4,3},{5,4},{6,5},{7,6},{8,7},{9,8},{10,9},{11,1... | collective-permute-start | bytes 1179656 | tf_op jit(solution)/shard_map/ppermute | solution.py:167
  203.9 1.3 copy.28
  205.7 1.3 pad_maximum_fusion.2
  207.1 2.0 collective-permute-done.4
  211.0 3.8 %pad_slice_fusion = (bf16[4,1,2,128,384]{4,3,2,0,1:T(8,128)(2,1)S(1)}, bf16[4,1,2,128,384]{4,3,2,0,1:T(8,128)(2,1)S(1)}, bf16[4,1,2,128,384]{4,3,2,0,1:T(8,128)(...) fusion(bf16[4,3,4,128,384]{4,3,2,0,1:T(8,128)(2,1)S(1)} %maximu, ...), kind=kLoop, calls=%fused_computation.106 | loop fusion | bytes 13369344 | tf_op jit(solution)/shard_map/slice | solution.py:94
  214.8 3.6 %pad_slice_fusion.1 = (bf16[4,1,2,128,384]{4,3,2,0,1:T(8,128)(2,1)S(1)}, bf16[4,1,2,128,384]{4,3,2,0,1:T(8,128)(2,1)S(1)}, bf16[4,1,2,128,384]{4,3,2,0,1:T(8,128...) fusion(bf16[4,3,4,128,384]{4,3,2,0,1:T(8,128)(2,1)S(1)} %maximu, ...), kind=kLoop, calls=%fused_computation.107 | loop fusion | bytes 15728640 | tf_op jit(solution)/shard_map/slice | solution.py:94
  220.4 1.0 constant_dynamic-update-slice_fusion.51
  222.4 1.0 constant_dynamic-update-slice_fusion.49
  223.5 1.0 constant_dynamic-update-slice_fusion.48
  231.5 1.0 constant_dynamic-update-slice_fusion.40
  233.6 1.1 constant_dynamic-update-slice_fusion.38
  235.7 1.0 constant_dynamic-update-slice_fusion.36
  238.7 1.1 constant_dynamic-update-slice_fusion.33
  240.8 1.0 constant_dynamic-update-slice_fusion.31
  241.8 1.1 constant_dynamic-update-slice_fusion.30
  243.9 1.1 constant_dynamic-update-slice_fusion.28
  246.0 14.8 %convolution_add_fusion = f32[1024,384]{1,0:T(8,128)S(1)} fusion(bf16[1024,10368]{1,0:T(8,128)(2,1)} %constant_dynamic-update-slice_fusion.27, bf16[10368,384]{1,0:T(8,128)(2,1)S(1)} %bitcast.166, f32[384]{0:T(512)S(1)} %copy-done.14), kind=kOutput, calls=%fused_computation.26 | convolution fusion | flops 8154120192 | bytes 30770688 | tf_op jit(solution)/shard_map/dot_general | solution.py:101
  260.8 1.1 fusion.10
  (103 shorter events, 45.0 us)
Async XLA Ops:
  0.6 1.4 copy-start
  2.0 1.4 copy-start.1
  3.5 13.5 %copy-start.8 = (s32[16]{0:T(128)S(1)}, s32[16]{0:T(128)}, u32[]{:S(2)}) copy-start(s32[16]{0:T(128)} %param.31) | copy-start | bytes 196
  3.5 13.5 %copy-start.9 = (s32[16]{0:T(128)S(1)}, s32[16]{0:T(128)}, u32[]{:S(2)}) copy-start(s32[16]{0:T(128)} %param.28) | copy-start | bytes 196
  3.5 13.5 %copy-start.10 = (s32[16]{0:T(128)S(1)}, s32[16]{0:T(128)}, u32[]{:S(2)}) copy-start(s32[16]{0:T(128)} %param.29) | copy-start | bytes 196
  3.5 13.5 %copy-start.11 = (s32[16]{0:T(128)S(1)}, s32[16]{0:T(128)}, u32[]{:S(2)}) copy-start(s32[16]{0:T(128)} %param.30) | copy-start | bytes 196
  3.5 13.5 %copy-start.12 = (s32[16]{0:T(128)S(1)}, s32[16]{0:T(128)}, u32[]{:S(2)}) copy-start(s32[16]{0:T(128)} %param.27) | copy-start | bytes 196
  5.8 53.0 %all-to-all-start = ((bf16[128,4,8,384]{3,2,1,0:T(8,128)(2,1)}), bf16[128,4,8,384]{3,2,1,0:T(8,128)(2,1)S(1)}, u32[]{:S(2)}, u32[]{:S(2)}) async-start(bf16[128,4,8,384]{3,2,1,0:T(8,128)(2,1)} %bitcast), calls=%async_computation | async-start | bytes 6291456 | tf_op jit(solution)/shard_map/all_to_all | solution.py:145
  61.5 54.4 %copy-start.2 = (bf16[4,2,128,384]{3,2,1,0:T(8,128)(2,1)S(1)}, bf16[4,2,128,384]{3,2,1,0:T(8,128)(2,1)}, u32[]{:S(2)}) copy-start(bf16[4,2,128,384]{3,2,1,0:T(8,128)(2,1)} %param.18) | copy-start | bytes 2359300
  107.8 8.4 %copy-start.6 = (f32[384]{0:T(512)S(1)}, f32[384]{0:T(512)}, u32[]{:S(2)}) copy-start(f32[384]{0:T(512)} %param.21) | copy-start | bytes 4612
  109.5 30.4 %collective-permute-start = (bf16[2,2,16,4,8,384]{5,4,2,3,1,0:T(8,128)(2,1)}, bf16[2,2,16,4,8,384]{5,4,2,3,1,0:T(8,128)(2,1)}, u32[]{:S(2)}, u32[]{:S(2)}) collective-permute-start(bf16[2,2,16,4,8,384]{5,4,2,3,1,0:T(8,128)(2,1)} %copy.23), channel_id=1, source_target_pairs={{0,1},{1,2},{2,3},{3,4},{4,5},{5,6},{6,7},{7,8},{8,9},{9,10},{10,1... | collective-permute-start | bytes 4718600 | tf_op jit(solution)/shard_map/ppermute | solution.py:154
  110.9 29.0 %collective-permute-start.1 = (bf16[2,2,16,4,8,384]{5,4,2,3,1,0:T(8,128)(2,1)}, bf16[2,2,16,4,8,384]{5,4,2,3,1,0:T(8,128)(2,1)}, u32[]{:S(2)}, u32[]{:S(2)}) collective-permute-start(bf16[2,2,16,4,8,384]{5,4,2,3,1,0:T(8,128)(2,1)} %copy.24), channel_id=1, source_target_pairs={{1,0},{2,1},{3,2},{4,3},{5,4},{6,5},{7,6},{8,7},{9,8},{10,9},{11,1... | collective-permute-start | bytes 4718600 | tf_op jit(solution)/shard_map/ppermute | solution.py:155
  116.7 0.9 copy-start.4
  118.6 18.5 %collective-permute-start.2 = (bf16[4,1,128,384]{3,2,1,0:T(8,128)(2,1)}, bf16[4,1,128,384]{3,2,1,0:T(8,128)(2,1)S(1)}, u32[]{:S(2)}, u32[]{:S(2)}) collective-permute-start(bf16[4,1,128,384]{3,2,1,0:T(8,128)(2,1)} %get-tuple-element.101), channel_id=1, source_target_pairs={{0,1},{1,2},{2,3},{3,4},{4,5},{5,6},{6,7},{7,8},{8,9},{9,10},{10,1... | collective-permute-start | bytes 1179656 | tf_op jit(solution)/shard_map/ppermute | solution.py:166
  118.6 19.8 %collective-permute-start.3 = (bf16[4,1,128,384]{3,2,1,0:T(8,128)(2,1)}, bf16[4,1,128,384]{3,2,1,0:T(8,128)(2,1)}, u32[]{:S(2)}, u32[]{:S(2)}) collective-permute-start(bf16[4,1,128,384]{3,2,1,0:T(8,128)(2,1)} %get-tuple-element.102), channel_id=1, source_target_pairs={{1,0},{2,1},{3,2},{4,3},{5,4},{6,5},{7,6},{8,7},{9,8},{10,9},{11,1... | collective-permute-start | bytes 1179656 | tf_op jit(solution)/shard_map/ppermute | solution.py:167
  171.6 10.3 %slice-start = ((s8[7962624]{0:T(1024)(128)(4,1)}), s8[4194304]{0:T(1024)(128)(4,1)S(1)}, s32[]{:S(2)}) async-start(s8[7962624]{0:T(1024)(128)(4,1)} %bitcast.161), calls=%async_computation.2 | async-start | bytes 8388608
  171.6 10.3 %copy-start.13 = (f32[384]{0:T(512)S(1)}, f32[384]{0:T(512)}, u32[]{:S(2)}) copy-start(f32[384]{0:T(512)} %param.25) | copy-start | bytes 4612
  176.8 5.2 %slice-start.1 = ((s8[7962624]{0:T(1024)(128)(4,1)}), s8[3768320]{0:T(1024)(128)(4,1)S(1)}, s32[]{:S(2)}) async-start(s8[7962624]{0:T(1024)(128)(4,1)} %bitcast.161), calls=%async_computation.3 | async-start | bytes 7536640
  182.0 15.7 %copy-start.7 = (f32[384]{0:T(512)S(1)}, f32[384]{0:T(512)}, u32[]{:S(2)}) copy-start(f32[384]{0:T(512)} %param.22) | copy-start | bytes 4612
  182.0 21.7 %copy-start.5 = (bf16[4,1,2,128,384]{4,3,2,0,1:T(8,128)(2,1)S(1)}, bf16[4,1,2,128,384]{4,3,2,0,1:T(8,128)(2,1)}, u32[]{:S(2)}) copy-start(bf16[4,1,2,128,384]{4,3,2,0,1:T(8,128)(2,1)} %fusion.24) | copy-start | bytes 2359300
  198.3 10.8 %collective-permute-start.4 = (bf16[4,1,128,384]{3,2,1,0:T(8,128)(2,1)S(1)}, bf16[4,1,128,384]{3,2,1,0:T(8,128)(2,1)S(1)}, u32[]{:S(2)}, u32[]{:S(2)}) collective-permute-start(bf16[4,1,128,384]{3,2,1,0:T(8,128)(2,1)S(1)} %get-tuple-element.99), channel_id=1, source_target_pairs={{0,1},{1,2},{2,3},{3,4},{4,5},{5,6},{6,7},{7,8},{8,9},{9,10},{10,1... | collective-permute-start | bytes 1179656 | tf_op jit(solution)/shard_map/ppermute | solution.py:166
  198.4 10.7 %collective-permute-start.5 = (bf16[4,1,128,384]{3,2,1,0:T(8,128)(2,1)S(1)}, bf16[4,1,128,384]{3,2,1,0:T(8,128)(2,1)S(1)}, u32[]{:S(2)}, u32[]{:S(2)}) collective-permute-start(bf16[4,1,128,384]{3,2,1,0:T(8,128)(2,1)S(1)} %get-tuple-element.100), channel_id=1, source_target_pairs={{1,0},{2,1},{3,2},{4,3},{5,4},{6,5},{7,6},{8,7},{9,8},{10,9},{11,1... | collective-permute-start | bytes 1179656 | tf_op jit(solution)/shard_map/ppermute | solution.py:167
  235.7 10.3 %slice-start.2 = ((s8[7962624]{0:T(1024)(128)(4,1)}), s8[4194304]{0:T(1024)(128)(4,1)S(1)}, s32[]{:S(2)}) async-start(s8[7962624]{0:T(1024)(128)(4,1)} %bitcast.164), calls=%async_computation.4 | async-start | bytes 8388608
  235.7 10.3 %copy-start.14 = (f32[384]{0:T(512)S(1)}, f32[384]{0:T(512)}, u32[]{:S(2)}) copy-start(f32[384]{0:T(512)} %param.26) | copy-start | bytes 4612
  240.8 5.2 %slice-start.3 = ((s8[7962624]{0:T(1024)(128)(4,1)}), s8[3768320]{0:T(1024)(128)(4,1)S(1)}, s32[]{:S(2)}) async-start(s8[7962624]{0:T(1024)(128)(4,1)} %bitcast.164), calls=%async_computation.5 | async-start | bytes 7536640
  246.0 14.8 %copy-start.3 = (bf16[4,2,128,384]{3,2,1,0:T(8,128)(2,1)S(1)}, bf16[4,2,128,384]{3,2,1,0:T(8,128)(2,1)}, u32[]{:S(2)}) copy-start(bf16[4,2,128,384]{3,2,1,0:T(8,128)(2,1)} %param.18) | copy-start | bytes 2359300

commit v2 on v1

--- a/solution.py
+++ b/solution.py
@@ -84,26 +84,150 @@
     )(source, rotation, keep, held)
 
 
-def convolve(padded, weight, bias_vec):
-    n_slots = padded.shape[0]
-    n_rows = padded.shape[2] - 2
-    n_cols = padded.shape[3]
-    channels = padded.shape[4]
-    widened = jnp.pad(padded, ((0, 0), (0, 0), (0, 0), (1, 1), (0, 0)))
-    pieces = [
-        widened[:, t_step, y_step : y_step + n_rows, x_step : x_step + n_cols, :]
-        for t_step in range(3)
-        for y_step in range(3)
-        for x_step in range(3)
-    ]
-    patches = jnp.concatenate(pieces, axis=-1).reshape(-1, 27 * channels)
-    result = (
-        jnp.dot(
-            patches, weight.reshape(27 * channels, channels), preferred_element_type=jnp.float32
-        )
-        + bias_vec
-    )
-    return result.reshape(n_slots, n_rows, n_cols, channels)
+def spread(weight):
+    n_t, n_y, n_x, ci, co = weight.shape
+
+    def body(w_ref, o_ref):
+        o_ref[0] = w_ref[0, 0, 0]
+
+    return pl.pallas_call(
+        body,
+        grid=(n_t, n_y, n_x),
+        in_specs=[pl.BlockSpec((1, 1, 1, ci, co), lambda t, y, x: (t, y, x, 0, 0))],
+        out_specs=pl.BlockSpec((1, ci, co), lambda t, y, x: (t, y, x)),
+        out_shape=jax.ShapeDtypeStruct((n_t, n_y * ci, n_x * co), weight.dtype),
+        cost_estimate=pl.CostEstimate(
+            flops=0, bytes_accessed=4 * weight.size, transcendentals=0
+        ),
+        compiler_params=pltpu.CompilerParams(vmem_limit_bytes=16 << 20),
+    )(weight)
+
+
+def conv_layer(which, got, above, below, act, act_above, act_below, weight, bias, extra, edges, normed):
+    n_slots, n_rows, n_cols, ch = act.shape
+    blocks = n_cols // CB
+    wide = weight.shape[2]
+    m_all = n_slots * n_rows * n_cols
+
+    def body(edge_ref, got_ref, above_ref, below_ref, act_ref, aa_ref, ab_ref, w_ref, b_ref, x_ref, o_ref, next_ref, lhs, acc):
+        t = pl.program_id(0)
+
+        def place(s, row, value):
+            for y in range(n_rows):
+                dy = row - y
+                if 0 <= dy <= 2:
+                    m = (s * n_rows + y) * n_cols
+                    lhs[m : m + n_cols, dy * ch : (dy + 1) * ch] = value
+
+        def edge(s, k, value):
+            return jnp.where(edge_ref[k, s] != 0, value, jnp.zeros_like(value))
+
+        @pl.when(t < 2)
+        def _():
+            for s in range(n_slots):
+                place(s, 0, edge(s, 0, above_ref[0, 0, :, s].reshape(n_cols, ch)))
+                place(s, n_rows + 1, edge(s, 1, below_ref[0, 0, :, s].reshape(n_cols, ch)))
+                for r in range(n_rows):
+                    own = got_ref[r, 0, 0, :, s].reshape(n_cols, ch)
+                    place(s, r + 1, own)
+                    next_ref[s, 0, r] = own
+
+        @pl.when(t == 2)
+        def _():
+            for s in range(n_slots):
+                place(s, 0, edge(s, 0, aa_ref[s]))
+                place(s, n_rows + 1, edge(s, 1, ab_ref[s]))
+                for r in range(n_rows):
+                    own = act_ref[s, r]
+                    place(s, r + 1, own)
+                    next_ref[s, 0, r] = own
+
+        half = m_all // 2
+
+        def product(k):
+            rows = pl.ds(k * half, half)
+            return rows, jnp.dot(lhs[rows], w_ref[0], preferred_element_type=jnp.float32)
+
+        @pl.when(t == 0)
+        def _():
+            for k in range(2):
+                rows, value = product(k)
+                acc[rows] = value
+
+        @pl.when(t > 0)
+        def _():
+            for k in range(2):
+                rows, value = product(k)
+                acc[rows] += value
+
+        @pl.when(t == 2)
+        def _():
+            col = lax.broadcasted_iota(jnp.int32, (n_cols, ch), 0)
+            for s in range(n_slots):
+                for y in range(n_rows):
+                    m = (s * n_rows + y) * n_cols
+                    left = pltpu.roll(acc[m : m + n_cols, 0:ch], 1, 0)
+                    right = pltpu.roll(acc[m : m + n_cols, 2 * ch : 3 * ch], n_cols - 1, 0)
+                    total = acc[m : m + n_cols, ch : 2 * ch] + b_ref[...]
+                    total += jnp.where(col == 0, 0.0, left)
+                    total += jnp.where(col == n_cols - 1, 0.0, right)
+                    if normed:
+                        scaled = total * lax.rsqrt(
+                            jnp.mean(total * total, axis=-1, keepdims=True) + 1e-06
+                        )
+                        u = scaled * x_ref[...]
+                        o_ref[s, y] = (u / (1.0 + jnp.exp(-u))).astype(o_ref.dtype)
+                    else:
+                        o_ref[s, y] = (total + x_ref[s, y].astype(jnp.float32)).astype(o_ref.dtype)
+
+    def whole(shape):
+        return pl.BlockSpec(shape, lambda t, e, zeros=(0,) * len(shape): zeros)
+
+    side = pl.BlockSpec(
+        (1, 1, blocks, n_slots, CB, ch), lambda t, e: (which, jnp.minimum(t, 1), 0, 0, 0, 0)
+    )
+    return pl.pallas_call(
+        body,
+        grid_spec=pltpu.PrefetchScalarGridSpec(
+            num_scalar_prefetch=1,
+            grid=(3,),
+            in_specs=[
+                pl.BlockSpec(
+                    (n_rows, 1, 1, blocks, n_slots, CB, ch),
+                    lambda t, e: (0, which, jnp.minimum(t, 1), 0, 0, 0, 0),
+                ),
+                side,
+                side,
+                whole(act.shape),
+                whole(act_above.shape),
+                whole(act_below.shape),
+                pl.BlockSpec((1,) + weight.shape[1:], lambda t, e: (t, 0, 0)),
+                whole(bias.shape),
+                whole(extra.shape),
+            ],
+            out_specs=[
+                whole(act.shape),
+                pl.BlockSpec(
+                    (n_slots, 1, n_rows, n_cols, ch),
+                    lambda t, e: (0, jnp.maximum(t - 1, 0), 0, 0, 0),
+                ),
+            ],
+            scratch_shapes=[
+                pltpu.VMEM((m_all, 3 * ch), jnp.bfloat16),
+                pltpu.VMEM((m_all, wide), jnp.float32),
+            ],
+        ),
+        out_shape=[
+            jax.ShapeDtypeStruct(act.shape, jnp.bfloat16),
+            jax.ShapeDtypeStruct((n_slots, 2) + act.shape[1:], jnp.bfloat16),
+        ],
+        cost_estimate=pl.CostEstimate(
+            flops=2 * m_all * weight.size,
+            bytes_accessed=2 * weight.size + 8 * act.size,
+            transcendentals=act.size,
+        ),
+        compiler_params=pltpu.CompilerParams(vmem_limit_bytes=40 << 20),
+    )(edges, got, above, below, act, act_above, act_below, weight, bias, extra)
 
 
 def local(
@@ -153,29 +277,25 @@
     up = [((i + 1) % n_tiles, i) for i in range(n_tiles)]
     above = lax.ppermute(got[n_rows - 1], "tile", down)
     below = lax.ppermute(got[0], "tile", up)
-    rows = jnp.concatenate([above[None], got, below[None]], axis=0)
-    rows = rows.transpose(1, 4, 2, 0, 3, 5, 6).reshape(
-        2, n_slots, 2, n_rows + 2, n_cols, ch
-    )
-    border = jnp.ones((n_slots, n_rows + 2), jnp.bfloat16)
-    border = border.at[:, 0].set((my_number != 0).astype(jnp.bfloat16))
-    border = border.at[:, -1].set((my_number != n_tiles - 1).astype(jnp.bfloat16))
-    border = border[:, None, :, None, None]
-
-    def conv_layer(kept, activation, weight, bias_vec):
-        head = lax.ppermute(activation[:, -1:], "tile", down)
-        tail = lax.ppermute(activation[:, :1], "tile", up)
-        act = jnp.concatenate([head, activation, tail], axis=1)
-        padded = jnp.concatenate([kept, act[:, None]], axis=1)
-        return convolve(padded * border, weight, bias_vec)
-
+    edges = jnp.stack([my_number != 0, my_number != n_tiles - 1]).astype(jnp.int32)
+
+    def sides(activation):
+        return (
+            lax.ppermute(activation[:, n_rows - 1], "tile", down),
+            lax.ppermute(activation[:, 0], "tile", up),
+        )
+
+    wide_first = spread(conv_first)
+    wide_second = spread(conv_second)
     act_first = activate(frame_in.astype(jnp.float32), gain_first).astype(jnp.bfloat16)
-    hidden = conv_layer(rows[0], act_first, conv_first, bias_first)
-    act_second = activate(hidden, gain_second).astype(jnp.bfloat16)
-    second_out = conv_layer(rows[1], act_second, conv_second, bias_second)
-    mixed_frame = (second_out + frame_in.astype(jnp.float32)).astype(jnp.bfloat16)
-    next_first = jnp.stack([rows[0, :, 1, 1:-1], act_first], axis=1)
-    next_second = jnp.stack([rows[1, :, 1, 1:-1], act_second], axis=1)
+    act_second, next_first = conv_layer(
+        0, got, above, below, act_first, *sides(act_first), wide_first,
+        bias_first[None], gain_second[None], edges, True,
+    )
+    mixed_frame, next_second = conv_layer(
+        1, got, above, below, act_second, *sides(act_second), wide_second,
+        bias_second[None], frame_in, edges, False,
+    )
     return (mixed_frame, next_first, next_second)
 
 

time: 262 us -> 187 us (0.71)
  local copies, waits for them, and re-layouts: 82.7 us -> 18.9 us
  Pallas kernels: 5.03 us -> 41.6 us
  matrix products: 30.3 us -> 0 us
  other arithmetic: 17 us -> 1.02 us
  starting transfers between devices: 26.6 us -> 21.8 us
  waiting for transfers between devices: 52.9 us -> 56.4 us
    unnamed x91 -> x40, local copies, waits for them, and re-layouts: 58.2 us -> 13.6 us
    pallas_call x0 -> x4, Pallas kernels: none -> 36.4 us  [the longest x2 32.3 us: conv_layer(): pl.pallas_call(body, grid_spec=pltpu.PrefetchScalarGridSpec(num_scalar_pr...]
    dot_general x2 -> x0, matrix products: 30.3 us -> none  [convolve(): jnp.dot(patches, weight.reshape(27 * channels, channels), preferred_eleme...]
    slice x9 -> x1, local copies, waits for them, and re-layouts: 17.8 us -> 1.98 us  [local(): below = lax.ppermute(got[0], 'tile', up)]
    another operation x5 -> x1, other arithmetic: 5.52 us -> 0.08 us  [local(): jnp.stack([my_number != 0, my_number != n_tiles - 1]).astype(jnp.int32)]
    ppermute x4, starting transfers between devices: 10.4 us -> 5.55 us  [the longest x2 5.04 us: sides(): lax.ppermute(activation[:, 0], 'tile', up)]
    reshape x1 -> x0, other arithmetic: 4.78 us -> none  [local(): rows.transpose(1, 4, 2, 0, 3, 5, 6)]
    ppermute x4, waiting for transfers between devices: 11.3 us -> 14.8 us  [the longest x2 9.44 us: sides(): lax.ppermute(activation[:, 0], 'tile', up)]
  transfers between devices with their start and end apart: 7 -> 7, of which waited for: 4 -> 5; matrix products, arithmetic and copies ran while one was open for 5% -> 2% of each run, Pallas kernels for 0% -> 2%
where the time goes in v2:
time: 187 us
  waiting for transfers between devices  56.4 us (30%)
  blocking collectives  46.2 us (25%)
  Pallas kernels  41.6 us (22%)
  starting transfers between devices  21.8 us (12%)
  local copies, waits for them, and re-layouts  18.9 us (10%)
    all_to_all x1, blocking collectives, local(): lax.all_to_all(moved.reshape(n_groups * n_tiles, n_slots, CB, ch), BOTH,...  46.2 us
    all_to_all x1, waiting for transfers between devices, local(): held = lax.all_to_all(sent, BOTH, 0, 0, tiled=True)  41.6 us
    pallas_call x2, Pallas kernels, conv_layer(): pl.pallas_call(body, grid_spec=pltpu.PrefetchScalarGridSpec(num_scalar_pr...  32.3 us
    unnamed x40, local copies, waits for them, and re-layouts  13.6 us
    all_to_all x1, starting transfers between devices, local(): held = lax.all_to_all(sent, BOTH, 0, 0, tiled=True)  11.1 us
    ppermute x2, waiting for transfers between devices, sides(): lax.ppermute(activation[:, 0], 'tile', up)  9.44 us
    ppermute x2, waiting for transfers between devices, sides(): lax.ppermute(activation[:, n_rows - 1], 'tile', down)  5.39 us
    ppermute x1, starting transfers between devices, local(): below = lax.ppermute(got[0], 'tile', up)  5.06 us
  transfers between devices with their start and end apart: 7, of which 5 were waited for; matrix products, arithmetic and copies ran while one was open for 2% of the time, Pallas kernels for 2%

profile of v2, /device:TPU:0, one launch (start us, length us, event | category | flops | bytes accessed | tf_op | source)
XLA Modules:
  0.0 186.8 jit_solution(18375164794309520353)
XLA Ops:
  0.6 0.0 copy-start.5
  0.6 1.4 copy-done.5
  2.0 1.4 copy-done.6
  3.4 2.4 %shard_map.157 = bf16[2,2,2,16,4,8,384]{6,5,4,3,2,1,0:T(8,128)(2,1)} custom-call(bf16[4,2,2,128,384]{4,3,2,1,0:T(8,128)(2,1)S(1)} %copy-done.5, bf16[4,2,2,128,384]{4,3,2,1,0:T(8,128)(2,1)S(1)} %copy-done.6), custom_call_target="tpu_custom_call" | custom-call | tf_op jit(solution)/shard_map/pallas_call | solution.py:32
  5.8 0.0 copy-start.17
  5.8 11.1 %all-to-all-start = ((bf16[128,4,8,384]{3,2,1,0:T(8,128)(2,1)}), bf16[128,4,8,384]{3,2,1,0:T(8,128)(2,1)S(1)}, u32[]{:S(2)}, u32[]{:S(2)}) async-start(bf16[128,4,8,384]{3,2,1,0:T(8,128)(2,1)} %bitcast.2), calls=%async_computation | async-start | bytes 6291456 | tf_op jit(solution)/shard_map/all_to_all | solution.py:269
  17.0 0.0 copy-done.13
  17.0 0.0 copy-done.14
  17.0 0.0 copy-done.15
  17.1 0.0 copy-done.16
  17.1 0.0 copy-done.17
  17.1 0.1 select_reduce_fusion
  17.3 41.6 %all-to-all-done = bf16[128,4,8,384]{3,2,1,0:T(8,128)(2,1)S(1)} async-done(((bf16[128,4,8,384]{3,2,1,0:T(8,128)(2,1)}), bf16[128,4,8,384]{3,2,1,0:T(8,128)(2,1)S(1)}, u32[]{:S(2)}, u32[]{:S(2)}) %all-to-all-start) | async-done | bytes 3145760 | tf_op jit(solution)/shard_map/all_to_all | solution.py:269
  58.8 2.8 %shard_map.158 = bf16[4,32,4,8,384]{4,3,2,1,0:T(8,128)(2,1)S(1)} custom-call(s32[16]{0:T(128)S(1)} %get-tuple-element.13.source_ref, s32[16]{0:T(128)S(1)} %get-tuple-element.21.rotation_ref, s32[16]{0:T(128)S(1)} %compare_convert_fusion.keep_ref, bf16[4,32,4,8,384]{4,3,2,1,0:T(8,128)(2,1)S(1)} %bitcast.20), custom_call_target="tpu_custom_call" | custom-call | tf_op jit(solution)/shard_map/pallas_call | solution.py:67
  61.7 46.2 %all_to_all.10 = bf16[128,4,8,384]{3,2,1,0:T(8,128)(2,1)S(1)} all-to-all(bf16[128,4,8,384]{3,2,1,0:T(8,128)(2,1)S(1)} %bitcast.21), channel_id=1, replica_groups=mesh['stream'=4,'tile'=32] {'stream','tile'}, dimensions={0} | all-to-all | bytes 6291456 | tf_op jit(solution)/shard_map/all_to_all | solution.py:271
  107.9 2.0 %fusion.10 = (bf16[64,4,8,384]{3,2,1,0:T(8,128)(2,1)}, bf16[64,4,8,384]{3,2,1,0:T(8,128)(2,1)}) fusion(bf16[128,4,8,384]{3,2,1,0:T(8,128)(2,1)S(1)} %all_to_all.10), kind=kLoop, calls=%fused_computation.32 | loop fusion | bytes 6291456 | tf_op jit(solution)/shard_map/slice | solution.py:279
  109.9 0.0 collective-permute-start
  109.9 5.1 %collective-permute-start.1 = (bf16[2,2,16,4,8,384]{5,4,3,2,1,0:T(8,128)(2,1)}, bf16[2,2,16,4,8,384]{5,4,3,2,1,0:T(8,128)(2,1)}, u32[]{:S(2)}, u32[]{:S(2)}) collective-permute-start(bf16[2,2,16,4,8,384]{5,4,3,2,1,0:T(8,128)(2,1)} %bitcast.7), channel_id=1, source_target_pairs={{1,0},{2,1},{3,2},{4,3},{5,4},{6,5},{7,6},{8,7},{9,8},{10,9},{11,1... | collective-permute-start | bytes 4718600 | tf_op jit(solution)/shard_map/ppermute | solution.py:279
  114.9 0.2 fusion
  115.2 0.5 fusion.7
  115.7 0.0 copy-start.8
  115.7 0.0 copy-start.10
  115.8 0.0 copy-start.11
  115.8 1.1 slice_bitcast_fusion.2
  116.9 0.0 collective-permute-start.3
  116.9 0.5 collective-permute-start.2
  117.4 2.1 %copy.22.act_ref = bf16[4,2,128,384]{3,2,1,0:T(8,128)(2,1)} copy(bf16[4,2,128,384]{3,2,0,1:T(8,128)(2,1)} %copy-done.8) | data formatting | bytes 1572864 | tf_op jit(solution)/shard_map/convert_element_type | solution.py:290
  119.5 0.0 copy-start
  119.6 3.3 %copy-done = bf16[3,3,3,384,384]{4,3,2,1,0:T(8,128)(2,1)S(1)} copy-done((bf16[3,3,3,384,384]{4,3,2,1,0:T(8,128)(2,1)S(1)}, bf16[3,3,3,384,384]{4,3,2,1,0:T(8,128)(2,1)}, u32[]{:S(2)}) %copy-start) | copy-done | bytes 7962648
  122.8 2.0 %shard_map.159.w_ref = bf16[3,1152,1152]{2,1,0:T(8,128)(2,1)S(1)} custom-call(bf16[3,3,3,384,384]{4,3,2,1,0:T(8,128)(2,1)S(1)} %copy-done), custom_call_target="tpu_custom_call" | custom-call | bytes 15925248 | tf_op jit(solution)/shard_map/pallas_call | solution.py:93
  124.9 3.1 %copy-done.1 = bf16[3,1152,1152]{2,1,0:T(8,128)(2,1)} copy-done((bf16[3,1152,1152]{2,1,0:T(8,128)(2,1)}, bf16[3,1152,1152]{2,1,0:T(8,128)(2,1)S(1)}, u32[]{:S(2)}) %copy-start.1) | copy-done | bytes 7962648
  127.9 0.1 compare_bitcast_fusion.1
  128.0 9.4 %collective-permute-done.3.ab_ref = bf16[4,128,384]{2,1,0:T(8,128)(2,1)S(1)} collective-permute-done((bf16[4,128,384]{2,1,0:T(8,128)(2,1)}, bf16[4,128,384]{2,1,0:T(8,128)(2,1)S(1)}, u32[]{:S(2)}, u32[]{:S(2)}) %collective-permute-start.3) | collective-permute-done | bytes 393248 | tf_op jit(solution)/shard_map/ppermute | solution.py:285
  137.4 0.2 collective-permute-done.2.aa_ref
  137.6 0.0 collective-permute-done.above_ref
  137.6 0.0 collective-permute-done.1.below_ref
  137.6 1.3 copy-done.7
  138.9 16.5 %shard_map.160 = (bf16[4,2,128,384]{3,2,1,0:T(8,128)(2,1)S(1)}, bf16[4,2,2,128,384]{4,3,2,1,0:T(8,128)(2,1)}) custom-call(s32[2,4]{1,0:T(2,128)S(1)} %add_convert_fusion.edge_ref, bf16[2,2,2,16,4,8,384]{6,5,4,3,2,1,0:T(8,128)(2,1)S(1)} %bitcast.18, bf16[2,2,16,4,8,384]{5,4,3,2,1,0:T(8,128)(2,1)} %collective-permute-done.above_ref, ...), custom_call_target="tpu_custom_call" | custom-call | flops 8153726976 | bytes 11108352 | tf_op jit(solution)/shard_map/pallas_call | solution.py:189
  155.4 0.1 slice_bitcast_fusion
  155.5 5.0 %collective-permute-start.5 = (bf16[4,128,384]{2,1,0:T(8,128)(2,1)S(1)}, bf16[4,128,384]{2,1,0:T(8,128)(2,1)S(1)}, u32[]{:S(2)}, u32[]{:S(2)}) collective-permute-start(bf16[4,128,384]{2,1,0:T(8,128)(2,1)S(1)} %get-tuple-element.17), channel_id=1, source_target_pairs={{1,0},{2,1},{3,2},{4,3},{5,4},{6,5},{7,6},{8,7},{9,8},{10,9},{11,1... | collective-permute-start | bytes 1179656 | tf_op jit(solution)/shard_map/ppermute | solution.py:285
  160.5 0.0 collective-permute-start.4
  160.5 0.0 copy-start.4
  160.5 2.1 %shard_map.161.w_ref = bf16[3,1152,1152]{2,1,0:T(8,128)(2,1)S(1)} custom-call(bf16[3,3,3,384,384]{4,3,2,1,0:T(8,128)(2,1)S(1)} %bitcast.23), custom_call_target="tpu_custom_call" | custom-call | bytes 15925248 | tf_op jit(solution)/shard_map/pallas_call | solution.py:93
  162.6 0.0 copy-start.2
  162.6 3.1 %copy-done.2 = bf16[3,1152,1152]{2,1,0:T(8,128)(2,1)} copy-done((bf16[3,1152,1152]{2,1,0:T(8,128)(2,1)}, bf16[3,1152,1152]{2,1,0:T(8,128)(2,1)S(1)}, u32[]{:S(2)}) %copy-start.2) | copy-done | bytes 7962648
  165.7 0.1 collective-permute-done.5.ab_ref
  165.8 5.2 %collective-permute-done.4.aa_ref = bf16[4,128,384]{2,1,0:T(8,128)(2,1)S(1)} collective-permute-done((bf16[4,128,384]{2,1,0:T(8,128)(2,1)S(1)}, bf16[4,128,384]{2,1,0:T(8,128)(2,1)S(1)}, u32[]{:S(2)}, u32[]{:S(2)}) %collective-permute-start.4) | collective-permute-done | bytes 393248 | tf_op jit(solution)/shard_map/ppermute | solution.py:284
  171.0 15.8 %shard_map.162 = (bf16[4,2,128,384]{3,2,1,0:T(8,128)(2,1)}, bf16[4,2,2,128,384]{4,3,2,1,0:T(8,128)(2,1)}) custom-call(s32[2,4]{1,0:T(2,128)S(1)} %add_convert_fusion.edge_ref, bf16[2,2,2,16,4,8,384]{6,5,4,3,2,1,0:T(8,128)(2,1)S(1)} %bitcast.19, bf16[2,2,16,4,8,384]{5,4,3,2,1,0:T(8,128)(2,1)} %collective-permute-done.above_ref, ...), custom_call_target="tpu_custom_call" | custom-call | flops 8153726976 | bytes 11108352 | tf_op jit(solution)/shard_map/pallas_call | solution.py:189
  (29 shorter events, 0.1 us)
Async XLA Ops:
  0.6 1.4 copy-start.5
  2.0 1.4 copy-start.6
  5.8 11.2 %copy-start.13 = (s32[16]{0:T(128)S(1)}, s32[16]{0:T(128)}, u32[]{:S(2)}) copy-start(s32[16]{0:T(128)} %param.27) | copy-start | bytes 196
  5.8 11.2 %copy-start.14 = (s32[16]{0:T(128)S(1)}, s32[16]{0:T(128)}, u32[]{:S(2)}) copy-start(s32[16]{0:T(128)} %param.24) | copy-start | bytes 196
  5.8 11.2 %copy-start.15 = (s32[16]{0:T(128)S(1)}, s32[16]{0:T(128)}, u32[]{:S(2)}) copy-start(s32[16]{0:T(128)} %param.25) | copy-start | bytes 196
  5.8 11.2 %copy-start.16 = (s32[16]{0:T(128)S(1)}, s32[16]{0:T(128)}, u32[]{:S(2)}) copy-start(s32[16]{0:T(128)} %param.23) | copy-start | bytes 196
  5.8 11.2 %copy-start.17 = (s32[16]{0:T(128)S(1)}, s32[16]{0:T(128)}, u32[]{:S(2)}) copy-start(s32[16]{0:T(128)} %param.26) | copy-start | bytes 196
  5.8 53.0 %all-to-all-start = ((bf16[128,4,8,384]{3,2,1,0:T(8,128)(2,1)}), bf16[128,4,8,384]{3,2,1,0:T(8,128)(2,1)S(1)}, u32[]{:S(2)}, u32[]{:S(2)}) async-start(bf16[128,4,8,384]{3,2,1,0:T(8,128)(2,1)} %bitcast.2), calls=%async_computation | async-start | bytes 6291456 | tf_op jit(solution)/shard_map/all_to_all | solution.py:269
  107.9 7.1 %copy-start.3 = (bf16[4,2,128,384]{3,2,1,0:T(8,128)(2,1)S(1)}, bf16[4,2,128,384]{3,2,1,0:T(8,128)(2,1)}, u32[]{:S(2)}) copy-start(bf16[4,2,128,384]{3,2,1,0:T(8,128)(2,1)} %x_ref.1) | copy-start | bytes 2359300
  107.9 7.3 %copy-start.9 = (f32[384]{0:T(512)S(1)}, f32[384]{0:T(512)}, u32[]{:S(2)}) copy-start(f32[384]{0:T(512)} %param.17) | copy-start | bytes 4612
  109.9 27.7 %collective-permute-start = (bf16[2,2,16,4,8,384]{5,4,3,2,1,0:T(8,128)(2,1)}, bf16[2,2,16,4,8,384]{5,4,3,2,1,0:T(8,128)(2,1)}, u32[]{:S(2)}, u32[]{:S(2)}) collective-permute-start(bf16[2,2,16,4,8,384]{5,4,3,2,1,0:T(8,128)(2,1)} %bitcast.6), channel_id=1, source_target_pairs={{0,1},{1,2},{2,3},{3,4},{4,5},{5,6},{6,7},{7,8},{8,9},{9,10},{10,1... | collective-permute-start | bytes 4718600 | tf_op jit(solution)/shard_map/ppermute | solution.py:278
  109.9 27.7 %collective-permute-start.1 = (bf16[2,2,16,4,8,384]{5,4,3,2,1,0:T(8,128)(2,1)}, bf16[2,2,16,4,8,384]{5,4,3,2,1,0:T(8,128)(2,1)}, u32[]{:S(2)}, u32[]{:S(2)}) collective-permute-start(bf16[2,2,16,4,8,384]{5,4,3,2,1,0:T(8,128)(2,1)} %bitcast.7), channel_id=1, source_target_pairs={{1,0},{2,1},{3,2},{4,3},{5,4},{6,5},{7,6},{8,7},{9,8},{10,9},{11,1... | collective-permute-start | bytes 4718600 | tf_op jit(solution)/shard_map/ppermute | solution.py:279
  115.7 1.2 copy-start.8
  115.7 3.8 %copy-start.10 = (f32[384]{0:T(512)S(1)}, f32[384]{0:T(512)}, u32[]{:S(2)}) copy-start(f32[384]{0:T(512)} %param.18) | copy-start | bytes 4612
  115.8 3.8 %copy-start.11 = (f32[384]{0:T(512)S(1)}, f32[384]{0:T(512)}, u32[]{:S(2)}) copy-start(f32[384]{0:T(512)} %param.21) | copy-start | bytes 4612
  116.9 20.5 %collective-permute-start.3 = (bf16[4,128,384]{2,1,0:T(8,128)(2,1)}, bf16[4,128,384]{2,1,0:T(8,128)(2,1)S(1)}, u32[]{:S(2)}, u32[]{:S(2)}) collective-permute-start(bf16[4,128,384]{2,1,0:T(8,128)(2,1)} %get-tuple-element.19), channel_id=1, source_target_pairs={{1,0},{2,1},{3,2},{4,3},{5,4},{6,5},{7,6},{8,7},{9,8},{10,9},{11,1... | collective-permute-start | bytes 1179656 | tf_op jit(solution)/shard_map/ppermute | solution.py:285
  116.9 20.7 %collective-permute-start.2 = (bf16[4,128,384]{2,1,0:T(8,128)(2,1)}, bf16[4,128,384]{2,1,0:T(8,128)(2,1)}, u32[]{:S(2)}, u32[]{:S(2)}) collective-permute-start(bf16[4,128,384]{2,1,0:T(8,128)(2,1)} %get-tuple-element.20), channel_id=1, source_target_pairs={{0,1},{1,2},{2,3},{3,4},{4,5},{5,6},{6,7},{7,8},{8,9},{9,10},{10,1... | collective-permute-start | bytes 1179656 | tf_op jit(solution)/shard_map/ppermute | solution.py:284
  119.5 3.3 %copy-start = (bf16[3,3,3,384,384]{4,3,2,1,0:T(8,128)(2,1)S(1)}, bf16[3,3,3,384,384]{4,3,2,1,0:T(8,128)(2,1)}, u32[]{:S(2)}) copy-start(bf16[3,3,3,384,384]{4,3,2,1,0:T(8,128)(2,1)} %w_ref.2) | copy-start | bytes 23887876
  124.9 3.1 %copy-start.1 = (bf16[3,1152,1152]{2,1,0:T(8,128)(2,1)}, bf16[3,1152,1152]{2,1,0:T(8,128)(2,1)S(1)}, u32[]{:S(2)}) copy-start(bf16[3,1152,1152]{2,1,0:T(8,128)(2,1)S(1)} %shard_map.159.w_ref) | copy-start | bytes 23887876
  137.6 22.9 %slice-start = ((s8[7962624]{0:T(1024)(128)(4,1)}), s8[4194304]{0:T(1024)(128)(4,1)S(1)}, s32[]{:S(2)}) async-start(s8[7962624]{0:T(1024)(128)(4,1)} %bitcast.22), calls=%async_computation.2 | async-start | bytes 8388608
  137.6 1.3 copy-start.7
  138.9 21.7 %slice-start.1 = ((s8[7962624]{0:T(1024)(128)(4,1)}), s8[3768320]{0:T(1024)(128)(4,1)S(1)}, s32[]{:S(2)}) async-start(s8[7962624]{0:T(1024)(128)(4,1)} %bitcast.22), calls=%async_computation.3 | async-start | bytes 7536640
  155.4 5.1 %copy-start.12 = (f32[384]{0:T(512)S(1)}, f32[384]{0:T(512)}, u32[]{:S(2)}) copy-start(f32[384]{0:T(512)} %param.22) | copy-start | bytes 4612
  155.5 10.3 %collective-permute-start.5 = (bf16[4,128,384]{2,1,0:T(8,128)(2,1)S(1)}, bf16[4,128,384]{2,1,0:T(8,128)(2,1)S(1)}, u32[]{:S(2)}, u32[]{:S(2)}) collective-permute-start(bf16[4,128,384]{2,1,0:T(8,128)(2,1)S(1)} %get-tuple-element.17), channel_id=1, source_target_pairs={{1,0},{2,1},{3,2},{4,3},{5,4},{6,5},{7,6},{8,7},{9,8},{10,9},{11,1... | collective-permute-start | bytes 1179656 | tf_op jit(solution)/shard_map/ppermute | solution.py:285
  160.5 10.5 %collective-permute-start.4 = (bf16[4,128,384]{2,1,0:T(8,128)(2,1)S(1)}, bf16[4,128,384]{2,1,0:T(8,128)(2,1)S(1)}, u32[]{:S(2)}, u32[]{:S(2)}) collective-permute-start(bf16[4,128,384]{2,1,0:T(8,128)(2,1)S(1)} %get-tuple-element.18), channel_id=1, source_target_pairs={{0,1},{1,2},{2,3},{3,4},{4,5},{5,6},{6,7},{7,8},{8,9},{9,10},{10,1... | collective-permute-start | bytes 1179656 | tf_op jit(solution)/shard_map/ppermute | solution.py:284
  160.5 10.5 %copy-start.4 = (bf16[4,2,128,384]{3,2,1,0:T(8,128)(2,1)S(1)}, bf16[4,2,128,384]{3,2,1,0:T(8,128)(2,1)}, u32[]{:S(2)}) copy-start(bf16[4,2,128,384]{3,2,1,0:T(8,128)(2,1)} %x_ref.1) | copy-start | bytes 2359300
  162.6 3.1 %copy-start.2 = (bf16[3,1152,1152]{2,1,0:T(8,128)(2,1)}, bf16[3,1152,1152]{2,1,0:T(8,128)(2,1)S(1)}, u32[]{:S(2)}) copy-start(bf16[3,1152,1152]{2,1,0:T(8,128)(2,1)S(1)} %shard_map.161.w_ref) | copy-start | bytes 23887876

commit v3 on v1

--- a/solution.py
+++ b/solution.py
@@ -11,11 +11,6 @@
 
 def lookup(held_table, values):
     return jnp.sum(jnp.where(held_table, values[None, :], 0), axis=1)
-
-
-def activate(values, gain):
-    scaled = values * lax.rsqrt(jnp.mean(values * values, axis=-1, keepdims=True) + 1e-06)
-    return jax.nn.silu(scaled * gain)
 
 
 def pack(first, second):
@@ -84,26 +79,321 @@
     )(source, rotation, keep, held)
 
 
-def convolve(padded, weight, bias_vec):
-    n_slots = padded.shape[0]
-    n_rows = padded.shape[2] - 2
-    n_cols = padded.shape[3]
-    channels = padded.shape[4]
-    widened = jnp.pad(padded, ((0, 0), (0, 0), (0, 0), (1, 1), (0, 0)))
-    pieces = [
-        widened[:, t_step, y_step : y_step + n_rows, x_step : x_step + n_cols, :]
-        for t_step in range(3)
-        for y_step in range(3)
-        for x_step in range(3)
-    ]
-    patches = jnp.concatenate(pieces, axis=-1).reshape(-1, 27 * channels)
-    result = (
-        jnp.dot(
-            patches, weight.reshape(27 * channels, channels), preferred_element_type=jnp.float32
-        )
-        + bias_vec
-    )
-    return result.reshape(n_slots, n_rows, n_cols, channels)
+VMEM_LIMIT = 40 << 20
+
+
+def call(body, out_shape, operands, scalars=(), scratch=(), flops=0, moved=0, anywhere=()):
+    in_specs = [pl.BlockSpec(memory_space=pltpu.SMEM) for _ in scalars]
+    for k, _ in enumerate(operands):
+        space = pl.ANY if k in anywhere else pltpu.VMEM
+        in_specs.append(pl.BlockSpec(memory_space=space))
+    return pl.pallas_call(
+        body,
+        in_specs=in_specs,
+        out_specs=[pl.BlockSpec(memory_space=pltpu.VMEM) for _ in out_shape],
+        out_shape=list(out_shape),
+        scratch_shapes=list(scratch),
+        cost_estimate=pl.CostEstimate(flops=flops, bytes_accessed=moved, transcendentals=0),
+        compiler_params=pltpu.CompilerParams(vmem_limit_bytes=VMEM_LIMIT),
+    )(*scalars, *operands)
+
+
+def spread(weight):
+    n_t, n_y, n_x, ci, co = weight.shape
+
+    def body(w_ref, p_ref, a_ref):
+        for x in range(n_x):
+            for t in range(n_t - 1):
+                p_ref[t * ci : (t + 1) * ci, x * co : (x + 1) * co] = w_ref[t, 0, x]
+            a_ref[:, x * co : (x + 1) * co] = w_ref[n_t - 1, 0, x]
+
+    return pl.pallas_call(
+        body,
+        grid=(n_y,),
+        in_specs=[pl.BlockSpec((n_t, 1, n_x, ci, co), lambda y: (0, y, 0, 0, 0))],
+        out_specs=[
+            pl.BlockSpec(((n_t - 1) * ci, n_x * co), lambda y: (y, 0)),
+            pl.BlockSpec((ci, n_x * co), lambda y: (y, 0)),
+        ],
+        out_shape=[
+            jax.ShapeDtypeStruct((n_y * (n_t - 1) * ci, n_x * co), weight.dtype),
+            jax.ShapeDtypeStruct((n_y * ci, n_x * co), weight.dtype),
+        ],
+        cost_estimate=pl.CostEstimate(flops=0, bytes_accessed=4 * weight.size, transcendentals=0),
+        compiler_params=pltpu.CompilerParams(vmem_limit_bytes=24 << 20),
+    )(weight)
+
+
+def activated(values, gain):
+    u = values * lax.rsqrt(jnp.mean(values * values, axis=-1, keepdims=True) + 1e-06) * gain
+    return u / (1.0 + jnp.exp(-u))
+
+
+def first_activation(frame, gain):
+    n_slots, n_rows, n_cols, ch = frame.shape
+
+    def body(f_ref, g_ref, o_ref, top_ref, bottom_ref):
+        for s in range(n_slots):
+            for r in range(n_rows):
+                value = activated(f_ref[s, r].astype(jnp.float32), g_ref[...]).astype(jnp.bfloat16)
+                o_ref[s, r] = value
+                if r == 0:
+                    top_ref[s] = value
+                if r == n_rows - 1:
+                    bottom_ref[s] = value
+
+    row = jax.ShapeDtypeStruct((n_slots, n_cols, ch), jnp.bfloat16)
+    return call(
+        body,
+        [jax.ShapeDtypeStruct(frame.shape, jnp.bfloat16), row, row],
+        (frame, gain),
+        flops=10 * frame.size,
+        moved=6 * frame.size,
+    )
+
+
+def folded(acc, ch, cols_first):
+    tiles = acc.shape[0] // CB
+    n_slots = 4
+    blocks = tiles // n_slots
+    lead = (blocks, n_slots) if cols_first else (n_slots, blocks)
+    axis = 0 if cols_first else 1
+
+    def plane(k):
+        value = acc[:, k * ch : (k + 1) * ch].reshape(tiles, CB, ch)
+        return value
+
+    at = lax.broadcasted_iota(jnp.int32, (1, 1, CB, ch), 2)
+    before = pltpu.roll(plane(0), 1, 1).reshape(lead + (CB, ch))
+    after = pltpu.roll(plane(2), CB - 1, 1).reshape(lead + (CB, ch))
+    gap = list(lead) + [CB, ch]
+    gap[axis] = 1
+    gap = jnp.zeros(gap, jnp.float32)
+    before_prev = jnp.concatenate([gap, lax.slice_in_dim(before, 0, blocks - 1, axis=axis)], axis)
+    after_next = jnp.concatenate([lax.slice_in_dim(after, 1, blocks, axis=axis), gap], axis)
+    total = plane(1).reshape(lead + (CB, ch))
+    total += jnp.where(at == 0, before_prev, before)
+    total += jnp.where(at == CB - 1, after_next, after)
+    return total
+
+
+def add_into(o_ref, y, total, cols_first, base=None):
+    if cols_first:
+        o_ref[y] = total if base is None else base[y] + total
+        return
+    for s in range(total.shape[0]):
+        o_ref[y, :, s] = total[s] if base is None else base[y, :, s] + total[s]
+
+
+def masked(edge_ref, k, s, value):
+    return jnp.where(edge_ref[k, s] != 0, value, jnp.zeros_like(value))
+
+
+def dot(a, b):
+    return jnp.dot(a, b, preferred_element_type=jnp.float32)
+
+
+def sums_shape(blocks, n_slots, n_rows, ch):
+    return jax.ShapeDtypeStruct((n_rows, blocks, n_slots, CB, ch), jnp.float32)
+
+
+def current_part(act, above, below, weight, edges):
+    n_slots, n_rows, n_cols, ch = act.shape
+    half = n_slots * n_cols
+
+    def body(edge_ref, act_ref, above_ref, below_ref, w_ref, o_ref, lhs):
+        for y in range(n_rows):
+            for s in range(n_slots):
+                m = s * n_cols
+                rows = [masked(edge_ref, 0, s, above_ref[s])]
+                rows += [act_ref[s, r] for r in range(n_rows)]
+                rows += [masked(edge_ref, 1, s, below_ref[s])]
+                for dy in range(3):
+                    lhs[m : m + n_cols, dy * ch : (dy + 1) * ch] = rows[y + dy]
+            add_into(o_ref, y, folded(dot(lhs[...], w_ref[...]), ch, False), False)
+
+    return call(
+        body,
+        [sums_shape(n_cols // CB, n_slots, n_rows, ch)],
+        (act, above, below, weight),
+        scalars=(edges,),
+        scratch=[pltpu.VMEM((half, 3 * ch), jnp.bfloat16)],
+        flops=2 * n_rows * half * weight.size,
+        moved=2 * weight.size + 8 * act.size,
+    )[0]
+
+
+def own_part(got, weights, sums):
+    n_rows, n_caches, n_frames, blocks, n_slots, _, ch = got.shape
+    half = blocks * n_slots * CB
+    deep = n_frames * ch
+
+    def body(got_ref, w0_ref, w1_ref, z_ref, o0_ref, o1_ref, w0, w1, lhs, sems):
+        copies = []
+        for k, (src, dst) in enumerate(((w0_ref, w0), (w1_ref, w1))):
+            for d in range(3):
+                rows = pl.ds(d * deep, deep)
+                copies.append(pltpu.make_async_copy(src.at[rows], dst.at[rows], sems.at[3 * k + d]))
+        for c in copies:
+            c.start()
+        for k, (w, o_ref, base) in enumerate(((w0, o0_ref, z_ref), (w1, o1_ref, None))):
+            for r in range(n_rows):
+                for f in range(n_frames):
+                    lo = r * deep + f * ch
+                    lhs[:, lo : lo + ch] = got_ref[r, k, f].reshape(half, ch)
+            copies[3 * k].wait()
+            copies[3 * k + 1].wait()
+            add_into(o_ref, 1, folded(dot(lhs[...], w[0 : 2 * deep]), ch, True), True, base)
+            copies[3 * k + 2].wait()
+            add_into(o_ref, 0, folded(dot(lhs[...], w[deep : 3 * deep]), ch, True), True, base)
+
+    out = sums_shape(blocks, n_slots, n_rows, ch)
+    whole = weights[0]
+    return call(
+        body,
+        [out, out],
+        (got, *weights, sums),
+        scratch=[
+            pltpu.VMEM(whole.shape, whole.dtype),
+            pltpu.VMEM(whole.shape, whole.dtype),
+            pltpu.VMEM((half, n_rows * deep), jnp.bfloat16),
+            pltpu.SemaphoreType.DMA((6,)),
+        ],
+        flops=2 * 4 * half * 2 * deep * whole.shape[1],
+        moved=4 * whole.size,
+        anywhere=(1, 2),
+    )
+
+
+def side_sums(edge_ref, k, side_ref, w, lhs):
+    n_frames, blocks, n_slots, _, ch = side_ref.shape
+    for s in range(n_slots):
+        for f in range(n_frames):
+            value = masked(edge_ref, k, s, side_ref[f, :, s])
+            lhs[:, s, :, f * ch : (f + 1) * ch] = value
+    half = blocks * n_slots * CB
+    return folded(dot(lhs[...].reshape(half, n_frames * ch), w), ch, True)
+
+
+def second_activation(above, below, weight, sums, bias, gain, edges):
+    n_frames, blocks, n_slots, _, ch = above.shape
+    n_rows, n_cols, deep = sums.shape[0], blocks * CB, n_frames * ch
+
+    def body(edge_ref, above_ref, below_ref, w_ref, z_ref, b_ref, g_ref, o_ref, top_ref, bottom_ref, lhs, wv, sems):
+        copies = [
+            pltpu.make_async_copy(w_ref.at[pl.ds(2 * k * deep, deep)], wv.at[k], sems.at[k])
+            for k in range(2)
+        ]
+        for c in copies:
+            c.start()
+        for y, side in enumerate((above_ref, below_ref)):
+            copies[y].wait()
+            total = side_sums(edge_ref, y, side, wv[y], lhs) + z_ref[y] + b_ref[...]
+            for s in range(n_slots):
+                value = activated(total[:, s].reshape(n_cols, ch), g_ref[...]).astype(jnp.bfloat16)
+                o_ref[s, y] = value
+                if y == 0:
+                    top_ref[s] = value
+                else:
+                    bottom_ref[s] = value
+
+    row = jax.ShapeDtypeStruct((n_slots, n_cols, ch), jnp.bfloat16)
+    return call(
+        body,
+        [jax.ShapeDtypeStruct((n_slots, n_rows, n_cols, ch), jnp.bfloat16), row, row],
+        (above, below, weight, sums, bias, gain),
+        scalars=(edges,),
+        scratch=[
+            pltpu.VMEM((blocks, n_slots, CB, deep), jnp.bfloat16),
+            pltpu.VMEM((2, deep, weight.shape[1]), weight.dtype),
+            pltpu.SemaphoreType.DMA((2,)),
+        ],
+        flops=4 * n_slots * n_cols * deep * weight.shape[1],
+        moved=4 * deep * weight.shape[1],
+        anywhere=(2,),
+    )
+
+
+def before_sides(above, below, act, w_prior, w_act, sums, got, act_first, edges):
+    n_frames, blocks, n_slots, _, ch = above.shape
+    n_rows, n_cols, deep = sums.shape[0], blocks * CB, n_frames * ch
+
+    def body(edge_ref, above_ref, below_ref, act_ref, w_ref, wa_ref, z_ref, got_ref, act1_ref, o_ref, n1_ref, n2_ref, lhs, lhs2, wv, wa, sems):
+        copies = [pltpu.make_async_copy(wa_ref, wa, sems.at[2])]
+        copies += [
+            pltpu.make_async_copy(w_ref.at[pl.ds(2 * k * deep, deep)], wv.at[k], sems.at[k])
+            for k in range(2)
+        ]
+        for c in copies:
+            c.start()
+        for s in range(n_slots):
+            for r in range(n_rows):
+                own = act_ref[s, r]
+                lhs2[s * n_cols : (s + 1) * n_cols, r * ch : (r + 1) * ch] = own
+                n2_ref[s, 1, r] = own
+                n1_ref[s, 1, r] = act1_ref[s, r]
+                n1_ref[s, 0, r] = got_ref[r, 0, 1, :, s].reshape(n_cols, ch)
+                n2_ref[s, 0, r] = got_ref[r, 1, 1, :, s].reshape(n_cols, ch)
+        copies[0].wait()
+        for y in range(n_rows):
+            lo = (1 - y) * ch
+            add_into(o_ref, y, folded(dot(lhs2[...], wa[lo : lo + 2 * ch]), ch, False), False, z_ref)
+        for y, side in enumerate((above_ref, below_ref)):
+            copies[1 + y].wait()
+            o_ref[y] += side_sums(edge_ref, y, side, wv[y], lhs)
+
+    nxt = jax.ShapeDtypeStruct((n_slots, 2, n_rows, n_cols, ch), jnp.bfloat16)
+    return call(
+        body,
+        [jax.ShapeDtypeStruct(sums.shape, jnp.float32), nxt, nxt],
+        (above, below, act, w_prior, w_act, sums, got, act_first),
+        scalars=(edges,),
+        scratch=[
+            pltpu.VMEM((blocks, n_slots, CB, deep), jnp.bfloat16),
+            pltpu.VMEM((n_slots * n_cols, 2 * ch), jnp.bfloat16),
+            pltpu.VMEM((2, deep, w_prior.shape[1]), w_prior.dtype),
+            pltpu.VMEM(w_act.shape, w_act.dtype),
+            pltpu.SemaphoreType.DMA((3,)),
+        ],
+        flops=8 * n_slots * n_cols * deep * w_prior.shape[1],
+        moved=4 * deep * w_prior.shape[1],
+        anywhere=(3, 4),
+    )
+
+
+def last_part(above, below, w_act, sums, bias, frame, edges):
+    n_slots, n_rows, n_cols, ch = frame.shape
+
+    def body(edge_ref, above_ref, below_ref, w_ref, z_ref, b_ref, f_ref, o_ref, lhs, wv, sems):
+        copies = [
+            pltpu.make_async_copy(w_ref.at[pl.ds(2 * k * ch, ch)], wv.at[k], sems.at[k])
+            for k in range(2)
+        ]
+        for c in copies:
+            c.start()
+        for y, side in enumerate((above_ref, below_ref)):
+            for s in range(n_slots):
+                lhs[s * n_cols : (s + 1) * n_cols] = masked(edge_ref, y, s, side[s])
+            copies[y].wait()
+            total = folded(dot(lhs[...], wv[y]), ch, False)
+            for s in range(n_slots):
+                value = (total[s] + z_ref[y, :, s] + b_ref[...]).reshape(n_cols, ch)
+                o_ref[s, y] = (value + f_ref[s, y].astype(jnp.float32)).astype(jnp.bfloat16)
+
+    return call(
+        body,
+        [jax.ShapeDtypeStruct(frame.shape, jnp.bfloat16)],
+        (above, below, w_act, sums, bias, frame),
+        scalars=(edges,),
+        scratch=[
+            pltpu.VMEM((n_slots * n_cols, ch), jnp.bfloat16),
+            pltpu.VMEM((2, ch, w_act.shape[1]), w_act.dtype),
+            pltpu.SemaphoreType.DMA((2,)),
+        ],
+        flops=4 * n_slots * n_cols * ch * w_act.shape[1],
+        moved=4 * ch * w_act.shape[1],
+        anywhere=(2,),
+    )[0]
 
 
 def local(
@@ -141,41 +431,48 @@
     start = my_group * n_slots
     my_number = lax.dynamic_slice_in_dim((my_tile - shift_after) % n_tiles, start, n_slots)
 
+    edges = jnp.stack([my_number != 0, my_number != n_tiles - 1]).astype(jnp.int32)
+    down = [(i, (i + 1) % n_tiles) for i in range(n_tiles)]
+    up = [((i + 1) % n_tiles, i) for i in range(n_tiles)]
+
+    def from_above(row):
+        return lax.ppermute(row, "tile", down)
+
+    def from_below(row):
+        return lax.ppermute(row, "tile", up)
+
     sent = pack(cache_first, cache_second).reshape(n_groups * n_tiles, n_slots, CB, ch)
     held = lax.all_to_all(sent, BOTH, 0, 0, tiled=True)
+
+    w_prior_1, w_act_1 = spread(conv_first)
+    w_prior_2, w_act_2 = spread(conv_second)
+    act_first, top, bottom = first_activation(frame_in, gain_first[None])
+    sums_1 = current_part(act_first, from_above(bottom), from_below(top), w_act_1, edges)
+    held, sums_1, w_prior_1, w_prior_2, w_act_2 = lax.optimization_barrier(
+        (held, sums_1, w_prior_1, w_prior_2, w_act_2)
+    )
+
     moved = permute(held.reshape(n_groups, n_tiles, n_slots, CB, ch), source, rotation, keep)
     got = lax.all_to_all(
         moved.reshape(n_groups * n_tiles, n_slots, CB, ch), BOTH, 0, 0, tiled=True
     )
     got = got.reshape(n_rows, 2, 2, blocks, n_slots, CB, ch)
 
-    down = [(i, (i + 1) % n_tiles) for i in range(n_tiles)]
-    up = [((i + 1) % n_tiles, i) for i in range(n_tiles)]
-    above = lax.ppermute(got[n_rows - 1], "tile", down)
-    below = lax.ppermute(got[0], "tile", up)
-    rows = jnp.concatenate([above[None], got, below[None]], axis=0)
-    rows = rows.transpose(1, 4, 2, 0, 3, 5, 6).reshape(
-        2, n_slots, 2, n_rows + 2, n_cols, ch
-    )
-    border = jnp.ones((n_slots, n_rows + 2), jnp.bfloat16)
-    border = border.at[:, 0].set((my_number != 0).astype(jnp.bfloat16))
-    border = border.at[:, -1].set((my_number != n_tiles - 1).astype(jnp.bfloat16))
-    border = border[:, None, :, None, None]
-
-    def conv_layer(kept, activation, weight, bias_vec):
-        head = lax.ppermute(activation[:, -1:], "tile", down)
-        tail = lax.ppermute(activation[:, :1], "tile", up)
-        act = jnp.concatenate([head, activation, tail], axis=1)
-        padded = jnp.concatenate([kept, act[:, None]], axis=1)
-        return convolve(padded * border, weight, bias_vec)
-
-    act_first = activate(frame_in.astype(jnp.float32), gain_first).astype(jnp.bfloat16)
-    hidden = conv_layer(rows[0], act_first, conv_first, bias_first)
-    act_second = activate(hidden, gain_second).astype(jnp.bfloat16)
-    second_out = conv_layer(rows[1], act_second, conv_second, bias_second)
-    mixed_frame = (second_out + frame_in.astype(jnp.float32)).astype(jnp.bfloat16)
-    next_first = jnp.stack([rows[0, :, 1, 1:-1], act_first], axis=1)
-    next_second = jnp.stack([rows[1, :, 1, 1:-1], act_second], axis=1)
+    above_1 = from_above(got[n_rows - 1, 0])
+    below_1 = from_below(got[0, 0])
+    above_2 = from_above(got[n_rows - 1, 1])
+    below_2 = from_below(got[0, 1])
+    sums_1, sums_2 = own_part(got, (w_prior_1, w_prior_2), sums_1)
+    act_second, top, bottom = second_activation(
+        above_1, below_1, w_prior_1, sums_1, bias_first[None], gain_second[None], edges
+    )
+    side_above, side_below = from_above(bottom), from_below(top)
+    sums_2, next_first, next_second = before_sides(
+        above_2, below_2, act_second, w_prior_2, w_act_2, sums_2, got, act_first, edges
+    )
+    mixed_frame = last_part(
+        side_above, side_below, w_act_2, sums_2, bias_second[None], frame_in, edges
+    )
     return (mixed_frame, next_first, next_second)
 
 

time: 262 us -> 164 us (0.63)
  local copies, waits for them, and re-layouts: 82.7 us -> 23.5 us
  waiting for transfers between devices: 52.9 us -> 17.3 us
  Pallas kernels: 5.03 us -> 40.6 us
  matrix products: 30.3 us -> 0 us
  other arithmetic: 17 us -> 0.95 us
  starting transfers between devices: 26.6 us -> 31.6 us
    all_to_all x1, waiting for transfers between devices: 41.6 us -> 0.01 us  [local(): held = lax.all_to_all(sent, BOTH, 0, 0, tiled=True)]
    pallas_call x0 -> x8, Pallas kernels: none -> 35.5 us  [the longest x6 32.4 us: call(): pl.pallas_call(body, in_specs=in_specs, out_specs=[pl.BlockSpec(memory_sp...]
    unnamed x91 -> x50, local copies, waits for them, and re-layouts: 58.2 us -> 23.1 us
    dot_general x2 -> x0, matrix products: 30.3 us -> none  [convolve(): jnp.dot(patches, weight.reshape(27 * channels, channels), preferred_eleme...]
    slice x9 -> x0, local copies, waits for them, and re-layouts: 17.8 us -> none  [the longest x6 16.4 us: convolve(): widened[:, t_step, y_step:y_step + n_rows, x_step:x_step + n_cols, :]]
    ppermute x6 -> x8, waiting for transfers between devices: 11.3 us -> 17.3 us  [the longest x4 17.2 us: from_above(): return lax.ppermute(row, 'tile', down)]
    another operation x5 -> x1, other arithmetic: 5.52 us -> 0.08 us  [local(): jnp.stack([my_number != 0, my_number != n_tiles - 1]).astype(jnp.int32)]
    ppermute x6 -> x8, starting transfers between devices: 15.5 us -> 20.4 us  [the longest x4 20.2 us: from_below(): return lax.ppermute(row, 'tile', up)]
  transfers between devices with their start and end apart: 7 -> 9, of which waited for: 4 -> 1; matrix products, arithmetic and copies ran while one was open for 5% -> 1% of each run, Pallas kernels for 0% -> 20%
where the time goes in v3:
time: 164 us; the launch traced here: 163 us
  blocking collectives  48.1 us (29%)
  Pallas kernels  40.6 us (25%)
  starting transfers between devices  31.6 us (19%)
  local copies, waits for them, and re-layouts  23.5 us (14%)
  waiting for transfers between devices  17.3 us (11%)
    all_to_all x1, blocking collectives, local(): lax.all_to_all(moved.reshape(n_groups * n_tiles, n_slots, CB, ch), BOTH,...  48.1 us
    pallas_call x6, Pallas kernels, call(): pl.pallas_call(body, in_specs=in_specs, out_specs=[pl.BlockSpec(memory_sp...  32.4 us
    unnamed x50, local copies, waits for them, and re-layouts  23.1 us
    ppermute x4, starting transfers between devices, from_below(): return lax.ppermute(row, 'tile', up)  20.2 us
    ppermute x4, waiting for transfers between devices, from_above(): return lax.ppermute(row, 'tile', down)  17.2 us
    all_to_all x1, starting transfers between devices, local(): held = lax.all_to_all(sent, BOTH, 0, 0, tiled=True)  11.1 us
  transfers between devices with their start and end apart: 9, of which 1 were waited for; matrix products, arithmetic and copies ran while one was open for 1% of the time, Pallas kernels for 20%

profile of v3, /device:TPU:0, one launch (start us, length us, event | category | flops | bytes accessed | tf_op | source)
XLA Modules:
  0.0 163.1 jit_solution(15054873301121021925)
XLA Ops:
  0.6 1.4 copy-done.8
  2.0 1.4 copy-done.9
  3.4 2.3 %shard_map.157 = bf16[2,2,2,16,4,8,384]{6,5,4,3,2,1,0:T(8,128)(2,1)} custom-call(bf16[4,2,2,128,384]{4,3,2,1,0:T(8,128)(2,1)S(1)} %copy-done.8, bf16[4,2,2,128,384]{4,3,2,1,0:T(8,128)(2,1)S(1)} %copy-done.9), custom_call_target="tpu_custom_call" | custom-call | tf_op jit(solution)/shard_map/pallas_call | solution.py:27
  5.8 11.1 %all-to-all-start = ((bf16[128,4,8,384]{3,2,1,0:T(8,128)(2,1)}), bf16[128,4,8,384]{3,2,1,0:T(8,128)(2,1)S(1)}, u32[]{:S(2)}, u32[]{:S(2)}) async-start(bf16[128,4,8,384]{3,2,1,0:T(8,128)(2,1)} %bitcast.2), calls=%async_computation | async-start | bytes 6291456 | tf_op jit(solution)/shard_map/all_to_all | solution.py:445
  17.0 0.0 copy-start.6
  17.0 1.1 copy-done.6
  18.1 1.3 shard_map.158
  19.4 0.9 copy-done.10
  20.3 0.0 collective-permute-start
  20.3 5.1 %collective-permute-start.1 = (bf16[4,128,384]{2,1,0:T(8,128)(2,1)S(1)}, bf16[4,128,384]{2,1,0:T(8,128)(2,1)}, u32[]{:S(2)}, u32[]{:S(2)}) collective-permute-start(bf16[4,128,384]{2,1,0:T(8,128)(2,1)S(1)} %get-tuple-element.25), channel_id=1, source_target_pairs={{1,0},{2,1},{3,2},{4,3},{5,4},{6,5},{7,6},{8,7},{9,8},{10,9},{11,1... | collective-permute-start | bytes 1179656 | tf_op jit(solution)/shard_map/ppermute | solution.py:442
  25.3 3.3 %copy-done.2 = bf16[3,3,3,384,384]{4,3,2,1,0:T(8,128)(2,1)S(1)} copy-done((bf16[3,3,3,384,384]{4,3,2,1,0:T(8,128)(2,1)S(1)}, bf16[3,3,3,384,384]{4,3,2,1,0:T(8,128)(2,1)}, u32[]{:S(2)}) %copy-start.2) | copy-done | bytes 7962648
  28.6 1.6 shard_map.159
  30.2 2.3 %copy-done.5 = bf16[2304,1152]{1,0:T(8,128)(2,1)} copy-done((bf16[2304,1152]{1,0:T(8,128)(2,1)}, bf16[2304,1152]{1,0:T(8,128)(2,1)S(1)}, u32[]{:S(2)}) %copy-start.5) | copy-done | bytes 5308440
  32.5 1.5 copy-done.13
  34.0 3.3 %copy-done.3 = bf16[3,3,3,384,384]{4,3,2,1,0:T(8,128)(2,1)S(1)} copy-done((bf16[3,3,3,384,384]{4,3,2,1,0:T(8,128)(2,1)S(1)}, bf16[3,3,3,384,384]{4,3,2,1,0:T(8,128)(2,1)}, u32[]{:S(2)}) %copy-start.3) | copy-done | bytes 7962648
  37.3 1.6 shard_map.161
  38.9 1.5 copy-done
  40.3 2.4 %copy-done.4 = bf16[2304,1152]{1,0:T(8,128)(2,1)} copy-done((bf16[2304,1152]{1,0:T(8,128)(2,1)}, bf16[2304,1152]{1,0:T(8,128)(2,1)S(1)}, u32[]{:S(2)}) %copy-start.4) | copy-done | bytes 5308440
  42.7 0.8 select_reduce_fusion
  43.6 0.1 compare_bitcast_fusion.1
  43.7 17.2 %collective-permute-done.above_ref = bf16[4,128,384]{2,1,0:T(8,128)(2,1)} collective-permute-done((bf16[4,128,384]{2,1,0:T(8,128)(2,1)}, bf16[4,128,384]{2,1,0:T(8,128)(2,1)}, u32[]{:S(2)}, u32[]{:S(2)}) %collective-permute-start) | collective-permute-done | bytes 393248 | tf_op jit(solution)/shard_map/ppermute | solution.py:439
  60.9 0.0 collective-permute-done.1.below_ref
  60.9 1.1 copy-done.11
  62.1 1.7 %copy-done.14 = bf16[1152,1152]{1,0:T(8,128)(2,1)S(1)} copy-done((bf16[1152,1152]{1,0:T(8,128)(2,1)S(1)}, bf16[1152,1152]{1,0:T(8,128)(2,1)}, u32[]{:S(2)}) %copy-start.14) | copy-done | bytes 2654232
  63.8 4.7 %shard_map.160.z_ref = f32[2,16,4,8,384]{4,3,2,1,0:T(8,128)S(1)} custom-call(s32[2,4]{1,0:T(2,128)S(1)} %add_convert_fusion.edge_ref, bf16[4,2,128,384]{3,2,1,0:T(8,128)(2,1)S(1)} %copy-done.11, bf16[4,128,384]{2,1,0:T(8,128)(2,1)} %collective-permute-done.above_ref, bf16[4,128,384]{2,1,0:T(8,128)(2,1)} %collective-permute-done.1.below_ref, ...), custom_call_target="tpu_custom_call" | custom-call | flops 2717908992 | bytes 5799936 | tf_op jit(solution)/shard_map/pallas_call | solution.py:90
  68.5 0.0 copy-start.15
  68.5 1.1 copy-done.15
  69.7 2.8 %shard_map.162 = bf16[4,32,4,8,384]{4,3,2,1,0:T(8,128)(2,1)S(1)} custom-call(s32[16]{0:T(128)S(1)} %get-tuple-element.45.source_ref, s32[16]{0:T(128)S(1)} %get-tuple-element.51.rotation_ref, s32[16]{0:T(128)S(1)} %compare_convert_fusion.keep_ref, bf16[4,32,4,8,384]{4,3,2,1,0:T(8,128)(2,1)S(1)} %bitcast.19), custom_call_target="tpu_custom_call" | custom-call | tf_op jit(solution)/shard_map/pallas_call | solution.py:62
  72.5 0.0 slice-start.1
  72.5 48.1 %all_to_all.10 = bf16[128,4,8,384]{3,2,1,0:T(8,128)(2,1)S(1)} all-to-all(bf16[128,4,8,384]{3,2,1,0:T(8,128)(2,1)S(1)} %bitcast.20), channel_id=1, replica_groups=mesh['stream'=4,'tile'=32] {'stream','tile'}, dimensions={0} | all-to-all | bytes 6291456 | tf_op jit(solution)/shard_map/all_to_all | solution.py:456
  120.6 0.4 slice_bitcast_fusion
  121.0 0.1 collective-permute-start.2
  121.1 5.1 %collective-permute-start.3 = (bf16[2,16,4,8,384]{4,3,2,1,0:T(8,128)(2,1)S(1)}, bf16[2,16,4,8,384]{4,3,2,1,0:T(8,128)(2,1)S(1)}, u32[]{:S(2)}, u32[]{:S(2)}) collective-permute-start(bf16[2,16,4,8,384]{4,3,2,1,0:T(8,128)(2,1)S(1)} %get-tuple-element.49), channel_id=1, source_target_pairs={{1,0},{2,1},{3,2},{4,3},{5,4},{6,5},{7,6},{8,7},{9,8},{10,9},{11,1... | collective-permute-start | bytes 2359304 | tf_op jit(solution)/shard_map/ppermute | solution.py:442
  126.1 0.1 collective-permute-start.6
  126.2 5.1 %collective-permute-start.7 = (bf16[2,16,4,8,384]{4,3,2,1,0:T(8,128)(2,1)S(1)}, bf16[2,16,4,8,384]{4,3,2,1,0:T(8,128)(2,1)S(1)}, u32[]{:S(2)}, u32[]{:S(2)}) collective-permute-start(bf16[2,16,4,8,384]{4,3,2,1,0:T(8,128)(2,1)S(1)} %get-tuple-element.47), channel_id=1, source_target_pairs={{1,0},{2,1},{3,2},{4,3},{5,4},{6,5},{7,6},{8,7},{9,8},{10,9},{11,1... | collective-permute-start | bytes 2359304 | tf_op jit(solution)/shard_map/ppermute | solution.py:442
  131.3 11.7 %shard_map.163 = (f32[2,16,4,8,384]{4,3,2,1,0:T(8,128)S(1)}, f32[2,16,4,8,384]{4,3,2,1,0:T(8,128)S(1)}) custom-call(bf16[2,2,2,16,4,8,384]{6,5,4,3,2,1,0:T(8,128)(2,1)S(1)} %bitcast.17, bf16[2304,1152]{1,0:T(8,128)(2,1)S(1)} %bitcast.22, bf16[2304,1152]{1,0:T(8,128)(2,1)} %copy-done.4, f32[2,16,4,8,384]{4,3,2,1,0:T(8,128)S(1)} %copy-done.16), custom_call_target="tpu_custom_call" | custom-call | flops 7247757312 | bytes 10616832 | tf_op jit(solution)/shard_map/pallas_call | solution.py:90
  143.0 0.0 collective-permute-done.3.below_ref
  143.0 0.0 copy-start.20
  143.0 0.0 copy-start.12
  143.0 4.7 %shard_map.164 = (bf16[4,2,128,384]{3,2,1,0:T(8,128)(2,1)S(1)}, bf16[4,128,384]{2,1,0:T(8,128)(2,1)S(1)}, bf16[4,128,384]{2,1,0:T(8,128)(2,1)S(1)}) custom-call(s32[2,4]{1,0:T(2,128)S(1)} %add_convert_fusion.edge_ref, bf16[2,16,4,8,384]{4,3,2,1,0:T(8,128)(2,1)S(1)} %collective-permute-done.2.above_ref, ...), custom_call_target="tpu_custom_call" | custom-call | flops 1811939328 | bytes 3538944 | tf_op jit(solution)/shard_map/pallas_call | solution.py:90
  147.7 0.1 collective-permute-start.4
  147.8 5.1 %collective-permute-start.5 = (bf16[4,128,384]{2,1,0:T(8,128)(2,1)S(1)}, bf16[4,128,384]{2,1,0:T(8,128)(2,1)S(1)}, u32[]{:S(2)}, u32[]{:S(2)}) collective-permute-start(bf16[4,128,384]{2,1,0:T(8,128)(2,1)S(1)} %get-tuple-element.36), channel_id=1, source_target_pairs={{1,0},{2,1},{3,2},{4,3},{5,4},{6,5},{7,6},{8,7},{9,8},{10,9},{11,1... | collective-permute-start | bytes 1179656 | tf_op jit(solution)/shard_map/ppermute | solution.py:442
  152.9 0.0 collective-permute-done.7.below_ref
  152.9 0.0 copy-start.7
  152.9 6.4 %shard_map.165 = (f32[2,16,4,8,384]{4,3,2,1,0:T(8,128)S(1)}, bf16[4,2,2,128,384]{4,3,2,1,0:T(8,128)(2,1)}, bf16[4,2,2,128,384]{4,3,2,1,0:T(8,128)(2,1)}) custom-call(s32[2,4]{1,0:T(2,128)S(1)} %add_convert_fusion.edge_ref, bf16[2,16,4,8,384]{4,3,2,1,0:T(8,128)(2,1)S(1)} %collective-permute-done.6.above_ref, ...), custom_call_target="tpu_custom_call" | custom-call | flops 3623878656 | bytes 3538944 | tf_op jit(solution)/shard_map/pallas_call | solution.py:90
  159.3 0.0 collective-permute-done.4.above_ref
  159.4 0.0 collective-permute-done.5.below_ref
  159.4 3.6 %shard_map.166 = bf16[4,2,128,384]{3,2,1,0:T(8,128)(2,1)} custom-call(s32[2,4]{1,0:T(2,128)S(1)} %add_convert_fusion.edge_ref, bf16[4,128,384]{2,1,0:T(8,128)(2,1)S(1)} %collective-permute-done.4.above_ref, bf16[4,128,384]{2,1,0:T(8,128)(2,1)S(1)} %collective-permute-done.5.below_ref, bf16[1152,1152]{1,0:T(8,128)(2,1)S(1)} %copy-done.1, ...), custom_call_target="tpu_custom_call" | custom-call | flops 905969664 | bytes 1769472 | tf_op jit(solution)/shard_map/pallas_call | solution.py:90
  (42 shorter events, 0.1 us)
Async XLA Ops:
  0.6 1.4 copy-start.8
  2.0 1.4 copy-start.9
  5.8 11.2 %copy-start.17 = (f32[384]{0:T(512)S(1)}, f32[384]{0:T(512)}, u32[]{:S(2)}) copy-start(f32[384]{0:T(512)} %param.17) | copy-start | bytes 4612
  5.8 63.9 %all-to-all-start = ((bf16[128,4,8,384]{3,2,1,0:T(8,128)(2,1)}), bf16[128,4,8,384]{3,2,1,0:T(8,128)(2,1)S(1)}, u32[]{:S(2)}, u32[]{:S(2)}) async-start(bf16[128,4,8,384]{3,2,1,0:T(8,128)(2,1)} %bitcast.2), calls=%async_computation | async-start | bytes 6291456 | tf_op jit(solution)/shard_map/all_to_all | solution.py:445
  17.0 1.1 copy-start.6
  19.4 0.9 copy-start.10
  20.3 40.7 %collective-permute-start = (bf16[4,128,384]{2,1,0:T(8,128)(2,1)}, bf16[4,128,384]{2,1,0:T(8,128)(2,1)}, u32[]{:S(2)}, u32[]{:S(2)}) collective-permute-start(bf16[4,128,384]{2,1,0:T(8,128)(2,1)} %get-tuple-element.24), channel_id=1, source_target_pairs={{0,1},{1,2},{2,3},{3,4},{4,5},{5,6},{6,7},{7,8},{8,9},{9,10},{10,1... | collective-permute-start | bytes 1179656 | tf_op jit(solution)/shard_map/ppermute | solution.py:439
  20.3 40.7 %collective-permute-start.1 = (bf16[4,128,384]{2,1,0:T(8,128)(2,1)S(1)}, bf16[4,128,384]{2,1,0:T(8,128)(2,1)}, u32[]{:S(2)}, u32[]{:S(2)}) collective-permute-start(bf16[4,128,384]{2,1,0:T(8,128)(2,1)S(1)} %get-tuple-element.25), channel_id=1, source_target_pairs={{1,0},{2,1},{3,2},{4,3},{5,4},{6,5},{7,6},{8,7},{9,8},{10,9},{11,1... | collective-permute-start | bytes 1179656 | tf_op jit(solution)/shard_map/ppermute | solution.py:442
  25.3 3.3 %copy-start.2 = (bf16[3,3,3,384,384]{4,3,2,1,0:T(8,128)(2,1)S(1)}, bf16[3,3,3,384,384]{4,3,2,1,0:T(8,128)(2,1)}, u32[]{:S(2)}) copy-start(bf16[3,3,3,384,384]{4,3,2,1,0:T(8,128)(2,1)} %w_ref.2) | copy-start | bytes 23887876
  30.2 2.3 %copy-start.5 = (bf16[2304,1152]{1,0:T(8,128)(2,1)}, bf16[2304,1152]{1,0:T(8,128)(2,1)S(1)}, u32[]{:S(2)}) copy-start(bf16[2304,1152]{1,0:T(8,128)(2,1)S(1)} %get-tuple-element.31.w0_ref.w_ref) | copy-start | bytes 15925252
  32.5 1.5 copy-start.13
  34.0 3.3 %copy-start.3 = (bf16[3,3,3,384,384]{4,3,2,1,0:T(8,128)(2,1)S(1)}, bf16[3,3,3,384,384]{4,3,2,1,0:T(8,128)(2,1)}, u32[]{:S(2)}) copy-start(bf16[3,3,3,384,384]{4,3,2,1,0:T(8,128)(2,1)} %w_ref.3) | copy-start | bytes 23887876
  37.3 5.4 %copy-start.21 = (s32[16]{0:T(128)S(1)}, s32[16]{0:T(128)}, u32[]{:S(2)}) copy-start(s32[16]{0:T(128)} %param.27) | copy-start | bytes 196
  37.3 5.4 %copy-start.22 = (s32[16]{0:T(128)S(1)}, s32[16]{0:T(128)}, u32[]{:S(2)}) copy-start(s32[16]{0:T(128)} %param.24) | copy-start | bytes 196
  38.8 1.5 copy-start
  40.3 2.4 %copy-start.4 = (bf16[2304,1152]{1,0:T(8,128)(2,1)}, bf16[2304,1152]{1,0:T(8,128)(2,1)S(1)}, u32[]{:S(2)}) copy-start(bf16[2304,1152]{1,0:T(8,128)(2,1)S(1)} %get-tuple-element.32.w1_ref.w_ref) | copy-start | bytes 15925252
  60.9 1.1 copy-start.11
  62.1 1.7 %copy-start.14 = (bf16[1152,1152]{1,0:T(8,128)(2,1)S(1)}, bf16[1152,1152]{1,0:T(8,128)(2,1)}, u32[]{:S(2)}) copy-start(bf16[1152,1152]{1,0:T(8,128)(2,1)} %copy-done.13) | copy-start | bytes 7962628
  68.5 1.1 copy-start.15
  69.7 61.6 %slice-start = ((s8[5308416]{0:T(1024)(128)(4,1)}), s8[4194304]{0:T(1024)(128)(4,1)S(1)}, s32[]{:S(2)}) async-start(s8[5308416]{0:T(1024)(128)(4,1)} %bitcast.21), calls=%async_computation.2 | async-start | bytes 8388608
  72.5 58.8 %slice-start.1 = ((s8[5308416]{0:T(1024)(128)(4,1)}), s8[1114112]{0:T(1024)(128)(4,1)S(1)}, s32[]{:S(2)}) async-start(s8[5308416]{0:T(1024)(128)(4,1)} %bitcast.21), calls=%async_computation.3 | async-start | bytes 2228224
  120.6 5.5 %copy-start.18 = (f32[384]{0:T(512)S(1)}, f32[384]{0:T(512)}, u32[]{:S(2)}) copy-start(f32[384]{0:T(512)} %param.21) | copy-start | bytes 4612
  120.6 5.5 %copy-start.19 = (f32[384]{0:T(512)S(1)}, f32[384]{0:T(512)}, u32[]{:S(2)}) copy-start(f32[384]{0:T(512)} %param.18) | copy-start | bytes 4612
  120.6 10.7 %copy-start.16 = (f32[2,16,4,8,384]{4,3,2,1,0:T(8,128)S(1)}, f32[2,16,4,8,384]{4,3,2,1,0:T(8,128)}, u32[]{:S(2)}) copy-start(f32[2,16,4,8,384]{4,3,2,1,0:T(8,128)} %copy-done.15) | copy-start | bytes 4718596
  121.0 22.0 %collective-permute-start.2 = (bf16[2,16,4,8,384]{4,3,2,1,0:T(8,128)(2,1)S(1)}, bf16[2,16,4,8,384]{4,3,2,1,0:T(8,128)(2,1)S(1)}, u32[]{:S(2)}, u32[]{:S(2)}) collective-permute-start(bf16[2,16,4,8,384]{4,3,2,1,0:T(8,128)(2,1)S(1)} %get-tuple-element.50), channel_id=1, source_target_pairs={{0,1},{1,2},{2,3},{3,4},{4,5},{5,6},{6,7},{7,8},{8,9},{9,10},{10,1... | collective-permute-start | bytes 2359304 | tf_op jit(solution)/shard_map/ppermute | solution.py:439
  121.1 21.9 %collective-permute-start.3 = (bf16[2,16,4,8,384]{4,3,2,1,0:T(8,128)(2,1)S(1)}, bf16[2,16,4,8,384]{4,3,2,1,0:T(8,128)(2,1)S(1)}, u32[]{:S(2)}, u32[]{:S(2)}) collective-permute-start(bf16[2,16,4,8,384]{4,3,2,1,0:T(8,128)(2,1)S(1)} %get-tuple-element.49), channel_id=1, source_target_pairs={{1,0},{2,1},{3,2},{4,3},{5,4},{6,5},{7,6},{8,7},{9,8},{10,9},{11,1... | collective-permute-start | bytes 2359304 | tf_op jit(solution)/shard_map/ppermute | solution.py:442
  126.1 26.7 %collective-permute-start.6 = (bf16[2,16,4,8,384]{4,3,2,1,0:T(8,128)(2,1)S(1)}, bf16[2,16,4,8,384]{4,3,2,1,0:T(8,128)(2,1)S(1)}, u32[]{:S(2)}, u32[]{:S(2)}) collective-permute-start(bf16[2,16,4,8,384]{4,3,2,1,0:T(8,128)(2,1)S(1)} %get-tuple-element.48), channel_id=1, source_target_pairs={{0,1},{1,2},{2,3},{3,4},{4,5},{5,6},{6,7},{7,8},{8,9},{9,10},{10,1... | collective-permute-start | bytes 2359304 | tf_op jit(solution)/shard_map/ppermute | solution.py:439
  126.2 26.6 %collective-permute-start.7 = (bf16[2,16,4,8,384]{4,3,2,1,0:T(8,128)(2,1)S(1)}, bf16[2,16,4,8,384]{4,3,2,1,0:T(8,128)(2,1)S(1)}, u32[]{:S(2)}, u32[]{:S(2)}) collective-permute-start(bf16[2,16,4,8,384]{4,3,2,1,0:T(8,128)(2,1)S(1)} %get-tuple-element.47), channel_id=1, source_target_pairs={{1,0},{2,1},{3,2},{4,3},{5,4},{6,5},{7,6},{8,7},{9,8},{10,9},{11,1... | collective-permute-start | bytes 2359304 | tf_op jit(solution)/shard_map/ppermute | solution.py:442
  143.0 9.8 %copy-start.20 = (f32[384]{0:T(512)S(1)}, f32[384]{0:T(512)}, u32[]{:S(2)}) copy-start(f32[384]{0:T(512)} %param.22) | copy-start | bytes 4612
  143.0 9.9 %copy-start.1 = (bf16[1152,1152]{1,0:T(8,128)(2,1)S(1)}, bf16[1152,1152]{1,0:T(8,128)(2,1)}, u32[]{:S(2)}) copy-start(bf16[1152,1152]{1,0:T(8,128)(2,1)} %copy-done) | copy-start | bytes 7962628
  143.0 9.9 %copy-start.12 = (bf16[4,2,128,384]{3,2,1,0:T(8,128)(2,1)S(1)}, bf16[4,2,128,384]{3,2,1,0:T(8,128)(2,1)}, u32[]{:S(2)}) copy-start(bf16[4,2,128,384]{3,2,1,0:T(8,128)(2,1)} %copy-done.10) | copy-start | bytes 2359300
  147.7 11.6 %collective-permute-start.4 = (bf16[4,128,384]{2,1,0:T(8,128)(2,1)S(1)}, bf16[4,128,384]{2,1,0:T(8,128)(2,1)S(1)}, u32[]{:S(2)}, u32[]{:S(2)}) collective-permute-start(bf16[4,128,384]{2,1,0:T(8,128)(2,1)S(1)} %get-tuple-element.35), channel_id=1, source_target_pairs={{0,1},{1,2},{2,3},{3,4},{4,5},{5,6},{6,7},{7,8},{8,9},{9,10},{10,1... | collective-permute-start | bytes 1179656 | tf_op jit(solution)/shard_map/ppermute | solution.py:439
  147.8 11.6 %collective-permute-start.5 = (bf16[4,128,384]{2,1,0:T(8,128)(2,1)S(1)}, bf16[4,128,384]{2,1,0:T(8,128)(2,1)S(1)}, u32[]{:S(2)}, u32[]{:S(2)}) collective-permute-start(bf16[4,128,384]{2,1,0:T(8,128)(2,1)S(1)} %get-tuple-element.36), channel_id=1, source_target_pairs={{1,0},{2,1},{3,2},{4,3},{5,4},{6,5},{7,6},{8,7},{9,8},{10,9},{11,1... | collective-permute-start | bytes 1179656 | tf_op jit(solution)/shard_map/ppermute | solution.py:442
  152.9 6.5 %copy-start.7 = (bf16[4,2,128,384]{3,2,1,0:T(8,128)(2,1)S(1)}, bf16[4,2,128,384]{3,2,1,0:T(8,128)(2,1)}, u32[]{:S(2)}) copy-start(bf16[4,2,128,384]{3,2,1,0:T(8,128)(2,1)} %f_ref.3) | copy-start | bytes 2359300

commit v4 on v3

v4 whole, which is shorter than its diff:
```python
import jax
import jax.numpy as jnp
from jax import lax
from jax.experimental import pallas as pl
from jax.experimental.pallas import tpu as pltpu
from jax.sharding import PartitionSpec as P

BOTH = ("stream", "tile")
CB = 8


def lookup(held_table, values):
    return jnp.sum(jnp.where(held_table, values[None, :], 0), axis=1)


def pack(first, second):
    n_slots, n_frames, n_rows, n_cols, ch = first.shape
    blocks = n_cols // CB

    def body(a_ref, b_ref, o_ref):
        for k, ref in enumerate((a_ref, b_ref)):
            for f in range(n_frames):
                for r in range(n_rows):
                    o_ref[r, k, f, :, 0] = ref[0, f, r].reshape(blocks, CB, ch)

    spec = pl.BlockSpec((1, n_frames, n_rows, n_cols, ch), lambda s: (s, 0, 0, 0, 0))
    return pl.pallas_call(
        body,
        grid=(n_slots,),
        in_specs=[spec, spec],
        out_specs=pl.BlockSpec(
            (n_rows, 2, n_frames, blocks, 1, CB, ch), lambda s: (0, 0, 0, 0, s, 0, 0)
        ),
        out_shape=jax.ShapeDtypeStruct(
            (n_rows, 2, n_frames, blocks, n_slots, CB, ch), first.dtype
        ),
        compiler_params=pltpu.CompilerParams(vmem_limit_bytes=58 << 20),
    )(first, second)


def permute(held, source, rotation, keep):
    n_groups, n_tiles, n_slots, cols, ch = held.shape

    def body(source_ref, rotation_ref, keep_ref, i_ref, o_ref):
        n = pl.program_id(0)
        by = rotation_ref[n]

        @pl.when(keep_ref[n] != 0)
        def _():
            def step(t, _):
                at = lax.rem(t + n_tiles - by, n_tiles)
                o_ref[0, t, 0] = i_ref[0, at, 0]
                return 0

            lax.fori_loop(0, n_tiles, step, 0, unroll=8)

        @pl.when(keep_ref[n] == 0)
        def _():
            o_ref[...] = jnp.zeros_like(o_ref)

    block = (1, n_tiles, 1, cols, ch)
    return pl.pallas_call(
        body,
        grid_spec=pltpu.PrefetchScalarGridSpec(
            num_scalar_prefetch=3,
            grid=(n_groups * n_slots,),
            in_specs=[
                pl.BlockSpec(
                    block,
                    lambda n, s, r, k: (lax.div(s[n], n_slots), 0, lax.rem(s[n], n_slots), 0, 0),
                )
            ],
            out_specs=pl.BlockSpec(
                block, lambda n, s, r, k: (lax.div(n, n_slots), 0, lax.rem(n, n_slots), 0, 0)
            ),
        ),
        out_shape=jax.ShapeDtypeStruct(held.shape, held.dtype),
        compiler_params=pltpu.CompilerParams(vmem_limit_bytes=32 << 20),
    )(source, rotation, keep, held)


VMEM_LIMIT = 24 << 20


def call(body, out_shape, operands, scalars=(), scratch=(), flops=0, moved=0):
    in_specs = [pl.BlockSpec(memory_space=pltpu.SMEM) for _ in scalars]
    in_specs += [pl.BlockSpec(memory_space=pltpu.VMEM) for _ in operands]
    return pl.pallas_call(
        body,
        in_specs=in_specs,
        out_specs=[pl.BlockSpec(memory_space=pltpu.VMEM) for _ in out_shape],
        out_shape=list(out_shape),
        scratch_shapes=list(scratch),
        cost_estimate=pl.CostEstimate(flops=flops, bytes_accessed=moved, transcendentals=0),
        compiler_params=pltpu.CompilerParams(vmem_limit_bytes=VMEM_LIMIT),
    )(*scalars, *operands)


def spread(weight):
    n_t, n_y, n_x, ci, co = weight.shape
    wide = n_x * co
    past = n_t - 1

    def body(w_ref, po_ref, ps_ref, ao_ref, as_ref):
        dy = pl.program_id(0)

        def at(t, x):
            return w_ref[t, 0, x]

        def side(y):
            for x in range(n_x):
                cols = slice(x * co, (x + 1) * co)
                for t in range(past):
                    ps_ref[y, t * ci : (t + 1) * ci, cols] = at(t, x)
                as_ref[y, :, cols] = at(past, x)

        def own(row, y):
            for x in range(n_x):
                cols = slice(y * wide + x * co, y * wide + (x + 1) * co)
                for t in range(past):
                    lo = (row * past + t) * ci
                    po_ref[lo : lo + ci, cols] = at(t, x)
                ao_ref[row * ci : (row + 1) * ci, cols] = at(past, x)

        @pl.when(dy == 0)
        def _():
            side(0)
            own(0, 1)

        @pl.when(dy == 1)
        def _():
            own(0, 0)
            own(1, 1)

        @pl.when(dy == 2)
        def _():
            side(1)
            own(1, 0)

    shapes = [(2 * past * ci, 2 * wide), (2, past * ci, wide), (2 * ci, 2 * wide), (2, ci, wide)]
    return pl.pallas_call(
        body,
        grid=(n_y,),
        in_specs=[pl.BlockSpec((n_t, 1, n_x, ci, co), lambda y: (0, y, 0, 0, 0))],
        out_specs=[
            pl.BlockSpec(shape, lambda y, zeros=(0,) * len(shape): zeros) for shape in shapes
        ],
        out_shape=[jax.ShapeDtypeStruct(shape, weight.dtype) for shape in shapes],
        cost_estimate=pl.CostEstimate(flops=0, bytes_accessed=5 * weight.size, transcendentals=0),
        compiler_params=pltpu.CompilerParams(vmem_limit_bytes=40 << 20),
    )(weight)


def activated(values, gain):
    u = values * lax.rsqrt(jnp.mean(values * values, axis=-1, keepdims=True) + 1e-06) * gain
    return u / (1.0 + jnp.exp(-u))


def first_activation(frame, gain):
    n_slots, n_rows, n_cols, ch = frame.shape

    def body(f_ref, g_ref, o_ref, top_ref, bottom_ref):
        for s in range(n_slots):
            for r in range(n_rows):
                value = activated(f_ref[s, r].astype(jnp.float32), g_ref[...]).astype(jnp.bfloat16)
                o_ref[s, r] = value
                if r == 0:
                    top_ref[s] = value
                if r == n_rows - 1:
                    bottom_ref[s] = value

    row = jax.ShapeDtypeStruct((n_slots, n_cols, ch), jnp.bfloat16)
    return call(
        body,
        [jax.ShapeDtypeStruct(frame.shape, jnp.bfloat16), row, row],
        (frame, gain),
        flops=10 * frame.size,
        moved=6 * frame.size,
    )


def folded(acc, ch, cols_first):
    tiles = acc.shape[0] // CB
    n_slots = 4
    blocks = tiles // n_slots
    lead = (blocks, n_slots) if cols_first else (n_slots, blocks)
    axis = 0 if cols_first else 1

    def plane(k):
        value = acc[:, k * ch : (k + 1) * ch].reshape(tiles, CB, ch)
        return value

    at = lax.broadcasted_iota(jnp.int32, (1, 1, CB, ch), 2)
    before = pltpu.roll(plane(0), 1, 1).reshape(lead + (CB, ch))
    after = pltpu.roll(plane(2), CB - 1, 1).reshape(lead + (CB, ch))
    gap = list(lead) + [CB, ch]
    gap[axis] = 1
    gap = jnp.zeros(gap, jnp.float32)
    before_prev = jnp.concatenate([gap, lax.slice_in_dim(before, 0, blocks - 1, axis=axis)], axis)
    after_next = jnp.concatenate([lax.slice_in_dim(after, 1, blocks, axis=axis), gap], axis)
    total = plane(1).reshape(lead + (CB, ch))
    total += jnp.where(at == 0, before_prev, before)
    total += jnp.where(at == CB - 1, after_next, after)
    return total


def add_into(o_ref, y, total, cols_first, base=None):
    if cols_first:
        o_ref[y] = total if base is None else base[y] + total
        return
    for s in range(total.shape[0]):
        o_ref[y, :, s] = total[s] if base is None else base[y, :, s] + total[s]


def masked(edge_ref, k, s, value):
    return jnp.where(edge_ref[k, s] != 0, value, jnp.zeros_like(value))


def dot(a, b):
    return jnp.dot(a, b, preferred_element_type=jnp.float32)


def sums_shape(blocks, n_slots, n_rows, ch):
    return jax.ShapeDtypeStruct((n_rows, blocks, n_slots, CB, ch), jnp.float32)


def add_sides(edge_ref, sides, w_ref, lhs, o_ref):
    n_slots, n_cols, ch = sides[0].shape
    for y, side in enumerate(sides):
        for s in range(n_slots):
            lhs[s * n_cols : (s + 1) * n_cols] = masked(edge_ref, y, s, side[s])
        add_into(o_ref, y, folded(dot(lhs[...], w_ref[y]), ch, False), False, o_ref)


def add_own(act_ref, w_ref, lhs, o_ref, base):
    n_slots, n_rows, n_cols, ch = act_ref.shape
    for s in range(n_slots):
        for r in range(n_rows):
            lhs[s * n_cols : (s + 1) * n_cols, r * ch : (r + 1) * ch] = act_ref[s, r]
    both = dot(lhs[...], w_ref[...])
    wide = both.shape[1] // 2
    for y in range(n_rows):
        add_into(o_ref, y, folded(both[:, y * wide : (y + 1) * wide], ch, False), False, base)


def current_part(act, above, below, w_own, w_sides, edges):
    n_slots, n_rows, n_cols, ch = act.shape
    half = n_slots * n_cols

    def body(edge_ref, act_ref, above_ref, below_ref, wo_ref, ws_ref, o_ref, lhs, side):
        add_own(act_ref, wo_ref, lhs, o_ref, None)
        add_sides(edge_ref, (above_ref, below_ref), ws_ref, side, o_ref)

    return call(
        body,
        [sums_shape(n_cols // CB, n_slots, n_rows, ch)],
        (act, above, below, w_own, w_sides),
        scalars=(edges,),
        scratch=[
            pltpu.VMEM((half, n_rows * ch), jnp.bfloat16),
            pltpu.VMEM((half, ch), jnp.bfloat16),
        ],
        flops=2 * half * (w_own.size + w_sides.size),
        moved=2 * w_own.size + 8 * act.size,
    )[0]


def own_part(got, weights, sums):
    n_rows, n_caches, n_frames, blocks, n_slots, _, ch = got.shape
    half = blocks * n_slots * CB
    deep = n_frames * ch

    def body(got_ref, w0_ref, w1_ref, z_ref, o0_ref, o1_ref, lhs):
        for k, (w, o_ref, base) in enumerate(((w0_ref, o0_ref, z_ref), (w1_ref, o1_ref, None))):
            for r in range(n_rows):
                for f in range(n_frames):
                    lo = r * deep + f * ch
                    lhs[:, lo : lo + ch] = got_ref[r, k, f].reshape(half, ch)
            both = dot(lhs[...], w[...])
            wide = both.shape[1] // 2
            for y in range(n_rows):
                total = folded(both[:, y * wide : (y + 1) * wide], ch, True)
                add_into(o_ref, y, total, True, base)

    out = sums_shape(blocks, n_slots, n_rows, ch)
    whole = weights[0]
    return call(
        body,
        [out, out],
        (got, *weights, sums),
        scratch=[pltpu.VMEM((half, n_rows * deep), jnp.bfloat16)],
        flops=4 * half * whole.size,
        moved=4 * whole.size,
    )


def side_sums(edge_ref, k, side_ref, w, lhs):
    n_frames, blocks, n_slots, _, ch = side_ref.shape
    for s in range(n_slots):
        for f in range(n_frames):
            value = masked(edge_ref, k, s, side_ref[f, :, s])
            lhs[:, s, :, f * ch : (f + 1) * ch] = value
    half = blocks * n_slots * CB
    return folded(dot(lhs[...].reshape(half, n_frames * ch), w), ch, True)


def second_activation(above, below, w_sides, sums, bias, gain, edges):
    n_frames, blocks, n_slots, _, ch = above.shape
    n_rows, n_cols, deep = sums.shape[0], blocks * CB, n_frames * ch

    def body(edge_ref, above_ref, below_ref, w_ref, z_ref, b_ref, g_ref, o_ref, top_ref, bottom_ref, lhs):
        for y, side in enumerate((above_ref, below_ref)):
            total = side_sums(edge_ref, y, side, w_ref[y], lhs) + z_ref[y] + b_ref[...]
            for s in range(n_slots):
                value = activated(total[:, s].reshape(n_cols, ch), g_ref[...]).astype(jnp.bfloat16)
                o_ref[s, y] = value
                if y == 0:
                    top_ref[s] = value
                else:
                    bottom_ref[s] = value

    row = jax.ShapeDtypeStruct((n_slots, n_cols, ch), jnp.bfloat16)
    return call(
        body,
        [jax.ShapeDtypeStruct((n_slots, n_rows, n_cols, ch), jnp.bfloat16), row, row],
        (above, below, w_sides, sums, bias, gain),
        scalars=(edges,),
        scratch=[pltpu.VMEM((blocks, n_slots, CB, deep), jnp.bfloat16)],
        flops=2 * n_slots * n_cols * w_sides.size,
        moved=2 * w_sides.size,
    )


def before_sides(above, below, act, w_sides, w_act, sums, got, act_first, edges):
    n_frames, blocks, n_slots, _, ch = above.shape
    n_rows, n_cols, deep = sums.shape[0], blocks * CB, n_frames * ch

    def body(edge_ref, above_ref, below_ref, act_ref, w_ref, wa_ref, z_ref, got_ref, act1_ref, o_ref, n1_ref, n2_ref, lhs, lhs2):
        add_own(act_ref, wa_ref, lhs2, o_ref, z_ref)
        for y, side in enumerate((above_ref, below_ref)):
            o_ref[y] += side_sums(edge_ref, y, side, w_ref[y], lhs)
        for s in range(n_slots):
            for r in range(n_rows):
                n2_ref[s, 1, r] = act_ref[s, r]
                n1_ref[s, 1, r] = act1_ref[s, r]
                n1_ref[s, 0, r] = got_ref[r, 0, 1, :, s].reshape(n_cols, ch)
                n2_ref[s, 0, r] = got_ref[r, 1, 1, :, s].reshape(n_cols, ch)

    nxt = jax.ShapeDtypeStruct((n_slots, 2, n_rows, n_cols, ch), jnp.bfloat16)
    return call(
        body,
        [jax.ShapeDtypeStruct(sums.shape, jnp.float32), nxt, nxt],
        (above, below, act, w_sides, w_act, sums, got, act_first),
        scalars=(edges,),
        scratch=[
            pltpu.VMEM((blocks, n_slots, CB, deep), jnp.bfloat16),
            pltpu.VMEM((n_slots * n_cols, n_rows * ch), jnp.bfloat16),
        ],
        flops=2 * n_slots * n_cols * (w_sides.size + w_act.size),
        moved=2 * (w_sides.size + w_act.size),
    )


def last_part(above, below, w_sides, sums, bias, frame, edges):
    n_slots, n_rows, n_cols, ch = frame.shape

    def body(edge_ref, above_ref, below_ref, w_ref, z_ref, b_ref, f_ref, o_ref, lhs):
        for y, side in enumerate((above_ref, below_ref)):
            for s in range(n_slots):
                lhs[s * n_cols : (s + 1) * n_cols] = masked(edge_ref, y, s, side[s])
            total = folded(dot(lhs[...], w_ref[y]), ch, False)
            for s in range(n_slots):
                value = (total[s] + z_ref[y, :, s] + b_ref[...]).reshape(n_cols, ch)
                o_ref[s, y] = (value + f_ref[s, y].astype(jnp.float32)).astype(jnp.bfloat16)

    return call(
        body,
        [jax.ShapeDtypeStruct(frame.shape, jnp.bfloat16)],
        (above, below, w_sides, sums, bias, frame),
        scalars=(edges,),
        scratch=[pltpu.VMEM((n_slots * n_cols, ch), jnp.bfloat16)],
        flops=2 * n_slots * n_cols * w_sides.size,
        moved=2 * w_sides.size,
    )[0]


def local(
    frame_in,
    cache_first,
    cache_second,
    gain_first,
    gain_second,
    conv_first,
    conv_second,
    bias_first,
    bias_second,
    old_slot,
    new_slot,
    old_shift,
    new_shift,
    frame_count,
):
    n_slots, n_rows, n_cols, ch = frame_in.shape
    n_groups = lax.axis_size("stream")
    n_tiles = lax.axis_size("tile")
    my_group = lax.axis_index("stream")
    my_tile = lax.axis_index("tile")
    n_flight = old_slot.shape[0]
    blocks = n_cols // CB
    slot_ids = jnp.arange(n_flight, dtype=jnp.int32)
    held_new = new_slot[None, :] == slot_ids[:, None]
    source = lookup(held_new, old_slot)
    shift_after = lookup(held_new, new_shift)
    rotation = (shift_after - lookup(held_new, old_shift)) % n_tiles
    frames_done = lookup(held_new, frame_count)
    my_piece = my_group * n_tiles + my_tile
    my_frame = (my_piece // blocks) % 2
    keep = (frames_done >= 2 - my_frame).astype(jnp.int32)
    start = my_group * n_slots
    my_number = lax.dynamic_slice_in_dim((my_tile - shift_after) % n_tiles, start, n_slots)

    edges = jnp.stack([my_number != 0, my_number != n_tiles - 1]).astype(jnp.int32)
    down = [(i, (i + 1) % n_tiles) for i in range(n_tiles)]
    up = [((i + 1) % n_tiles, i) for i in range(n_tiles)]

    def from_above(row):
        return lax.ppermute(row, "tile", down)

    def from_below(row):
        return lax.ppermute(row, "tile", up)

    sent = pack(cache_first, cache_second).reshape(n_groups * n_tiles, n_slots, CB, ch)
    held = lax.all_to_all(sent, BOTH, 0, 0, tiled=True)

    own_1, sides_1, act_own_1, act_sides_1 = spread(conv_first)
    own_2, sides_2, act_own_2, act_sides_2 = spread(conv_second)
    act_first, top, bottom = first_activation(frame_in, gain_first[None])
    act_above, act_below = from_above(bottom), from_below(top)
    held, act_first, own_1, own_2 = lax.optimization_barrier((held, act_first, own_1, own_2))

    moved = permute(held.reshape(n_groups, n_tiles, n_slots, CB, ch), source, rotation, keep)
    moved, act_later = lax.optimization_barrier((moved, act_first))
    got = lax.all_to_all(
        moved.reshape(n_groups * n_tiles, n_slots, CB, ch), BOTH, 0, 0, tiled=True
    )
    sums_1 = current_part(act_later, act_above, act_below, act_own_1, act_sides_1, edges)
    got, sums_1 = lax.optimization_barrier((got, sums_1))
    got = got.reshape(n_rows, 2, 2, blocks, n_slots, CB, ch)

    above_1 = from_above(got[n_rows - 1, 0])
    below_1 = from_below(got[0, 0])
    above_2 = from_above(got[n_rows - 1, 1])
    below_2 = from_below(got[0, 1])
    sums_1, sums_2 = own_part(got, (own_1, own_2), sums_1)
    act_second, top, bottom = second_activation(
        above_1, below_1, sides_1, sums_1, bias_first[None], gain_second[None], edges
    )
    side_above, side_below = from_above(bottom), from_below(top)
    sums_2, next_first, next_second = before_sides(
        above_2, below_2, act_second, sides_2, act_own_2, sums_2, got, act_first, edges
    )
    mixed_frame = last_part(
        side_above, side_below, act_sides_2, sums_2, bias_second[None], frame_in, edges
    )
    return (mixed_frame, next_first, next_second)


def solution(mesh):
    frame = P("stream", "tile", None, None)
    cache = P("stream", None, "tile", None, None)
    return jax.shard_map(
        local,
        mesh=mesh,
        in_specs=(frame, cache, cache) + (P(),) * 11,
        out_specs=(frame, cache, cache),
        check_vma=False,
    )
```

time: 164 us -> 161 us (0.982)
  blocking collectives: 48.1 us -> 0 us
  waiting for transfers between devices: 17.3 us -> 53.6 us
  Pallas kernels: 40.6 us -> 48 us
    all_to_all x1 -> x0, blocking collectives: 48.1 us -> none  [local(): lax.all_to_all(moved.reshape(n_groups * n_tiles, n_slots, CB, ch), BOTH,...]
    ppermute x4, waiting for transfers between devices: 17.2 us -> 38.8 us  [from_above(): return lax.ppermute(row, 'tile', down)]
    all_to_all x1, waiting for transfers between devices: 0.01 us -> 14.8 us  [local(): held = lax.all_to_all(sent, BOTH, 0, 0, tiled=True)]
    pallas_call x2, Pallas kernels: 3.12 us -> 14.9 us  [spread(): pl.pallas_call(body, grid=(n_y,), in_specs=[pl.BlockSpec((n_t, 1, n_x, ci...]
    pallas_call x6, Pallas kernels: 32.4 us -> 25.9 us  [call(): pl.pallas_call(body, in_specs=in_specs, out_specs=[pl.BlockSpec(memory_sp...]
    all_to_all x0 -> x1, starting transfers between devices: none -> 4.67 us  [local(): lax.all_to_all(moved.reshape(n_groups * n_tiles, n_slots, CB, ch), BOTH,...]
    ppermute x4, starting transfers between devices: 20.2 us -> 16.9 us  [from_below(): return lax.ppermute(row, 'tile', up)]
    pallas_call x1, Pallas kernels: 2.33 us -> 4.3 us  [pack(): pl.pallas_call(body, grid=(n_slots,), in_specs=[spec, spec], out_specs=pl...]
  transfers between devices with their start and end apart: 9 -> 10, of which waited for: 1 -> 2; matrix products, arithmetic and copies ran while one was open for 1% -> 0% of each run, Pallas kernels for 20% -> 23%
where the time goes in v4:
time: 161 us
  waiting for transfers between devices  53.6 us (33%)
  Pallas kernels  48 us (30%)
  starting transfers between devices  32.9 us (20%)
  local copies, waits for them, and re-layouts  25.1 us (16%)
    ppermute x4, waiting for transfers between devices, from_above(): return lax.ppermute(row, 'tile', down)  38.8 us
    pallas_call x6, Pallas kernels, call(): pl.pallas_call(body, in_specs=in_specs, out_specs=[pl.BlockSpec(memory_sp...  25.9 us
    unnamed x64, local copies, waits for them, and re-layouts  24.7 us
    ppermute x4, starting transfers between devices, from_below(): return lax.ppermute(row, 'tile', up)  16.9 us
    pallas_call x2, Pallas kernels, spread(): pl.pallas_call(body, grid=(n_y,), in_specs=[pl.BlockSpec((n_t, 1, n_x, ci...  14.9 us
    all_to_all x1, waiting for transfers between devices, local(): held = lax.all_to_all(sent, BOTH, 0, 0, tiled=True)  14.8 us
    all_to_all x1, starting transfers between devices, local(): held = lax.all_to_all(sent, BOTH, 0, 0, tiled=True)  11.1 us
    all_to_all x1, starting transfers between devices, local(): lax.all_to_all(moved.reshape(n_groups * n_tiles, n_slots, CB, ch), BOTH,...  4.67 us
  transfers between devices with their start and end apart: 10, of which 2 were waited for; matrix products, arithmetic and copies ran while one was open for 0% of the time, Pallas kernels for 23%

profile of v4, /device:TPU:0, one launch (start us, length us, event | category | flops | bytes accessed | tf_op | source)
XLA Modules:
  0.0 160.8 jit_solution(8945492566739441799)
XLA Ops:
  0.6 4.3 %shard_map.157 = bf16[2,2,2,16,4,8,384]{6,5,4,3,2,1,0:T(8,128)(2,1)} custom-call(bf16[4,2,2,128,384]{4,3,2,1,0:T(8,128)(2,1)} %a_ref.1, bf16[4,2,2,128,384]{4,3,2,1,0:T(8,128)(2,1)} %b_ref.1), custom_call_target="tpu_custom_call" | custom-call | tf_op jit(solution)/shard_map/pallas_call | solution.py:27
  4.9 11.1 %all-to-all-start = ((bf16[128,4,8,384]{3,2,1,0:T(8,128)(2,1)}), bf16[128,4,8,384]{3,2,1,0:T(8,128)(2,1)S(1)}, u32[]{:S(2)}, u32[]{:S(2)}) async-start(bf16[128,4,8,384]{3,2,1,0:T(8,128)(2,1)} %bitcast.21), calls=%async_computation | async-start | bytes 6291456 | tf_op jit(solution)/shard_map/all_to_all | solution.py:433
  16.1 7.4 %shard_map.159 = (bf16[1536,2304]{1,0:T(8,128)(2,1)}, bf16[2,768,1152]{2,1,0:T(8,128)(2,1)S(1)}, bf16[768,2304]{1,0:T(8,128)(2,1)S(1)}, bf16[2,384,1152]{2,1,0:T(8,128)(2,1)S(1)}) custom-call(bf16[3,3,3,384,384]{4,3,2,1,0:T(8,128)(2,1)} %w_ref.2), custom_call_target="tpu_custom_call" | custom-call | bytes 19906560 | tf_op jit(solution)/shard_map/pallas_call | solution.py:141
  23.5 1.8 %copy-done.14 = bf16[2,768,1152]{2,1,0:T(8,128)(2,1)} copy-done((bf16[2,768,1152]{2,1,0:T(8,128)(2,1)}, bf16[2,768,1152]{2,1,0:T(8,128)(2,1)S(1)}, u32[]{:S(2)}) %copy-start.14) | copy-done | bytes 3538968
  25.3 1.8 %copy-done.16 = bf16[768,2304]{1,0:T(8,128)(2,1)} copy-done((bf16[768,2304]{1,0:T(8,128)(2,1)}, bf16[768,2304]{1,0:T(8,128)(2,1)S(1)}, u32[]{:S(2)}) %copy-start.16) | copy-done | bytes 3538968
  27.1 1.2 copy-done.18
  28.3 0.0 copy-start.30
  28.3 0.0 copy-start.31
  28.3 7.5 %shard_map.160 = (bf16[1536,2304]{1,0:T(8,128)(2,1)}, bf16[2,768,1152]{2,1,0:T(8,128)(2,1)S(1)}, bf16[768,2304]{1,0:T(8,128)(2,1)S(1)}, bf16[2,384,1152]{2,1,0:T(8,128)(2,1)S(1)}) custom-call(bf16[3,3,3,384,384]{4,3,2,1,0:T(8,128)(2,1)} %w_ref.3), custom_call_target="tpu_custom_call" | custom-call | bytes 19906560 | tf_op jit(solution)/shard_map/pallas_call | solution.py:141
  35.8 1.8 %copy-done.1 = bf16[2,768,1152]{2,1,0:T(8,128)(2,1)} copy-done((bf16[2,768,1152]{2,1,0:T(8,128)(2,1)}, bf16[2,768,1152]{2,1,0:T(8,128)(2,1)S(1)}, u32[]{:S(2)}) %copy-start.1) | copy-done | bytes 3538968
  37.6 1.8 %copy-done.3 = bf16[768,2304]{1,0:T(8,128)(2,1)} copy-done((bf16[768,2304]{1,0:T(8,128)(2,1)}, bf16[768,2304]{1,0:T(8,128)(2,1)S(1)}, u32[]{:S(2)}) %copy-start.3) | copy-done | bytes 3538968
  39.4 1.2 copy-done.7
  40.6 0.7 shard_map.158
  41.3 0.0 copy-start.9
  41.3 0.9 copy-done.9
  42.2 0.7 copy-done.20
  43.0 0.1 select_reduce_fusion
  43.2 14.8 %all-to-all-done = bf16[128,4,8,384]{3,2,1,0:T(8,128)(2,1)S(1)} async-done(((bf16[128,4,8,384]{3,2,1,0:T(8,128)(2,1)}), bf16[128,4,8,384]{3,2,1,0:T(8,128)(2,1)S(1)}, u32[]{:S(2)}, u32[]{:S(2)}) %all-to-all-start) | async-done | bytes 3145760 | tf_op jit(solution)/shard_map/all_to_all | solution.py:433
  57.9 2.9 %shard_map.161 = bf16[4,32,4,8,384]{4,3,2,1,0:T(8,128)(2,1)S(1)} custom-call(s32[16]{0:T(128)S(1)} %get-tuple-element.59.source_ref, s32[16]{0:T(128)S(1)} %get-tuple-element.65.rotation_ref, s32[16]{0:T(128)S(1)} %compare_convert_fusion.keep_ref, bf16[4,32,4,8,384]{4,3,2,1,0:T(8,128)(2,1)S(1)} %bitcast.19), custom_call_target="tpu_custom_call" | custom-call | tf_op jit(solution)/shard_map/pallas_call | solution.py:62
  60.9 1.7 %copy-done = bf16[4,32,4,8,384]{4,3,2,1,0:T(8,128)(2,1)} copy-done((bf16[4,32,4,8,384]{4,3,2,1,0:T(8,128)(2,1)}, bf16[4,32,4,8,384]{4,3,2,1,0:T(8,128)(2,1)S(1)}, u32[]{:S(2)}) %copy-start) | copy-done | bytes 3145752
  62.5 4.7 %all-to-all-start.1 = ((bf16[128,4,8,384]{3,2,1,0:T(8,128)(2,1)}), bf16[128,4,8,384]{3,2,1,0:T(8,128)(2,1)S(1)}, u32[]{:S(2)}, u32[]{:S(2)}) async-start(bf16[128,4,8,384]{3,2,1,0:T(8,128)(2,1)} %bitcast.20), calls=%async_computation.1 | async-start | bytes 6291456 | tf_op jit(solution)/shard_map/all_to_all | solution.py:443
  67.2 0.1 collective-permute-start
  67.3 5.1 %collective-permute-start.1 = (bf16[4,128,384]{2,1,0:T(8,128)(2,1)S(1)}, bf16[4,128,384]{2,1,0:T(8,128)(2,1)}, u32[]{:S(2)}, u32[]{:S(2)}) collective-permute-start(bf16[4,128,384]{2,1,0:T(8,128)(2,1)S(1)} %get-tuple-element.38), channel_id=1, source_target_pairs={{1,0},{2,1},{3,2},{4,3},{5,4},{6,5},{7,6},{8,7},{9,8},{10,9},{11,1... | collective-permute-start | bytes 1179656 | tf_op jit(solution)/shard_map/ppermute | solution.py:430
  72.3 0.1 compare_bitcast_fusion.1
  72.4 38.8 %collective-permute-done.above_ref = bf16[4,128,384]{2,1,0:T(8,128)(2,1)} collective-permute-done((bf16[4,128,384]{2,1,0:T(8,128)(2,1)}, bf16[4,128,384]{2,1,0:T(8,128)(2,1)}, u32[]{:S(2)}, u32[]{:S(2)}) %collective-permute-start) | collective-permute-done | bytes 393248 | tf_op jit(solution)/shard_map/ppermute | solution.py:427
  111.2 1.1 copy-done.10
  112.3 2.0 %copy-done.17 = bf16[768,2304]{1,0:T(8,128)(2,1)S(1)} copy-done((bf16[768,2304]{1,0:T(8,128)(2,1)S(1)}, bf16[768,2304]{1,0:T(8,128)(2,1)}, u32[]{:S(2)}) %copy-start.17) | copy-done | bytes 3538968
  114.3 1.5 copy-done.19
  115.8 4.5 %shard_map.162.z_ref = f32[2,16,4,8,384]{4,3,2,1,0:T(8,128)S(1)} custom-call(s32[2,4]{1,0:T(2,128)S(1)} %add_convert_fusion.edge_ref, bf16[4,2,128,384]{3,2,1,0:T(8,128)(2,1)S(1)} %copy-done.10, bf16[4,128,384]{2,1,0:T(8,128)(2,1)} %collective-permute-done.above_ref, bf16[4,128,384]{2,1,0:T(8,128)(2,1)} %collective-permute-done.1.below_ref, ...), custom_call_target="tpu_custom_call" | custom-call | flops 2717908992 | bytes 6684672 | tf_op jit(solution)/shard_map/pallas_call | solution.py:88
  120.3 0.0 copy-start.21
  120.3 1.1 copy-done.21
  121.4 0.0 all-to-all-done.1
  121.4 0.4 slice_bitcast_fusion
  121.9 1.4 collective-permute-start.3
  123.3 5.1 %collective-permute-start.7 = (bf16[2,16,4,8,384]{4,3,2,1,0:T(8,128)(2,1)S(1)}, bf16[2,16,4,8,384]{4,3,2,1,0:T(8,128)(2,1)S(1)}, u32[]{:S(2)}, u32[]{:S(2)}) collective-permute-start(bf16[2,16,4,8,384]{4,3,2,1,0:T(8,128)(2,1)S(1)} %get-tuple-element.61), channel_id=1, source_target_pairs={{1,0},{2,1},{3,2},{4,3},{5,4},{6,5},{7,6},{8,7},{9,8},{10,9},{11,1... | collective-permute-start | bytes 2359304 | tf_op jit(solution)/shard_map/ppermute | solution.py:430
  128.4 0.0 collective-permute-start.6
  128.4 3.0 %copy-done.12 = bf16[1536,2304]{1,0:T(8,128)(2,1)S(1)} copy-done((bf16[1536,2304]{1,0:T(8,128)(2,1)S(1)}, bf16[1536,2304]{1,0:T(8,128)(2,1)}, u32[]{:S(2)}) %copy-start.12) | copy-done | bytes 7077912
  131.4 3.0 %copy-done.13 = bf16[1536,2304]{1,0:T(8,128)(2,1)S(1)} copy-done((bf16[1536,2304]{1,0:T(8,128)(2,1)S(1)}, bf16[1536,2304]{1,0:T(8,128)(2,1)}, u32[]{:S(2)}) %copy-start.13) | copy-done | bytes 7077912
  134.5 7.8 %shard_map.163 = (f32[2,16,4,8,384]{4,3,2,1,0:T(8,128)S(1)}, f32[2,16,4,8,384]{4,3,2,1,0:T(8,128)S(1)}) custom-call(bf16[2,2,2,16,4,8,384]{6,5,4,3,2,1,0:T(8,128)(2,1)S(1)} %bitcast.17, bf16[1536,2304]{1,0:T(8,128)(2,1)S(1)} %copy-done.12, bf16[1536,2304]{1,0:T(8,128)(2,1)S(1)} %copy-done.13, f32[2,16,4,8,384]{4,3,2,1,0:T(8,128)S(1)} %copy-done.22), custom_call_target="tpu_custom_call" | custom-call | flops 7247757312 | bytes 14155776 | tf_op jit(solution)/shard_map/pallas_call | solution.py:88
  142.3 0.0 collective-permute-done.2.above_ref
  142.3 0.0 copy-start.26
  142.3 0.0 copy-start.11
  142.4 3.4 %shard_map.164 = (bf16[4,2,128,384]{3,2,1,0:T(8,128)(2,1)S(1)}, bf16[4,128,384]{2,1,0:T(8,128)(2,1)S(1)}, bf16[4,128,384]{2,1,0:T(8,128)(2,1)S(1)}) custom-call(s32[2,4]{1,0:T(2,128)S(1)} %add_convert_fusion.edge_ref, bf16[2,16,4,8,384]{4,3,2,1,0:T(8,128)(2,1)S(1)} %collective-permute-done.2.above_ref, ...), custom_call_target="tpu_custom_call" | custom-call | flops 1811939328 | bytes 3538944 | tf_op jit(solution)/shard_map/pallas_call | solution.py:88
  145.7 0.1 collective-permute-start.4
  145.8 5.3 %collective-permute-start.5 = (bf16[4,128,384]{2,1,0:T(8,128)(2,1)S(1)}, bf16[4,128,384]{2,1,0:T(8,128)(2,1)S(1)}, u32[]{:S(2)}, u32[]{:S(2)}) collective-permute-start(bf16[4,128,384]{2,1,0:T(8,128)(2,1)S(1)} %get-tuple-element.48), channel_id=1, source_target_pairs={{1,0},{2,1},{3,2},{4,3},{5,4},{6,5},{7,6},{8,7},{9,8},{10,9},{11,1... | collective-permute-start | bytes 1179656 | tf_op jit(solution)/shard_map/ppermute | solution.py:430
  151.2 0.0 copy-start.6
  151.2 6.5 %shard_map.165 = (f32[2,16,4,8,384]{4,3,2,1,0:T(8,128)S(1)}, bf16[4,2,2,128,384]{4,3,2,1,0:T(8,128)(2,1)}, bf16[4,2,2,128,384]{4,3,2,1,0:T(8,128)(2,1)}) custom-call(s32[2,4]{1,0:T(2,128)S(1)} %add_convert_fusion.edge_ref, bf16[2,16,4,8,384]{4,3,2,1,0:T(8,128)(2,1)S(1)} %collective-permute-done.6.above_ref, ...), custom_call_target="tpu_custom_call" | custom-call | flops 3623878656 | bytes 7077888 | tf_op jit(solution)/shard_map/pallas_call | solution.py:88
  157.8 3.1 %shard_map.166 = bf16[4,2,128,384]{3,2,1,0:T(8,128)(2,1)} custom-call(s32[2,4]{1,0:T(2,128)S(1)} %add_convert_fusion.edge_ref, bf16[4,128,384]{2,1,0:T(8,128)(2,1)S(1)} %collective-permute-done.4.above_ref, bf16[4,128,384]{2,1,0:T(8,128)(2,1)S(1)} %collective-permute-done.5.below_ref, bf16[2,384,1152]{2,1,0:T(8,128)(2,1)S(1)} %copy-done.8, ...), custom_call_target="tpu_custom_call" | custom-call | flops 905969664 | bytes 1769472 | tf_op jit(solution)/shard_map/pallas_call | solution.py:88
  (56 shorter events, 0.1 us)
Async XLA Ops:
  4.9 11.2 %copy-start.23 = (f32[384]{0:T(512)S(1)}, f32[384]{0:T(512)}, u32[]{:S(2)}) copy-start(f32[384]{0:T(512)} %param.17) | copy-start | bytes 4612
  4.9 53.0 %all-to-all-start = ((bf16[128,4,8,384]{3,2,1,0:T(8,128)(2,1)}), bf16[128,4,8,384]{3,2,1,0:T(8,128)(2,1)S(1)}, u32[]{:S(2)}, u32[]{:S(2)}) async-start(bf16[128,4,8,384]{3,2,1,0:T(8,128)(2,1)} %bitcast.21), calls=%async_computation | async-start | bytes 6291456 | tf_op jit(solution)/shard_map/all_to_all | solution.py:433
  23.5 1.8 %copy-start.14 = (bf16[2,768,1152]{2,1,0:T(8,128)(2,1)}, bf16[2,768,1152]{2,1,0:T(8,128)(2,1)S(1)}, u32[]{:S(2)}) copy-start(bf16[2,768,1152]{2,1,0:T(8,128)(2,1)S(1)} %get-tuple-element.42.w_ref) | copy-start | bytes 10616836
  25.3 1.8 %copy-start.16 = (bf16[768,2304]{1,0:T(8,128)(2,1)}, bf16[768,2304]{1,0:T(8,128)(2,1)S(1)}, u32[]{:S(2)}) copy-start(bf16[768,2304]{1,0:T(8,128)(2,1)S(1)} %get-tuple-element.39.wo_ref) | copy-start | bytes 10616836
  27.1 1.2 copy-start.18
  28.3 12.3 %copy-start.5 = (bf16[4,2,128,384]{3,2,1,0:T(8,128)(2,1)S(1)}, bf16[4,2,128,384]{3,2,1,0:T(8,128)(2,1)}, u32[]{:S(2)}) copy-start(bf16[4,2,128,384]{3,2,1,0:T(8,128)(2,1)} %f_ref.3) | copy-start | bytes 2359300
  28.3 14.7 %copy-start.27 = (s32[16]{0:T(128)S(1)}, s32[16]{0:T(128)}, u32[]{:S(2)}) copy-start(s32[16]{0:T(128)} %param.27) | copy-start | bytes 196
  28.3 14.7 %copy-start.28 = (s32[16]{0:T(128)S(1)}, s32[16]{0:T(128)}, u32[]{:S(2)}) copy-start(s32[16]{0:T(128)} %param.24) | copy-start | bytes 196
  28.3 14.7 %copy-start.29 = (s32[16]{0:T(128)S(1)}, s32[16]{0:T(128)}, u32[]{:S(2)}) copy-start(s32[16]{0:T(128)} %param.25) | copy-start | bytes 196
  28.3 14.7 %copy-start.30 = (s32[16]{0:T(128)S(1)}, s32[16]{0:T(128)}, u32[]{:S(2)}) copy-start(s32[16]{0:T(128)} %param.23) | copy-start | bytes 196
  28.3 14.7 %copy-start.31 = (s32[16]{0:T(128)S(1)}, s32[16]{0:T(128)}, u32[]{:S(2)}) copy-start(s32[16]{0:T(128)} %param.26) | copy-start | bytes 196
  35.8 1.8 %copy-start.1 = (bf16[2,768,1152]{2,1,0:T(8,128)(2,1)}, bf16[2,768,1152]{2,1,0:T(8,128)(2,1)S(1)}, u32[]{:S(2)}) copy-start(bf16[2,768,1152]{2,1,0:T(8,128)(2,1)S(1)} %get-tuple-element.51.w_ref) | copy-start | bytes 10616836
  37.6 1.8 %copy-start.3 = (bf16[768,2304]{1,0:T(8,128)(2,1)}, bf16[768,2304]{1,0:T(8,128)(2,1)S(1)}, u32[]{:S(2)}) copy-start(bf16[768,2304]{1,0:T(8,128)(2,1)S(1)} %get-tuple-element.52.wa_ref) | copy-start | bytes 10616836
  39.4 1.2 copy-start.7
  41.3 0.9 copy-start.9
  42.2 0.7 copy-start.20
  60.8 1.7 %copy-start = (bf16[4,32,4,8,384]{4,3,2,1,0:T(8,128)(2,1)}, bf16[4,32,4,8,384]{4,3,2,1,0:T(8,128)(2,1)S(1)}, u32[]{:S(2)}) copy-start(bf16[4,32,4,8,384]{4,3,2,1,0:T(8,128)(2,1)S(1)} %shard_map.161) | copy-start | bytes 9437188
  62.5 58.9 %all-to-all-start.1 = ((bf16[128,4,8,384]{3,2,1,0:T(8,128)(2,1)}), bf16[128,4,8,384]{3,2,1,0:T(8,128)(2,1)S(1)}, u32[]{:S(2)}, u32[]{:S(2)}) async-start(bf16[128,4,8,384]{3,2,1,0:T(8,128)(2,1)} %bitcast.20), calls=%async_computation.1 | async-start | bytes 6291456 | tf_op jit(solution)/shard_map/all_to_all | solution.py:443
  67.2 44.0 %collective-permute-start = (bf16[4,128,384]{2,1,0:T(8,128)(2,1)}, bf16[4,128,384]{2,1,0:T(8,128)(2,1)}, u32[]{:S(2)}, u32[]{:S(2)}) collective-permute-start(bf16[4,128,384]{2,1,0:T(8,128)(2,1)} %copy-done.20), channel_id=1, source_target_pairs={{0,1},{1,2},{2,3},{3,4},{4,5},{5,6},{6,7},{7,8},{8,9},{9,10},{10,1... | collective-permute-start | bytes 1179656 | tf_op jit(solution)/shard_map/ppermute | solution.py:427
  67.3 43.9 %collective-permute-start.1 = (bf16[4,128,384]{2,1,0:T(8,128)(2,1)S(1)}, bf16[4,128,384]{2,1,0:T(8,128)(2,1)}, u32[]{:S(2)}, u32[]{:S(2)}) collective-permute-start(bf16[4,128,384]{2,1,0:T(8,128)(2,1)S(1)} %get-tuple-element.38), channel_id=1, source_target_pairs={{1,0},{2,1},{3,2},{4,3},{5,4},{6,5},{7,6},{8,7},{9,8},{10,9},{11,1... | collective-permute-start | bytes 1179656 | tf_op jit(solution)/shard_map/ppermute | solution.py:430
  111.2 1.1 copy-start.10
  112.3 2.0 %copy-start.17 = (bf16[768,2304]{1,0:T(8,128)(2,1)S(1)}, bf16[768,2304]{1,0:T(8,128)(2,1)}, u32[]{:S(2)}) copy-start(bf16[768,2304]{1,0:T(8,128)(2,1)} %copy-done.16) | copy-start | bytes 10616836
  114.3 1.5 copy-start.19
  120.3 1.1 copy-start.21
  121.4 1.8 %copy-start.24 = (f32[384]{0:T(512)S(1)}, f32[384]{0:T(512)}, u32[]{:S(2)}) copy-start(f32[384]{0:T(512)} %param.18) | copy-start | bytes 4612
  121.4 1.9 %copy-start.25 = (f32[384]{0:T(512)S(1)}, f32[384]{0:T(512)}, u32[]{:S(2)}) copy-start(f32[384]{0:T(512)} %param.21) | copy-start | bytes 4612
  121.4 7.0 %copy-start.22 = (f32[2,16,4,8,384]{4,3,2,1,0:T(8,128)S(1)}, f32[2,16,4,8,384]{4,3,2,1,0:T(8,128)}, u32[]{:S(2)}) copy-start(f32[2,16,4,8,384]{4,3,2,1,0:T(8,128)} %copy-done.21) | copy-start | bytes 4718596
  121.9 20.4 %collective-permute-start.3 = (bf16[2,16,4,8,384]{4,3,2,1,0:T(8,128)(2,1)S(1)}, bf16[2,16,4,8,384]{4,3,2,1,0:T(8,128)(2,1)S(1)}, u32[]{:S(2)}, u32[]{:S(2)}) collective-permute-start(bf16[2,16,4,8,384]{4,3,2,1,0:T(8,128)(2,1)S(1)} %get-tuple-element.63), channel_id=1, source_target_pairs={{1,0},{2,1},{3,2},{4,3},{5,4},{6,5},{7,6},{8,7},{9,8},{10,9},{11,1... | collective-permute-start | bytes 2359304 | tf_op jit(solution)/shard_map/ppermute | solution.py:430
  123.3 19.0 %collective-permute-start.2 = (bf16[2,16,4,8,384]{4,3,2,1,0:T(8,128)(2,1)S(1)}, bf16[2,16,4,8,384]{4,3,2,1,0:T(8,128)(2,1)S(1)}, u32[]{:S(2)}, u32[]{:S(2)}) collective-permute-start(bf16[2,16,4,8,384]{4,3,2,1,0:T(8,128)(2,1)S(1)} %get-tuple-element.64), channel_id=1, source_target_pairs={{0,1},{1,2},{2,3},{3,4},{4,5},{5,6},{6,7},{7,8},{8,9},{9,10},{10,1... | collective-permute-start | bytes 2359304 | tf_op jit(solution)/shard_map/ppermute | solution.py:427
  123.3 27.9 %collective-permute-start.7 = (bf16[2,16,4,8,384]{4,3,2,1,0:T(8,128)(2,1)S(1)}, bf16[2,16,4,8,384]{4,3,2,1,0:T(8,128)(2,1)S(1)}, u32[]{:S(2)}, u32[]{:S(2)}) collective-permute-start(bf16[2,16,4,8,384]{4,3,2,1,0:T(8,128)(2,1)S(1)} %get-tuple-element.61), channel_id=1, source_target_pairs={{1,0},{2,1},{3,2},{4,3},{5,4},{6,5},{7,6},{8,7},{9,8},{10,9},{11,1... | collective-permute-start | bytes 2359304 | tf_op jit(solution)/shard_map/ppermute | solution.py:430
  128.4 22.8 %collective-permute-start.6 = (bf16[2,16,4,8,384]{4,3,2,1,0:T(8,128)(2,1)S(1)}, bf16[2,16,4,8,384]{4,3,2,1,0:T(8,128)(2,1)S(1)}, u32[]{:S(2)}, u32[]{:S(2)}) collective-permute-start(bf16[2,16,4,8,384]{4,3,2,1,0:T(8,128)(2,1)S(1)} %get-tuple-element.62), channel_id=1, source_target_pairs={{0,1},{1,2},{2,3},{3,4},{4,5},{5,6},{6,7},{7,8},{8,9},{9,10},{10,1... | collective-permute-start | bytes 2359304 | tf_op jit(solution)/shard_map/ppermute | solution.py:427
  128.4 3.0 %copy-start.12 = (bf16[1536,2304]{1,0:T(8,128)(2,1)S(1)}, bf16[1536,2304]{1,0:T(8,128)(2,1)}, u32[]{:S(2)}) copy-start(bf16[1536,2304]{1,0:T(8,128)(2,1)} %get-tuple-element.43.w0_ref) | copy-start | bytes 21233668
  131.4 3.0 %copy-start.13 = (bf16[1536,2304]{1,0:T(8,128)(2,1)S(1)}, bf16[1536,2304]{1,0:T(8,128)(2,1)}, u32[]{:S(2)}) copy-start(bf16[1536,2304]{1,0:T(8,128)(2,1)} %get-tuple-element.44.w1_ref) | copy-start | bytes 21233668
  134.4 7.9 %copy-start.15 = (bf16[2,768,1152]{2,1,0:T(8,128)(2,1)S(1)}, bf16[2,768,1152]{2,1,0:T(8,128)(2,1)}, u32[]{:S(2)}) copy-start(bf16[2,768,1152]{2,1,0:T(8,128)(2,1)} %copy-done.14) | copy-start | bytes 10616836
  134.5 16.7 %copy-start.4 = (bf16[768,2304]{1,0:T(8,128)(2,1)S(1)}, bf16[768,2304]{1,0:T(8,128)(2,1)}, u32[]{:S(2)}) copy-start(bf16[768,2304]{1,0:T(8,128)(2,1)} %copy-done.3) | copy-start | bytes 10616836
  142.3 8.8 %copy-start.26 = (f32[384]{0:T(512)S(1)}, f32[384]{0:T(512)}, u32[]{:S(2)}) copy-start(f32[384]{0:T(512)} %param.22) | copy-start | bytes 4612
  142.3 8.9 %copy-start.2 = (bf16[2,768,1152]{2,1,0:T(8,128)(2,1)S(1)}, bf16[2,768,1152]{2,1,0:T(8,128)(2,1)}, u32[]{:S(2)}) copy-start(bf16[2,768,1152]{2,1,0:T(8,128)(2,1)} %copy-done.1) | copy-start | bytes 10616836
  142.3 8.9 %copy-start.11 = (bf16[4,2,128,384]{3,2,1,0:T(8,128)(2,1)S(1)}, bf16[4,2,128,384]{3,2,1,0:T(8,128)(2,1)}, u32[]{:S(2)}) copy-start(bf16[4,2,128,384]{3,2,1,0:T(8,128)(2,1)} %copy-done.9) | copy-start | bytes 2359300
  145.7 12.0 %collective-permute-start.4 = (bf16[4,128,384]{2,1,0:T(8,128)(2,1)S(1)}, bf16[4,128,384]{2,1,0:T(8,128)(2,1)S(1)}, u32[]{:S(2)}, u32[]{:S(2)}) collective-permute-start(bf16[4,128,384]{2,1,0:T(8,128)(2,1)S(1)} %get-tuple-element.47), channel_id=1, source_target_pairs={{0,1},{1,2},{2,3},{3,4},{4,5},{5,6},{6,7},{7,8},{8,9},{9,10},{10,1... | collective-permute-start | bytes 1179656 | tf_op jit(solution)/shard_map/ppermute | solution.py:427
  145.8 11.9 %collective-permute-start.5 = (bf16[4,128,384]{2,1,0:T(8,128)(2,1)S(1)}, bf16[4,128,384]{2,1,0:T(8,128)(2,1)S(1)}, u32[]{:S(2)}, u32[]{:S(2)}) collective-permute-start(bf16[4,128,384]{2,1,0:T(8,128)(2,1)S(1)} %get-tuple-element.48), channel_id=1, source_target_pairs={{1,0},{2,1},{3,2},{4,3},{5,4},{6,5},{7,6},{8,7},{9,8},{10,9},{11,1... | collective-permute-start | bytes 1179656 | tf_op jit(solution)/shard_map/ppermute | solution.py:430
  151.2 6.5 %copy-start.6 = (bf16[4,2,128,384]{3,2,1,0:T(8,128)(2,1)S(1)}, bf16[4,2,128,384]{3,2,1,0:T(8,128)(2,1)}, u32[]{:S(2)}) copy-start(bf16[4,2,128,384]{3,2,1,0:T(8,128)(2,1)} %f_ref.3) | copy-start | bytes 2359300
  151.2 6.5 %copy-start.8 = (bf16[2,384,1152]{2,1,0:T(8,128)(2,1)S(1)}, bf16[2,384,1152]{2,1,0:T(8,128)(2,1)}, u32[]{:S(2)}) copy-start(bf16[2,384,1152]{2,1,0:T(8,128)(2,1)} %copy-done.7) | copy-start | bytes 5308420

commit v5 on v4

--- a/solution.py
+++ b/solution.py
@@ -75,22 +75,27 @@
             ),
         ),
         out_shape=jax.ShapeDtypeStruct(held.shape, held.dtype),
-        compiler_params=pltpu.CompilerParams(vmem_limit_bytes=32 << 20),
+        compiler_params=pltpu.CompilerParams(vmem_limit_bytes=58 << 20),
     )(source, rotation, keep, held)
 
 
-VMEM_LIMIT = 24 << 20
-
-
-def call(body, out_shape, operands, scalars=(), scratch=(), flops=0, moved=0):
+VMEM_LIMIT = 36 << 20
+
+
+def call(body, out_shape, operands, scalars=(), scratch=(), flops=0, moved=0, far=(), far_out=(), aliases=None):
     in_specs = [pl.BlockSpec(memory_space=pltpu.SMEM) for _ in scalars]
-    in_specs += [pl.BlockSpec(memory_space=pltpu.VMEM) for _ in operands]
+    for k, _ in enumerate(operands):
+        in_specs.append(pl.BlockSpec(memory_space=pl.ANY if k in far else pltpu.VMEM))
+    out_specs = []
+    for k, _ in enumerate(out_shape):
+        out_specs.append(pl.BlockSpec(memory_space=pl.ANY if k in far_out else pltpu.VMEM))
     return pl.pallas_call(
         body,
         in_specs=in_specs,
-        out_specs=[pl.BlockSpec(memory_space=pltpu.VMEM) for _ in out_shape],
+        out_specs=out_specs,
         out_shape=list(out_shape),
         scratch_shapes=list(scratch),
+        input_output_aliases=aliases or {},
         cost_estimate=pl.CostEstimate(flops=flops, bytes_accessed=moved, transcendentals=0),
         compiler_params=pltpu.CompilerParams(vmem_limit_bytes=VMEM_LIMIT),
     )(*scalars, *operands)
@@ -265,32 +270,74 @@
     )[0]
 
 
-def own_part(got, weights, sums):
+def own_part(got, weights, sums, act):
     n_rows, n_caches, n_frames, blocks, n_slots, _, ch = got.shape
     half = blocks * n_slots * CB
     deep = n_frames * ch
-
-    def body(got_ref, w0_ref, w1_ref, z_ref, o0_ref, o1_ref, lhs):
-        for k, (w, o_ref, base) in enumerate(((w0_ref, o0_ref, z_ref), (w1_ref, o1_ref, None))):
+    parts = 3
+    whole = weights[0]
+    part = whole.shape[1] // parts
+
+    def body(got_ref, w0_ref, w1_ref, z_ref, act_ref, o0_ref, o1_ref, n1_ref, n2_ref, w, lhs, acc, sems, kept_sems, act_sem):
+        loads = []
+        for k, src in enumerate((w0_ref, w1_ref)):
+            for p in range(parts):
+                cols = pl.ds(p * part, part)
+                n = k * parts + p
+                loads.append(pltpu.make_async_copy(src.at[:, cols], w.at[k, :, cols], sems.at[n]))
+        loads[0].start()
+        loads[1].start()
+        keeps = []
+        for k, dst in enumerate((n1_ref, n2_ref)):
+            for r in range(n_rows):
+                for s in range(n_slots):
+                    n = (k * n_rows + r) * n_slots + s
+                    keeps.append(
+                        pltpu.make_async_copy(
+                            got_ref.at[r, k, n_frames - 1, :, s], dst.at[s, 0, r], kept_sems.at[n]
+                        )
+                    )
+        keeps.append(pltpu.make_async_copy(act_ref, n1_ref.at[:, 1], act_sem))
+        for k, (o_ref, base) in enumerate(((o0_ref, z_ref), (o1_ref, None))):
             for r in range(n_rows):
                 for f in range(n_frames):
                     lo = r * deep + f * ch
                     lhs[:, lo : lo + ch] = got_ref[r, k, f].reshape(half, ch)
-            both = dot(lhs[...], w[...])
-            wide = both.shape[1] // 2
+            for p in range(parts):
+                n = k * parts + p
+                loads[n].wait()
+                if n + 2 < len(loads):
+                    loads[n + 2].start()
+                if n == 3:
+                    for c in keeps:
+                        c.start()
+                cols = slice(p * part, (p + 1) * part)
+                acc[:, cols] = dot(lhs[...], w[k, :, cols])
+            wide = whole.shape[1] // 2
             for y in range(n_rows):
-                total = folded(both[:, y * wide : (y + 1) * wide], ch, True)
+                total = folded(acc[:, y * wide : (y + 1) * wide], ch, True)
                 add_into(o_ref, y, total, True, base)
+        for c in keeps:
+            c.wait()
 
     out = sums_shape(blocks, n_slots, n_rows, ch)
-    whole = weights[0]
+    nxt = jax.ShapeDtypeStruct((n_slots, 2, n_rows, blocks, CB, ch), jnp.bfloat16)
     return call(
         body,
-        [out, out],
-        (got, *weights, sums),
-        scratch=[pltpu.VMEM((half, n_rows * deep), jnp.bfloat16)],
+        [out, out, nxt, nxt],
+        (got, *weights, sums, act),
+        scratch=[
+            pltpu.VMEM((2,) + whole.shape, whole.dtype),
+            pltpu.VMEM((half, n_rows * deep), jnp.bfloat16),
+            pltpu.VMEM((half, whole.shape[1]), jnp.float32),
+            pltpu.SemaphoreType.DMA((2 * parts,)),
+            pltpu.SemaphoreType.DMA((2 * n_rows * n_slots,)),
+            pltpu.SemaphoreType.DMA,
+        ],
         flops=4 * half * whole.size,
         moved=4 * whole.size,
+        far=(1, 2),
+        far_out=(2, 3),
     )
 
 
@@ -331,33 +378,33 @@
     )
 
 
-def before_sides(above, below, act, w_sides, w_act, sums, got, act_first, edges):
+def before_sides(above, below, act, w_sides, w_act, sums, kept, edges):
     n_frames, blocks, n_slots, _, ch = above.shape
     n_rows, n_cols, deep = sums.shape[0], blocks * CB, n_frames * ch
 
-    def body(edge_ref, above_ref, below_ref, act_ref, w_ref, wa_ref, z_ref, got_ref, act1_ref, o_ref, n1_ref, n2_ref, lhs, lhs2):
+    def body(edge_ref, above_ref, below_ref, act_ref, tiles_ref, w_ref, wa_ref, z_ref, kept_ref, o_ref, next_ref, lhs, lhs2, sem):
+        copy = pltpu.make_async_copy(tiles_ref, next_ref.at[:, 1], sem)
+        copy.start()
         add_own(act_ref, wa_ref, lhs2, o_ref, z_ref)
         for y, side in enumerate((above_ref, below_ref)):
             o_ref[y] += side_sums(edge_ref, y, side, w_ref[y], lhs)
-        for s in range(n_slots):
-            for r in range(n_rows):
-                n2_ref[s, 1, r] = act_ref[s, r]
-                n1_ref[s, 1, r] = act1_ref[s, r]
-                n1_ref[s, 0, r] = got_ref[r, 0, 1, :, s].reshape(n_cols, ch)
-                n2_ref[s, 0, r] = got_ref[r, 1, 1, :, s].reshape(n_cols, ch)
-
-    nxt = jax.ShapeDtypeStruct((n_slots, 2, n_rows, n_cols, ch), jnp.bfloat16)
+        copy.wait()
+
     return call(
         body,
-        [jax.ShapeDtypeStruct(sums.shape, jnp.float32), nxt, nxt],
-        (above, below, act, w_sides, w_act, sums, got, act_first),
+        [jax.ShapeDtypeStruct(sums.shape, jnp.float32), jax.ShapeDtypeStruct(kept.shape, kept.dtype)],
+        (above, below, act, act.reshape(n_slots, n_rows, blocks, CB, ch), w_sides, w_act, sums, kept),
         scalars=(edges,),
         scratch=[
             pltpu.VMEM((blocks, n_slots, CB, deep), jnp.bfloat16),
             pltpu.VMEM((n_slots * n_cols, n_rows * ch), jnp.bfloat16),
+            pltpu.SemaphoreType.DMA,
         ],
         flops=2 * n_slots * n_cols * (w_sides.size + w_act.size),
         moved=2 * (w_sides.size + w_act.size),
+        far=(7,),
+        far_out=(1,),
+        aliases={8: 1},
     )
 
 
@@ -436,7 +483,9 @@
     own_2, sides_2, act_own_2, act_sides_2 = spread(conv_second)
     act_first, top, bottom = first_activation(frame_in, gain_first[None])
     act_above, act_below = from_above(bottom), from_below(top)
-    held, act_first, own_1, own_2 = lax.optimization_barrier((held, act_first, own_1, own_2))
+    held, act_first, act_above, act_below, own_1, own_2 = lax.optimization_barrier(
+        (held, act_first, act_above, act_below, own_1, own_2)
+    )
 
     moved = permute(held.reshape(n_groups, n_tiles, n_slots, CB, ch), source, rotation, keep)
     moved, act_later = lax.optimization_barrier((moved, act_first))
@@ -451,18 +500,20 @@
     below_1 = from_below(got[0, 0])
     above_2 = from_above(got[n_rows - 1, 1])
     below_2 = from_below(got[0, 1])
-    sums_1, sums_2 = own_part(got, (own_1, own_2), sums_1)
+    act_tiles = act_first.reshape(n_slots, n_rows, blocks, CB, ch)
+    sums_1, sums_2, next_first, kept = own_part(got, (own_1, own_2), sums_1, act_tiles)
     act_second, top, bottom = second_activation(
         above_1, below_1, sides_1, sums_1, bias_first[None], gain_second[None], edges
     )
     side_above, side_below = from_above(bottom), from_below(top)
-    sums_2, next_first, next_second = before_sides(
-        above_2, below_2, act_second, sides_2, act_own_2, sums_2, got, act_first, edges
+    sums_2, next_second = before_sides(
+        above_2, below_2, act_second, sides_2, act_own_2, sums_2, kept, edges
     )
     mixed_frame = last_part(
         side_above, side_below, act_sides_2, sums_2, bias_second[None], frame_in, edges
     )
-    return (mixed_frame, next_first, next_second)
+    whole = (n_slots, 2, n_rows, n_cols, ch)
+    return (mixed_frame, next_first.reshape(whole), next_second.reshape(whole))
 
 
 def solution(mesh):

time: 161 us -> 162 us (level)
  waiting for transfers between devices: 53.6 us -> 41.6 us
  Pallas kernels: 48 us -> 58.4 us
  other arithmetic: 0.25 us -> 1.89 us
    all_to_all x1, waiting for transfers between devices: 0.01 us -> 31.1 us  [local(): lax.all_to_all(moved.reshape(n_groups * n_tiles, n_slots, CB, ch), BOTH,...]
    ppermute x4, waiting for transfers between devices: 38.8 us -> 10.5 us  [from_above(): return lax.ppermute(row, 'tile', down)]
    all_to_all x1, waiting for transfers between devices: 14.8 us -> 0.01 us  [local(): held = lax.all_to_all(sent, BOTH, 0, 0, tiled=True)]
    pallas_call x1, Pallas kernels: 2.91 us -> 10.9 us  [permute(): pl.pallas_call(body, grid_spec=pltpu.PrefetchScalarGridSpec(num_scalar_pr...]
    pallas_call x6, Pallas kernels: 25.9 us -> 28.3 us  [call(): pl.pallas_call(body, in_specs=in_specs, out_specs=out_specs, out_shape=li...]
    unnamed x64 -> x66, local copies, waits for them, and re-layouts: 24.7 us -> 24.2 us
  transfers between devices with their start and end apart: 10 -> 10, of which waited for: 2 -> 2; matrix products, arithmetic and copies ran while one was open for 0% -> 1% of each run, Pallas kernels for 23% -> 25%
where the time goes in v5:
time: 162 us; the launch traced here: 161 us
  Pallas kernels  58.4 us (36%)
  waiting for transfers between devices  41.6 us (26%)
  starting transfers between devices  33.5 us (21%)
  local copies, waits for them, and re-layouts  24.5 us (15%)
  other arithmetic  1.89 us (1%)
    all_to_all x1, waiting for transfers between devices, local(): lax.all_to_all(moved.reshape(n_groups * n_tiles, n_slots, CB, ch), BOTH,...  31.1 us
    pallas_call x6, Pallas kernels, call(): pl.pallas_call(body, in_specs=in_specs, out_specs=out_specs, out_shape=li...  28.3 us
    unnamed x66, local copies, waits for them, and re-layouts  24.2 us
    ppermute x4, starting transfers between devices, from_below(): return lax.ppermute(row, 'tile', up)  15.5 us
    pallas_call x2, Pallas kernels, spread(): pl.pallas_call(body, grid=(n_y,), in_specs=[pl.BlockSpec((n_t, 1, n_x, ci...  14.9 us
    all_to_all x1, starting transfers between devices, local(): held = lax.all_to_all(sent, BOTH, 0, 0, tiled=True)  11.6 us
    pallas_call x1, Pallas kernels, permute(): pl.pallas_call(body, grid_spec=pltpu.PrefetchScalarGridSpec(num_scalar_pr...  10.9 us
    ppermute x4, waiting for transfers between devices, from_above(): return lax.ppermute(row, 'tile', down)  10.5 us
  transfers between devices with their start and end apart: 10, of which 2 were waited for; matrix products, arithmetic and copies ran while one was open for 1% of the time, Pallas kernels for 25%

profile of v5, /device:TPU:0, one launch (start us, length us, event | category | flops | bytes accessed | tf_op | source)
XLA Modules:
  0.0 160.9 jit_solution(9518149646166656670)
XLA Ops:
  0.6 4.3 %shard_map.157 = bf16[2,2,2,16,4,8,384]{6,5,4,3,2,1,0:T(8,128)(2,1)} custom-call(bf16[4,2,2,128,384]{4,3,2,1,0:T(8,128)(2,1)} %a_ref.1, bf16[4,2,2,128,384]{4,3,2,1,0:T(8,128)(2,1)} %b_ref.1), custom_call_target="tpu_custom_call" | custom-call | tf_op jit(solution)/shard_map/pallas_call | solution.py:27
  4.9 11.6 %all-to-all-start = ((bf16[128,4,8,384]{3,2,1,0:T(8,128)(2,1)}), bf16[128,4,8,384]{3,2,1,0:T(8,128)(2,1)}, u32[]{:S(2)}, u32[]{:S(2)}) async-start(bf16[128,4,8,384]{3,2,1,0:T(8,128)(2,1)} %bitcast.24), calls=%async_computation | async-start | bytes 6291456 | tf_op jit(solution)/shard_map/all_to_all | solution.py:480
  16.6 0.7 shard_map.158
  17.3 0.0 copy-start.15
  17.3 0.9 copy-done.15
  18.2 0.0 collective-permute-start
  18.2 5.1 %collective-permute-start.1 = (bf16[4,128,384]{2,1,0:T(8,128)(2,1)S(1)}, bf16[4,128,384]{2,1,0:T(8,128)(2,1)S(1)}, u32[]{:S(2)}, u32[]{:S(2)}) collective-permute-start(bf16[4,128,384]{2,1,0:T(8,128)(2,1)S(1)} %get-tuple-element.35), channel_id=1, source_target_pairs={{1,0},{2,1},{3,2},{4,3},{5,4},{6,5},{7,6},{8,7},{9,8},{10,9},{11,1... | collective-permute-start | bytes 1179656 | tf_op jit(solution)/shard_map/ppermute | solution.py:477
  23.2 7.4 %shard_map.159 = (bf16[1536,2304]{1,0:T(8,128)(2,1)}, bf16[2,768,1152]{2,1,0:T(8,128)(2,1)S(1)}, bf16[768,2304]{1,0:T(8,128)(2,1)S(1)}, bf16[2,384,1152]{2,1,0:T(8,128)(2,1)S(1)}) custom-call(bf16[3,3,3,384,384]{4,3,2,1,0:T(8,128)(2,1)} %w_ref.2), custom_call_target="tpu_custom_call" | custom-call | bytes 19906560 | tf_op jit(solution)/shard_map/pallas_call | solution.py:146
  30.6 1.8 %copy-done.9 = bf16[2,768,1152]{2,1,0:T(8,128)(2,1)} copy-done((bf16[2,768,1152]{2,1,0:T(8,128)(2,1)}, bf16[2,768,1152]{2,1,0:T(8,128)(2,1)S(1)}, u32[]{:S(2)}) %copy-start.9) | copy-done | bytes 3538968
  32.4 1.8 %copy-done.11 = bf16[768,2304]{1,0:T(8,128)(2,1)} copy-done((bf16[768,2304]{1,0:T(8,128)(2,1)}, bf16[768,2304]{1,0:T(8,128)(2,1)S(1)}, u32[]{:S(2)}) %copy-start.11) | copy-done | bytes 3538968
  34.1 1.2 copy-done.13
  35.4 0.0 copy-start.32
  35.4 7.5 %shard_map.160 = (bf16[1536,2304]{1,0:T(8,128)(2,1)}, bf16[2,768,1152]{2,1,0:T(8,128)(2,1)S(1)}, bf16[768,2304]{1,0:T(8,128)(2,1)S(1)}, bf16[2,384,1152]{2,1,0:T(8,128)(2,1)S(1)}) custom-call(bf16[3,3,3,384,384]{4,3,2,1,0:T(8,128)(2,1)} %w_ref.3), custom_call_target="tpu_custom_call" | custom-call | bytes 19906560 | tf_op jit(solution)/shard_map/pallas_call | solution.py:146
  42.9 1.2 copy-done.2
  44.1 1.8 %copy-done.5 = bf16[2,768,1152]{2,1,0:T(8,128)(2,1)} copy-done((bf16[2,768,1152]{2,1,0:T(8,128)(2,1)}, bf16[2,768,1152]{2,1,0:T(8,128)(2,1)S(1)}, u32[]{:S(2)}) %copy-start.5) | copy-done | bytes 3538968
  45.9 1.8 %copy-done.7 = bf16[768,2304]{1,0:T(8,128)(2,1)} copy-done((bf16[768,2304]{1,0:T(8,128)(2,1)}, bf16[768,2304]{1,0:T(8,128)(2,1)S(1)}, u32[]{:S(2)}) %copy-start.7) | copy-done | bytes 3538968
  47.7 0.6 select_reduce_fusion
  48.3 0.6 compare_convert_fusion.keep_ref
  48.9 0.6 and_select_fusion
  49.5 10.5 %collective-permute-done.above_ref = bf16[4,128,384]{2,1,0:T(8,128)(2,1)S(1)} collective-permute-done((bf16[4,128,384]{2,1,0:T(8,128)(2,1)S(1)}, bf16[4,128,384]{2,1,0:T(8,128)(2,1)S(1)}, u32[]{:S(2)}, u32[]{:S(2)}) %collective-permute-start) | collective-permute-done | bytes 393248 | tf_op jit(solution)/shard_map/ppermute | solution.py:474
  60.0 10.9 %shard_map.161 = bf16[4,32,4,8,384]{4,3,2,1,0:T(8,128)(2,1)} custom-call(s32[16]{0:T(128)} %get-tuple-element.65.source_ref, s32[16]{0:T(128)} %get-tuple-element.71.rotation_ref, s32[16]{0:T(128)} %compare_convert_fusion.keep_ref, bf16[4,32,4,8,384]{4,3,2,1,0:T(8,128)(2,1)} %bitcast.3.i_ref), custom_call_target="tpu_custom_call" | custom-call | tf_op jit(solution)/shard_map/pallas_call | solution.py:62
  70.9 6.0 %all-to-all-start.1 = ((bf16[128,4,8,384]{3,2,1,0:T(8,128)(2,1)}), bf16[128,4,8,384]{3,2,1,0:T(8,128)(2,1)S(1)}, u32[]{:S(2)}, u32[]{:S(2)}) async-start(bf16[128,4,8,384]{3,2,1,0:T(8,128)(2,1)} %bitcast.25), calls=%async_computation.1 | async-start | bytes 6291456 | tf_op jit(solution)/shard_map/all_to_all | solution.py:492
  77.0 0.1 compare_bitcast_fusion.1
  77.1 2.0 %copy-done.12 = bf16[768,2304]{1,0:T(8,128)(2,1)S(1)} copy-done((bf16[768,2304]{1,0:T(8,128)(2,1)S(1)}, bf16[768,2304]{1,0:T(8,128)(2,1)}, u32[]{:S(2)}) %copy-start.12) | copy-done | bytes 3538968
  79.0 1.5 copy-done.14
  80.5 1.1 copy-done.16
  81.7 1.0 copy-done.19
  82.7 3.9 %shard_map.162.z_ref = f32[2,16,4,8,384]{4,3,2,1,0:T(8,128)S(1)} custom-call(s32[2,4]{1,0:T(2,128)S(1)} %add_convert_fusion.edge_ref, bf16[4,2,128,384]{3,2,1,0:T(8,128)(2,1)S(1)} %copy-done.16, bf16[4,128,384]{2,1,0:T(8,128)(2,1)S(1)} %collective-permute-done.above_ref, bf16[4,128,384]{2,1,0:T(8,128)(2,1)S(1)} %copy-done.19, ...), custom_call_target="tpu_custom_call" | custom-call | flops 2717908992 | bytes 6684672 | tf_op jit(solution)/shard_map/pallas_call | solution.py:92
  86.5 0.0 copy-start.22
  86.6 1.1 copy-done.22
  87.7 31.1 %all-to-all-done.1 = bf16[128,4,8,384]{3,2,1,0:T(8,128)(2,1)S(1)} async-done(((bf16[128,4,8,384]{3,2,1,0:T(8,128)(2,1)}), bf16[128,4,8,384]{3,2,1,0:T(8,128)(2,1)S(1)}, u32[]{:S(2)}, u32[]{:S(2)}) %all-to-all-start.1) | async-done | bytes 3145760 | tf_op jit(solution)/shard_map/all_to_all | solution.py:492
  118.8 0.3 slice_bitcast_fusion
  119.1 0.3 collective-permute-start.3
  119.4 0.3 collective-permute-start.2
  119.7 4.8 %collective-permute-start.7 = (bf16[2,16,4,8,384]{4,3,2,1,0:T(8,128)(2,1)S(1)}, bf16[2,16,4,8,384]{4,3,2,1,0:T(8,128)(2,1)S(1)}, u32[]{:S(2)}, u32[]{:S(2)}) collective-permute-start(bf16[2,16,4,8,384]{4,3,2,1,0:T(8,128)(2,1)S(1)} %get-tuple-element.67), channel_id=1, source_target_pairs={{1,0},{2,1},{3,2},{4,3},{5,4},{6,5},{7,6},{8,7},{9,8},{10,9},{11,1... | collective-permute-start | bytes 2359304 | tf_op jit(solution)/shard_map/ppermute | solution.py:477
  124.6 0.0 collective-permute-start.6
  124.6 3.0 %copy-done.4 = bf16[1536,2304]{1,0:T(8,128)(2,1)S(1)} copy-done((bf16[1536,2304]{1,0:T(8,128)(2,1)S(1)}, bf16[1536,2304]{1,0:T(8,128)(2,1)}, u32[]{:S(2)}) %copy-start.4) | copy-done | bytes 7077912
  127.6 12.2 %shard_map.163 = (f32[2,16,4,8,384]{4,3,2,1,0:T(8,128)S(1)}, f32[2,16,4,8,384]{4,3,2,1,0:T(8,128)S(1)}, bf16[4,2,2,16,8,384]{5,4,3,2,1,0:T(8,128)(2,1)}, bf16[4,2,2,16,8,384]{5,4,3,2,1,0:T(8,128)(2,1)}) custom-call(bf16[2,2,2,16,4,8,384]{6,5,4,3,2,1,0:T(8,128)(2,1)S(1)} %bitcast.21, bf16[1536,2304]{1,0:T(8,128)(2,1)S(1)} %copy-done.4, ...), custom_call_target="tpu_custom_call" | custom-call | flops 7247757312 | bytes 14155776 | tf_op jit(solution)/shard_map/pallas_call | solution.py:92
  139.8 0.0 collective-permute-done.3.below_ref
  139.8 0.0 collective-permute-done.2.above_ref
  139.8 2.5 %copy-done.10 = bf16[2,768,1152]{2,1,0:T(8,128)(2,1)S(1)} copy-done((bf16[2,768,1152]{2,1,0:T(8,128)(2,1)S(1)}, bf16[2,768,1152]{2,1,0:T(8,128)(2,1)}, u32[]{:S(2)}) %copy-start.10) | copy-done | bytes 3538968
  142.4 3.4 %shard_map.164 = (bf16[4,2,128,384]{3,2,1,0:T(8,128)(2,1)S(1)}, bf16[4,128,384]{2,1,0:T(8,128)(2,1)S(1)}, bf16[4,128,384]{2,1,0:T(8,128)(2,1)S(1)}) custom-call(s32[2,4]{1,0:T(2,128)S(1)} %add_convert_fusion.edge_ref, bf16[2,16,4,8,384]{4,3,2,1,0:T(8,128)(2,1)S(1)} %collective-permute-done.2.above_ref, ...), custom_call_target="tpu_custom_call" | custom-call | flops 1811939328 | bytes 3538944 | tf_op jit(solution)/shard_map/pallas_call | solution.py:92
  145.8 0.1 collective-permute-start.4
  145.9 5.4 %collective-permute-start.5 = (bf16[4,128,384]{2,1,0:T(8,128)(2,1)S(1)}, bf16[4,128,384]{2,1,0:T(8,128)(2,1)S(1)}, u32[]{:S(2)}, u32[]{:S(2)}) collective-permute-start(bf16[4,128,384]{2,1,0:T(8,128)(2,1)S(1)} %get-tuple-element.53), channel_id=1, source_target_pairs={{1,0},{2,1},{3,2},{4,3},{5,4},{6,5},{7,6},{8,7},{9,8},{10,9},{11,1... | collective-permute-start | bytes 1179656 | tf_op jit(solution)/shard_map/ppermute | solution.py:477
  151.2 0.0 collective-permute-done.6.above_ref
  151.3 1.4 copy-done.21
  152.7 5.2 %shard_map.165 = (f32[2,16,4,8,384]{4,3,2,1,0:T(8,128)S(1)}, bf16[4,2,2,16,8,384]{5,4,3,2,1,0:T(8,128)(2,1)}) custom-call(s32[2,4]{1,0:T(2,128)S(1)} %add_convert_fusion.edge_ref, bf16[2,16,4,8,384]{4,3,2,1,0:T(8,128)(2,1)S(1)} %collective-permute-done.6.above_ref, ...), custom_call_target="tpu_custom_call", output_to_operand_aliasing={{1}: (8, {})} | custom-call | flops 3623878656 | bytes 7077888 | tf_op jit(solution)/shard_map/pallas_call | solution.py:92
  157.9 2.9 %shard_map.166 = bf16[4,2,128,384]{3,2,1,0:T(8,128)(2,1)} custom-call(s32[2,4]{1,0:T(2,128)S(1)} %add_convert_fusion.edge_ref, bf16[4,128,384]{2,1,0:T(8,128)(2,1)S(1)} %collective-permute-done.4.above_ref, bf16[4,128,384]{2,1,0:T(8,128)(2,1)S(1)} %collective-permute-done.5.below_ref, bf16[2,384,1152]{2,1,0:T(8,128)(2,1)S(1)} %copy-done.3, ...), custom_call_target="tpu_custom_call" | custom-call | flops 905969664 | bytes 1769472 | tf_op jit(solution)/shard_map/pallas_call | solution.py:92
  (58 shorter events, 0.1 us)
Async XLA Ops:
  4.9 11.6 %copy-start.24 = (f32[384]{0:T(512)S(1)}, f32[384]{0:T(512)}, u32[]{:S(2)}) copy-start(f32[384]{0:T(512)} %param.17) | copy-start | bytes 4612
  4.9 11.6 %copy-start = (bf16[4,2,128,384]{3,2,1,0:T(8,128)(2,1)S(1)}, bf16[4,2,128,384]{3,2,1,0:T(8,128)(2,1)}, u32[]{:S(2)}) copy-start(bf16[4,2,128,384]{3,2,1,0:T(8,128)(2,1)} %f_ref.3) | copy-start | bytes 2359300
  4.9 55.1 %all-to-all-start = ((bf16[128,4,8,384]{3,2,1,0:T(8,128)(2,1)}), bf16[128,4,8,384]{3,2,1,0:T(8,128)(2,1)}, u32[]{:S(2)}, u32[]{:S(2)}) async-start(bf16[128,4,8,384]{3,2,1,0:T(8,128)(2,1)} %bitcast.24), calls=%async_computation | async-start | bytes 6291456 | tf_op jit(solution)/shard_map/all_to_all | solution.py:480
  17.3 0.9 copy-start.15
  18.2 41.9 %collective-permute-start = (bf16[4,128,384]{2,1,0:T(8,128)(2,1)S(1)}, bf16[4,128,384]{2,1,0:T(8,128)(2,1)S(1)}, u32[]{:S(2)}, u32[]{:S(2)}) collective-permute-start(bf16[4,128,384]{2,1,0:T(8,128)(2,1)S(1)} %get-tuple-element.34), channel_id=1, source_target_pairs={{0,1},{1,2},{2,3},{3,4},{4,5},{5,6},{6,7},{7,8},{8,9},{9,10},{10,1... | collective-permute-start | bytes 1179656 | tf_op jit(solution)/shard_map/ppermute | solution.py:474
  18.2 41.9 %collective-permute-start.1 = (bf16[4,128,384]{2,1,0:T(8,128)(2,1)S(1)}, bf16[4,128,384]{2,1,0:T(8,128)(2,1)S(1)}, u32[]{:S(2)}, u32[]{:S(2)}) collective-permute-start(bf16[4,128,384]{2,1,0:T(8,128)(2,1)S(1)} %get-tuple-element.35), channel_id=1, source_target_pairs={{1,0},{2,1},{3,2},{4,3},{5,4},{6,5},{7,6},{8,7},{9,8},{10,9},{11,1... | collective-permute-start | bytes 1179656 | tf_op jit(solution)/shard_map/ppermute | solution.py:477
  30.6 1.8 %copy-start.9 = (bf16[2,768,1152]{2,1,0:T(8,128)(2,1)}, bf16[2,768,1152]{2,1,0:T(8,128)(2,1)S(1)}, u32[]{:S(2)}) copy-start(bf16[2,768,1152]{2,1,0:T(8,128)(2,1)S(1)} %get-tuple-element.47.w_ref) | copy-start | bytes 10616836
  32.4 1.8 %copy-start.11 = (bf16[768,2304]{1,0:T(8,128)(2,1)}, bf16[768,2304]{1,0:T(8,128)(2,1)S(1)}, u32[]{:S(2)}) copy-start(bf16[768,2304]{1,0:T(8,128)(2,1)S(1)} %get-tuple-element.44.wo_ref) | copy-start | bytes 10616836
  34.1 1.2 copy-start.13
  35.4 12.3 %copy-start.28 = (s32[16]{0:T(128)S(1)}, s32[16]{0:T(128)}, u32[]{:S(2)}) copy-start(s32[16]{0:T(128)} %param.27) | copy-start | bytes 196
  35.4 12.3 %copy-start.29 = (s32[16]{0:T(128)S(1)}, s32[16]{0:T(128)}, u32[]{:S(2)}) copy-start(s32[16]{0:T(128)} %param.24) | copy-start | bytes 196
  35.4 12.3 %copy-start.30 = (s32[16]{0:T(128)S(1)}, s32[16]{0:T(128)}, u32[]{:S(2)}) copy-start(s32[16]{0:T(128)} %param.25) | copy-start | bytes 196
  35.4 12.3 %copy-start.31 = (s32[16]{0:T(128)S(1)}, s32[16]{0:T(128)}, u32[]{:S(2)}) copy-start(s32[16]{0:T(128)} %param.23) | copy-start | bytes 196
  35.4 12.3 %copy-start.32 = (s32[16]{0:T(128)S(1)}, s32[16]{0:T(128)}, u32[]{:S(2)}) copy-start(s32[16]{0:T(128)} %param.26) | copy-start | bytes 196
  42.9 1.2 copy-start.2
  44.1 1.8 %copy-start.5 = (bf16[2,768,1152]{2,1,0:T(8,128)(2,1)}, bf16[2,768,1152]{2,1,0:T(8,128)(2,1)S(1)}, u32[]{:S(2)}) copy-start(bf16[2,768,1152]{2,1,0:T(8,128)(2,1)S(1)} %get-tuple-element.56.w_ref) | copy-start | bytes 10616836
  45.9 1.8 %copy-start.7 = (bf16[768,2304]{1,0:T(8,128)(2,1)}, bf16[768,2304]{1,0:T(8,128)(2,1)S(1)}, u32[]{:S(2)}) copy-start(bf16[768,2304]{1,0:T(8,128)(2,1)S(1)} %get-tuple-element.57.wa_ref) | copy-start | bytes 10616836
  60.0 10.9 %copy-start.18 = (bf16[4,128,384]{2,1,0:T(8,128)(2,1)}, bf16[4,128,384]{2,1,0:T(8,128)(2,1)S(1)}, u32[]{:S(2)}) copy-start(bf16[4,128,384]{2,1,0:T(8,128)(2,1)S(1)} %collective-permute-done.1.below_ref) | copy-start | bytes 1179652
  70.9 47.9 %all-to-all-start.1 = ((bf16[128,4,8,384]{3,2,1,0:T(8,128)(2,1)}), bf16[128,4,8,384]{3,2,1,0:T(8,128)(2,1)S(1)}, u32[]{:S(2)}, u32[]{:S(2)}) async-start(bf16[128,4,8,384]{3,2,1,0:T(8,128)(2,1)} %bitcast.25), calls=%async_computation.1 | async-start | bytes 6291456 | tf_op jit(solution)/shard_map/all_to_all | solution.py:492
  77.0 2.0 %copy-start.12 = (bf16[768,2304]{1,0:T(8,128)(2,1)S(1)}, bf16[768,2304]{1,0:T(8,128)(2,1)}, u32[]{:S(2)}) copy-start(bf16[768,2304]{1,0:T(8,128)(2,1)} %copy-done.11) | copy-start | bytes 10616836
  79.0 1.5 copy-start.14
  80.5 1.1 copy-start.16
  81.7 1.0 copy-start.19
  86.5 1.1 copy-start.22
  118.8 0.9 copy-start.25
  118.8 0.9 copy-start.26
  118.8 5.8 %copy-start.17 = (bf16[4,2,128,384]{3,2,1,0:T(8,128)(2,1)S(1)}, bf16[4,2,128,384]{3,2,1,0:T(8,128)(2,1)}, u32[]{:S(2)}) copy-start(bf16[4,2,128,384]{3,2,1,0:T(8,128)(2,1)} %copy-done.15) | copy-start | bytes 2359300
  118.8 5.8 %copy-start.23 = (f32[2,16,4,8,384]{4,3,2,1,0:T(8,128)S(1)}, f32[2,16,4,8,384]{4,3,2,1,0:T(8,128)}, u32[]{:S(2)}) copy-start(f32[2,16,4,8,384]{4,3,2,1,0:T(8,128)} %copy-done.22) | copy-start | bytes 4718596
  119.1 20.7 %collective-permute-start.3 = (bf16[2,16,4,8,384]{4,3,2,1,0:T(8,128)(2,1)S(1)}, bf16[2,16,4,8,384]{4,3,2,1,0:T(8,128)(2,1)S(1)}, u32[]{:S(2)}, u32[]{:S(2)}) collective-permute-start(bf16[2,16,4,8,384]{4,3,2,1,0:T(8,128)(2,1)S(1)} %get-tuple-element.69), channel_id=1, source_target_pairs={{1,0},{2,1},{3,2},{4,3},{5,4},{6,5},{7,6},{8,7},{9,8},{10,9},{11,1... | collective-permute-start | bytes 2359304 | tf_op jit(solution)/shard_map/ppermute | solution.py:477
  119.4 20.4 %collective-permute-start.2 = (bf16[2,16,4,8,384]{4,3,2,1,0:T(8,128)(2,1)S(1)}, bf16[2,16,4,8,384]{4,3,2,1,0:T(8,128)(2,1)S(1)}, u32[]{:S(2)}, u32[]{:S(2)}) collective-permute-start(bf16[2,16,4,8,384]{4,3,2,1,0:T(8,128)(2,1)S(1)} %get-tuple-element.70), channel_id=1, source_target_pairs={{0,1},{1,2},{2,3},{3,4},{4,5},{5,6},{6,7},{7,8},{8,9},{9,10},{10,1... | collective-permute-start | bytes 2359304 | tf_op jit(solution)/shard_map/ppermute | solution.py:474
  119.7 31.5 %collective-permute-start.7 = (bf16[2,16,4,8,384]{4,3,2,1,0:T(8,128)(2,1)S(1)}, bf16[2,16,4,8,384]{4,3,2,1,0:T(8,128)(2,1)S(1)}, u32[]{:S(2)}, u32[]{:S(2)}) collective-permute-start(bf16[2,16,4,8,384]{4,3,2,1,0:T(8,128)(2,1)S(1)} %get-tuple-element.67), channel_id=1, source_target_pairs={{1,0},{2,1},{3,2},{4,3},{5,4},{6,5},{7,6},{8,7},{9,8},{10,9},{11,1... | collective-permute-start | bytes 2359304 | tf_op jit(solution)/shard_map/ppermute | solution.py:477
  124.6 26.7 %collective-permute-start.6 = (bf16[2,16,4,8,384]{4,3,2,1,0:T(8,128)(2,1)S(1)}, bf16[2,16,4,8,384]{4,3,2,1,0:T(8,128)(2,1)S(1)}, u32[]{:S(2)}, u32[]{:S(2)}) collective-permute-start(bf16[2,16,4,8,384]{4,3,2,1,0:T(8,128)(2,1)S(1)} %get-tuple-element.68), channel_id=1, source_target_pairs={{0,1},{1,2},{2,3},{3,4},{4,5},{5,6},{6,7},{7,8},{8,9},{9,10},{10,1... | collective-permute-start | bytes 2359304 | tf_op jit(solution)/shard_map/ppermute | solution.py:474
  124.6 3.0 %copy-start.4 = (bf16[1536,2304]{1,0:T(8,128)(2,1)S(1)}, bf16[1536,2304]{1,0:T(8,128)(2,1)}, u32[]{:S(2)}) copy-start(bf16[1536,2304]{1,0:T(8,128)(2,1)} %get-tuple-element.48.w0_ref) | copy-start | bytes 21233668
  127.6 23.7 %copy-start.8 = (bf16[768,2304]{1,0:T(8,128)(2,1)S(1)}, bf16[768,2304]{1,0:T(8,128)(2,1)}, u32[]{:S(2)}) copy-start(bf16[768,2304]{1,0:T(8,128)(2,1)} %copy-done.7) | copy-start | bytes 10616836
  139.8 6.0 %copy-start.20 = (f32[2,16,4,8,384]{4,3,2,1,0:T(8,128)}, f32[2,16,4,8,384]{4,3,2,1,0:T(8,128)S(1)}, u32[]{:S(2)}) copy-start(f32[2,16,4,8,384]{4,3,2,1,0:T(8,128)S(1)} %get-tuple-element.58.z_ref) | copy-start | bytes 4718596
  139.8 2.6 %copy-start.10 = (bf16[2,768,1152]{2,1,0:T(8,128)(2,1)S(1)}, bf16[2,768,1152]{2,1,0:T(8,128)(2,1)}, u32[]{:S(2)}) copy-start(bf16[2,768,1152]{2,1,0:T(8,128)(2,1)} %copy-done.9) | copy-start | bytes 10616836
  142.4 8.8 %copy-start.27 = (f32[384]{0:T(512)S(1)}, f32[384]{0:T(512)}, u32[]{:S(2)}) copy-start(f32[384]{0:T(512)} %param.22) | copy-start | bytes 4612
  142.4 8.9 %copy-start.6 = (bf16[2,768,1152]{2,1,0:T(8,128)(2,1)S(1)}, bf16[2,768,1152]{2,1,0:T(8,128)(2,1)}, u32[]{:S(2)}) copy-start(bf16[2,768,1152]{2,1,0:T(8,128)(2,1)} %copy-done.5) | copy-start | bytes 10616836
  145.8 12.1 %collective-permute-start.4 = (bf16[4,128,384]{2,1,0:T(8,128)(2,1)S(1)}, bf16[4,128,384]{2,1,0:T(8,128)(2,1)S(1)}, u32[]{:S(2)}, u32[]{:S(2)}) collective-permute-start(bf16[4,128,384]{2,1,0:T(8,128)(2,1)S(1)} %get-tuple-element.52), channel_id=1, source_target_pairs={{0,1},{1,2},{2,3},{3,4},{4,5},{5,6},{6,7},{7,8},{8,9},{9,10},{10,1... | collective-permute-start | bytes 1179656 | tf_op jit(solution)/shard_map/ppermute | solution.py:474
  145.9 12.0 %collective-permute-start.5 = (bf16[4,128,384]{2,1,0:T(8,128)(2,1)S(1)}, bf16[4,128,384]{2,1,0:T(8,128)(2,1)S(1)}, u32[]{:S(2)}, u32[]{:S(2)}) collective-permute-start(bf16[4,128,384]{2,1,0:T(8,128)(2,1)S(1)} %get-tuple-element.53), channel_id=1, source_target_pairs={{1,0},{2,1},{3,2},{4,3},{5,4},{6,5},{7,6},{8,7},{9,8},{10,9},{11,1... | collective-permute-start | bytes 1179656 | tf_op jit(solution)/shard_map/ppermute | solution.py:477
  151.3 1.4 copy-start.21
  152.7 5.2 %copy-start.1 = (bf16[4,2,128,384]{3,2,1,0:T(8,128)(2,1)S(1)}, bf16[4,2,128,384]{3,2,1,0:T(8,128)(2,1)}, u32[]{:S(2)}) copy-start(bf16[4,2,128,384]{3,2,1,0:T(8,128)(2,1)} %f_ref.3) | copy-start | bytes 2359300
  152.7 5.2 %copy-start.3 = (bf16[2,384,1152]{2,1,0:T(8,128)(2,1)S(1)}, bf16[2,384,1152]{2,1,0:T(8,128)(2,1)}, u32[]{:S(2)}) copy-start(bf16[2,384,1152]{2,1,0:T(8,128)(2,1)} %copy-done.2) | copy-start | bytes 5308420

commit v6 on v5

--- a/solution.py
+++ b/solution.py
@@ -75,11 +75,11 @@
             ),
         ),
         out_shape=jax.ShapeDtypeStruct(held.shape, held.dtype),
-        compiler_params=pltpu.CompilerParams(vmem_limit_bytes=58 << 20),
+        compiler_params=pltpu.CompilerParams(vmem_limit_bytes=32 << 20),
     )(source, rotation, keep, held)
 
 
-VMEM_LIMIT = 36 << 20
+VMEM_LIMIT = 16 << 20
 
 
 def call(body, out_shape, operands, scalars=(), scratch=(), flops=0, moved=0, far=(), far_out=(), aliases=None):
@@ -101,31 +101,25 @@
     )(*scalars, *operands)
 
 
-def spread(weight):
+def spread(weight, past):
     n_t, n_y, n_x, ci, co = weight.shape
     wide = n_x * co
-    past = n_t - 1
-
-    def body(w_ref, po_ref, ps_ref, ao_ref, as_ref):
+    times = n_t - 1 if past else 1
+
+    def body(w_ref, own_ref, side_ref):
         dy = pl.program_id(0)
-
-        def at(t, x):
-            return w_ref[t, 0, x]
 
         def side(y):
             for x in range(n_x):
-                cols = slice(x * co, (x + 1) * co)
-                for t in range(past):
-                    ps_ref[y, t * ci : (t + 1) * ci, cols] = at(t, x)
-                as_ref[y, :, cols] = at(past, x)
+                for t in range(times):
+                    side_ref[y, t * ci : (t + 1) * ci, x * co : (x + 1) * co] = w_ref[t, 0, x]
 
         def own(row, y):
             for x in range(n_x):
-                cols = slice(y * wide + x * co, y * wide + (x + 1) * co)
-                for t in range(past):
-                    lo = (row * past + t) * ci
-                    po_ref[lo : lo + ci, cols] = at(t, x)
-                ao_ref[row * ci : (row + 1) * ci, cols] = at(past, x)
+                for t in range(times):
+                    lo = (row * times + t) * ci
+                    at = y * wide + x * co
+                    own_ref[lo : lo + ci, at : at + co] = w_ref[t, 0, x]
 
         @pl.when(dy == 0)
         def _():
@@ -142,17 +136,16 @@
             side(1)
             own(1, 0)
 
-    shapes = [(2 * past * ci, 2 * wide), (2, past * ci, wide), (2 * ci, 2 * wide), (2, ci, wide)]
+    shapes = [(2 * times * ci, 2 * wide), (2, times * ci, wide)]
+    first = 0 if past else n_t - 1
     return pl.pallas_call(
         body,
         grid=(n_y,),
-        in_specs=[pl.BlockSpec((n_t, 1, n_x, ci, co), lambda y: (0, y, 0, 0, 0))],
-        out_specs=[
-            pl.BlockSpec(shape, lambda y, zeros=(0,) * len(shape): zeros) for shape in shapes
-        ],
+        in_specs=[pl.BlockSpec((times, 1, n_x, ci, co), lambda y: (first, y, 0, 0, 0))],
+        out_specs=[pl.BlockSpec(memory_space=pltpu.VMEM) for _ in shapes],
         out_shape=[jax.ShapeDtypeStruct(shape, weight.dtype) for shape in shapes],
-        cost_estimate=pl.CostEstimate(flops=0, bytes_accessed=5 * weight.size, transcendentals=0),
-        compiler_params=pltpu.CompilerParams(vmem_limit_bytes=40 << 20),
+        cost_estimate=pl.CostEstimate(flops=0, bytes_accessed=4 * weight.size, transcendentals=0),
+        compiler_params=pltpu.CompilerParams(vmem_limit_bytes=16 << 20),
     )(weight)
 
 
@@ -274,19 +267,9 @@
     n_rows, n_caches, n_frames, blocks, n_slots, _, ch = got.shape
     half = blocks * n_slots * CB
     deep = n_frames * ch
-    parts = 3
     whole = weights[0]
-    part = whole.shape[1] // parts
-
-    def body(got_ref, w0_ref, w1_ref, z_ref, act_ref, o0_ref, o1_ref, n1_ref, n2_ref, w, lhs, acc, sems, kept_sems, act_sem):
-        loads = []
-        for k, src in enumerate((w0_ref, w1_ref)):
-            for p in range(parts):
-                cols = pl.ds(p * part, part)
-                n = k * parts + p
-                loads.append(pltpu.make_async_copy(src.at[:, cols], w.at[k, :, cols], sems.at[n]))
-        loads[0].start()
-        loads[1].start()
+
+    def body(got_ref, w0_ref, w1_ref, z_ref, act_ref, o0_ref, o1_ref, n1_ref, n2_ref, lhs, sems, act_sem):
         keeps = []
         for k, dst in enumerate((n1_ref, n2_ref)):
             for r in range(n_rows):
@@ -294,28 +277,21 @@
                     n = (k * n_rows + r) * n_slots + s
                     keeps.append(
                         pltpu.make_async_copy(
-                            got_ref.at[r, k, n_frames - 1, :, s], dst.at[s, 0, r], kept_sems.at[n]
+                            got_ref.at[r, k, n_frames - 1, :, s], dst.at[s, 0, r], sems.at[n]
                         )
                     )
         keeps.append(pltpu.make_async_copy(act_ref, n1_ref.at[:, 1], act_sem))
-        for k, (o_ref, base) in enumerate(((o0_ref, z_ref), (o1_ref, None))):
+        for c in keeps:
+            c.start()
+        for k, (w, o_ref, base) in enumerate(((w0_ref, o0_ref, z_ref), (w1_ref, o1_ref, None))):
             for r in range(n_rows):
                 for f in range(n_frames):
                     lo = r * deep + f * ch
                     lhs[:, lo : lo + ch] = got_ref[r, k, f].reshape(half, ch)
-            for p in range(parts):
-                n = k * parts + p
-                loads[n].wait()
-                if n + 2 < len(loads):
-                    loads[n + 2].start()
-                if n == 3:
-                    for c in keeps:
-                        c.start()
-                cols = slice(p * part, (p + 1) * part)
-                acc[:, cols] = dot(lhs[...], w[k, :, cols])
-            wide = whole.shape[1] // 2
+            both = dot(lhs[...], w[...])
+            wide = both.shape[1] // 2
             for y in range(n_rows):
-                total = folded(acc[:, y * wide : (y + 1) * wide], ch, True)
+                total = folded(both[:, y * wide : (y + 1) * wide], ch, True)
                 add_into(o_ref, y, total, True, base)
         for c in keeps:
             c.wait()
@@ -327,16 +303,12 @@
         [out, out, nxt, nxt],
         (got, *weights, sums, act),
         scratch=[
-            pltpu.VMEM((2,) + whole.shape, whole.dtype),
             pltpu.VMEM((half, n_rows * deep), jnp.bfloat16),
-            pltpu.VMEM((half, whole.shape[1]), jnp.float32),
-            pltpu.SemaphoreType.DMA((2 * parts,)),
             pltpu.SemaphoreType.DMA((2 * n_rows * n_slots,)),
             pltpu.SemaphoreType.DMA,
         ],
         flops=4 * half * whole.size,
         moved=4 * whole.size,
-        far=(1, 2),
         far_out=(2, 3),
     )
 
@@ -479,12 +451,11 @@
     sent = pack(cache_first, cache_second).reshape(n_groups * n_tiles, n_slots, CB, ch)
     held = lax.all_to_all(sent, BOTH, 0, 0, tiled=True)
 
-    own_1, sides_1, act_own_1, act_sides_1 = spread(conv_first)
-    own_2, sides_2, act_own_2, act_sides_2 = spread(conv_second)
+    act_own_1, act_sides_1 = spread(conv_first, False)
     act_first, top, bottom = first_activation(frame_in, gain_first[None])
     act_above, act_below = from_above(bottom), from_below(top)
-    held, act_first, act_above, act_below, own_1, own_2 = lax.optimization_barrier(
-        (held, act_first, act_above, act_below, own_1, own_2)
+    held, act_first, act_above, act_below, act_own_1, act_sides_1 = lax.optimization_barrier(
+        (held, act_first, act_above, act_below, act_own_1, act_sides_1)
     )
 
     moved = permute(held.reshape(n_groups, n_tiles, n_slots, CB, ch), source, rotation, keep)
@@ -493,7 +464,13 @@
         moved.reshape(n_groups * n_tiles, n_slots, CB, ch), BOTH, 0, 0, tiled=True
     )
     sums_1 = current_part(act_later, act_above, act_below, act_own_1, act_sides_1, edges)
-    got, sums_1 = lax.optimization_barrier((got, sums_1))
+    sums_1, conv_first, conv_second = lax.optimization_barrier((sums_1, conv_first, conv_second))
+    act_own_2, act_sides_2 = spread(conv_second, False)
+    own_1, sides_1 = spread(conv_first, True)
+    own_2, sides_2 = spread(conv_second, True)
+    got, sums_1, own_1, own_2, sides_1, sides_2, act_own_2, act_sides_2 = lax.optimization_barrier(
+        (got, sums_1, own_1, own_2, sides_1, sides_2, act_own_2, act_sides_2)
+    )
     got = got.reshape(n_rows, 2, 2, blocks, n_slots, CB, ch)
 
     above_1 = from_above(got[n_rows - 1, 0])

time: 162 us -> 156 us (0.963)
  Pallas kernels: 58.4 us -> 38 us
  local copies, waits for them, and re-layouts: 24.5 us -> 37.3 us
  starting transfers between devices: 33.5 us -> 38 us
  other arithmetic: 1.89 us -> 0.26 us
    all_to_all x1, waiting for transfers between devices: 31.1 us -> 12.7 us  [local(): lax.all_to_all(moved.reshape(n_groups * n_tiles, n_slots, CB, ch), BOTH,...]
    ppermute x4, waiting for transfers between devices: 10.5 us -> 28.4 us  [from_above(): return lax.ppermute(row, 'tile', down)]
    unnamed x66 -> x74, local copies, waits for them, and re-layouts: 24.2 us -> 37 us
    pallas_call x2 -> x4, Pallas kernels: 14.9 us -> 4.14 us  [spread(): pl.pallas_call(body, grid=(n_y,), in_specs=[pl.BlockSpec((times, 1, n_x,...]
    pallas_call x1, Pallas kernels: 10.9 us -> 3 us  [permute(): pl.pallas_call(body, grid_spec=pltpu.PrefetchScalarGridSpec(num_scalar_pr...]
    ppermute x4, starting transfers between devices: 15.5 us -> 20.2 us  [from_below(): return lax.ppermute(row, 'tile', up)]
    pallas_call x6, Pallas kernels: 28.3 us -> 26.6 us  [call(): pl.pallas_call(body, in_specs=in_specs, out_specs=out_specs, out_shape=li...]
  transfers between devices with their start and end apart: 10 -> 10, of which waited for: 2 -> 3; matrix products, arithmetic and copies ran while one was open for 1% -> 0% of each run, Pallas kernels for 25% -> 18%
where the time goes in v6:
time: 156 us
  waiting for transfers between devices  41.1 us (26%)
  Pallas kernels  38 us (24%)
  starting transfers between devices  38 us (24%)
  local copies, waits for them, and re-layouts  37.3 us (24%)
    unnamed x74, local copies, waits for them, and re-layouts  37 us
    ppermute x4, waiting for transfers between devices, from_above(): return lax.ppermute(row, 'tile', down)  28.4 us
    pallas_call x6, Pallas kernels, call(): pl.pallas_call(body, in_specs=in_specs, out_specs=out_specs, out_shape=li...  26.6 us
    ppermute x4, starting transfers between devices, from_below(): return lax.ppermute(row, 'tile', up)  20.2 us
    all_to_all x1, waiting for transfers between devices, local(): lax.all_to_all(moved.reshape(n_groups * n_tiles, n_slots, CB, ch), BOTH,...  12.7 us
    all_to_all x1, starting transfers between devices, local(): held = lax.all_to_all(sent, BOTH, 0, 0, tiled=True)  11.1 us
    all_to_all x1, starting transfers between devices, local(): lax.all_to_all(moved.reshape(n_groups * n_tiles, n_slots, CB, ch), BOTH,...  6.45 us
    pallas_call x1, Pallas kernels, pack(): pl.pallas_call(body, grid=(n_slots,), in_specs=[spec, spec], out_specs=pl...  4.34 us
  transfers between devices with their start and end apart: 10, of which 3 were waited for; matrix products, arithmetic and copies ran while one was open for 0% of the time, Pallas kernels for 18%

profile of v6, /device:TPU:0, one launch (start us, length us, event | category | flops | bytes accessed | tf_op | source)
XLA Modules:
  0.0 155.7 jit_solution(7302088717021394353)
XLA Ops:
  0.6 4.3 %shard_map.157 = bf16[2,2,2,16,4,8,384]{6,5,4,3,2,1,0:T(8,128)(2,1)} custom-call(bf16[4,2,2,128,384]{4,3,2,1,0:T(8,128)(2,1)} %a_ref.1, bf16[4,2,2,128,384]{4,3,2,1,0:T(8,128)(2,1)} %b_ref.1), custom_call_target="tpu_custom_call" | custom-call | tf_op jit(solution)/shard_map/pallas_call | solution.py:27
  5.0 11.1 %all-to-all-start = ((bf16[128,4,8,384]{3,2,1,0:T(8,128)(2,1)}), bf16[128,4,8,384]{3,2,1,0:T(8,128)(2,1)S(1)}, u32[]{:S(2)}, u32[]{:S(2)}) async-start(bf16[128,4,8,384]{3,2,1,0:T(8,128)(2,1)} %bitcast.28), calls=%async_computation | async-start | bytes 6291456 | tf_op jit(solution)/shard_map/all_to_all | solution.py:452
  16.1 0.0 copy-start.3
  16.2 1.1 copy-done.3
  17.3 1.5 shard_map.158
  18.8 0.9 copy-done.21
  19.7 5.1 %collective-permute-start.1 = (bf16[4,128,384]{2,1,0:T(8,128)(2,1)}, bf16[4,128,384]{2,1,0:T(8,128)(2,1)}, u32[]{:S(2)}, u32[]{:S(2)}) collective-permute-start(bf16[4,128,384]{2,1,0:T(8,128)(2,1)} %get-tuple-element.44), channel_id=1, source_target_pairs={{1,0},{2,1},{3,2},{4,3},{5,4},{6,5},{7,6},{8,7},{9,8},{10,9},{11,1... | collective-permute-start | bytes 1179656 | tf_op jit(solution)/shard_map/ppermute | solution.py:449
  24.7 3.3 %copy-done.1 = bf16[3,3,3,384,384]{4,3,2,1,0:T(8,128)(2,1)S(1)} copy-done((bf16[3,3,3,384,384]{4,3,2,1,0:T(8,128)(2,1)S(1)}, bf16[3,3,3,384,384]{4,3,2,1,0:T(8,128)(2,1)}, u32[]{:S(2)}) %copy-start.1) | copy-done | bytes 7962648
  28.0 0.0 copy-start.34
  28.0 0.5 shard_map.159
  28.6 1.8 %copy-done.15 = bf16[768,2304]{1,0:T(8,128)(2,1)} copy-done((bf16[768,2304]{1,0:T(8,128)(2,1)}, bf16[768,2304]{1,0:T(8,128)(2,1)S(1)}, u32[]{:S(2)}) %copy-start.15) | copy-done | bytes 3538968
  30.3 1.3 copy-done.19
  31.6 0.1 select_reduce_fusion
  31.8 28.2 %collective-permute-done.above_ref = bf16[4,128,384]{2,1,0:T(8,128)(2,1)S(1)} collective-permute-done((bf16[4,128,384]{2,1,0:T(8,128)(2,1)}, bf16[4,128,384]{2,1,0:T(8,128)(2,1)S(1)}, u32[]{:S(2)}, u32[]{:S(2)}) %collective-permute-start) | collective-permute-done | bytes 393248 | tf_op jit(solution)/shard_map/ppermute | solution.py:446
  60.0 3.0 %shard_map.160 = bf16[4,32,4,8,384]{4,3,2,1,0:T(8,128)(2,1)S(1)} custom-call(s32[16]{0:T(128)S(1)} %get-tuple-element.83.source_ref, s32[16]{0:T(128)S(1)} %get-tuple-element.89.rotation_ref, s32[16]{0:T(128)S(1)} %compare_convert_fusion.keep_ref, bf16[4,32,4,8,384]{4,3,2,1,0:T(8,128)(2,1)S(1)} %bitcast.24), custom_call_target="tpu_custom_call" | custom-call | tf_op jit(solution)/shard_map/pallas_call | solution.py:62
  63.0 1.7 %copy-done.2 = bf16[4,32,4,8,384]{4,3,2,1,0:T(8,128)(2,1)} copy-done((bf16[4,32,4,8,384]{4,3,2,1,0:T(8,128)(2,1)}, bf16[4,32,4,8,384]{4,3,2,1,0:T(8,128)(2,1)S(1)}, u32[]{:S(2)}) %copy-start.2) | copy-done | bytes 3145752
  64.7 6.4 %all-to-all-start.1 = ((bf16[128,4,8,384]{3,2,1,0:T(8,128)(2,1)}), bf16[128,4,8,384]{3,2,1,0:T(8,128)(2,1)S(1)}, u32[]{:S(2)}, u32[]{:S(2)}) async-start(bf16[128,4,8,384]{3,2,1,0:T(8,128)(2,1)} %bitcast.25), calls=%async_computation.1 | async-start | bytes 6291456 | tf_op jit(solution)/shard_map/all_to_all | solution.py:463
  71.2 0.1 compare_bitcast_fusion.1
  71.3 2.0 %copy-done.16 = bf16[768,2304]{1,0:T(8,128)(2,1)S(1)} copy-done((bf16[768,2304]{1,0:T(8,128)(2,1)S(1)}, bf16[768,2304]{1,0:T(8,128)(2,1)}, u32[]{:S(2)}) %copy-start.16) | copy-done | bytes 3538968
  73.3 1.5 copy-done.20
  74.8 1.1 copy-done.22
  75.9 4.5 %shard_map.161.z_ref = f32[2,16,4,8,384]{4,3,2,1,0:T(8,128)S(1)} custom-call(s32[2,4]{1,0:T(2,128)S(1)} %add_convert_fusion.edge_ref, bf16[4,2,128,384]{3,2,1,0:T(8,128)(2,1)S(1)} %copy-done.22, bf16[4,128,384]{2,1,0:T(8,128)(2,1)S(1)} %collective-permute-done.above_ref, bf16[4,128,384]{2,1,0:T(8,128)(2,1)} %collective-permute-done.1.below_ref, ...), custom_call_target="tpu_custom_call" | custom-call | flops 2717908992 | bytes 6684672 | tf_op jit(solution)/shard_map/pallas_call | solution.py:92
  80.4 1.1 copy-done.24
  81.5 3.3 %copy-done = bf16[3,3,3,384,384]{4,3,2,1,0:T(8,128)(2,1)S(1)} copy-done((bf16[3,3,3,384,384]{4,3,2,1,0:T(8,128)(2,1)S(1)}, bf16[3,3,3,384,384]{4,3,2,1,0:T(8,128)(2,1)}, u32[]{:S(2)}) %copy-start) | copy-done | bytes 7962648
  84.8 1.5 shard_map.163
  86.3 2.8 %copy-done.7 = bf16[1536,2304]{1,0:T(8,128)(2,1)} copy-done((bf16[1536,2304]{1,0:T(8,128)(2,1)}, bf16[1536,2304]{1,0:T(8,128)(2,1)S(1)}, u32[]{:S(2)}) %copy-start.7) | copy-done | bytes 7077912
  89.2 0.5 shard_map.164
  89.7 1.2 copy-done.11
  90.9 1.3 copy-done.5
  92.2 1.8 %copy-done.13 = bf16[768,2304]{1,0:T(8,128)(2,1)} copy-done((bf16[768,2304]{1,0:T(8,128)(2,1)}, bf16[768,2304]{1,0:T(8,128)(2,1)S(1)}, u32[]{:S(2)}) %copy-start.13) | copy-done | bytes 3538968
  94.0 1.5 shard_map.162
  95.6 2.9 %copy-done.9 = bf16[1536,2304]{1,0:T(8,128)(2,1)} copy-done((bf16[1536,2304]{1,0:T(8,128)(2,1)}, bf16[1536,2304]{1,0:T(8,128)(2,1)S(1)}, u32[]{:S(2)}) %copy-start.9) | copy-done | bytes 7077912
  98.5 1.8 %copy-done.17 = bf16[2,768,1152]{2,1,0:T(8,128)(2,1)} copy-done((bf16[2,768,1152]{2,1,0:T(8,128)(2,1)}, bf16[2,768,1152]{2,1,0:T(8,128)(2,1)S(1)}, u32[]{:S(2)}) %copy-start.17) | copy-done | bytes 3538968
  100.3 12.7 %all-to-all-done.1 = bf16[128,4,8,384]{3,2,1,0:T(8,128)(2,1)S(1)} async-done(((bf16[128,4,8,384]{3,2,1,0:T(8,128)(2,1)}), bf16[128,4,8,384]{3,2,1,0:T(8,128)(2,1)S(1)}, u32[]{:S(2)}, u32[]{:S(2)}) %all-to-all-start.1) | async-done | bytes 3145760 | tf_op jit(solution)/shard_map/all_to_all | solution.py:463
  113.0 0.3 slice_bitcast_fusion
  113.4 0.1 collective-permute-start.2
  113.4 5.1 %collective-permute-start.3 = (bf16[2,16,4,8,384]{4,3,2,1,0:T(8,128)(2,1)S(1)}, bf16[2,16,4,8,384]{4,3,2,1,0:T(8,128)(2,1)S(1)}, u32[]{:S(2)}, u32[]{:S(2)}) collective-permute-start(bf16[2,16,4,8,384]{4,3,2,1,0:T(8,128)(2,1)S(1)} %get-tuple-element.87), channel_id=1, source_target_pairs={{1,0},{2,1},{3,2},{4,3},{5,4},{6,5},{7,6},{8,7},{9,8},{10,9},{11,1... | collective-permute-start | bytes 2359304 | tf_op jit(solution)/shard_map/ppermute | solution.py:449
  118.5 0.1 collective-permute-start.6
  118.6 5.1 %collective-permute-start.7 = (bf16[2,16,4,8,384]{4,3,2,1,0:T(8,128)(2,1)S(1)}, bf16[2,16,4,8,384]{4,3,2,1,0:T(8,128)(2,1)S(1)}, u32[]{:S(2)}, u32[]{:S(2)}) collective-permute-start(bf16[2,16,4,8,384]{4,3,2,1,0:T(8,128)(2,1)S(1)} %get-tuple-element.85), channel_id=1, source_target_pairs={{1,0},{2,1},{3,2},{4,3},{5,4},{6,5},{7,6},{8,7},{9,8},{10,9},{11,1... | collective-permute-start | bytes 2359304 | tf_op jit(solution)/shard_map/ppermute | solution.py:449
  123.7 3.0 %copy-done.8 = bf16[1536,2304]{1,0:T(8,128)(2,1)S(1)} copy-done((bf16[1536,2304]{1,0:T(8,128)(2,1)S(1)}, bf16[1536,2304]{1,0:T(8,128)(2,1)}, u32[]{:S(2)}) %copy-start.8) | copy-done | bytes 7077912
  126.7 3.0 %copy-done.10 = bf16[1536,2304]{1,0:T(8,128)(2,1)S(1)} copy-done((bf16[1536,2304]{1,0:T(8,128)(2,1)S(1)}, bf16[1536,2304]{1,0:T(8,128)(2,1)}, u32[]{:S(2)}) %copy-start.10) | copy-done | bytes 7077912
  129.7 9.1 %shard_map.165 = (f32[2,16,4,8,384]{4,3,2,1,0:T(8,128)S(1)}, f32[2,16,4,8,384]{4,3,2,1,0:T(8,128)S(1)}, bf16[4,2,2,16,8,384]{5,4,3,2,1,0:T(8,128)(2,1)}, bf16[4,2,2,16,8,384]{5,4,3,2,1,0:T(8,128)(2,1)}) custom-call(bf16[2,2,2,16,4,8,384]{6,5,4,3,2,1,0:T(8,128)(2,1)S(1)} %bitcast.23, bf16[1536,2304]{1,0:T(8,128)(2,1)S(1)} %copy-done.10, ...), custom_call_target="tpu_custom_call" | custom-call | flops 7247757312 | bytes 14155776 | tf_op jit(solution)/shard_map/pallas_call | solution.py:92
  138.8 3.4 %shard_map.166 = (bf16[4,2,128,384]{3,2,1,0:T(8,128)(2,1)S(1)}, bf16[4,128,384]{2,1,0:T(8,128)(2,1)S(1)}, bf16[4,128,384]{2,1,0:T(8,128)(2,1)S(1)}) custom-call(s32[2,4]{1,0:T(2,128)S(1)} %add_convert_fusion.edge_ref, bf16[2,16,4,8,384]{4,3,2,1,0:T(8,128)(2,1)S(1)} %collective-permute-done.2.above_ref, ...), custom_call_target="tpu_custom_call" | custom-call | flops 1811939328 | bytes 3538944 | tf_op jit(solution)/shard_map/pallas_call | solution.py:92
  142.2 0.1 collective-permute-start.4
  142.3 5.1 %collective-permute-start.5 = (bf16[4,128,384]{2,1,0:T(8,128)(2,1)S(1)}, bf16[4,128,384]{2,1,0:T(8,128)(2,1)S(1)}, u32[]{:S(2)}, u32[]{:S(2)}) collective-permute-start(bf16[4,128,384]{2,1,0:T(8,128)(2,1)S(1)} %get-tuple-element.71), channel_id=1, source_target_pairs={{1,0},{2,1},{3,2},{4,3},{5,4},{6,5},{7,6},{8,7},{9,8},{10,9},{11,1... | collective-permute-start | bytes 1179656 | tf_op jit(solution)/shard_map/ppermute | solution.py:449
  147.4 5.2 %shard_map.167 = (f32[2,16,4,8,384]{4,3,2,1,0:T(8,128)S(1)}, bf16[4,2,2,16,8,384]{5,4,3,2,1,0:T(8,128)(2,1)}) custom-call(s32[2,4]{1,0:T(2,128)S(1)} %add_convert_fusion.edge_ref, bf16[2,16,4,8,384]{4,3,2,1,0:T(8,128)(2,1)S(1)} %collective-permute-done.6.above_ref, ...), custom_call_target="tpu_custom_call", output_to_operand_aliasing={{1}: (8, {})} | custom-call | flops 3623878656 | bytes 7077888 | tf_op jit(solution)/shard_map/pallas_call | solution.py:92
  152.6 0.2 collective-permute-done.4.above_ref
  152.8 2.9 %shard_map.168 = bf16[4,2,128,384]{3,2,1,0:T(8,128)(2,1)} custom-call(s32[2,4]{1,0:T(2,128)S(1)} %add_convert_fusion.edge_ref, bf16[4,128,384]{2,1,0:T(8,128)(2,1)S(1)} %collective-permute-done.4.above_ref, bf16[4,128,384]{2,1,0:T(8,128)(2,1)S(1)} %collective-permute-done.5.below_ref, bf16[2,384,1152]{2,1,0:T(8,128)(2,1)S(1)} %copy-done.6, ...), custom_call_target="tpu_custom_call" | custom-call | flops 905969664 | bytes 1769472 | tf_op jit(solution)/shard_map/pallas_call | solution.py:92
  (69 shorter events, 0.2 us)
Async XLA Ops:
  5.0 11.2 %copy-start.26 = (f32[384]{0:T(512)S(1)}, f32[384]{0:T(512)}, u32[]{:S(2)}) copy-start(f32[384]{0:T(512)} %param.17) | copy-start | bytes 4612
  5.0 55.1 %all-to-all-start = ((bf16[128,4,8,384]{3,2,1,0:T(8,128)(2,1)}), bf16[128,4,8,384]{3,2,1,0:T(8,128)(2,1)S(1)}, u32[]{:S(2)}, u32[]{:S(2)}) async-start(bf16[128,4,8,384]{3,2,1,0:T(8,128)(2,1)} %bitcast.28), calls=%async_computation | async-start | bytes 6291456 | tf_op jit(solution)/shard_map/all_to_all | solution.py:452
  16.1 1.1 copy-start.3
  18.8 0.9 copy-start.21
  19.7 40.4 %collective-permute-start = (bf16[4,128,384]{2,1,0:T(8,128)(2,1)}, bf16[4,128,384]{2,1,0:T(8,128)(2,1)S(1)}, u32[]{:S(2)}, u32[]{:S(2)}) collective-permute-start(bf16[4,128,384]{2,1,0:T(8,128)(2,1)} %get-tuple-element.43), channel_id=1, source_target_pairs={{0,1},{1,2},{2,3},{3,4},{4,5},{5,6},{6,7},{7,8},{8,9},{9,10},{10,1... | collective-permute-start | bytes 1179656 | tf_op jit(solution)/shard_map/ppermute | solution.py:446
  19.7 40.4 %collective-permute-start.1 = (bf16[4,128,384]{2,1,0:T(8,128)(2,1)}, bf16[4,128,384]{2,1,0:T(8,128)(2,1)}, u32[]{:S(2)}, u32[]{:S(2)}) collective-permute-start(bf16[4,128,384]{2,1,0:T(8,128)(2,1)} %get-tuple-element.44), channel_id=1, source_target_pairs={{1,0},{2,1},{3,2},{4,3},{5,4},{6,5},{7,6},{8,7},{9,8},{10,9},{11,1... | collective-permute-start | bytes 1179656 | tf_op jit(solution)/shard_map/ppermute | solution.py:449
  24.7 3.3 %copy-start.1 = (bf16[3,3,3,384,384]{4,3,2,1,0:T(8,128)(2,1)S(1)}, bf16[3,3,3,384,384]{4,3,2,1,0:T(8,128)(2,1)}, u32[]{:S(2)}) copy-start(bf16[3,3,3,384,384]{4,3,2,1,0:T(8,128)(2,1)} %w_ref.2) | copy-start | bytes 23887876
  28.0 3.6 %copy-start.30 = (s32[16]{0:T(128)S(1)}, s32[16]{0:T(128)}, u32[]{:S(2)}) copy-start(s32[16]{0:T(128)} %param.27) | copy-start | bytes 196
  28.0 3.6 %copy-start.31 = (s32[16]{0:T(128)S(1)}, s32[16]{0:T(128)}, u32[]{:S(2)}) copy-start(s32[16]{0:T(128)} %param.24) | copy-start | bytes 196
  28.0 3.6 %copy-start.32 = (s32[16]{0:T(128)S(1)}, s32[16]{0:T(128)}, u32[]{:S(2)}) copy-start(s32[16]{0:T(128)} %param.25) | copy-start | bytes 196
  28.0 3.6 %copy-start.33 = (s32[16]{0:T(128)S(1)}, s32[16]{0:T(128)}, u32[]{:S(2)}) copy-start(s32[16]{0:T(128)} %param.23) | copy-start | bytes 196
  28.0 3.6 %copy-start.34 = (s32[16]{0:T(128)S(1)}, s32[16]{0:T(128)}, u32[]{:S(2)}) copy-start(s32[16]{0:T(128)} %param.26) | copy-start | bytes 196
  28.6 1.8 %copy-start.15 = (bf16[768,2304]{1,0:T(8,128)(2,1)}, bf16[768,2304]{1,0:T(8,128)(2,1)S(1)}, u32[]{:S(2)}) copy-start(bf16[768,2304]{1,0:T(8,128)(2,1)S(1)} %get-tuple-element.53.wo_ref) | copy-start | bytes 10616836
  30.3 1.3 copy-start.19
  63.0 1.7 %copy-start.2 = (bf16[4,32,4,8,384]{4,3,2,1,0:T(8,128)(2,1)}, bf16[4,32,4,8,384]{4,3,2,1,0:T(8,128)(2,1)S(1)}, u32[]{:S(2)}) copy-start(bf16[4,32,4,8,384]{4,3,2,1,0:T(8,128)(2,1)S(1)} %shard_map.160) | copy-start | bytes 9437188
  64.7 48.3 %all-to-all-start.1 = ((bf16[128,4,8,384]{3,2,1,0:T(8,128)(2,1)}), bf16[128,4,8,384]{3,2,1,0:T(8,128)(2,1)S(1)}, u32[]{:S(2)}, u32[]{:S(2)}) async-start(bf16[128,4,8,384]{3,2,1,0:T(8,128)(2,1)} %bitcast.25), calls=%async_computation.1 | async-start | bytes 6291456 | tf_op jit(solution)/shard_map/all_to_all | solution.py:463
  71.3 2.0 %copy-start.16 = (bf16[768,2304]{1,0:T(8,128)(2,1)S(1)}, bf16[768,2304]{1,0:T(8,128)(2,1)}, u32[]{:S(2)}) copy-start(bf16[768,2304]{1,0:T(8,128)(2,1)} %copy-done.15) | copy-start | bytes 10616836
  73.3 1.5 copy-start.20
  74.8 1.1 copy-start.22
  75.9 18.1 %slice-start = ((s8[7962624]{0:T(1024)(128)(4,1)}), s8[4194304]{0:T(1024)(128)(4,1)S(1)}, s32[]{:S(2)}) async-start(s8[7962624]{0:T(1024)(128)(4,1)} %bitcast.20), calls=%async_computation.2 | async-start | bytes 8388608
  80.4 1.1 copy-start.24
  81.5 3.3 %copy-start = (bf16[3,3,3,384,384]{4,3,2,1,0:T(8,128)(2,1)S(1)}, bf16[3,3,3,384,384]{4,3,2,1,0:T(8,128)(2,1)}, u32[]{:S(2)}) copy-start(bf16[3,3,3,384,384]{4,3,2,1,0:T(8,128)(2,1)} %w_ref.4) | copy-start | bytes 23887876
  84.8 9.2 %slice-start.1 = ((s8[7962624]{0:T(1024)(128)(4,1)}), s8[3768320]{0:T(1024)(128)(4,1)S(1)}, s32[]{:S(2)}) async-start(s8[7962624]{0:T(1024)(128)(4,1)} %bitcast.20), calls=%async_computation.3 | async-start | bytes 7536640
  86.3 2.8 %copy-start.7 = (bf16[1536,2304]{1,0:T(8,128)(2,1)}, bf16[1536,2304]{1,0:T(8,128)(2,1)S(1)}, u32[]{:S(2)}) copy-start(bf16[1536,2304]{1,0:T(8,128)(2,1)S(1)} %get-tuple-element.67.w1_ref) | copy-start | bytes 21233668
  89.2 1.8 %copy-start.11 = (bf16[2,768,1152]{2,1,0:T(8,128)(2,1)}, bf16[2,768,1152]{2,1,0:T(8,128)(2,1)S(1)}, u32[]{:S(2)}) copy-start(bf16[2,768,1152]{2,1,0:T(8,128)(2,1)S(1)} %get-tuple-element.74.w_ref) | copy-start | bytes 10616836
  90.9 1.3 copy-start.5
  92.2 1.8 %copy-start.13 = (bf16[768,2304]{1,0:T(8,128)(2,1)}, bf16[768,2304]{1,0:T(8,128)(2,1)S(1)}, u32[]{:S(2)}) copy-start(bf16[768,2304]{1,0:T(8,128)(2,1)S(1)} %get-tuple-element.75.wa_ref) | copy-start | bytes 10616836
  95.6 2.9 %copy-start.9 = (bf16[1536,2304]{1,0:T(8,128)(2,1)}, bf16[1536,2304]{1,0:T(8,128)(2,1)S(1)}, u32[]{:S(2)}) copy-start(bf16[1536,2304]{1,0:T(8,128)(2,1)S(1)} %get-tuple-element.66.w0_ref) | copy-start | bytes 21233668
  98.5 1.8 %copy-start.17 = (bf16[2,768,1152]{2,1,0:T(8,128)(2,1)}, bf16[2,768,1152]{2,1,0:T(8,128)(2,1)S(1)}, u32[]{:S(2)}) copy-start(bf16[2,768,1152]{2,1,0:T(8,128)(2,1)S(1)} %get-tuple-element.65.w_ref) | copy-start | bytes 10616836
  113.0 5.5 %copy-start.27 = (f32[384]{0:T(512)S(1)}, f32[384]{0:T(512)}, u32[]{:S(2)}) copy-start(f32[384]{0:T(512)} %param.21) | copy-start | bytes 4612
  113.0 5.5 %copy-start.28 = (f32[384]{0:T(512)S(1)}, f32[384]{0:T(512)}, u32[]{:S(2)}) copy-start(f32[384]{0:T(512)} %param.18) | copy-start | bytes 4612
  113.0 10.6 %copy-start.23 = (bf16[4,2,128,384]{3,2,1,0:T(8,128)(2,1)S(1)}, bf16[4,2,128,384]{3,2,1,0:T(8,128)(2,1)}, u32[]{:S(2)}) copy-start(bf16[4,2,128,384]{3,2,1,0:T(8,128)(2,1)} %copy-done.21) | copy-start | bytes 2359300
  113.0 10.6 %copy-start.25 = (f32[2,16,4,8,384]{4,3,2,1,0:T(8,128)S(1)}, f32[2,16,4,8,384]{4,3,2,1,0:T(8,128)}, u32[]{:S(2)}) copy-start(f32[2,16,4,8,384]{4,3,2,1,0:T(8,128)} %copy-done.24) | copy-start | bytes 4718596
  113.4 25.4 %collective-permute-start.2 = (bf16[2,16,4,8,384]{4,3,2,1,0:T(8,128)(2,1)S(1)}, bf16[2,16,4,8,384]{4,3,2,1,0:T(8,128)(2,1)S(1)}, u32[]{:S(2)}, u32[]{:S(2)}) collective-permute-start(bf16[2,16,4,8,384]{4,3,2,1,0:T(8,128)(2,1)S(1)} %get-tuple-element.88), channel_id=1, source_target_pairs={{0,1},{1,2},{2,3},{3,4},{4,5},{5,6},{6,7},{7,8},{8,9},{9,10},{10,1... | collective-permute-start | bytes 2359304 | tf_op jit(solution)/shard_map/ppermute | solution.py:446
  113.4 25.3 %collective-permute-start.3 = (bf16[2,16,4,8,384]{4,3,2,1,0:T(8,128)(2,1)S(1)}, bf16[2,16,4,8,384]{4,3,2,1,0:T(8,128)(2,1)S(1)}, u32[]{:S(2)}, u32[]{:S(2)}) collective-permute-start(bf16[2,16,4,8,384]{4,3,2,1,0:T(8,128)(2,1)S(1)} %get-tuple-element.87), channel_id=1, source_target_pairs={{1,0},{2,1},{3,2},{4,3},{5,4},{6,5},{7,6},{8,7},{9,8},{10,9},{11,1... | collective-permute-start | bytes 2359304 | tf_op jit(solution)/shard_map/ppermute | solution.py:449
  118.5 28.8 %collective-permute-start.6 = (bf16[2,16,4,8,384]{4,3,2,1,0:T(8,128)(2,1)S(1)}, bf16[2,16,4,8,384]{4,3,2,1,0:T(8,128)(2,1)S(1)}, u32[]{:S(2)}, u32[]{:S(2)}) collective-permute-start(bf16[2,16,4,8,384]{4,3,2,1,0:T(8,128)(2,1)S(1)} %get-tuple-element.86), channel_id=1, source_target_pairs={{0,1},{1,2},{2,3},{3,4},{4,5},{5,6},{6,7},{7,8},{8,9},{9,10},{10,1... | collective-permute-start | bytes 2359304 | tf_op jit(solution)/shard_map/ppermute | solution.py:446
  118.6 28.7 %collective-permute-start.7 = (bf16[2,16,4,8,384]{4,3,2,1,0:T(8,128)(2,1)S(1)}, bf16[2,16,4,8,384]{4,3,2,1,0:T(8,128)(2,1)S(1)}, u32[]{:S(2)}, u32[]{:S(2)}) collective-permute-start(bf16[2,16,4,8,384]{4,3,2,1,0:T(8,128)(2,1)S(1)} %get-tuple-element.85), channel_id=1, source_target_pairs={{1,0},{2,1},{3,2},{4,3},{5,4},{6,5},{7,6},{8,7},{9,8},{10,9},{11,1... | collective-permute-start | bytes 2359304 | tf_op jit(solution)/shard_map/ppermute | solution.py:449
  123.7 3.0 %copy-start.8 = (bf16[1536,2304]{1,0:T(8,128)(2,1)S(1)}, bf16[1536,2304]{1,0:T(8,128)(2,1)}, u32[]{:S(2)}) copy-start(bf16[1536,2304]{1,0:T(8,128)(2,1)} %copy-done.7) | copy-start | bytes 21233668
  126.7 3.0 %copy-start.10 = (bf16[1536,2304]{1,0:T(8,128)(2,1)S(1)}, bf16[1536,2304]{1,0:T(8,128)(2,1)}, u32[]{:S(2)}) copy-start(bf16[1536,2304]{1,0:T(8,128)(2,1)} %copy-done.9) | copy-start | bytes 21233668
  129.7 9.1 %copy-start.18 = (bf16[2,768,1152]{2,1,0:T(8,128)(2,1)S(1)}, bf16[2,768,1152]{2,1,0:T(8,128)(2,1)}, u32[]{:S(2)}) copy-start(bf16[2,768,1152]{2,1,0:T(8,128)(2,1)} %copy-done.17) | copy-start | bytes 10616836
  129.7 17.7 %copy-start.14 = (bf16[768,2304]{1,0:T(8,128)(2,1)S(1)}, bf16[768,2304]{1,0:T(8,128)(2,1)}, u32[]{:S(2)}) copy-start(bf16[768,2304]{1,0:T(8,128)(2,1)} %copy-done.13) | copy-start | bytes 10616836
  138.8 8.5 %copy-start.29 = (f32[384]{0:T(512)S(1)}, f32[384]{0:T(512)}, u32[]{:S(2)}) copy-start(f32[384]{0:T(512)} %param.22) | copy-start | bytes 4612
  138.8 8.6 %copy-start.12 = (bf16[2,768,1152]{2,1,0:T(8,128)(2,1)S(1)}, bf16[2,768,1152]{2,1,0:T(8,128)(2,1)}, u32[]{:S(2)}) copy-start(bf16[2,768,1152]{2,1,0:T(8,128)(2,1)} %copy-done.11) | copy-start | bytes 10616836
  142.2 10.6 %collective-permute-start.4 = (bf16[4,128,384]{2,1,0:T(8,128)(2,1)S(1)}, bf16[4,128,384]{2,1,0:T(8,128)(2,1)S(1)}, u32[]{:S(2)}, u32[]{:S(2)}) collective-permute-start(bf16[4,128,384]{2,1,0:T(8,128)(2,1)S(1)} %get-tuple-element.70), channel_id=1, source_target_pairs={{0,1},{1,2},{2,3},{3,4},{4,5},{5,6},{6,7},{7,8},{8,9},{9,10},{10,1... | collective-permute-start | bytes 1179656 | tf_op jit(solution)/shard_map/ppermute | solution.py:446
  142.3 10.5 %collective-permute-start.5 = (bf16[4,128,384]{2,1,0:T(8,128)(2,1)S(1)}, bf16[4,128,384]{2,1,0:T(8,128)(2,1)S(1)}, u32[]{:S(2)}, u32[]{:S(2)}) collective-permute-start(bf16[4,128,384]{2,1,0:T(8,128)(2,1)S(1)} %get-tuple-element.71), channel_id=1, source_target_pairs={{1,0},{2,1},{3,2},{4,3},{5,4},{6,5},{7,6},{8,7},{9,8},{10,9},{11,1... | collective-permute-start | bytes 1179656 | tf_op jit(solution)/shard_map/ppermute | solution.py:449
  147.3 5.4 %copy-start.4 = (bf16[4,2,128,384]{3,2,1,0:T(8,128)(2,1)S(1)}, bf16[4,2,128,384]{3,2,1,0:T(8,128)(2,1)}, u32[]{:S(2)}) copy-start(bf16[4,2,128,384]{3,2,1,0:T(8,128)(2,1)} %f_ref.3) | copy-start | bytes 2359300
  147.4 5.4 %copy-start.6 = (bf16[2,384,1152]{2,1,0:T(8,128)(2,1)S(1)}, bf16[2,384,1152]{2,1,0:T(8,128)(2,1)}, u32[]{:S(2)}) copy-start(bf16[2,384,1152]{2,1,0:T(8,128)(2,1)} %copy-done.5) | copy-start | bytes 5308420

commit v7 on v6

--- a/solution.py
+++ b/solution.py
@@ -42,40 +42,33 @@
     n_groups, n_tiles, n_slots, cols, ch = held.shape
 
     def body(source_ref, rotation_ref, keep_ref, i_ref, o_ref):
-        n = pl.program_id(0)
-        by = rotation_ref[n]
-
-        @pl.when(keep_ref[n] != 0)
-        def _():
-            def step(t, _):
-                at = lax.rem(t + n_tiles - by, n_tiles)
-                o_ref[0, t, 0] = i_ref[0, at, 0]
-                return 0
-
-            lax.fori_loop(0, n_tiles, step, 0, unroll=8)
-
-        @pl.when(keep_ref[n] == 0)
-        def _():
-            o_ref[...] = jnp.zeros_like(o_ref)
-
-    block = (1, n_tiles, 1, cols, ch)
+        def stream(n, _):
+            by = rotation_ref[n]
+            old = source_ref[n]
+            to, slot = lax.div(n, n_slots), lax.rem(n, n_slots)
+            of, place = lax.div(old, n_slots), lax.rem(old, n_slots)
+
+            @pl.when(keep_ref[n] != 0)
+            def _():
+                for t in range(n_tiles):
+                    at = lax.rem(t + n_tiles - by, n_tiles)
+                    o_ref[to, t, slot] = i_ref[of, at, place]
+
+            @pl.when(keep_ref[n] == 0)
+            def _():
+                o_ref[to, :, slot] = jnp.zeros((n_tiles, cols, ch), o_ref.dtype)
+
+            return 0
+
+        lax.fori_loop(0, n_groups * n_slots, stream, 0)
+
+    smem, vmem = pl.BlockSpec(memory_space=pltpu.SMEM), pl.BlockSpec(memory_space=pltpu.VMEM)
     return pl.pallas_call(
         body,
-        grid_spec=pltpu.PrefetchScalarGridSpec(
-            num_scalar_prefetch=3,
-            grid=(n_groups * n_slots,),
-            in_specs=[
-                pl.BlockSpec(
-                    block,
-                    lambda n, s, r, k: (lax.div(s[n], n_slots), 0, lax.rem(s[n], n_slots), 0, 0),
-                )
-            ],
-            out_specs=pl.BlockSpec(
-                block, lambda n, s, r, k: (lax.div(n, n_slots), 0, lax.rem(n, n_slots), 0, 0)
-            ),
-        ),
+        in_specs=[smem, smem, smem, vmem],
+        out_specs=vmem,
         out_shape=jax.ShapeDtypeStruct(held.shape, held.dtype),
-        compiler_params=pltpu.CompilerParams(vmem_limit_bytes=32 << 20),
+        compiler_params=pltpu.CompilerParams(vmem_limit_bytes=16 << 20),
     )(source, rotation, keep, held)
 
 
@@ -101,49 +94,62 @@
     )(*scalars, *operands)
 
 
-def spread(weight, past):
-    n_t, n_y, n_x, ci, co = weight.shape
+def spread_own(weight, first, times):
+    _, n_y, n_x, ci, co = weight.shape
     wide = n_x * co
-    times = n_t - 1 if past else 1
-
-    def body(w_ref, own_ref, side_ref):
+
+    def body(w_ref, o_ref):
         dy = pl.program_id(0)
 
-        def side(y):
-            for x in range(n_x):
-                for t in range(times):
-                    side_ref[y, t * ci : (t + 1) * ci, x * co : (x + 1) * co] = w_ref[t, 0, x]
-
-        def own(row, y):
+        def fill(row, y):
             for x in range(n_x):
                 for t in range(times):
                     lo = (row * times + t) * ci
                     at = y * wide + x * co
-                    own_ref[lo : lo + ci, at : at + co] = w_ref[t, 0, x]
+                    o_ref[lo : lo + ci, at : at + co] = w_ref[t, 0, x]
 
         @pl.when(dy == 0)
         def _():
-            side(0)
-            own(0, 1)
+            fill(0, 1)
 
         @pl.when(dy == 1)
         def _():
-            own(0, 0)
-            own(1, 1)
+            fill(0, 0)
+            fill(1, 1)
 
         @pl.when(dy == 2)
         def _():
-            side(1)
-            own(1, 0)
-
-    shapes = [(2 * times * ci, 2 * wide), (2, times * ci, wide)]
-    first = 0 if past else n_t - 1
+            fill(1, 0)
+
     return pl.pallas_call(
         body,
         grid=(n_y,),
-        in_specs=[pl.BlockSpec((times, 1, n_x, ci, co), lambda y: (first, y, 0, 0, 0))],
-        out_specs=[pl.BlockSpec(memory_space=pltpu.VMEM) for _ in shapes],
-        out_shape=[jax.ShapeDtypeStruct(shape, weight.dtype) for shape in shapes],
+        in_specs=[
+            pl.BlockSpec((times, 1, n_x, ci, co), lambda y: (first // times, y, 0, 0, 0))
+        ],
+        out_specs=pl.BlockSpec(memory_space=pltpu.VMEM),
+        out_shape=jax.ShapeDtypeStruct((2 * times * ci, 2 * wide), weight.dtype),
+        cost_estimate=pl.CostEstimate(flops=0, bytes_accessed=4 * weight.size, transcendentals=0),
+        compiler_params=pltpu.CompilerParams(vmem_limit_bytes=16 << 20),
+    )(weight)
+
+
+def spread_sides(weight, first, times):
+    _, _, n_x, ci, co = weight.shape
+
+    def body(w_ref, o_ref):
+        for x in range(n_x):
+            for t in range(times):
+                o_ref[0, t * ci : (t + 1) * ci, x * co : (x + 1) * co] = w_ref[t, 0, x]
+
+    return pl.pallas_call(
+        body,
+        grid=(2,),
+        in_specs=[
+            pl.BlockSpec((times, 1, n_x, ci, co), lambda y: (first // times, 2 * y, 0, 0, 0))
+        ],
+        out_specs=pl.BlockSpec((1, times * ci, n_x * co), lambda y: (y, 0, 0)),
+        out_shape=jax.ShapeDtypeStruct((2, times * ci, n_x * co), weight.dtype),
         cost_estimate=pl.CostEstimate(flops=0, bytes_accessed=4 * weight.size, transcendentals=0),
         compiler_params=pltpu.CompilerParams(vmem_limit_bytes=16 << 20),
     )(weight)
@@ -222,14 +228,6 @@
     return jax.ShapeDtypeStruct((n_rows, blocks, n_slots, CB, ch), jnp.float32)
 
 
-def add_sides(edge_ref, sides, w_ref, lhs, o_ref):
-    n_slots, n_cols, ch = sides[0].shape
-    for y, side in enumerate(sides):
-        for s in range(n_slots):
-            lhs[s * n_cols : (s + 1) * n_cols] = masked(edge_ref, y, s, side[s])
-        add_into(o_ref, y, folded(dot(lhs[...], w_ref[y]), ch, False), False, o_ref)
-
-
 def add_own(act_ref, w_ref, lhs, o_ref, base):
     n_slots, n_rows, n_cols, ch = act_ref.shape
     for s in range(n_slots):
@@ -241,24 +239,19 @@
         add_into(o_ref, y, folded(both[:, y * wide : (y + 1) * wide], ch, False), False, base)
 
 
-def current_part(act, above, below, w_own, w_sides, edges):
+def current_part(act, w_own):
     n_slots, n_rows, n_cols, ch = act.shape
     half = n_slots * n_cols
 
-    def body(edge_ref, act_ref, above_ref, below_ref, wo_ref, ws_ref, o_ref, lhs, side):
-        add_own(act_ref, wo_ref, lhs, o_ref, None)
-        add_sides(edge_ref, (above_ref, below_ref), ws_ref, side, o_ref)
+    def body(act_ref, w_ref, o_ref, lhs):
+        add_own(act_ref, w_ref, lhs, o_ref, None)
 
     return call(
         body,
         [sums_shape(n_cols // CB, n_slots, n_rows, ch)],
-        (act, above, below, w_own, w_sides),
-        scalars=(edges,),
-        scratch=[
-            pltpu.VMEM((half, n_rows * ch), jnp.bfloat16),
-            pltpu.VMEM((half, ch), jnp.bfloat16),
-        ],
-        flops=2 * half * (w_own.size + w_sides.size),
+        (act, w_own),
+        scratch=[pltpu.VMEM((half, n_rows * ch), jnp.bfloat16)],
+        flops=2 * half * w_own.size,
         moved=2 * w_own.size + 8 * act.size,
     )[0]
 
@@ -313,23 +306,26 @@
     )
 
 
-def side_sums(edge_ref, k, side_ref, w, lhs):
+def side_sums(edge_ref, k, side_ref, w, lhs, current=None):
     n_frames, blocks, n_slots, _, ch = side_ref.shape
     for s in range(n_slots):
         for f in range(n_frames):
             value = masked(edge_ref, k, s, side_ref[f, :, s])
             lhs[:, s, :, f * ch : (f + 1) * ch] = value
+        if current is not None:
+            value = masked(edge_ref, k, s, current[s]).reshape(blocks, CB, ch)
+            lhs[:, s, :, n_frames * ch : (n_frames + 1) * ch] = value
     half = blocks * n_slots * CB
-    return folded(dot(lhs[...].reshape(half, n_frames * ch), w), ch, True)
-
-
-def second_activation(above, below, w_sides, sums, bias, gain, edges):
+    return folded(dot(lhs[...].reshape(half, lhs.shape[3]), w), ch, True)
+
+
+def second_activation(above, below, act_above, act_below, w_sides, sums, bias, gain, edges):
     n_frames, blocks, n_slots, _, ch = above.shape
     n_rows, n_cols, deep = sums.shape[0], blocks * CB, n_frames * ch
 
-    def body(edge_ref, above_ref, below_ref, w_ref, z_ref, b_ref, g_ref, o_ref, top_ref, bottom_ref, lhs):
-        for y, side in enumerate((above_ref, below_ref)):
-            total = side_sums(edge_ref, y, side, w_ref[y], lhs) + z_ref[y] + b_ref[...]
+    def body(edge_ref, above_ref, below_ref, aa_ref, ab_ref, w_ref, z_ref, b_ref, g_ref, o_ref, top_ref, bottom_ref, lhs):
+        for y, (side, row) in enumerate(((above_ref, aa_ref), (below_ref, ab_ref))):
+            total = side_sums(edge_ref, y, side, w_ref[y], lhs, row) + z_ref[y] + b_ref[...]
             for s in range(n_slots):
                 value = activated(total[:, s].reshape(n_cols, ch), g_ref[...]).astype(jnp.bfloat16)
                 o_ref[s, y] = value
@@ -342,9 +338,9 @@
     return call(
         body,
         [jax.ShapeDtypeStruct((n_slots, n_rows, n_cols, ch), jnp.bfloat16), row, row],
-        (above, below, w_sides, sums, bias, gain),
+        (above, below, act_above, act_below, w_sides, sums, bias, gain),
         scalars=(edges,),
-        scratch=[pltpu.VMEM((blocks, n_slots, CB, deep), jnp.bfloat16)],
+        scratch=[pltpu.VMEM((blocks, n_slots, CB, deep + ch), jnp.bfloat16)],
         flops=2 * n_slots * n_cols * w_sides.size,
         moved=2 * w_sides.size,
     )
@@ -451,25 +447,20 @@
     sent = pack(cache_first, cache_second).reshape(n_groups * n_tiles, n_slots, CB, ch)
     held = lax.all_to_all(sent, BOTH, 0, 0, tiled=True)
 
-    act_own_1, act_sides_1 = spread(conv_first, False)
+    act_own_1 = spread_own(conv_first, 2, 1)
     act_first, top, bottom = first_activation(frame_in, gain_first[None])
     act_above, act_below = from_above(bottom), from_below(top)
-    held, act_first, act_above, act_below, act_own_1, act_sides_1 = lax.optimization_barrier(
-        (held, act_first, act_above, act_below, act_own_1, act_sides_1)
+    sums_1 = current_part(act_first, act_own_1)
+    own_1, sides_1 = spread_own(conv_first, 0, 2), spread_sides(conv_first, 0, 3)
+    own_2, sides_2 = spread_own(conv_second, 0, 2), spread_sides(conv_second, 0, 2)
+    act_own_2, act_sides_2 = spread_own(conv_second, 2, 1), spread_sides(conv_second, 2, 1)
+    held, sums_1, own_1, sides_1, own_2, sides_2, act_own_2, act_sides_2 = lax.optimization_barrier(
+        (held, sums_1, own_1, sides_1, own_2, sides_2, act_own_2, act_sides_2)
     )
 
     moved = permute(held.reshape(n_groups, n_tiles, n_slots, CB, ch), source, rotation, keep)
-    moved, act_later = lax.optimization_barrier((moved, act_first))
     got = lax.all_to_all(
         moved.reshape(n_groups * n_tiles, n_slots, CB, ch), BOTH, 0, 0, tiled=True
-    )
-    sums_1 = current_part(act_later, act_above, act_below, act_own_1, act_sides_1, edges)
-    sums_1, conv_first, conv_second = lax.optimization_barrier((sums_1, conv_first, conv_second))
-    act_own_2, act_sides_2 = spread(conv_second, False)
-    own_1, sides_1 = spread(conv_first, True)
-    own_2, sides_2 = spread(conv_second, True)
-    got, sums_1, own_1, own_2, sides_1, sides_2, act_own_2, act_sides_2 = lax.optimization_barrier(
-        (got, sums_1, own_1, own_2, sides_1, sides_2, act_own_2, act_sides_2)
     )
     got = got.reshape(n_rows, 2, 2, blocks, n_slots, CB, ch)
 
@@ -480,7 +471,8 @@
     act_tiles = act_first.reshape(n_slots, n_rows, blocks, CB, ch)
     sums_1, sums_2, next_first, kept = own_part(got, (own_1, own_2), sums_1, act_tiles)
     act_second, top, bottom = second_activation(
-        above_1, below_1, sides_1, sums_1, bias_first[None], gain_second[None], edges
+        above_1, below_1, act_above, act_below, sides_1, sums_1, bias_first[None],
+        gain_second[None], edges,
     )
     side_above, side_below = from_above(bottom), from_below(top)
     sums_2, next_second = before_sides(

time: 156 us -> 156 us (level)
  waiting for transfers between devices: 41.1 us -> 47.4 us
  local copies, waits for them, and re-layouts: 37.3 us -> 32.5 us
  starting transfers between devices: 38 us -> 36.4 us
    ppermute x4, waiting for transfers between devices: 28.4 us -> 0.08 us  [from_above(): return lax.ppermute(row, 'tile', down)]
    all_to_all x1, waiting for transfers between devices: 12.7 us -> 36.3 us  [local(): lax.all_to_all(moved.reshape(n_groups * n_tiles, n_slots, CB, ch), BOTH,...]
    all_to_all x1, waiting for transfers between devices: 0.01 us -> 10.9 us  [local(): held = lax.all_to_all(sent, BOTH, 0, 0, tiled=True)]
    unnamed x74 -> x66, local copies, waits for them, and re-layouts: 37 us -> 32.1 us
    all_to_all x1, starting transfers between devices: 6.45 us -> 4.8 us  [local(): lax.all_to_all(moved.reshape(n_groups * n_tiles, n_slots, CB, ch), BOTH,...]
    pallas_call x5 -> x8, Pallas kernels: 7.14 us -> 6.91 us  [the longest x4 3.22 us: spread_own(): pl.pallas_call(body, grid=(n_y,), in_specs=[pl.BlockSpec((times, 1, n_x,...]
  transfers between devices with their start and end apart: 10 -> 10, of which waited for: 3 -> 3; matrix products, arithmetic and copies ran while one was open for 0% -> 1% of each run, Pallas kernels for 18% -> 18%
where the time goes in v7:
time: 156 us
  waiting for transfers between devices  47.4 us (30%)
  Pallas kernels  36.7 us (24%)
  starting transfers between devices  36.4 us (23%)
  local copies, waits for them, and re-layouts  32.5 us (21%)
  other arithmetic  1.58 us (1%)
    all_to_all x1, waiting for transfers between devices, local(): lax.all_to_all(moved.reshape(n_groups * n_tiles, n_slots, CB, ch), BOTH,...  36.3 us
    unnamed x66, local copies, waits for them, and re-layouts  32.1 us
    pallas_call x6, Pallas kernels, call(): pl.pallas_call(body, in_specs=in_specs, out_specs=out_specs, out_shape=li...  25.5 us
    ppermute x4, starting transfers between devices, from_below(): return lax.ppermute(row, 'tile', up)  20.2 us
    all_to_all x1, starting transfers between devices, local(): held = lax.all_to_all(sent, BOTH, 0, 0, tiled=True)  11.1 us
    all_to_all x1, waiting for transfers between devices, local(): held = lax.all_to_all(sent, BOTH, 0, 0, tiled=True)  10.9 us
    all_to_all x1, starting transfers between devices, local(): lax.all_to_all(moved.reshape(n_groups * n_tiles, n_slots, CB, ch), BOTH,...  4.8 us
    pallas_call x1, Pallas kernels, pack(): pl.pallas_call(body, grid=(n_slots,), in_specs=[spec, spec], out_specs=pl...  4.33 us
  transfers between devices with their start and end apart: 10, of which 3 were waited for; matrix products, arithmetic and copies ran while one was open for 1% of the time, Pallas kernels for 18%

profile of v7, /device:TPU:0, one launch (start us, length us, event | category | flops | bytes accessed | tf_op | source)
XLA Modules:
  0.0 155.7 jit_solution(9078620113706753864)
XLA Ops:
  0.6 4.3 %shard_map.157 = bf16[2,2,2,16,4,8,384]{6,5,4,3,2,1,0:T(8,128)(2,1)} custom-call(bf16[4,2,2,128,384]{4,3,2,1,0:T(8,128)(2,1)} %a_ref.1, bf16[4,2,2,128,384]{4,3,2,1,0:T(8,128)(2,1)} %b_ref.1), custom_call_target="tpu_custom_call" | custom-call | tf_op jit(solution)/shard_map/pallas_call | solution.py:27
  5.0 11.1 %all-to-all-start = ((bf16[128,4,8,384]{3,2,1,0:T(8,128)(2,1)}), bf16[128,4,8,384]{3,2,1,0:T(8,128)(2,1)S(1)}, u32[]{:S(2)}, u32[]{:S(2)}) async-start(bf16[128,4,8,384]{3,2,1,0:T(8,128)(2,1)} %bitcast.28), calls=%async_computation | async-start | bytes 6291456 | tf_op jit(solution)/shard_map/all_to_all | solution.py:448
  16.2 3.3 %copy-done = bf16[3,3,3,384,384]{4,3,2,1,0:T(8,128)(2,1)S(1)} copy-done((bf16[3,3,3,384,384]{4,3,2,1,0:T(8,128)(2,1)S(1)}, bf16[3,3,3,384,384]{4,3,2,1,0:T(8,128)(2,1)}, u32[]{:S(2)}) %copy-start) | copy-done | bytes 7962648
  19.4 0.4 shard_map.159.w_ref
  19.8 1.9 %copy-done.14 = bf16[768,2304]{1,0:T(8,128)(2,1)} copy-done((bf16[768,2304]{1,0:T(8,128)(2,1)}, bf16[768,2304]{1,0:T(8,128)(2,1)S(1)}, u32[]{:S(2)}) %copy-start.14) | copy-done | bytes 3538968
  21.7 1.2 shard_map.161.w0_ref
  22.9 2.9 %copy-done.2 = bf16[1536,2304]{1,0:T(8,128)(2,1)} copy-done((bf16[1536,2304]{1,0:T(8,128)(2,1)}, bf16[1536,2304]{1,0:T(8,128)(2,1)S(1)}, u32[]{:S(2)}) %copy-start.2) | copy-done | bytes 7077912
  25.8 1.1 shard_map.162.w_ref
  26.9 1.2 shard_map.163.w1_ref
  28.1 1.0 copy-done.8
  29.2 2.9 %copy-done.4 = bf16[1536,2304]{1,0:T(8,128)(2,1)} copy-done((bf16[1536,2304]{1,0:T(8,128)(2,1)}, bf16[1536,2304]{1,0:T(8,128)(2,1)S(1)}, u32[]{:S(2)}) %copy-start.4) | copy-done | bytes 7077912
  32.1 0.7 shard_map.164.w_ref
  32.8 1.8 %copy-done.10 = bf16[2,768,1152]{2,1,0:T(8,128)(2,1)} copy-done((bf16[2,768,1152]{2,1,0:T(8,128)(2,1)}, bf16[2,768,1152]{2,1,0:T(8,128)(2,1)S(1)}, u32[]{:S(2)}) %copy-start.10) | copy-done | bytes 3538968
  34.6 0.4 shard_map.165.wa_ref
  35.0 1.8 %copy-done.12 = bf16[768,2304]{1,0:T(8,128)(2,1)} copy-done((bf16[768,2304]{1,0:T(8,128)(2,1)}, bf16[768,2304]{1,0:T(8,128)(2,1)S(1)}, u32[]{:S(2)}) %copy-start.12) | copy-done | bytes 3538968
  36.9 0.2 shard_map.166.w_ref
  37.1 1.2 copy-done.6
  38.3 1.1 copy-done.16
  39.4 0.7 shard_map.158
  40.1 0.0 copy-start.20
  40.1 0.7 copy-done.20
  40.9 0.9 select_reduce_fusion
  41.8 2.0 %copy-done.15 = bf16[768,2304]{1,0:T(8,128)(2,1)S(1)} copy-done((bf16[768,2304]{1,0:T(8,128)(2,1)S(1)}, bf16[768,2304]{1,0:T(8,128)(2,1)}, u32[]{:S(2)}) %copy-start.15) | copy-done | bytes 3538968
  43.8 2.0 %shard_map.160.z_ref = f32[2,16,4,8,384]{4,3,2,1,0:T(8,128)S(1)} custom-call(bf16[4,2,128,384]{3,2,1,0:T(8,128)(2,1)S(1)} %get-tuple-element.23.act_ref, bf16[768,2304]{1,0:T(8,128)(2,1)S(1)} %copy-done.15), custom_call_target="tpu_custom_call" | custom-call | flops 1811939328 | bytes 6684672 | tf_op jit(solution)/shard_map/pallas_call | solution.py:85
  45.9 1.1 copy-done.21
  47.0 10.9 %all-to-all-done = bf16[128,4,8,384]{3,2,1,0:T(8,128)(2,1)S(1)} async-done(((bf16[128,4,8,384]{3,2,1,0:T(8,128)(2,1)}), bf16[128,4,8,384]{3,2,1,0:T(8,128)(2,1)S(1)}, u32[]{:S(2)}, u32[]{:S(2)}) %all-to-all-start) | async-done | bytes 3145760 | tf_op jit(solution)/shard_map/all_to_all | solution.py:448
  58.0 1.7 %shard_map.167 = bf16[4,32,4,8,384]{4,3,2,1,0:T(8,128)(2,1)S(1)} custom-call(s32[16]{0:T(128)S(1)} %get-tuple-element.45.source_ref, s32[16]{0:T(128)S(1)} %get-tuple-element.51.rotation_ref, s32[16]{0:T(128)S(1)} %compare_convert_fusion.keep_ref, bf16[4,32,4,8,384]{4,3,2,1,0:T(8,128)(2,1)S(1)} %bitcast.24), custom_call_target="tpu_custom_call" | custom-call | tf_op jit(solution)/shard_map/pallas_call | solution.py:66
  59.7 1.7 %copy-done.1 = bf16[4,32,4,8,384]{4,3,2,1,0:T(8,128)(2,1)} copy-done((bf16[4,32,4,8,384]{4,3,2,1,0:T(8,128)(2,1)}, bf16[4,32,4,8,384]{4,3,2,1,0:T(8,128)(2,1)S(1)}, u32[]{:S(2)}) %copy-start.1) | copy-done | bytes 3145752
  61.4 4.8 %all-to-all-start.1 = ((bf16[128,4,8,384]{3,2,1,0:T(8,128)(2,1)}), bf16[128,4,8,384]{3,2,1,0:T(8,128)(2,1)S(1)}, u32[]{:S(2)}, u32[]{:S(2)}) async-start(bf16[128,4,8,384]{3,2,1,0:T(8,128)(2,1)} %bitcast.25), calls=%async_computation.1 | async-start | bytes 6291456 | tf_op jit(solution)/shard_map/all_to_all | solution.py:462
  66.2 0.1 collective-permute-start.2
  66.3 5.1 %collective-permute-start.3 = (bf16[4,128,384]{2,1,0:T(8,128)(2,1)S(1)}, bf16[4,128,384]{2,1,0:T(8,128)(2,1)}, u32[]{:S(2)}, u32[]{:S(2)}) collective-permute-start(bf16[4,128,384]{2,1,0:T(8,128)(2,1)S(1)} %get-tuple-element.26), channel_id=1, source_target_pairs={{1,0},{2,1},{3,2},{4,3},{5,4},{6,5},{7,6},{8,7},{9,8},{10,9},{11,1... | collective-permute-start | bytes 1179656 | tf_op jit(solution)/shard_map/ppermute | solution.py:445
  71.4 0.7 compare_bitcast_fusion.1
  72.1 36.3 %all-to-all-done.1 = bf16[128,4,8,384]{3,2,1,0:T(8,128)(2,1)S(1)} async-done(((bf16[128,4,8,384]{3,2,1,0:T(8,128)(2,1)}), bf16[128,4,8,384]{3,2,1,0:T(8,128)(2,1)S(1)}, u32[]{:S(2)}, u32[]{:S(2)}) %all-to-all-start.1) | async-done | bytes 3145760 | tf_op jit(solution)/shard_map/all_to_all | solution.py:462
  108.4 0.3 slice_bitcast_fusion
  108.7 0.1 collective-permute-start
  108.8 5.1 %collective-permute-start.1 = (bf16[2,16,4,8,384]{4,3,2,1,0:T(8,128)(2,1)S(1)}, bf16[2,16,4,8,384]{4,3,2,1,0:T(8,128)(2,1)S(1)}, u32[]{:S(2)}, u32[]{:S(2)}) collective-permute-start(bf16[2,16,4,8,384]{4,3,2,1,0:T(8,128)(2,1)S(1)} %get-tuple-element.49), channel_id=1, source_target_pairs={{1,0},{2,1},{3,2},{4,3},{5,4},{6,5},{7,6},{8,7},{9,8},{10,9},{11,1... | collective-permute-start | bytes 2359304 | tf_op jit(solution)/shard_map/ppermute | solution.py:445
  113.9 0.1 collective-permute-start.6
  114.0 5.0 %collective-permute-start.7 = (bf16[2,16,4,8,384]{4,3,2,1,0:T(8,128)(2,1)S(1)}, bf16[2,16,4,8,384]{4,3,2,1,0:T(8,128)(2,1)S(1)}, u32[]{:S(2)}, u32[]{:S(2)}) collective-permute-start(bf16[2,16,4,8,384]{4,3,2,1,0:T(8,128)(2,1)S(1)} %get-tuple-element.47), channel_id=1, source_target_pairs={{1,0},{2,1},{3,2},{4,3},{5,4},{6,5},{7,6},{8,7},{9,8},{10,9},{11,1... | collective-permute-start | bytes 2359304 | tf_op jit(solution)/shard_map/ppermute | solution.py:445
  119.0 3.0 %copy-done.3 = bf16[1536,2304]{1,0:T(8,128)(2,1)S(1)} copy-done((bf16[1536,2304]{1,0:T(8,128)(2,1)S(1)}, bf16[1536,2304]{1,0:T(8,128)(2,1)}, u32[]{:S(2)}) %copy-start.3) | copy-done | bytes 7077912
  122.1 3.0 %copy-done.5 = bf16[1536,2304]{1,0:T(8,128)(2,1)S(1)} copy-done((bf16[1536,2304]{1,0:T(8,128)(2,1)S(1)}, bf16[1536,2304]{1,0:T(8,128)(2,1)}, u32[]{:S(2)}) %copy-start.5) | copy-done | bytes 7077912
  125.1 9.0 %shard_map.168 = (f32[2,16,4,8,384]{4,3,2,1,0:T(8,128)S(1)}, f32[2,16,4,8,384]{4,3,2,1,0:T(8,128)S(1)}, bf16[4,2,2,16,8,384]{5,4,3,2,1,0:T(8,128)(2,1)}, bf16[4,2,2,16,8,384]{5,4,3,2,1,0:T(8,128)(2,1)}) custom-call(bf16[2,2,2,16,4,8,384]{6,5,4,3,2,1,0:T(8,128)(2,1)S(1)} %bitcast.23, bf16[1536,2304]{1,0:T(8,128)(2,1)S(1)} %copy-done.3, ...), custom_call_target="tpu_custom_call" | custom-call | flops 7247757312 | bytes 14155776 | tf_op jit(solution)/shard_map/pallas_call | solution.py:85
  134.1 2.5 %copy-done.9 = bf16[2,1152,1152]{2,1,0:T(8,128)(2,1)S(1)} copy-done((bf16[2,1152,1152]{2,1,0:T(8,128)(2,1)S(1)}, bf16[2,1152,1152]{2,1,0:T(8,128)(2,1)}, u32[]{:S(2)}) %copy-start.9) | copy-done | bytes 5308440
  136.6 5.4 %shard_map.169 = (bf16[4,2,128,384]{3,2,1,0:T(8,128)(2,1)S(1)}, bf16[4,128,384]{2,1,0:T(8,128)(2,1)S(1)}, bf16[4,128,384]{2,1,0:T(8,128)(2,1)S(1)}) custom-call(s32[2,4]{1,0:T(2,128)S(1)} %add_convert_fusion.edge_ref, bf16[2,16,4,8,384]{4,3,2,1,0:T(8,128)(2,1)S(1)} %collective-permute-done.above_ref, ...), custom_call_target="tpu_custom_call" | custom-call | flops 2717908992 | bytes 5308416 | tf_op jit(solution)/shard_map/pallas_call | solution.py:85
  142.0 0.1 collective-permute-start.4
  142.1 5.1 %collective-permute-start.5 = (bf16[4,128,384]{2,1,0:T(8,128)(2,1)S(1)}, bf16[4,128,384]{2,1,0:T(8,128)(2,1)S(1)}, u32[]{:S(2)}, u32[]{:S(2)}) collective-permute-start(bf16[4,128,384]{2,1,0:T(8,128)(2,1)S(1)} %get-tuple-element.33), channel_id=1, source_target_pairs={{1,0},{2,1},{3,2},{4,3},{5,4},{6,5},{7,6},{8,7},{9,8},{10,9},{11,1... | collective-permute-start | bytes 1179656 | tf_op jit(solution)/shard_map/ppermute | solution.py:445
  147.2 5.3 %shard_map.170 = (f32[2,16,4,8,384]{4,3,2,1,0:T(8,128)S(1)}, bf16[4,2,2,16,8,384]{5,4,3,2,1,0:T(8,128)(2,1)}) custom-call(s32[2,4]{1,0:T(2,128)S(1)} %add_convert_fusion.edge_ref, bf16[2,16,4,8,384]{4,3,2,1,0:T(8,128)(2,1)S(1)} %collective-permute-done.6.above_ref, ...), custom_call_target="tpu_custom_call", output_to_operand_aliasing={{1}: (8, {})} | custom-call | flops 3623878656 | bytes 7077888 | tf_op jit(solution)/shard_map/pallas_call | solution.py:85
  152.5 0.1 collective-permute-done.4.above_ref
  152.6 3.1 %shard_map.171 = bf16[4,2,128,384]{3,2,1,0:T(8,128)(2,1)} custom-call(s32[2,4]{1,0:T(2,128)S(1)} %add_convert_fusion.edge_ref, bf16[4,128,384]{2,1,0:T(8,128)(2,1)S(1)} %collective-permute-done.4.above_ref, bf16[4,128,384]{2,1,0:T(8,128)(2,1)S(1)} %collective-permute-done.5.below_ref, bf16[2,384,1152]{2,1,0:T(8,128)(2,1)S(1)} %copy-done.7, ...), custom_call_target="tpu_custom_call" | custom-call | flops 905969664 | bytes 1769472 | tf_op jit(solution)/shard_map/pallas_call | solution.py:85
  (64 shorter events, 0.1 us)
Async XLA Ops:
  5.0 53.0 %all-to-all-start = ((bf16[128,4,8,384]{3,2,1,0:T(8,128)(2,1)}), bf16[128,4,8,384]{3,2,1,0:T(8,128)(2,1)S(1)}, u32[]{:S(2)}, u32[]{:S(2)}) async-start(bf16[128,4,8,384]{3,2,1,0:T(8,128)(2,1)} %bitcast.28), calls=%async_computation | async-start | bytes 6291456 | tf_op jit(solution)/shard_map/all_to_all | solution.py:448
  16.1 3.3 %copy-start = (bf16[3,3,3,384,384]{4,3,2,1,0:T(8,128)(2,1)S(1)}, bf16[3,3,3,384,384]{4,3,2,1,0:T(8,128)(2,1)}, u32[]{:S(2)}) copy-start(bf16[3,3,3,384,384]{4,3,2,1,0:T(8,128)(2,1)} %w_ref.9) | copy-start | bytes 23887876
  19.4 7.4 %slice-start = ((s8[7962624]{0:T(1024)(128)(4,1)}), s8[4194304]{0:T(1024)(128)(4,1)S(1)}, s32[]{:S(2)}) async-start(s8[7962624]{0:T(1024)(128)(4,1)} %bitcast.20), calls=%async_computation.2 | async-start | bytes 8388608
  19.8 1.9 %copy-start.14 = (bf16[768,2304]{1,0:T(8,128)(2,1)}, bf16[768,2304]{1,0:T(8,128)(2,1)S(1)}, u32[]{:S(2)}) copy-start(bf16[768,2304]{1,0:T(8,128)(2,1)S(1)} %shard_map.159.w_ref) | copy-start | bytes 10616836
  21.7 5.2 %slice-start.1 = ((s8[7962624]{0:T(1024)(128)(4,1)}), s8[3768320]{0:T(1024)(128)(4,1)S(1)}, s32[]{:S(2)}) async-start(s8[7962624]{0:T(1024)(128)(4,1)} %bitcast.20), calls=%async_computation.3 | async-start | bytes 7536640
  22.9 2.9 %copy-start.2 = (bf16[1536,2304]{1,0:T(8,128)(2,1)}, bf16[1536,2304]{1,0:T(8,128)(2,1)S(1)}, u32[]{:S(2)}) copy-start(bf16[1536,2304]{1,0:T(8,128)(2,1)S(1)} %shard_map.161.w0_ref) | copy-start | bytes 21233668
  26.9 2.3 %copy-start.8 = (bf16[2,1152,1152]{2,1,0:T(8,128)(2,1)}, bf16[2,1152,1152]{2,1,0:T(8,128)(2,1)S(1)}, u32[]{:S(2)}) copy-start(bf16[2,1152,1152]{2,1,0:T(8,128)(2,1)S(1)} %shard_map.162.w_ref) | copy-start | bytes 15925252
  29.2 2.9 %copy-start.4 = (bf16[1536,2304]{1,0:T(8,128)(2,1)}, bf16[1536,2304]{1,0:T(8,128)(2,1)S(1)}, u32[]{:S(2)}) copy-start(bf16[1536,2304]{1,0:T(8,128)(2,1)S(1)} %shard_map.163.w1_ref) | copy-start | bytes 21233668
  32.8 1.8 %copy-start.10 = (bf16[2,768,1152]{2,1,0:T(8,128)(2,1)}, bf16[2,768,1152]{2,1,0:T(8,128)(2,1)S(1)}, u32[]{:S(2)}) copy-start(bf16[2,768,1152]{2,1,0:T(8,128)(2,1)S(1)} %shard_map.164.w_ref) | copy-start | bytes 10616836
  35.0 1.8 %copy-start.12 = (bf16[768,2304]{1,0:T(8,128)(2,1)}, bf16[768,2304]{1,0:T(8,128)(2,1)S(1)}, u32[]{:S(2)}) copy-start(bf16[768,2304]{1,0:T(8,128)(2,1)S(1)} %shard_map.165.wa_ref) | copy-start | bytes 10616836
  36.9 1.4 copy-start.23
  36.9 4.0 %copy-start.28 = (s32[16]{0:T(128)S(1)}, s32[16]{0:T(128)}, u32[]{:S(2)}) copy-start(s32[16]{0:T(128)} %param.27) | copy-start | bytes 196
  36.9 4.0 %copy-start.29 = (s32[16]{0:T(128)S(1)}, s32[16]{0:T(128)}, u32[]{:S(2)}) copy-start(s32[16]{0:T(128)} %param.24) | copy-start | bytes 196
  36.9 4.0 %copy-start.30 = (s32[16]{0:T(128)S(1)}, s32[16]{0:T(128)}, u32[]{:S(2)}) copy-start(s32[16]{0:T(128)} %param.25) | copy-start | bytes 196
  37.1 1.2 copy-start.6
  38.3 1.1 copy-start.16
  40.1 0.7 copy-start.20
  40.9 5.0 %copy-start.18 = (bf16[4,2,128,384]{3,2,1,0:T(8,128)(2,1)}, bf16[4,2,128,384]{3,2,1,0:T(8,128)(2,1)S(1)}, u32[]{:S(2)}) copy-start(bf16[4,2,128,384]{3,2,1,0:T(8,128)(2,1)S(1)} %get-tuple-element.23.act_ref) | copy-start | bytes 2359300
  41.8 2.0 %copy-start.15 = (bf16[768,2304]{1,0:T(8,128)(2,1)S(1)}, bf16[768,2304]{1,0:T(8,128)(2,1)}, u32[]{:S(2)}) copy-start(bf16[768,2304]{1,0:T(8,128)(2,1)} %copy-done.14) | copy-start | bytes 10616836
  45.8 1.1 copy-start.21
  59.7 1.8 %copy-start.1 = (bf16[4,32,4,8,384]{4,3,2,1,0:T(8,128)(2,1)}, bf16[4,32,4,8,384]{4,3,2,1,0:T(8,128)(2,1)S(1)}, u32[]{:S(2)}) copy-start(bf16[4,32,4,8,384]{4,3,2,1,0:T(8,128)(2,1)S(1)} %shard_map.167) | copy-start | bytes 9437188
  61.4 10.0 %copy-start.24 = (f32[384]{0:T(512)S(1)}, f32[384]{0:T(512)}, u32[]{:S(2)}) copy-start(f32[384]{0:T(512)} %param.21) | copy-start | bytes 4612
  61.4 10.0 %copy-start.25 = (f32[384]{0:T(512)S(1)}, f32[384]{0:T(512)}, u32[]{:S(2)}) copy-start(f32[384]{0:T(512)} %param.18) | copy-start | bytes 4612
  61.4 47.0 %all-to-all-start.1 = ((bf16[128,4,8,384]{3,2,1,0:T(8,128)(2,1)}), bf16[128,4,8,384]{3,2,1,0:T(8,128)(2,1)S(1)}, u32[]{:S(2)}, u32[]{:S(2)}) async-start(bf16[128,4,8,384]{3,2,1,0:T(8,128)(2,1)} %bitcast.25), calls=%async_computation.1 | async-start | bytes 6291456 | tf_op jit(solution)/shard_map/all_to_all | solution.py:462
  66.2 47.7 %collective-permute-start.2 = (bf16[4,128,384]{2,1,0:T(8,128)(2,1)}, bf16[4,128,384]{2,1,0:T(8,128)(2,1)}, u32[]{:S(2)}, u32[]{:S(2)}) collective-permute-start(bf16[4,128,384]{2,1,0:T(8,128)(2,1)} %copy-done.20), channel_id=1, source_target_pairs={{0,1},{1,2},{2,3},{3,4},{4,5},{5,6},{6,7},{7,8},{8,9},{9,10},{10,1... | collective-permute-start | bytes 1179656 | tf_op jit(solution)/shard_map/ppermute | solution.py:442
  66.3 67.7 %collective-permute-start.3 = (bf16[4,128,384]{2,1,0:T(8,128)(2,1)S(1)}, bf16[4,128,384]{2,1,0:T(8,128)(2,1)}, u32[]{:S(2)}, u32[]{:S(2)}) collective-permute-start(bf16[4,128,384]{2,1,0:T(8,128)(2,1)S(1)} %get-tuple-element.26), channel_id=1, source_target_pairs={{1,0},{2,1},{3,2},{4,3},{5,4},{6,5},{7,6},{8,7},{9,8},{10,9},{11,1... | collective-permute-start | bytes 1179656 | tf_op jit(solution)/shard_map/ppermute | solution.py:445
  108.4 5.5 %copy-start.27 = (pred[1,4]{1,0:T(4,128)(4,1)S(1)}, pred[1,4]{1,0:T(4,128)(4,1)}, u32[]{:S(2)}) copy-start(pred[1,4]{1,0:T(4,128)(4,1)} %get-tuple-element.54) | copy-start | bytes 16
  108.4 10.6 %copy-start.19 = (bf16[4,2,128,384]{3,2,1,0:T(8,128)(2,1)S(1)}, bf16[4,2,128,384]{3,2,1,0:T(8,128)(2,1)}, u32[]{:S(2)}) copy-start(bf16[4,2,128,384]{3,2,1,0:T(8,128)(2,1)} %copy-done.18) | copy-start | bytes 2359300
  108.4 10.6 %copy-start.22 = (f32[2,16,4,8,384]{4,3,2,1,0:T(8,128)S(1)}, f32[2,16,4,8,384]{4,3,2,1,0:T(8,128)}, u32[]{:S(2)}) copy-start(f32[2,16,4,8,384]{4,3,2,1,0:T(8,128)} %copy-done.21) | copy-start | bytes 4718596
  108.7 25.3 %collective-permute-start = (bf16[2,16,4,8,384]{4,3,2,1,0:T(8,128)(2,1)S(1)}, bf16[2,16,4,8,384]{4,3,2,1,0:T(8,128)(2,1)S(1)}, u32[]{:S(2)}, u32[]{:S(2)}) collective-permute-start(bf16[2,16,4,8,384]{4,3,2,1,0:T(8,128)(2,1)S(1)} %get-tuple-element.50), channel_id=1, source_target_pairs={{0,1},{1,2},{2,3},{3,4},{4,5},{5,6},{6,7},{7,8},{8,9},{9,10},{10,1... | collective-permute-start | bytes 2359304 | tf_op jit(solution)/shard_map/ppermute | solution.py:442
  108.8 25.3 %collective-permute-start.1 = (bf16[2,16,4,8,384]{4,3,2,1,0:T(8,128)(2,1)S(1)}, bf16[2,16,4,8,384]{4,3,2,1,0:T(8,128)(2,1)S(1)}, u32[]{:S(2)}, u32[]{:S(2)}) collective-permute-start(bf16[2,16,4,8,384]{4,3,2,1,0:T(8,128)(2,1)S(1)} %get-tuple-element.49), channel_id=1, source_target_pairs={{1,0},{2,1},{3,2},{4,3},{5,4},{6,5},{7,6},{8,7},{9,8},{10,9},{11,1... | collective-permute-start | bytes 2359304 | tf_op jit(solution)/shard_map/ppermute | solution.py:445
  113.9 33.3 %collective-permute-start.6 = (bf16[2,16,4,8,384]{4,3,2,1,0:T(8,128)(2,1)S(1)}, bf16[2,16,4,8,384]{4,3,2,1,0:T(8,128)(2,1)S(1)}, u32[]{:S(2)}, u32[]{:S(2)}) collective-permute-start(bf16[2,16,4,8,384]{4,3,2,1,0:T(8,128)(2,1)S(1)} %get-tuple-element.48), channel_id=1, source_target_pairs={{0,1},{1,2},{2,3},{3,4},{4,5},{5,6},{6,7},{7,8},{8,9},{9,10},{10,1... | collective-permute-start | bytes 2359304 | tf_op jit(solution)/shard_map/ppermute | solution.py:442
  114.0 33.2 %collective-permute-start.7 = (bf16[2,16,4,8,384]{4,3,2,1,0:T(8,128)(2,1)S(1)}, bf16[2,16,4,8,384]{4,3,2,1,0:T(8,128)(2,1)S(1)}, u32[]{:S(2)}, u32[]{:S(2)}) collective-permute-start(bf16[2,16,4,8,384]{4,3,2,1,0:T(8,128)(2,1)S(1)} %get-tuple-element.47), channel_id=1, source_target_pairs={{1,0},{2,1},{3,2},{4,3},{5,4},{6,5},{7,6},{8,7},{9,8},{10,9},{11,1... | collective-permute-start | bytes 2359304 | tf_op jit(solution)/shard_map/ppermute | solution.py:445
  119.0 3.0 %copy-start.3 = (bf16[1536,2304]{1,0:T(8,128)(2,1)S(1)}, bf16[1536,2304]{1,0:T(8,128)(2,1)}, u32[]{:S(2)}) copy-start(bf16[1536,2304]{1,0:T(8,128)(2,1)} %copy-done.2) | copy-start | bytes 21233668
  122.1 3.0 %copy-start.5 = (bf16[1536,2304]{1,0:T(8,128)(2,1)S(1)}, bf16[1536,2304]{1,0:T(8,128)(2,1)}, u32[]{:S(2)}) copy-start(bf16[1536,2304]{1,0:T(8,128)(2,1)} %copy-done.4) | copy-start | bytes 21233668
  134.1 2.5 %copy-start.9 = (bf16[2,1152,1152]{2,1,0:T(8,128)(2,1)S(1)}, bf16[2,1152,1152]{2,1,0:T(8,128)(2,1)}, u32[]{:S(2)}) copy-start(bf16[2,1152,1152]{2,1,0:T(8,128)(2,1)} %copy-done.8) | copy-start | bytes 15925252
  136.6 10.6 %copy-start.26 = (f32[384]{0:T(512)S(1)}, f32[384]{0:T(512)}, u32[]{:S(2)}) copy-start(f32[384]{0:T(512)} %param.22) | copy-start | bytes 4612
  136.6 10.6 %copy-start.11 = (bf16[2,768,1152]{2,1,0:T(8,128)(2,1)S(1)}, bf16[2,768,1152]{2,1,0:T(8,128)(2,1)}, u32[]{:S(2)}) copy-start(bf16[2,768,1152]{2,1,0:T(8,128)(2,1)} %copy-done.10) | copy-start | bytes 10616836
  136.6 10.6 %copy-start.13 = (bf16[768,2304]{1,0:T(8,128)(2,1)S(1)}, bf16[768,2304]{1,0:T(8,128)(2,1)}, u32[]{:S(2)}) copy-start(bf16[768,2304]{1,0:T(8,128)(2,1)} %copy-done.12) | copy-start | bytes 10616836
  142.0 10.6 %collective-permute-start.4 = (bf16[4,128,384]{2,1,0:T(8,128)(2,1)S(1)}, bf16[4,128,384]{2,1,0:T(8,128)(2,1)S(1)}, u32[]{:S(2)}, u32[]{:S(2)}) collective-permute-start(bf16[4,128,384]{2,1,0:T(8,128)(2,1)S(1)} %get-tuple-element.32), channel_id=1, source_target_pairs={{0,1},{1,2},{2,3},{3,4},{4,5},{5,6},{6,7},{7,8},{8,9},{9,10},{10,1... | collective-permute-start | bytes 1179656 | tf_op jit(solution)/shard_map/ppermute | solution.py:442
  142.1 10.5 %collective-permute-start.5 = (bf16[4,128,384]{2,1,0:T(8,128)(2,1)S(1)}, bf16[4,128,384]{2,1,0:T(8,128)(2,1)S(1)}, u32[]{:S(2)}, u32[]{:S(2)}) collective-permute-start(bf16[4,128,384]{2,1,0:T(8,128)(2,1)S(1)} %get-tuple-element.33), channel_id=1, source_target_pairs={{1,0},{2,1},{3,2},{4,3},{5,4},{6,5},{7,6},{8,7},{9,8},{10,9},{11,1... | collective-permute-start | bytes 1179656 | tf_op jit(solution)/shard_map/ppermute | solution.py:445
  147.2 5.4 %copy-start.7 = (bf16[2,384,1152]{2,1,0:T(8,128)(2,1)S(1)}, bf16[2,384,1152]{2,1,0:T(8,128)(2,1)}, u32[]{:S(2)}) copy-start(bf16[2,384,1152]{2,1,0:T(8,128)(2,1)} %copy-done.6) | copy-start | bytes 5308420
  147.2 5.4 %copy-start.17 = (bf16[4,2,128,384]{3,2,1,0:T(8,128)(2,1)S(1)}, bf16[4,2,128,384]{3,2,1,0:T(8,128)(2,1)}, u32[]{:S(2)}) copy-start(bf16[4,2,128,384]{3,2,1,0:T(8,128)(2,1)} %f_ref.3) | copy-start | bytes 2359300

commit v8 on v6

--- a/solution.py
+++ b/solution.py
@@ -16,73 +16,96 @@
 def pack(first, second):
     n_slots, n_frames, n_rows, n_cols, ch = first.shape
     blocks = n_cols // CB
-
-    def body(a_ref, b_ref, o_ref):
-        for k, ref in enumerate((a_ref, b_ref)):
-            for f in range(n_frames):
-                for r in range(n_rows):
-                    o_ref[r, k, f, :, 0] = ref[0, f, r].reshape(blocks, CB, ch)
-
-    spec = pl.BlockSpec((1, n_frames, n_rows, n_cols, ch), lambda s: (s, 0, 0, 0, 0))
+    parts = n_rows * 2 * n_frames
+
+    def body(a_ref, b_ref, o_ref, held, in_sems, out_sems):
+        whole = []
+        for r in range(n_rows):
+            for k, ref in enumerate((a_ref, b_ref)):
+                for f in range(n_frames):
+                    whole.append((r, k, f, ref))
+        loads = []
+        for p, (r, k, f, ref) in enumerate(whole):
+            for s in range(n_slots):
+                n = p * n_slots + s
+                loads.append(
+                    pltpu.make_async_copy(ref.at[s, f, r], held.at[r, k, f, :, s], in_sems.at[n])
+                )
+                loads[-1].start()
+        stores = []
+        for p, (r, k, f, _) in enumerate(whole):
+            for s in range(n_slots):
+                loads[p * n_slots + s].wait()
+            stores.append(pltpu.make_async_copy(held.at[r, k, f], o_ref.at[r, k, f], out_sems.at[p]))
+            stores[-1].start()
+        for c in stores:
+            c.wait()
+
+    shape = (n_rows, 2, n_frames, blocks, n_slots, CB, ch)
+    tiles = (n_slots, n_frames, n_rows, blocks, CB, ch)
+    far = pl.BlockSpec(memory_space=pl.ANY)
     return pl.pallas_call(
         body,
-        grid=(n_slots,),
-        in_specs=[spec, spec],
-        out_specs=pl.BlockSpec(
-            (n_rows, 2, n_frames, blocks, 1, CB, ch), lambda s: (0, 0, 0, 0, s, 0, 0)
-        ),
-        out_shape=jax.ShapeDtypeStruct(
-            (n_rows, 2, n_frames, blocks, n_slots, CB, ch), first.dtype
-        ),
+        in_specs=[far, far],
+        out_specs=far,
+        out_shape=jax.ShapeDtypeStruct(shape, first.dtype),
+        scratch_shapes=[
+            pltpu.VMEM(shape, first.dtype),
+            pltpu.SemaphoreType.DMA((parts * n_slots,)),
+            pltpu.SemaphoreType.DMA((parts,)),
+        ],
         compiler_params=pltpu.CompilerParams(vmem_limit_bytes=58 << 20),
-    )(first, second)
+    )(first.reshape(tiles), second.reshape(tiles))
 
 
 def permute(held, source, rotation, keep):
     n_groups, n_tiles, n_slots, cols, ch = held.shape
 
-    def body(source_ref, rotation_ref, keep_ref, i_ref, o_ref):
-        n = pl.program_id(0)
-        by = rotation_ref[n]
-
-        @pl.when(keep_ref[n] != 0)
-        def _():
-            def step(t, _):
-                at = lax.rem(t + n_tiles - by, n_tiles)
-                o_ref[0, t, 0] = i_ref[0, at, 0]
-                return 0
-
-            lax.fori_loop(0, n_tiles, step, 0, unroll=8)
-
-        @pl.when(keep_ref[n] == 0)
-        def _():
-            o_ref[...] = jnp.zeros_like(o_ref)
-
-    block = (1, n_tiles, 1, cols, ch)
+    def body(source_ref, rotation_ref, keep_ref, i_ref, o_ref, made, sems):
+        def stream(n, to):
+            by = rotation_ref[n]
+            old = source_ref[n]
+            slot = lax.rem(n, n_slots)
+            of, place = lax.div(old, n_slots), lax.rem(old, n_slots)
+
+            @pl.when(keep_ref[n] != 0)
+            def _():
+                for t in range(n_tiles):
+                    at = lax.rem(t + n_tiles - by, n_tiles)
+                    made[to, t, slot] = i_ref[of, at, place]
+
+            @pl.when(keep_ref[n] == 0)
+            def _():
+                made[to, :, slot] = jnp.zeros((n_tiles, cols, ch), made.dtype)
+
+            return to
+
+        copies = []
+        for to in range(n_groups):
+            lax.fori_loop(to * n_slots, (to + 1) * n_slots, stream, to)
+            copies.append(pltpu.make_async_copy(made.at[to], o_ref.at[to], sems.at[to]))
+            copies[-1].start()
+        for c in copies:
+            c.wait()
+
+    smem = pl.BlockSpec(memory_space=pltpu.SMEM)
     return pl.pallas_call(
         body,
-        grid_spec=pltpu.PrefetchScalarGridSpec(
-            num_scalar_prefetch=3,
-            grid=(n_groups * n_slots,),
-            in_specs=[
-                pl.BlockSpec(
-                    block,
-                    lambda n, s, r, k: (lax.div(s[n], n_slots), 0, lax.rem(s[n], n_slots), 0, 0),
-                )
-            ],
-            out_specs=pl.BlockSpec(
-                block, lambda n, s, r, k: (lax.div(n, n_slots), 0, lax.rem(n, n_slots), 0, 0)
-            ),
-        ),
+        in_specs=[smem, smem, smem, pl.BlockSpec(memory_space=pltpu.VMEM)],
+        out_specs=pl.BlockSpec(memory_space=pl.ANY),
         out_shape=jax.ShapeDtypeStruct(held.shape, held.dtype),
-        compiler_params=pltpu.CompilerParams(vmem_limit_bytes=32 << 20),
+        scratch_shapes=[
+            pltpu.VMEM(held.shape, held.dtype),
+            pltpu.SemaphoreType.DMA((n_groups,)),
+        ],
+        compiler_params=pltpu.CompilerParams(vmem_limit_bytes=52 << 20),
     )(source, rotation, keep, held)
 
 
 VMEM_LIMIT = 16 << 20
 
 
-def call(body, out_shape, operands, scalars=(), scratch=(), flops=0, moved=0, far=(), far_out=(), aliases=None):
+def call(body, out_shape, operands, scalars=(), scratch=(), flops=0, moved=0, far=(), far_out=(), aliases=None, limit=VMEM_LIMIT):
     in_specs = [pl.BlockSpec(memory_space=pltpu.SMEM) for _ in scalars]
     for k, _ in enumerate(operands):
         in_specs.append(pl.BlockSpec(memory_space=pl.ANY if k in far else pltpu.VMEM))
@@ -97,7 +120,7 @@
         scratch_shapes=list(scratch),
         input_output_aliases=aliases or {},
         cost_estimate=pl.CostEstimate(flops=flops, bytes_accessed=moved, transcendentals=0),
-        compiler_params=pltpu.CompilerParams(vmem_limit_bytes=VMEM_LIMIT),
+        compiler_params=pltpu.CompilerParams(vmem_limit_bytes=limit),
     )(*scalars, *operands)
 
 
@@ -263,53 +286,82 @@
     )[0]
 
 
-def own_part(got, weights, sums, act):
+def own_part(got, weights, sums, act, sides):
     n_rows, n_caches, n_frames, blocks, n_slots, _, ch = got.shape
     half = blocks * n_slots * CB
     deep = n_frames * ch
     whole = weights[0]
 
-    def body(got_ref, w0_ref, w1_ref, z_ref, act_ref, o0_ref, o1_ref, n1_ref, n2_ref, lhs, sems, act_sem):
-        keeps = []
+    def body(got_ref, w0_ref, w1_ref, z_ref, act_ref, sides_ref, o0_ref, o1_ref, n1_ref, n2_ref, near_ref, w0, w1, lhs, acc, sems, keep_sems):
+        loads = []
+        for r in range(n_rows):
+            rows = pl.ds(r * deep, deep)
+            loads.append(pltpu.make_async_copy(w0_ref.at[rows], w0.at[r], sems.at[r]))
+        loads.append(pltpu.make_async_copy(w1_ref, w1, sems.at[2]))
+        near = pltpu.make_async_copy(sides_ref, near_ref, sems.at[3])
+        keeps = [pltpu.make_async_copy(act_ref, n1_ref.at[:, 1], sems.at[4])]
         for k, dst in enumerate((n1_ref, n2_ref)):
             for r in range(n_rows):
                 for s in range(n_slots):
                     n = (k * n_rows + r) * n_slots + s
                     keeps.append(
                         pltpu.make_async_copy(
-                            got_ref.at[r, k, n_frames - 1, :, s], dst.at[s, 0, r], sems.at[n]
+                            got_ref.at[r, k, n_frames - 1, :, s], dst.at[s, 0, r], keep_sems.at[n]
                         )
                     )
-        keeps.append(pltpu.make_async_copy(act_ref, n1_ref.at[:, 1], act_sem))
+        for c in loads:
+            c.start()
+        near.start()
+
+        def fill(k, r, f):
+            lo = r * deep + f * ch
+            lhs[:, lo : lo + ch] = got_ref[r, k, f].reshape(half, ch)
+
+        def give(o_ref, base):
+            wide = whole.shape[1] // 2
+            for y in range(n_rows):
+                total = folded(acc[:, y * wide : (y + 1) * wide], ch, True)
+                add_into(o_ref, y, total, True, base)
+
+        for r in range(n_rows):
+            for f in range(n_frames):
+                fill(0, r, f)
+        loads[0].wait()
+        acc[...] = dot(lhs[:, 0:deep], w0[0])
+        loads[1].wait()
+        acc[...] += dot(lhs[:, deep : 2 * deep], w0[1])
+        give(o0_ref, z_ref)
+        for r in range(n_rows):
+            for f in range(n_frames):
+                fill(1, r, f)
         for c in keeps:
             c.start()
-        for k, (w, o_ref, base) in enumerate(((w0_ref, o0_ref, z_ref), (w1_ref, o1_ref, None))):
-            for r in range(n_rows):
-                for f in range(n_frames):
-                    lo = r * deep + f * ch
-                    lhs[:, lo : lo + ch] = got_ref[r, k, f].reshape(half, ch)
-            both = dot(lhs[...], w[...])
-            wide = both.shape[1] // 2
-            for y in range(n_rows):
-                total = folded(both[:, y * wide : (y + 1) * wide], ch, True)
-                add_into(o_ref, y, total, True, base)
+        loads[2].wait()
+        acc[...] = dot(lhs[...], w1[...])
+        give(o1_ref, None)
         for c in keeps:
             c.wait()
+        near.wait()
 
     out = sums_shape(blocks, n_slots, n_rows, ch)
     nxt = jax.ShapeDtypeStruct((n_slots, 2, n_rows, blocks, CB, ch), jnp.bfloat16)
     return call(
         body,
-        [out, out, nxt, nxt],
-        (got, *weights, sums, act),
+        [out, out, nxt, nxt, jax.ShapeDtypeStruct(sides.shape, sides.dtype)],
+        (got, *weights, sums, act, sides),
         scratch=[
+            pltpu.VMEM((n_rows, deep, whole.shape[1]), whole.dtype),
+            pltpu.VMEM(whole.shape, whole.dtype),
             pltpu.VMEM((half, n_rows * deep), jnp.bfloat16),
+            pltpu.VMEM((half, whole.shape[1]), jnp.float32),
+            pltpu.SemaphoreType.DMA((5,)),
             pltpu.SemaphoreType.DMA((2 * n_rows * n_slots,)),
-            pltpu.SemaphoreType.DMA,
         ],
         flops=4 * half * whole.size,
         moved=4 * whole.size,
+        far=(1, 2, 5),
         far_out=(2, 3),
+        limit=45 << 20,
     )
 
 
@@ -478,7 +530,9 @@
     above_2 = from_above(got[n_rows - 1, 1])
     below_2 = from_below(got[0, 1])
     act_tiles = act_first.reshape(n_slots, n_rows, blocks, CB, ch)
-    sums_1, sums_2, next_first, kept = own_part(got, (own_1, own_2), sums_1, act_tiles)
+    sums_1, sums_2, next_first, kept, sides_1 = own_part(
+        got, (own_1, own_2), sums_1, act_tiles, sides_1
+    )
     act_second, top, bottom = second_activation(
         above_1, below_1, sides_1, sums_1, bias_first[None], gain_second[None], edges
     )

time: 156 us -> 154 us (0.987)
  local copies, waits for them, and re-layouts: 37.3 us -> 31.9 us
  Pallas kernels: 38 us -> 40.1 us
    unnamed x74 -> x72, local copies, waits for them, and re-layouts: 37 us -> 31.6 us
    pallas_call x6, Pallas kernels: 26.6 us -> 28.8 us  [call(): pl.pallas_call(body, in_specs=in_specs, out_specs=out_specs, out_shape=li...]
    ppermute x4, waiting for transfers between devices: 28.4 us -> 30 us  [from_above(): return lax.ppermute(row, 'tile', down)]
  transfers between devices with their start and end apart: 10 -> 10, of which waited for: 3 -> 3; matrix products, arithmetic and copies ran while one was open for 0% -> 0% of each run, Pallas kernels for 18% -> 20%
where the time goes in v8:
time: 154 us; the launch traced here: 153 us
  waiting for transfers between devices  41.8 us (27%)
  Pallas kernels  40.1 us (26%)
  starting transfers between devices  38.2 us (25%)
  local copies, waits for them, and re-layouts  31.9 us (21%)
    unnamed x72, local copies, waits for them, and re-layouts  31.6 us
    ppermute x4, waiting for transfers between devices, from_above(): return lax.ppermute(row, 'tile', down)  30 us
    pallas_call x6, Pallas kernels, call(): pl.pallas_call(body, in_specs=in_specs, out_specs=out_specs, out_shape=li...  28.8 us
    ppermute x4, starting transfers between devices, from_below(): return lax.ppermute(row, 'tile', up)  20.2 us
    all_to_all x1, waiting for transfers between devices, local(): lax.all_to_all(moved.reshape(n_groups * n_tiles, n_slots, CB, ch), BOTH,...  11.8 us
    all_to_all x1, starting transfers between devices, local(): held = lax.all_to_all(sent, BOTH, 0, 0, tiled=True)  11.6 us
    all_to_all x1, starting transfers between devices, local(): lax.all_to_all(moved.reshape(n_groups * n_tiles, n_slots, CB, ch), BOTH,...  6.09 us
    pallas_call x4, Pallas kernels, spread(): pl.pallas_call(body, grid=(n_y,), in_specs=[pl.BlockSpec((times, 1, n_x,...  4.14 us
  transfers between devices with their start and end apart: 10, of which 3 were waited for; matrix products, arithmetic and copies ran while one was open for 0% of the time, Pallas kernels for 20%

profile of v8, /device:TPU:0, one launch (start us, length us, event | category | flops | bytes accessed | tf_op | source)
XLA Modules:
  0.0 153.2 jit_solution(18068310374465756034)
XLA Ops:
  0.6 3.2 %shard_map.157 = bf16[2,2,2,16,4,8,384]{6,5,4,3,2,1,0:T(8,128)(2,1)} custom-call(bf16[4,2,2,16,8,384]{5,4,3,2,1,0:T(8,128)(2,1)} %bitcast.30, bf16[4,2,2,16,8,384]{5,4,3,2,1,0:T(8,128)(2,1)} %bitcast.31), custom_call_target="tpu_custom_call" | custom-call | tf_op jit(solution)/shard_map/pallas_call | solution.py:47
  3.8 0.0 copy-start.2
  3.8 11.6 %all-to-all-start = ((bf16[128,4,8,384]{3,2,1,0:T(8,128)(2,1)}), bf16[128,4,8,384]{3,2,1,0:T(8,128)(2,1)}, u32[]{:S(2)}, u32[]{:S(2)}) async-start(bf16[128,4,8,384]{3,2,1,0:T(8,128)(2,1)} %bitcast.28), calls=%async_computation | async-start | bytes 6291456 | tf_op jit(solution)/shard_map/all_to_all | solution.py:504
  15.5 0.7 shard_map.158
  16.2 0.9 copy-done.17
  17.0 5.1 %collective-permute-start.1 = (bf16[4,128,384]{2,1,0:T(8,128)(2,1)S(1)}, bf16[4,128,384]{2,1,0:T(8,128)(2,1)S(1)}, u32[]{:S(2)}, u32[]{:S(2)}) collective-permute-start(bf16[4,128,384]{2,1,0:T(8,128)(2,1)S(1)} %get-tuple-element.45), channel_id=1, source_target_pairs={{1,0},{2,1},{3,2},{4,3},{5,4},{6,5},{7,6},{8,7},{9,8},{10,9},{11,1... | collective-permute-start | bytes 1179656 | tf_op jit(solution)/shard_map/ppermute | solution.py:501
  22.1 3.3 %copy-done.1 = bf16[3,3,3,384,384]{4,3,2,1,0:T(8,128)(2,1)S(1)} copy-done((bf16[3,3,3,384,384]{4,3,2,1,0:T(8,128)(2,1)S(1)}, bf16[3,3,3,384,384]{4,3,2,1,0:T(8,128)(2,1)}, u32[]{:S(2)}) %copy-start.1) | copy-done | bytes 7962648
  25.4 0.0 copy-start.33
  25.4 0.5 shard_map.159
  26.0 1.7 %copy-done.12 = bf16[768,2304]{1,0:T(8,128)(2,1)} copy-done((bf16[768,2304]{1,0:T(8,128)(2,1)}, bf16[768,2304]{1,0:T(8,128)(2,1)S(1)}, u32[]{:S(2)}) %copy-start.12) | copy-done | bytes 3538968
  27.7 1.2 copy-done.15
  28.9 0.1 select_reduce_fusion
  29.1 29.8 %collective-permute-done.above_ref = bf16[4,128,384]{2,1,0:T(8,128)(2,1)S(1)} collective-permute-done((bf16[4,128,384]{2,1,0:T(8,128)(2,1)S(1)}, bf16[4,128,384]{2,1,0:T(8,128)(2,1)S(1)}, u32[]{:S(2)}, u32[]{:S(2)}) %collective-permute-start) | collective-permute-done | bytes 393248 | tf_op jit(solution)/shard_map/ppermute | solution.py:498
  58.9 4.0 %shard_map.160 = bf16[4,32,4,8,384]{4,3,2,1,0:T(8,128)(2,1)} custom-call(s32[16]{0:T(128)S(1)} %get-tuple-element.85.source_ref, s32[16]{0:T(128)S(1)} %get-tuple-element.91.rotation_ref, s32[16]{0:T(128)S(1)} %compare_convert_fusion.keep_ref, bf16[4,32,4,8,384]{4,3,2,1,0:T(8,128)(2,1)} %bitcast.5.i_ref), custom_call_target="tpu_custom_call" | custom-call | tf_op jit(solution)/shard_map/pallas_call | solution.py:92
  63.0 6.1 %all-to-all-start.1 = ((bf16[128,4,8,384]{3,2,1,0:T(8,128)(2,1)}), bf16[128,4,8,384]{3,2,1,0:T(8,128)(2,1)S(1)}, u32[]{:S(2)}, u32[]{:S(2)}) async-start(bf16[128,4,8,384]{3,2,1,0:T(8,128)(2,1)} %bitcast.29), calls=%async_computation.1 | async-start | bytes 6291456 | tf_op jit(solution)/shard_map/all_to_all | solution.py:515
  69.1 0.1 compare_bitcast_fusion.1
  69.2 2.0 %copy-done.13 = bf16[768,2304]{1,0:T(8,128)(2,1)S(1)} copy-done((bf16[768,2304]{1,0:T(8,128)(2,1)S(1)}, bf16[768,2304]{1,0:T(8,128)(2,1)}, u32[]{:S(2)}) %copy-start.13) | copy-done | bytes 3538968
  71.2 1.5 copy-done.16
  72.6 1.1 copy-done.18
  73.8 1.0 copy-done.21
  74.8 3.9 %shard_map.161.z_ref = f32[2,16,4,8,384]{4,3,2,1,0:T(8,128)S(1)} custom-call(s32[2,4]{1,0:T(2,128)S(1)} %add_convert_fusion.edge_ref, bf16[4,2,128,384]{3,2,1,0:T(8,128)(2,1)S(1)} %copy-done.18, bf16[4,128,384]{2,1,0:T(8,128)(2,1)S(1)} %collective-permute-done.above_ref, bf16[4,128,384]{2,1,0:T(8,128)(2,1)S(1)} %copy-done.21, ...), custom_call_target="tpu_custom_call" | custom-call | flops 2717908992 | bytes 6684672 | tf_op jit(solution)/shard_map/pallas_call | solution.py:115
  78.7 0.0 copy-start.23
  78.7 1.1 copy-done.23
  79.8 3.3 %copy-done = bf16[3,3,3,384,384]{4,3,2,1,0:T(8,128)(2,1)S(1)} copy-done((bf16[3,3,3,384,384]{4,3,2,1,0:T(8,128)(2,1)S(1)}, bf16[3,3,3,384,384]{4,3,2,1,0:T(8,128)(2,1)}, u32[]{:S(2)}) %copy-start) | copy-done | bytes 7962648
  83.1 1.5 %shard_map.163 = (bf16[1536,2304]{1,0:T(8,128)(2,1)S(1)}, bf16[2,768,1152]{2,1,0:T(8,128)(2,1)S(1)}) custom-call(bf16[3,3,3,384,384]{4,3,2,1,0:T(8,128)(2,1)S(1)} %copy-done), custom_call_target="tpu_custom_call" | custom-call | bytes 15925248 | tf_op jit(solution)/shard_map/pallas_call | solution.py:164
  84.6 2.8 %copy-done.6 = bf16[1536,2304]{1,0:T(8,128)(2,1)} copy-done((bf16[1536,2304]{1,0:T(8,128)(2,1)}, bf16[1536,2304]{1,0:T(8,128)(2,1)S(1)}, u32[]{:S(2)}) %copy-start.6) | copy-done | bytes 7077912
  87.5 1.8 %copy-done.8 = bf16[2,768,1152]{2,1,0:T(8,128)(2,1)} copy-done((bf16[2,768,1152]{2,1,0:T(8,128)(2,1)}, bf16[2,768,1152]{2,1,0:T(8,128)(2,1)S(1)}, u32[]{:S(2)}) %copy-start.8) | copy-done | bytes 3538968
  89.2 0.5 shard_map.164
  89.7 1.3 copy-done.4
  91.0 1.8 %copy-done.10 = bf16[768,2304]{1,0:T(8,128)(2,1)} copy-done((bf16[768,2304]{1,0:T(8,128)(2,1)}, bf16[768,2304]{1,0:T(8,128)(2,1)S(1)}, u32[]{:S(2)}) %copy-start.10) | copy-done | bytes 3538968
  92.8 1.5 %shard_map.162 = (bf16[1536,2304]{1,0:T(8,128)(2,1)S(1)}, bf16[2,768,1152]{2,1,0:T(8,128)(2,1)S(1)}) custom-call(bf16[3,3,3,384,384]{4,3,2,1,0:T(8,128)(2,1)S(1)} %bitcast.23), custom_call_target="tpu_custom_call" | custom-call | bytes 15925248 | tf_op jit(solution)/shard_map/pallas_call | solution.py:164
  94.4 2.9 %copy-done.7 = bf16[1536,2304]{1,0:T(8,128)(2,1)} copy-done((bf16[1536,2304]{1,0:T(8,128)(2,1)}, bf16[1536,2304]{1,0:T(8,128)(2,1)S(1)}, u32[]{:S(2)}) %copy-start.7) | copy-done | bytes 7077912
  97.3 1.8 %copy-done.14 = bf16[2,768,1152]{2,1,0:T(8,128)(2,1)} copy-done((bf16[2,768,1152]{2,1,0:T(8,128)(2,1)}, bf16[2,768,1152]{2,1,0:T(8,128)(2,1)S(1)}, u32[]{:S(2)}) %copy-start.14) | copy-done | bytes 3538968
  99.1 11.8 %all-to-all-done.1 = bf16[128,4,8,384]{3,2,1,0:T(8,128)(2,1)S(1)} async-done(((bf16[128,4,8,384]{3,2,1,0:T(8,128)(2,1)}), bf16[128,4,8,384]{3,2,1,0:T(8,128)(2,1)S(1)}, u32[]{:S(2)}, u32[]{:S(2)}) %all-to-all-start.1) | async-done | bytes 3145760 | tf_op jit(solution)/shard_map/all_to_all | solution.py:515
  110.9 0.3 slice_bitcast_fusion
  111.2 0.1 collective-permute-start.2
  111.3 5.1 %collective-permute-start.3 = (bf16[2,16,4,8,384]{4,3,2,1,0:T(8,128)(2,1)S(1)}, bf16[2,16,4,8,384]{4,3,2,1,0:T(8,128)(2,1)S(1)}, u32[]{:S(2)}, u32[]{:S(2)}) collective-permute-start(bf16[2,16,4,8,384]{4,3,2,1,0:T(8,128)(2,1)S(1)} %get-tuple-element.89), channel_id=1, source_target_pairs={{1,0},{2,1},{3,2},{4,3},{5,4},{6,5},{7,6},{8,7},{9,8},{10,9},{11,1... | collective-permute-start | bytes 2359304 | tf_op jit(solution)/shard_map/ppermute | solution.py:501
  116.4 0.1 collective-permute-start.6
  116.5 5.1 %collective-permute-start.7 = (bf16[2,16,4,8,384]{4,3,2,1,0:T(8,128)(2,1)S(1)}, bf16[2,16,4,8,384]{4,3,2,1,0:T(8,128)(2,1)S(1)}, u32[]{:S(2)}, u32[]{:S(2)}) collective-permute-start(bf16[2,16,4,8,384]{4,3,2,1,0:T(8,128)(2,1)S(1)} %get-tuple-element.87), channel_id=1, source_target_pairs={{1,0},{2,1},{3,2},{4,3},{5,4},{6,5},{7,6},{8,7},{9,8},{10,9},{11,1... | collective-permute-start | bytes 2359304 | tf_op jit(solution)/shard_map/ppermute | solution.py:501
  121.5 12.8 %shard_map.165 = (f32[2,16,4,8,384]{4,3,2,1,0:T(8,128)S(1)}, f32[2,16,4,8,384]{4,3,2,1,0:T(8,128)S(1)}, bf16[4,2,2,16,8,384]{5,4,3,2,1,0:T(8,128)(2,1)}, bf16[4,...) custom-call(bf16[2,2,2,16,4,8,384]{6,5,4,3,2,1,0:T(8,128)(2,1)S(1)} %bitcast.25, bf16[1536,2304]{1,0:T(8,128)(2,1)} %copy-done.7, ...), custom_call_target="tpu_custom_call" | custom-call | flops 7247757312 | bytes 14155776 | tf_op jit(solution)/shard_map/pallas_call | solution.py:115
  134.3 2.0 %copy-done.22 = bf16[2,768,1152]{2,1,0:T(8,128)(2,1)S(1)} copy-done((bf16[2,768,1152]{2,1,0:T(8,128)(2,1)S(1)}, bf16[2,768,1152]{2,1,0:T(8,128)(2,1)}, u32[]{:S(2)}) %copy-start.22) | copy-done | bytes 3538968
  136.3 3.3 %shard_map.166 = (bf16[4,2,128,384]{3,2,1,0:T(8,128)(2,1)S(1)}, bf16[4,128,384]{2,1,0:T(8,128)(2,1)S(1)}, bf16[4,128,384]{2,1,0:T(8,128)(2,1)S(1)}) custom-call(s32[2,4]{1,0:T(2,128)S(1)} %add_convert_fusion.edge_ref, bf16[2,16,4,8,384]{4,3,2,1,0:T(8,128)(2,1)S(1)} %collective-permute-done.2.above_ref, ...), custom_call_target="tpu_custom_call" | custom-call | flops 1811939328 | bytes 3538944 | tf_op jit(solution)/shard_map/pallas_call | solution.py:115
  139.7 0.1 collective-permute-start.4
  139.7 5.1 %collective-permute-start.5 = (bf16[4,128,384]{2,1,0:T(8,128)(2,1)S(1)}, bf16[4,128,384]{2,1,0:T(8,128)(2,1)S(1)}, u32[]{:S(2)}, u32[]{:S(2)}) collective-permute-start(bf16[4,128,384]{2,1,0:T(8,128)(2,1)S(1)} %get-tuple-element.73), channel_id=1, source_target_pairs={{1,0},{2,1},{3,2},{4,3},{5,4},{6,5},{7,6},{8,7},{9,8},{10,9},{11,1... | collective-permute-start | bytes 1179656 | tf_op jit(solution)/shard_map/ppermute | solution.py:501
  144.8 0.0 copy-start.3
  144.9 5.2 %shard_map.167 = (f32[2,16,4,8,384]{4,3,2,1,0:T(8,128)S(1)}, bf16[4,2,2,16,8,384]{5,4,3,2,1,0:T(8,128)(2,1)}) custom-call(s32[2,4]{1,0:T(2,128)S(1)} %add_convert_fusion.edge_ref, bf16[2,16,4,8,384]{4,3,2,1,0:T(8,128)(2,1)S(1)} %collective-permute-done.6.above_ref, ...), custom_call_target="tpu_custom_call", output_to_operand_aliasing={{1}: (8, {})} | custom-call | flops 3623878656 | bytes 7077888 | tf_op jit(solution)/shard_map/pallas_call | solution.py:115
  150.1 0.2 collective-permute-done.4.above_ref
  150.3 2.9 %shard_map.168 = bf16[4,2,128,384]{3,2,1,0:T(8,128)(2,1)} custom-call(s32[2,4]{1,0:T(2,128)S(1)} %add_convert_fusion.edge_ref, bf16[4,128,384]{2,1,0:T(8,128)(2,1)S(1)} %collective-permute-done.4.above_ref, bf16[4,128,384]{2,1,0:T(8,128)(2,1)S(1)} %collective-permute-done.5.below_ref, bf16[2,384,1152]{2,1,0:T(8,128)(2,1)S(1)} %copy-done.5, ...), custom_call_target="tpu_custom_call" | custom-call | flops 905969664 | bytes 1769472 | tf_op jit(solution)/shard_map/pallas_call | solution.py:115
  (67 shorter events, 0.2 us)
Async XLA Ops:
  3.8 11.7 %copy-start.25 = (f32[384]{0:T(512)S(1)}, f32[384]{0:T(512)}, u32[]{:S(2)}) copy-start(f32[384]{0:T(512)} %param.17) | copy-start | bytes 4612
  3.8 11.7 %copy-start.2 = (bf16[4,2,128,384]{3,2,1,0:T(8,128)(2,1)S(1)}, bf16[4,2,128,384]{3,2,1,0:T(8,128)(2,1)}, u32[]{:S(2)}) copy-start(bf16[4,2,128,384]{3,2,1,0:T(8,128)(2,1)} %f_ref.3) | copy-start | bytes 2359300
  3.8 55.1 %all-to-all-start = ((bf16[128,4,8,384]{3,2,1,0:T(8,128)(2,1)}), bf16[128,4,8,384]{3,2,1,0:T(8,128)(2,1)}, u32[]{:S(2)}, u32[]{:S(2)}) async-start(bf16[128,4,8,384]{3,2,1,0:T(8,128)(2,1)} %bitcast.28), calls=%async_computation | async-start | bytes 6291456 | tf_op jit(solution)/shard_map/all_to_all | solution.py:504
  16.2 0.9 copy-start.17
  17.0 41.9 %collective-permute-start = (bf16[4,128,384]{2,1,0:T(8,128)(2,1)S(1)}, bf16[4,128,384]{2,1,0:T(8,128)(2,1)S(1)}, u32[]{:S(2)}, u32[]{:S(2)}) collective-permute-start(bf16[4,128,384]{2,1,0:T(8,128)(2,1)S(1)} %get-tuple-element.44), channel_id=1, source_target_pairs={{0,1},{1,2},{2,3},{3,4},{4,5},{5,6},{6,7},{7,8},{8,9},{9,10},{10,1... | collective-permute-start | bytes 1179656 | tf_op jit(solution)/shard_map/ppermute | solution.py:498
  17.0 41.9 %collective-permute-start.1 = (bf16[4,128,384]{2,1,0:T(8,128)(2,1)S(1)}, bf16[4,128,384]{2,1,0:T(8,128)(2,1)S(1)}, u32[]{:S(2)}, u32[]{:S(2)}) collective-permute-start(bf16[4,128,384]{2,1,0:T(8,128)(2,1)S(1)} %get-tuple-element.45), channel_id=1, source_target_pairs={{1,0},{2,1},{3,2},{4,3},{5,4},{6,5},{7,6},{8,7},{9,8},{10,9},{11,1... | collective-permute-start | bytes 1179656 | tf_op jit(solution)/shard_map/ppermute | solution.py:501
  22.1 3.3 %copy-start.1 = (bf16[3,3,3,384,384]{4,3,2,1,0:T(8,128)(2,1)S(1)}, bf16[3,3,3,384,384]{4,3,2,1,0:T(8,128)(2,1)}, u32[]{:S(2)}) copy-start(bf16[3,3,3,384,384]{4,3,2,1,0:T(8,128)(2,1)} %w_ref.2) | copy-start | bytes 23887876
  25.4 3.5 %copy-start.29 = (s32[16]{0:T(128)S(1)}, s32[16]{0:T(128)}, u32[]{:S(2)}) copy-start(s32[16]{0:T(128)} %param.27) | copy-start | bytes 196
  25.4 3.5 %copy-start.30 = (s32[16]{0:T(128)S(1)}, s32[16]{0:T(128)}, u32[]{:S(2)}) copy-start(s32[16]{0:T(128)} %param.24) | copy-start | bytes 196
  25.4 3.5 %copy-start.31 = (s32[16]{0:T(128)S(1)}, s32[16]{0:T(128)}, u32[]{:S(2)}) copy-start(s32[16]{0:T(128)} %param.25) | copy-start | bytes 196
  25.4 3.5 %copy-start.32 = (s32[16]{0:T(128)S(1)}, s32[16]{0:T(128)}, u32[]{:S(2)}) copy-start(s32[16]{0:T(128)} %param.23) | copy-start | bytes 196
  25.4 3.5 %copy-start.33 = (s32[16]{0:T(128)S(1)}, s32[16]{0:T(128)}, u32[]{:S(2)}) copy-start(s32[16]{0:T(128)} %param.26) | copy-start | bytes 196
  25.9 1.8 %copy-start.12 = (bf16[768,2304]{1,0:T(8,128)(2,1)}, bf16[768,2304]{1,0:T(8,128)(2,1)S(1)}, u32[]{:S(2)}) copy-start(bf16[768,2304]{1,0:T(8,128)(2,1)S(1)} %get-tuple-element.54.wo_ref) | copy-start | bytes 10616836
  27.7 1.2 copy-start.15
  58.9 4.0 %copy-start.20 = (bf16[4,128,384]{2,1,0:T(8,128)(2,1)}, bf16[4,128,384]{2,1,0:T(8,128)(2,1)S(1)}, u32[]{:S(2)}) copy-start(bf16[4,128,384]{2,1,0:T(8,128)(2,1)S(1)} %collective-permute-done.1.below_ref) | copy-start | bytes 1179652
  63.0 47.9 %all-to-all-start.1 = ((bf16[128,4,8,384]{3,2,1,0:T(8,128)(2,1)}), bf16[128,4,8,384]{3,2,1,0:T(8,128)(2,1)S(1)}, u32[]{:S(2)}, u32[]{:S(2)}) async-start(bf16[128,4,8,384]{3,2,1,0:T(8,128)(2,1)} %bitcast.29), calls=%async_computation.1 | async-start | bytes 6291456 | tf_op jit(solution)/shard_map/all_to_all | solution.py:515
  69.2 2.0 %copy-start.13 = (bf16[768,2304]{1,0:T(8,128)(2,1)S(1)}, bf16[768,2304]{1,0:T(8,128)(2,1)}, u32[]{:S(2)}) copy-start(bf16[768,2304]{1,0:T(8,128)(2,1)} %copy-done.12) | copy-start | bytes 10616836
  71.2 1.5 copy-start.16
  72.6 1.1 copy-start.18
  73.8 1.0 copy-start.21
  74.8 18.0 %slice-start = ((s8[7962624]{0:T(1024)(128)(4,1)}), s8[4194304]{0:T(1024)(128)(4,1)S(1)}, s32[]{:S(2)}) async-start(s8[7962624]{0:T(1024)(128)(4,1)} %bitcast.22), calls=%async_computation.2 | async-start | bytes 8388608
  78.7 1.1 copy-start.23
  79.8 3.3 %copy-start = (bf16[3,3,3,384,384]{4,3,2,1,0:T(8,128)(2,1)S(1)}, bf16[3,3,3,384,384]{4,3,2,1,0:T(8,128)(2,1)}, u32[]{:S(2)}) copy-start(bf16[3,3,3,384,384]{4,3,2,1,0:T(8,128)(2,1)} %w_ref.4) | copy-start | bytes 23887876
  83.1 9.7 %slice-start.1 = ((s8[7962624]{0:T(1024)(128)(4,1)}), s8[3768320]{0:T(1024)(128)(4,1)S(1)}, s32[]{:S(2)}) async-start(s8[7962624]{0:T(1024)(128)(4,1)} %bitcast.22), calls=%async_computation.3 | async-start | bytes 7536640
  84.6 2.8 %copy-start.6 = (bf16[1536,2304]{1,0:T(8,128)(2,1)}, bf16[1536,2304]{1,0:T(8,128)(2,1)S(1)}, u32[]{:S(2)}) copy-start(bf16[1536,2304]{1,0:T(8,128)(2,1)S(1)} %get-tuple-element.67.w1_ref) | copy-start | bytes 21233668
  87.5 1.8 %copy-start.8 = (bf16[2,768,1152]{2,1,0:T(8,128)(2,1)}, bf16[2,768,1152]{2,1,0:T(8,128)(2,1)S(1)}, u32[]{:S(2)}) copy-start(bf16[2,768,1152]{2,1,0:T(8,128)(2,1)S(1)} %get-tuple-element.76.w_ref) | copy-start | bytes 10616836
  89.7 1.3 copy-start.4
  91.0 1.8 %copy-start.10 = (bf16[768,2304]{1,0:T(8,128)(2,1)}, bf16[768,2304]{1,0:T(8,128)(2,1)S(1)}, u32[]{:S(2)}) copy-start(bf16[768,2304]{1,0:T(8,128)(2,1)S(1)} %get-tuple-element.77.wa_ref) | copy-start | bytes 10616836
  94.4 2.9 %copy-start.7 = (bf16[1536,2304]{1,0:T(8,128)(2,1)}, bf16[1536,2304]{1,0:T(8,128)(2,1)S(1)}, u32[]{:S(2)}) copy-start(bf16[1536,2304]{1,0:T(8,128)(2,1)S(1)} %get-tuple-element.66.w0_ref) | copy-start | bytes 21233668
  97.3 1.8 %copy-start.14 = (bf16[2,768,1152]{2,1,0:T(8,128)(2,1)}, bf16[2,768,1152]{2,1,0:T(8,128)(2,1)S(1)}, u32[]{:S(2)}) copy-start(bf16[2,768,1152]{2,1,0:T(8,128)(2,1)S(1)} %get-tuple-element.69.sides_ref) | copy-start | bytes 10616836
  110.9 5.5 %copy-start.26 = (f32[384]{0:T(512)S(1)}, f32[384]{0:T(512)}, u32[]{:S(2)}) copy-start(f32[384]{0:T(512)} %param.21) | copy-start | bytes 4612
  110.9 5.5 %copy-start.27 = (f32[384]{0:T(512)S(1)}, f32[384]{0:T(512)}, u32[]{:S(2)}) copy-start(f32[384]{0:T(512)} %param.18) | copy-start | bytes 4612
  110.9 10.6 %copy-start.19 = (bf16[4,2,128,384]{3,2,1,0:T(8,128)(2,1)S(1)}, bf16[4,2,128,384]{3,2,1,0:T(8,128)(2,1)}, u32[]{:S(2)}) copy-start(bf16[4,2,128,384]{3,2,1,0:T(8,128)(2,1)} %copy-done.17) | copy-start | bytes 2359300
  110.9 10.6 %copy-start.24 = (f32[2,16,4,8,384]{4,3,2,1,0:T(8,128)S(1)}, f32[2,16,4,8,384]{4,3,2,1,0:T(8,128)}, u32[]{:S(2)}) copy-start(f32[2,16,4,8,384]{4,3,2,1,0:T(8,128)} %copy-done.23) | copy-start | bytes 4718596
  111.2 23.1 %collective-permute-start.2 = (bf16[2,16,4,8,384]{4,3,2,1,0:T(8,128)(2,1)S(1)}, bf16[2,16,4,8,384]{4,3,2,1,0:T(8,128)(2,1)S(1)}, u32[]{:S(2)}, u32[]{:S(2)}) collective-permute-start(bf16[2,16,4,8,384]{4,3,2,1,0:T(8,128)(2,1)S(1)} %get-tuple-element.90), channel_id=1, source_target_pairs={{0,1},{1,2},{2,3},{3,4},{4,5},{5,6},{6,7},{7,8},{8,9},{9,10},{10,1... | collective-permute-start | bytes 2359304 | tf_op jit(solution)/shard_map/ppermute | solution.py:498
  111.3 23.0 %collective-permute-start.3 = (bf16[2,16,4,8,384]{4,3,2,1,0:T(8,128)(2,1)S(1)}, bf16[2,16,4,8,384]{4,3,2,1,0:T(8,128)(2,1)S(1)}, u32[]{:S(2)}, u32[]{:S(2)}) collective-permute-start(bf16[2,16,4,8,384]{4,3,2,1,0:T(8,128)(2,1)S(1)} %get-tuple-element.89), channel_id=1, source_target_pairs={{1,0},{2,1},{3,2},{4,3},{5,4},{6,5},{7,6},{8,7},{9,8},{10,9},{11,1... | collective-permute-start | bytes 2359304 | tf_op jit(solution)/shard_map/ppermute | solution.py:501
  116.4 28.4 %collective-permute-start.6 = (bf16[2,16,4,8,384]{4,3,2,1,0:T(8,128)(2,1)S(1)}, bf16[2,16,4,8,384]{4,3,2,1,0:T(8,128)(2,1)S(1)}, u32[]{:S(2)}, u32[]{:S(2)}) collective-permute-start(bf16[2,16,4,8,384]{4,3,2,1,0:T(8,128)(2,1)S(1)} %get-tuple-element.88), channel_id=1, source_target_pairs={{0,1},{1,2},{2,3},{3,4},{4,5},{5,6},{6,7},{7,8},{8,9},{9,10},{10,1... | collective-permute-start | bytes 2359304 | tf_op jit(solution)/shard_map/ppermute | solution.py:498
  116.5 28.3 %collective-permute-start.7 = (bf16[2,16,4,8,384]{4,3,2,1,0:T(8,128)(2,1)S(1)}, bf16[2,16,4,8,384]{4,3,2,1,0:T(8,128)(2,1)S(1)}, u32[]{:S(2)}, u32[]{:S(2)}) collective-permute-start(bf16[2,16,4,8,384]{4,3,2,1,0:T(8,128)(2,1)S(1)} %get-tuple-element.87), channel_id=1, source_target_pairs={{1,0},{2,1},{3,2},{4,3},{5,4},{6,5},{7,6},{8,7},{9,8},{10,9},{11,1... | collective-permute-start | bytes 2359304 | tf_op jit(solution)/shard_map/ppermute | solution.py:501
  121.5 23.3 %copy-start.11 = (bf16[768,2304]{1,0:T(8,128)(2,1)S(1)}, bf16[768,2304]{1,0:T(8,128)(2,1)}, u32[]{:S(2)}) copy-start(bf16[768,2304]{1,0:T(8,128)(2,1)} %copy-done.10) | copy-start | bytes 10616836
  134.3 2.0 %copy-start.22 = (bf16[2,768,1152]{2,1,0:T(8,128)(2,1)S(1)}, bf16[2,768,1152]{2,1,0:T(8,128)(2,1)}, u32[]{:S(2)}) copy-start(bf16[2,768,1152]{2,1,0:T(8,128)(2,1)} %get-tuple-element.70.w_ref) | copy-start | bytes 10616836
  136.3 8.5 %copy-start.28 = (f32[384]{0:T(512)S(1)}, f32[384]{0:T(512)}, u32[]{:S(2)}) copy-start(f32[384]{0:T(512)} %param.22) | copy-start | bytes 4612
  136.3 8.5 %copy-start.9 = (bf16[2,768,1152]{2,1,0:T(8,128)(2,1)S(1)}, bf16[2,768,1152]{2,1,0:T(8,128)(2,1)}, u32[]{:S(2)}) copy-start(bf16[2,768,1152]{2,1,0:T(8,128)(2,1)} %copy-done.8) | copy-start | bytes 10616836
  139.7 10.6 %collective-permute-start.4 = (bf16[4,128,384]{2,1,0:T(8,128)(2,1)S(1)}, bf16[4,128,384]{2,1,0:T(8,128)(2,1)S(1)}, u32[]{:S(2)}, u32[]{:S(2)}) collective-permute-start(bf16[4,128,384]{2,1,0:T(8,128)(2,1)S(1)} %get-tuple-element.72), channel_id=1, source_target_pairs={{0,1},{1,2},{2,3},{3,4},{4,5},{5,6},{6,7},{7,8},{8,9},{9,10},{10,1... | collective-permute-start | bytes 1179656 | tf_op jit(solution)/shard_map/ppermute | solution.py:498
  139.7 10.5 %collective-permute-start.5 = (bf16[4,128,384]{2,1,0:T(8,128)(2,1)S(1)}, bf16[4,128,384]{2,1,0:T(8,128)(2,1)S(1)}, u32[]{:S(2)}, u32[]{:S(2)}) collective-permute-start(bf16[4,128,384]{2,1,0:T(8,128)(2,1)S(1)} %get-tuple-element.73), channel_id=1, source_target_pairs={{1,0},{2,1},{3,2},{4,3},{5,4},{6,5},{7,6},{8,7},{9,8},{10,9},{11,1... | collective-permute-start | bytes 1179656 | tf_op jit(solution)/shard_map/ppermute | solution.py:501
  144.8 5.4 %copy-start.3 = (bf16[4,2,128,384]{3,2,1,0:T(8,128)(2,1)S(1)}, bf16[4,2,128,384]{3,2,1,0:T(8,128)(2,1)}, u32[]{:S(2)}) copy-start(bf16[4,2,128,384]{3,2,1,0:T(8,128)(2,1)} %f_ref.3) | copy-start | bytes 2359300
  144.8 5.4 %copy-start.5 = (bf16[2,384,1152]{2,1,0:T(8,128)(2,1)S(1)}, bf16[2,384,1152]{2,1,0:T(8,128)(2,1)}, u32[]{:S(2)}) copy-start(bf16[2,384,1152]{2,1,0:T(8,128)(2,1)} %copy-done.4) | copy-start | bytes 5308420

commit v9 on v8

--- a/solution.py
+++ b/solution.py
@@ -177,27 +177,38 @@
     return u / (1.0 + jnp.exp(-u))
 
 
-def first_activation(frame, gain):
+def first_activation(frame, gain, edges):
     n_slots, n_rows, n_cols, ch = frame.shape
 
-    def body(f_ref, g_ref, o_ref, top_ref, bottom_ref):
+    def body(edge_ref, f_ref, g_ref, o_ref, near_ref, far_ref):
+        odd = edge_ref[2, 0]
         for s in range(n_slots):
             for r in range(n_rows):
                 value = activated(f_ref[s, r].astype(jnp.float32), g_ref[...]).astype(jnp.bfloat16)
                 o_ref[s, r] = value
-                if r == 0:
-                    top_ref[s] = value
-                if r == n_rows - 1:
-                    bottom_ref[s] = value
+
+                @pl.when(odd != r)
+                def _(s=s, value=value):
+                    near_ref[s] = value
+
+                @pl.when(odd == r)
+                def _(s=s, value=value):
+                    far_ref[s] = value
 
     row = jax.ShapeDtypeStruct((n_slots, n_cols, ch), jnp.bfloat16)
     return call(
         body,
         [jax.ShapeDtypeStruct(frame.shape, jnp.bfloat16), row, row],
         (frame, gain),
+        scalars=(edges,),
         flops=10 * frame.size,
         moved=6 * frame.size,
     )
+
+
+def beside(edge_ref, near_ref, far_ref):
+    odd = edge_ref[2, 0]
+    return ((near_ref, 1 - odd), (far_ref, odd))
 
 
 def folded(acc, ch, cols_first):
@@ -247,7 +258,7 @@
 
 def add_sides(edge_ref, sides, w_ref, lhs, o_ref):
     n_slots, n_cols, ch = sides[0].shape
-    for y, side in enumerate(sides):
+    for side, y in beside(edge_ref, *sides):
         for s in range(n_slots):
             lhs[s * n_cols : (s + 1) * n_cols] = masked(edge_ref, y, s, side[s])
         add_into(o_ref, y, folded(dot(lhs[...], w_ref[y]), ch, False), False, o_ref)
@@ -264,18 +275,18 @@
         add_into(o_ref, y, folded(both[:, y * wide : (y + 1) * wide], ch, False), False, base)
 
 
-def current_part(act, above, below, w_own, w_sides, edges):
+def current_part(act, near, far, w_own, w_sides, edges):
     n_slots, n_rows, n_cols, ch = act.shape
     half = n_slots * n_cols
 
-    def body(edge_ref, act_ref, above_ref, below_ref, wo_ref, ws_ref, o_ref, lhs, side):
+    def body(edge_ref, act_ref, near_ref, far_ref, wo_ref, ws_ref, o_ref, lhs, side):
         add_own(act_ref, wo_ref, lhs, o_ref, None)
-        add_sides(edge_ref, (above_ref, below_ref), ws_ref, side, o_ref)
+        add_sides(edge_ref, (near_ref, far_ref), ws_ref, side, o_ref)
 
     return call(
         body,
         [sums_shape(n_cols // CB, n_slots, n_rows, ch)],
-        (act, above, below, w_own, w_sides),
+        (act, near, far, w_own, w_sides),
         scalars=(edges,),
         scratch=[
             pltpu.VMEM((half, n_rows * ch), jnp.bfloat16),
@@ -309,9 +320,7 @@
                             got_ref.at[r, k, n_frames - 1, :, s], dst.at[s, 0, r], keep_sems.at[n]
                         )
                     )
-        for c in loads:
-            c.start()
-        near.start()
+        loads[0].start()
 
         def fill(k, r, f):
             lo = r * deep + f * ch
@@ -327,16 +336,19 @@
             for f in range(n_frames):
                 fill(0, r, f)
         loads[0].wait()
+        loads[1].start()
         acc[...] = dot(lhs[:, 0:deep], w0[0])
         loads[1].wait()
+        loads[2].start()
         acc[...] += dot(lhs[:, deep : 2 * deep], w0[1])
         give(o0_ref, z_ref)
         for r in range(n_rows):
             for f in range(n_frames):
                 fill(1, r, f)
+        loads[2].wait()
+        near.start()
         for c in keeps:
             c.start()
-        loads[2].wait()
         acc[...] = dot(lhs[...], w1[...])
         give(o1_ref, None)
         for c in keeps:
@@ -361,7 +373,7 @@
         moved=4 * whole.size,
         far=(1, 2, 5),
         far_out=(2, 3),
-        limit=45 << 20,
+        limit=40 << 20,
     )
 
 
@@ -375,26 +387,23 @@
     return folded(dot(lhs[...].reshape(half, n_frames * ch), w), ch, True)
 
 
-def second_activation(above, below, w_sides, sums, bias, gain, edges):
-    n_frames, blocks, n_slots, _, ch = above.shape
+def second_activation(near, far, w_sides, sums, bias, gain, edges):
+    n_frames, blocks, n_slots, _, ch = near.shape
     n_rows, n_cols, deep = sums.shape[0], blocks * CB, n_frames * ch
 
-    def body(edge_ref, above_ref, below_ref, w_ref, z_ref, b_ref, g_ref, o_ref, top_ref, bottom_ref, lhs):
-        for y, side in enumerate((above_ref, below_ref)):
+    def body(edge_ref, near_ref, far_ref, w_ref, z_ref, b_ref, g_ref, o_ref, near_out, far_out, lhs):
+        for (side, y), out in zip(beside(edge_ref, near_ref, far_ref), (near_out, far_out)):
             total = side_sums(edge_ref, y, side, w_ref[y], lhs) + z_ref[y] + b_ref[...]
             for s in range(n_slots):
                 value = activated(total[:, s].reshape(n_cols, ch), g_ref[...]).astype(jnp.bfloat16)
                 o_ref[s, y] = value
-                if y == 0:
-                    top_ref[s] = value
-                else:
-                    bottom_ref[s] = value
+                out[s] = value
 
     row = jax.ShapeDtypeStruct((n_slots, n_cols, ch), jnp.bfloat16)
     return call(
         body,
         [jax.ShapeDtypeStruct((n_slots, n_rows, n_cols, ch), jnp.bfloat16), row, row],
-        (above, below, w_sides, sums, bias, gain),
+        (near, far, w_sides, sums, bias, gain),
         scalars=(edges,),
         scratch=[pltpu.VMEM((blocks, n_slots, CB, deep), jnp.bfloat16)],
         flops=2 * n_slots * n_cols * w_sides.size,
@@ -402,22 +411,22 @@
     )
 
 
-def before_sides(above, below, act, w_sides, w_act, sums, kept, edges):
-    n_frames, blocks, n_slots, _, ch = above.shape
+def before_sides(near, far, act, w_sides, w_act, sums, kept, edges):
+    n_frames, blocks, n_slots, _, ch = near.shape
     n_rows, n_cols, deep = sums.shape[0], blocks * CB, n_frames * ch
 
-    def body(edge_ref, above_ref, below_ref, act_ref, tiles_ref, w_ref, wa_ref, z_ref, kept_ref, o_ref, next_ref, lhs, lhs2, sem):
+    def body(edge_ref, near_ref, far_ref, act_ref, tiles_ref, w_ref, wa_ref, z_ref, kept_ref, o_ref, next_ref, lhs, lhs2, sem):
         copy = pltpu.make_async_copy(tiles_ref, next_ref.at[:, 1], sem)
         copy.start()
         add_own(act_ref, wa_ref, lhs2, o_ref, z_ref)
-        for y, side in enumerate((above_ref, below_ref)):
+        for side, y in beside(edge_ref, near_ref, far_ref):
             o_ref[y] += side_sums(edge_ref, y, side, w_ref[y], lhs)
         copy.wait()
 
     return call(
         body,
         [jax.ShapeDtypeStruct(sums.shape, jnp.float32), jax.ShapeDtypeStruct(kept.shape, kept.dtype)],
-        (above, below, act, act.reshape(n_slots, n_rows, blocks, CB, ch), w_sides, w_act, sums, kept),
+        (near, far, act, act.reshape(n_slots, n_rows, blocks, CB, ch), w_sides, w_act, sums, kept),
         scalars=(edges,),
         scratch=[
             pltpu.VMEM((blocks, n_slots, CB, deep), jnp.bfloat16),
@@ -432,11 +441,11 @@
     )
 
 
-def last_part(above, below, w_sides, sums, bias, frame, edges):
+def last_part(near, far, w_sides, sums, bias, frame, edges):
     n_slots, n_rows, n_cols, ch = frame.shape
 
-    def body(edge_ref, above_ref, below_ref, w_ref, z_ref, b_ref, f_ref, o_ref, lhs):
-        for y, side in enumerate((above_ref, below_ref)):
+    def body(edge_ref, near_ref, far_ref, w_ref, z_ref, b_ref, f_ref, o_ref, lhs):
+        for side, y in beside(edge_ref, near_ref, far_ref):
             for s in range(n_slots):
                 lhs[s * n_cols : (s + 1) * n_cols] = masked(edge_ref, y, s, side[s])
             total = folded(dot(lhs[...], w_ref[y]), ch, False)
@@ -447,7 +456,7 @@
     return call(
         body,
         [jax.ShapeDtypeStruct(frame.shape, jnp.bfloat16)],
-        (above, below, w_sides, sums, bias, frame),
+        (near, far, w_sides, sums, bias, frame),
         scalars=(edges,),
         scratch=[pltpu.VMEM((n_slots * n_cols, ch), jnp.bfloat16)],
         flops=2 * n_slots * n_cols * w_sides.size,
@@ -490,24 +499,27 @@
     start = my_group * n_slots
     my_number = lax.dynamic_slice_in_dim((my_tile - shift_after) % n_tiles, start, n_slots)
 
-    edges = jnp.stack([my_number != 0, my_number != n_tiles - 1]).astype(jnp.int32)
-    down = [(i, (i + 1) % n_tiles) for i in range(n_tiles)]
-    up = [((i + 1) % n_tiles, i) for i in range(n_tiles)]
-
-    def from_above(row):
-        return lax.ppermute(row, "tile", down)
-
-    def from_below(row):
-        return lax.ppermute(row, "tile", up)
+    odd = my_tile % 2
+    edges = jnp.stack(
+        [my_number != 0, my_number != n_tiles - 1, jnp.broadcast_to(odd == 1, my_number.shape)]
+    ).astype(jnp.int32)
+
+    def swap_near(row):
+        return lax.ppermute(row, "tile", [(i, i ^ 1) for i in range(n_tiles)])
+
+    def swap_far(row):
+        return lax.ppermute(
+            row, "tile", [(i, (i + 2 * (i % 2) - 1) % n_tiles) for i in range(n_tiles)]
+        )
 
     sent = pack(cache_first, cache_second).reshape(n_groups * n_tiles, n_slots, CB, ch)
     held = lax.all_to_all(sent, BOTH, 0, 0, tiled=True)
 
     act_own_1, act_sides_1 = spread(conv_first, False)
-    act_first, top, bottom = first_activation(frame_in, gain_first[None])
-    act_above, act_below = from_above(bottom), from_below(top)
-    held, act_first, act_above, act_below, act_own_1, act_sides_1 = lax.optimization_barrier(
-        (held, act_first, act_above, act_below, act_own_1, act_sides_1)
+    act_first, near, far = first_activation(frame_in, gain_first[None], edges)
+    act_near, act_far = swap_near(near), swap_far(far)
+    held, act_first, act_near, act_far, act_own_1, act_sides_1 = lax.optimization_barrier(
+        (held, act_first, act_near, act_far, act_own_1, act_sides_1)
     )
 
     moved = permute(held.reshape(n_groups, n_tiles, n_slots, CB, ch), source, rotation, keep)
@@ -515,7 +527,7 @@
     got = lax.all_to_all(
         moved.reshape(n_groups * n_tiles, n_slots, CB, ch), BOTH, 0, 0, tiled=True
     )
-    sums_1 = current_part(act_later, act_above, act_below, act_own_1, act_sides_1, edges)
+    sums_1 = current_part(act_later, act_near, act_far, act_own_1, act_sides_1, edges)
     sums_1, conv_first, conv_second = lax.optimization_barrier((sums_1, conv_first, conv_second))
     act_own_2, act_sides_2 = spread(conv_second, False)
     own_1, sides_1 = spread(conv_first, True)
@@ -525,23 +537,24 @@
     )
     got = got.reshape(n_rows, 2, 2, blocks, n_slots, CB, ch)
 
-    above_1 = from_above(got[n_rows - 1, 0])
-    below_1 = from_below(got[0, 0])
-    above_2 = from_above(got[n_rows - 1, 1])
-    below_2 = from_below(got[0, 1])
+    def picked(cache, row):
+        return lax.dynamic_index_in_dim(got[:, cache], row, 0, keepdims=False)
+
+    near_1, far_1 = swap_near(picked(0, 1 - odd)), swap_far(picked(0, odd))
+    near_2, far_2 = swap_near(picked(1, 1 - odd)), swap_far(picked(1, odd))
     act_tiles = act_first.reshape(n_slots, n_rows, blocks, CB, ch)
     sums_1, sums_2, next_first, kept, sides_1 = own_part(
         got, (own_1, own_2), sums_1, act_tiles, sides_1
     )
-    act_second, top, bottom = second_activation(
-        above_1, below_1, sides_1, sums_1, bias_first[None], gain_second[None], edges
-    )
-    side_above, side_below = from_above(bottom), from_below(top)
+    act_second, near, far = second_activation(
+        near_1, far_1, sides_1, sums_1, bias_first[None], gain_second[None], edges
+    )
+    act_near, act_far = swap_near(near), swap_far(far)
     sums_2, next_second = before_sides(
-        above_2, below_2, act_second, sides_2, act_own_2, sums_2, kept, edges
+        near_2, far_2, act_second, sides_2, act_own_2, sums_2, kept, edges
     )
     mixed_frame = last_part(
-        side_above, side_below, act_sides_2, sums_2, bias_second[None], frame_in, edges
+        act_near, act_far, act_sides_2, sums_2, bias_second[None], frame_in, edges
     )
     whole = (n_slots, 2, n_rows, n_cols, ch)
     return (mixed_frame, next_first.reshape(whole), next_second.reshape(whole))

time: 154 us -> 148 us (0.961)
  starting transfers between devices: 38.2 us -> 29.7 us
  waiting for transfers between devices: 41.8 us -> 44.6 us
  local copies, waits for them, and re-layouts: 31.9 us -> 29.3 us
  Pallas kernels: 40.1 us -> 41.8 us
    ppermute x8, starting transfers between devices: 20.4 us -> 12 us  [the longest x4 11.8 us: swap_far(): lax.ppermute(row, 'tile', [(i, (i + 2 * (i % 2) - 1) % n_tiles) for i in...]
    unnamed x72 -> x70, local copies, waits for them, and re-layouts: 31.6 us -> 28.4 us
    ppermute x8, waiting for transfers between devices: 30 us -> 32.9 us  [the longest x4 32.9 us: swap_far(): lax.ppermute(row, 'tile', [(i, (i + 2 * (i % 2) - 1) % n_tiles) for i in...]
  transfers between devices with their start and end apart: 10 -> 10, of which waited for: 3 -> 4; matrix products, arithmetic and copies ran while one was open for 0% -> 0% of each run, Pallas kernels for 20% -> 21%
where the time goes in v9:
time: 148 us; the launch traced here: 147 us
  waiting for transfers between devices  44.6 us (30%)
  Pallas kernels  41.8 us (28%)
  starting transfers between devices  29.7 us (20%)
  local copies, waits for them, and re-layouts  29.3 us (20%)
    ppermute x4, waiting for transfers between devices, swap_far(): lax.ppermute(row, 'tile', [(i, (i + 2 * (i % 2) - 1) % n_tiles) for i in...  32.9 us
    pallas_call x6, Pallas kernels, call(): pl.pallas_call(body, in_specs=in_specs, out_specs=out_specs, out_shape=li...  30.3 us
    unnamed x70, local copies, waits for them, and re-layouts  28.4 us
    ppermute x4, starting transfers between devices, swap_far(): lax.ppermute(row, 'tile', [(i, (i + 2 * (i % 2) - 1) % n_tiles) for i in...  11.8 us
    all_to_all x1, waiting for transfers between devices, local(): lax.all_to_all(moved.reshape(n_groups * n_tiles, n_slots, CB, ch), BOTH,...  11.7 us
    all_to_all x1, starting transfers between devices, local(): held = lax.all_to_all(sent, BOTH, 0, 0, tiled=True)  11.6 us
    all_to_all x1, starting transfers between devices, local(): lax.all_to_all(moved.reshape(n_groups * n_tiles, n_slots, CB, ch), BOTH,...  6.12 us
    pallas_call x1, Pallas kernels, permute(): pl.pallas_call(body, in_specs=[smem, smem, smem, pl.BlockSpec(memory_spac...  4.26 us
  transfers between devices with their start and end apart: 10, of which 4 were waited for; matrix products, arithmetic and copies ran while one was open for 0% of the time, Pallas kernels for 21%

profile of v9, /device:TPU:0, one launch (start us, length us, event | category | flops | bytes accessed | tf_op | source)
XLA Modules:
  0.0 146.9 jit_solution(12303004593064793502)
XLA Ops:
  0.6 3.2 %shard_map.157 = bf16[2,2,2,16,4,8,384]{6,5,4,3,2,1,0:T(8,128)(2,1)} custom-call(bf16[4,2,2,16,8,384]{5,4,3,2,1,0:T(8,128)(2,1)} %bitcast.31, bf16[4,2,2,16,8,384]{5,4,3,2,1,0:T(8,128)(2,1)} %bitcast.32), custom_call_target="tpu_custom_call" | custom-call | tf_op jit(solution)/shard_map/pallas_call | solution.py:47
  3.8 0.0 copy-start.24
  3.9 11.6 %all-to-all-start = ((bf16[128,4,8,384]{3,2,1,0:T(8,128)(2,1)}), bf16[128,4,8,384]{3,2,1,0:T(8,128)(2,1)}, u32[]{:S(2)}, u32[]{:S(2)}) async-start(bf16[128,4,8,384]{3,2,1,0:T(8,128)(2,1)} %bitcast.29), calls=%async_computation | async-start | bytes 6291456 | tf_op jit(solution)/shard_map/all_to_all | solution.py:516
  15.6 0.1 pad.2.clone
  15.7 0.1 select_reduce_fusion
  15.8 0.1 compare_bitcast_fusion.1
  15.9 0.1 add_convert_fusion.edge_ref
  16.0 2.8 %shard_map.158 = (bf16[4,2,128,384]{3,2,1,0:T(8,128)(2,1)S(1)}, bf16[4,128,384]{2,1,0:T(8,128)(2,1)}, bf16[4,128,384]{2,1,0:T(8,128)(2,1)}) custom-call(s32[3,4]{1,0:T(4,128)S(1)} %add_convert_fusion.edge_ref, bf16[4,2,128,384]{3,2,1,0:T(8,128)(2,1)S(1)} %copy-done.2, f32[1,384]{1,0:T(1,128)S(1)} %broadcast_in_dim.53.g_ref), custom_call_target="tpu_custom_call" | custom-call | flops 3932160 | bytes 2359296 | tf_op jit(solution)/shard_map/pallas_call | solution.py:115
  18.8 0.9 copy-done.17
  19.6 5.2 %collective-permute-start.1 = (bf16[4,128,384]{2,1,0:T(8,128)(2,1)}, bf16[4,128,384]{2,1,0:T(8,128)(2,1)S(1)}, u32[]{:S(2)}, u32[]{:S(2)}) collective-permute-start(bf16[4,128,384]{2,1,0:T(8,128)(2,1)} %get-tuple-element.45), channel_id=1, source_target_pairs={{0,31},{1,2},{2,1},{3,4},{4,3},{5,6},{6,5},{7,8},{8,7},{9,10},{10,... | collective-permute-start | bytes 1179656 | tf_op jit(solution)/shard_map/ppermute | solution.py:511
  24.8 3.3 %copy-done.1 = bf16[3,3,3,384,384]{4,3,2,1,0:T(8,128)(2,1)S(1)} copy-done((bf16[3,3,3,384,384]{4,3,2,1,0:T(8,128)(2,1)S(1)}, bf16[3,3,3,384,384]{4,3,2,1,0:T(8,128)(2,1)}, u32[]{:S(2)}) %copy-start.1) | copy-done | bytes 7962648
  28.1 0.5 shard_map.159
  28.6 1.8 %copy-done.12 = bf16[768,2304]{1,0:T(8,128)(2,1)} copy-done((bf16[768,2304]{1,0:T(8,128)(2,1)}, bf16[768,2304]{1,0:T(8,128)(2,1)S(1)}, u32[]{:S(2)}) %copy-start.12) | copy-done | bytes 3538968
  30.4 28.6 %collective-permute-done.1.far_ref = bf16[4,128,384]{2,1,0:T(8,128)(2,1)S(1)} collective-permute-done((bf16[4,128,384]{2,1,0:T(8,128)(2,1)}, bf16[4,128,384]{2,1,0:T(8,128)(2,1)S(1)}, u32[]{:S(2)}, u32[]{:S(2)}) %collective-permute-start.1) | collective-permute-done | bytes 393248 | tf_op jit(solution)/shard_map/ppermute | solution.py:511
  59.0 4.3 %shard_map.160 = bf16[4,32,4,8,384]{4,3,2,1,0:T(8,128)(2,1)} custom-call(s32[16]{0:T(128)S(1)} %get-tuple-element.85.source_ref, s32[16]{0:T(128)S(1)} %get-tuple-element.93.rotation_ref, s32[16]{0:T(128)S(1)} %compare_convert_fusion.keep_ref, bf16[4,32,4,8,384]{4,3,2,1,0:T(8,128)(2,1)} %bitcast.5.i_ref), custom_call_target="tpu_custom_call" | custom-call | tf_op jit(solution)/shard_map/pallas_call | solution.py:92
  63.3 6.1 %all-to-all-start.1 = ((bf16[128,4,8,384]{3,2,1,0:T(8,128)(2,1)}), bf16[128,4,8,384]{3,2,1,0:T(8,128)(2,1)S(1)}, u32[]{:S(2)}, u32[]{:S(2)}) async-start(bf16[128,4,8,384]{3,2,1,0:T(8,128)(2,1)} %bitcast.30), calls=%async_computation.1 | async-start | bytes 6291456 | tf_op jit(solution)/shard_map/all_to_all | solution.py:527
  69.5 2.0 %copy-done.13 = bf16[768,2304]{1,0:T(8,128)(2,1)S(1)} copy-done((bf16[768,2304]{1,0:T(8,128)(2,1)S(1)}, bf16[768,2304]{1,0:T(8,128)(2,1)}, u32[]{:S(2)}) %copy-start.13) | copy-done | bytes 3538968
  71.5 1.5 %copy-done.16 = bf16[2,384,1152]{2,1,0:T(8,128)(2,1)S(1)} copy-done((bf16[2,384,1152]{2,1,0:T(8,128)(2,1)S(1)}, bf16[2,384,1152]{2,1,0:T(8,128)(2,1)}, u32[]{:S(2)}) %copy-start.16) | copy-done | bytes 1769496
  73.0 1.1 copy-done.18
  74.1 1.0 copy-done.21
  75.1 4.0 %shard_map.161.z_ref = f32[2,16,4,8,384]{4,3,2,1,0:T(8,128)S(1)} custom-call(s32[3,4]{1,0:T(4,128)S(1)} %add_convert_fusion.edge_ref, bf16[4,2,128,384]{3,2,1,0:T(8,128)(2,1)S(1)} %copy-done.18, bf16[4,128,384]{2,1,0:T(8,128)(2,1)S(1)} %collective-permute-done.near_ref, bf16[4,128,384]{2,1,0:T(8,128)(2,1)S(1)} %copy-done.21, ...), custom_call_target="tpu_custom_call" | custom-call | flops 2717908992 | bytes 6684672 | tf_op jit(solution)/shard_map/pallas_call | solution.py:115
  79.1 1.1 copy-done.22
  80.2 3.3 %copy-done = bf16[3,3,3,384,384]{4,3,2,1,0:T(8,128)(2,1)S(1)} copy-done((bf16[3,3,3,384,384]{4,3,2,1,0:T(8,128)(2,1)S(1)}, bf16[3,3,3,384,384]{4,3,2,1,0:T(8,128)(2,1)}, u32[]{:S(2)}) %copy-start) | copy-done | bytes 7962648
  83.5 1.5 %shard_map.163 = (bf16[1536,2304]{1,0:T(8,128)(2,1)S(1)}, bf16[2,768,1152]{2,1,0:T(8,128)(2,1)S(1)}) custom-call(bf16[3,3,3,384,384]{4,3,2,1,0:T(8,128)(2,1)S(1)} %copy-done), custom_call_target="tpu_custom_call" | custom-call | bytes 15925248 | tf_op jit(solution)/shard_map/pallas_call | solution.py:164
  85.1 2.8 %copy-done.6 = bf16[1536,2304]{1,0:T(8,128)(2,1)} copy-done((bf16[1536,2304]{1,0:T(8,128)(2,1)}, bf16[1536,2304]{1,0:T(8,128)(2,1)S(1)}, u32[]{:S(2)}) %copy-start.6) | copy-done | bytes 7077912
  87.9 1.8 %copy-done.8 = bf16[2,768,1152]{2,1,0:T(8,128)(2,1)} copy-done((bf16[2,768,1152]{2,1,0:T(8,128)(2,1)}, bf16[2,768,1152]{2,1,0:T(8,128)(2,1)S(1)}, u32[]{:S(2)}) %copy-start.8) | copy-done | bytes 3538968
  89.6 0.5 shard_map.164
  90.2 1.3 copy-done.4
  91.5 1.8 %copy-done.10 = bf16[768,2304]{1,0:T(8,128)(2,1)} copy-done((bf16[768,2304]{1,0:T(8,128)(2,1)}, bf16[768,2304]{1,0:T(8,128)(2,1)S(1)}, u32[]{:S(2)}) %copy-start.10) | copy-done | bytes 3538968
  93.3 1.5 %shard_map.162 = (bf16[1536,2304]{1,0:T(8,128)(2,1)S(1)}, bf16[2,768,1152]{2,1,0:T(8,128)(2,1)S(1)}) custom-call(bf16[3,3,3,384,384]{4,3,2,1,0:T(8,128)(2,1)S(1)} %bitcast.24), custom_call_target="tpu_custom_call" | custom-call | bytes 15925248 | tf_op jit(solution)/shard_map/pallas_call | solution.py:164
  94.8 2.9 %copy-done.7 = bf16[1536,2304]{1,0:T(8,128)(2,1)} copy-done((bf16[1536,2304]{1,0:T(8,128)(2,1)}, bf16[1536,2304]{1,0:T(8,128)(2,1)S(1)}, u32[]{:S(2)}) %copy-start.7) | copy-done | bytes 7077912
  97.7 1.8 %copy-done.14 = bf16[2,768,1152]{2,1,0:T(8,128)(2,1)} copy-done((bf16[2,768,1152]{2,1,0:T(8,128)(2,1)}, bf16[2,768,1152]{2,1,0:T(8,128)(2,1)S(1)}, u32[]{:S(2)}) %copy-start.14) | copy-done | bytes 3538968
  99.6 11.7 %all-to-all-done.1 = bf16[128,4,8,384]{3,2,1,0:T(8,128)(2,1)S(1)} async-done(((bf16[128,4,8,384]{3,2,1,0:T(8,128)(2,1)}), bf16[128,4,8,384]{3,2,1,0:T(8,128)(2,1)S(1)}, u32[]{:S(2)}, u32[]{:S(2)}) %all-to-all-start.1) | async-done | bytes 3145760 | tf_op jit(solution)/shard_map/all_to_all | solution.py:527
  111.3 0.5 fusion.2
  111.7 0.2 dynamic-slice_bitcast_fusion.2
  112.0 0.1 collective-permute-start.2
  112.0 0.9 collective-permute-start.3
  113.0 0.2 dynamic-slice_bitcast_fusion
  113.2 0.1 collective-permute-start.6
  113.3 4.5 %collective-permute-start.7 = (bf16[2,16,4,8,384]{4,3,2,1,0:T(8,128)(2,1)S(1)}, bf16[2,16,4,8,384]{4,3,2,1,0:T(8,128)(2,1)S(1)}, u32[]{:S(2)}, u32[]{:S(2)}) collective-permute-start(bf16[2,16,4,8,384]{4,3,2,1,0:T(8,128)(2,1)S(1)} %get-tuple-element.89), channel_id=1, source_target_pairs={{0,31},{1,2},{2,1},{3,4},{4,3},{5,6},{6,5},{7,8},{8,7},{9,10},{10,... | collective-permute-start | bytes 2359304 | tf_op jit(solution)/shard_map/ppermute | solution.py:511
  117.7 11.8 %shard_map.165 = (f32[2,16,4,8,384]{4,3,2,1,0:T(8,128)S(1)}, f32[2,16,4,8,384]{4,3,2,1,0:T(8,128)S(1)}, bf16[4,2,2,16,8,384]{5,4,3,2,1,0:T(8,128)(2,1)}, bf16[4,...) custom-call(bf16[2,2,2,16,4,8,384]{6,5,4,3,2,1,0:T(8,128)(2,1)S(1)} %bitcast.26, bf16[1536,2304]{1,0:T(8,128)(2,1)} %copy-done.7, ...), custom_call_target="tpu_custom_call" | custom-call | flops 7247757312 | bytes 14155776 | tf_op jit(solution)/shard_map/pallas_call | solution.py:115
  129.6 3.4 %shard_map.166 = (bf16[4,2,128,384]{3,2,1,0:T(8,128)(2,1)S(1)}, bf16[4,128,384]{2,1,0:T(8,128)(2,1)S(1)}, bf16[4,128,384]{2,1,0:T(8,128)(2,1)S(1)}) custom-call(s32[3,4]{1,0:T(4,128)S(1)} %add_convert_fusion.edge_ref, bf16[2,16,4,8,384]{4,3,2,1,0:T(8,128)(2,1)S(1)} %collective-permute-done.2.near_ref, ...), custom_call_target="tpu_custom_call" | custom-call | flops 1811939328 | bytes 3538944 | tf_op jit(solution)/shard_map/pallas_call | solution.py:115
  133.0 0.1 collective-permute-start.4
  133.1 1.2 collective-permute-start.5
  134.2 1.1 collective-permute-done.7.far_ref
  135.3 5.3 %shard_map.167 = (f32[2,16,4,8,384]{4,3,2,1,0:T(8,128)S(1)}, bf16[4,2,2,16,8,384]{5,4,3,2,1,0:T(8,128)(2,1)}) custom-call(s32[3,4]{1,0:T(4,128)S(1)} %add_convert_fusion.edge_ref, bf16[2,16,4,8,384]{4,3,2,1,0:T(8,128)(2,1)S(1)} %collective-permute-done.6.near_ref, ...), custom_call_target="tpu_custom_call", output_to_operand_aliasing={{1}: (8, {})} | custom-call | flops 3623878656 | bytes 7077888 | tf_op jit(solution)/shard_map/pallas_call | solution.py:115
  140.7 3.2 %collective-permute-done.5.far_ref = bf16[4,128,384]{2,1,0:T(8,128)(2,1)S(1)} collective-permute-done((bf16[4,128,384]{2,1,0:T(8,128)(2,1)S(1)}, bf16[4,128,384]{2,1,0:T(8,128)(2,1)S(1)}, u32[]{:S(2)}, u32[]{:S(2)}) %collective-permute-start.5) | collective-permute-done | bytes 393248 | tf_op jit(solution)/shard_map/ppermute | solution.py:511
  143.9 3.1 %shard_map.168 = bf16[4,2,128,384]{3,2,1,0:T(8,128)(2,1)} custom-call(s32[3,4]{1,0:T(4,128)S(1)} %add_convert_fusion.edge_ref, bf16[4,128,384]{2,1,0:T(8,128)(2,1)S(1)} %collective-permute-done.4.near_ref, bf16[4,128,384]{2,1,0:T(8,128)(2,1)S(1)} %collective-permute-done.5.far_ref, bf16[2,384,1152]{2,1,0:T(8,128)(2,1)S(1)} %copy-done.5, ...), custom_call_target="tpu_custom_call" | custom-call | flops 905969664 | bytes 1769472 | tf_op jit(solution)/shard_map/pallas_call | solution.py:115
  (68 shorter events, 0.2 us)
Async XLA Ops:
  3.8 11.7 %copy-start.24 = (f32[384]{0:T(512)S(1)}, f32[384]{0:T(512)}, u32[]{:S(2)}) copy-start(f32[384]{0:T(512)} %param.17) | copy-start | bytes 4612
  3.8 11.8 %copy-start.28 = (s32[16]{0:T(128)S(1)}, s32[16]{0:T(128)}, u32[]{:S(2)}) copy-start(s32[16]{0:T(128)} %param.27) | copy-start | bytes 196
  3.8 11.8 %copy-start.29 = (s32[16]{0:T(128)S(1)}, s32[16]{0:T(128)}, u32[]{:S(2)}) copy-start(s32[16]{0:T(128)} %param.24) | copy-start | bytes 196
  3.8 11.8 %copy-start.30 = (s32[16]{0:T(128)S(1)}, s32[16]{0:T(128)}, u32[]{:S(2)}) copy-start(s32[16]{0:T(128)} %param.25) | copy-start | bytes 196
  3.9 11.8 %copy-start.31 = (s32[16]{0:T(128)S(1)}, s32[16]{0:T(128)}, u32[]{:S(2)}) copy-start(s32[16]{0:T(128)} %param.23) | copy-start | bytes 196
  3.9 11.8 %copy-start.32 = (s32[16]{0:T(128)S(1)}, s32[16]{0:T(128)}, u32[]{:S(2)}) copy-start(s32[16]{0:T(128)} %param.26) | copy-start | bytes 196
  3.9 12.1 %copy-start.2 = (bf16[4,2,128,384]{3,2,1,0:T(8,128)(2,1)S(1)}, bf16[4,2,128,384]{3,2,1,0:T(8,128)(2,1)}, u32[]{:S(2)}) copy-start(bf16[4,2,128,384]{3,2,1,0:T(8,128)(2,1)} %f_ref.3) | copy-start | bytes 2359300
  3.9 55.1 %all-to-all-start = ((bf16[128,4,8,384]{3,2,1,0:T(8,128)(2,1)}), bf16[128,4,8,384]{3,2,1,0:T(8,128)(2,1)}, u32[]{:S(2)}, u32[]{:S(2)}) async-start(bf16[128,4,8,384]{3,2,1,0:T(8,128)(2,1)} %bitcast.29), calls=%async_computation | async-start | bytes 6291456 | tf_op jit(solution)/shard_map/all_to_all | solution.py:516
  18.8 0.9 copy-start.17
  19.6 10.7 %collective-permute-start = (bf16[4,128,384]{2,1,0:T(8,128)(2,1)}, bf16[4,128,384]{2,1,0:T(8,128)(2,1)S(1)}, u32[]{:S(2)}, u32[]{:S(2)}) collective-permute-start(bf16[4,128,384]{2,1,0:T(8,128)(2,1)} %get-tuple-element.44), channel_id=1, source_target_pairs={{0,1},{1,0},{2,3},{3,2},{4,5},{5,4},{6,7},{7,6},{8,9},{9,8},{10,11... | collective-permute-start | bytes 1179656 | tf_op jit(solution)/shard_map/ppermute | solution.py:508
  19.6 39.3 %collective-permute-start.1 = (bf16[4,128,384]{2,1,0:T(8,128)(2,1)}, bf16[4,128,384]{2,1,0:T(8,128)(2,1)S(1)}, u32[]{:S(2)}, u32[]{:S(2)}) collective-permute-start(bf16[4,128,384]{2,1,0:T(8,128)(2,1)} %get-tuple-element.45), channel_id=1, source_target_pairs={{0,31},{1,2},{2,1},{3,4},{4,3},{5,6},{6,5},{7,8},{8,7},{9,10},{10,... | collective-permute-start | bytes 1179656 | tf_op jit(solution)/shard_map/ppermute | solution.py:511
  24.8 3.3 %copy-start.1 = (bf16[3,3,3,384,384]{4,3,2,1,0:T(8,128)(2,1)S(1)}, bf16[3,3,3,384,384]{4,3,2,1,0:T(8,128)(2,1)}, u32[]{:S(2)}) copy-start(bf16[3,3,3,384,384]{4,3,2,1,0:T(8,128)(2,1)} %w_ref.2) | copy-start | bytes 23887876
  28.6 1.8 %copy-start.12 = (bf16[768,2304]{1,0:T(8,128)(2,1)}, bf16[768,2304]{1,0:T(8,128)(2,1)S(1)}, u32[]{:S(2)}) copy-start(bf16[768,2304]{1,0:T(8,128)(2,1)S(1)} %get-tuple-element.54.wo_ref) | copy-start | bytes 10616836
  30.4 32.9 %copy-start.15 = (bf16[2,384,1152]{2,1,0:T(8,128)(2,1)}, bf16[2,384,1152]{2,1,0:T(8,128)(2,1)S(1)}, u32[]{:S(2)}) copy-start(bf16[2,384,1152]{2,1,0:T(8,128)(2,1)S(1)} %get-tuple-element.55.ws_ref) | copy-start | bytes 5308420
  59.0 4.3 %copy-start.20 = (bf16[4,128,384]{2,1,0:T(8,128)(2,1)}, bf16[4,128,384]{2,1,0:T(8,128)(2,1)S(1)}, u32[]{:S(2)}) copy-start(bf16[4,128,384]{2,1,0:T(8,128)(2,1)S(1)} %collective-permute-done.1.far_ref) | copy-start | bytes 1179652
  63.3 6.2 %copy-start.25 = (f32[384]{0:T(512)S(1)}, f32[384]{0:T(512)}, u32[]{:S(2)}) copy-start(f32[384]{0:T(512)} %param.21) | copy-start | bytes 4612
  63.3 6.2 %copy-start.26 = (f32[384]{0:T(512)S(1)}, f32[384]{0:T(512)}, u32[]{:S(2)}) copy-start(f32[384]{0:T(512)} %param.18) | copy-start | bytes 4612
  63.3 48.0 %all-to-all-start.1 = ((bf16[128,4,8,384]{3,2,1,0:T(8,128)(2,1)}), bf16[128,4,8,384]{3,2,1,0:T(8,128)(2,1)S(1)}, u32[]{:S(2)}, u32[]{:S(2)}) async-start(bf16[128,4,8,384]{3,2,1,0:T(8,128)(2,1)} %bitcast.30), calls=%async_computation.1 | async-start | bytes 6291456 | tf_op jit(solution)/shard_map/all_to_all | solution.py:527
  69.5 2.0 %copy-start.13 = (bf16[768,2304]{1,0:T(8,128)(2,1)S(1)}, bf16[768,2304]{1,0:T(8,128)(2,1)}, u32[]{:S(2)}) copy-start(bf16[768,2304]{1,0:T(8,128)(2,1)} %copy-done.12) | copy-start | bytes 10616836
  71.5 1.5 %copy-start.16 = (bf16[2,384,1152]{2,1,0:T(8,128)(2,1)S(1)}, bf16[2,384,1152]{2,1,0:T(8,128)(2,1)}, u32[]{:S(2)}) copy-start(bf16[2,384,1152]{2,1,0:T(8,128)(2,1)} %copy-done.15) | copy-start | bytes 5308420
  73.0 1.1 copy-start.18
  74.1 1.0 copy-start.21
  75.1 18.2 %slice-start = ((s8[7962624]{0:T(1024)(128)(4,1)}), s8[4194304]{0:T(1024)(128)(4,1)S(1)}, s32[]{:S(2)}) async-start(s8[7962624]{0:T(1024)(128)(4,1)} %bitcast.23), calls=%async_computation.2 | async-start | bytes 8388608
  79.1 1.1 copy-start.22
  80.2 3.3 %copy-start = (bf16[3,3,3,384,384]{4,3,2,1,0:T(8,128)(2,1)S(1)}, bf16[3,3,3,384,384]{4,3,2,1,0:T(8,128)(2,1)}, u32[]{:S(2)}) copy-start(bf16[3,3,3,384,384]{4,3,2,1,0:T(8,128)(2,1)} %w_ref.4) | copy-start | bytes 23887876
  83.5 9.8 %slice-start.1 = ((s8[7962624]{0:T(1024)(128)(4,1)}), s8[3768320]{0:T(1024)(128)(4,1)S(1)}, s32[]{:S(2)}) async-start(s8[7962624]{0:T(1024)(128)(4,1)} %bitcast.23), calls=%async_computation.3 | async-start | bytes 7536640
  85.0 2.8 %copy-start.6 = (bf16[1536,2304]{1,0:T(8,128)(2,1)}, bf16[1536,2304]{1,0:T(8,128)(2,1)S(1)}, u32[]{:S(2)}) copy-start(bf16[1536,2304]{1,0:T(8,128)(2,1)S(1)} %get-tuple-element.67.w1_ref) | copy-start | bytes 21233668
  87.9 1.8 %copy-start.8 = (bf16[2,768,1152]{2,1,0:T(8,128)(2,1)}, bf16[2,768,1152]{2,1,0:T(8,128)(2,1)S(1)}, u32[]{:S(2)}) copy-start(bf16[2,768,1152]{2,1,0:T(8,128)(2,1)S(1)} %get-tuple-element.76.w_ref) | copy-start | bytes 10616836
  90.2 1.3 copy-start.4
  91.5 1.8 %copy-start.10 = (bf16[768,2304]{1,0:T(8,128)(2,1)}, bf16[768,2304]{1,0:T(8,128)(2,1)S(1)}, u32[]{:S(2)}) copy-start(bf16[768,2304]{1,0:T(8,128)(2,1)S(1)} %get-tuple-element.77.wa_ref) | copy-start | bytes 10616836
  94.8 2.9 %copy-start.7 = (bf16[1536,2304]{1,0:T(8,128)(2,1)}, bf16[1536,2304]{1,0:T(8,128)(2,1)S(1)}, u32[]{:S(2)}) copy-start(bf16[1536,2304]{1,0:T(8,128)(2,1)S(1)} %get-tuple-element.66.w0_ref) | copy-start | bytes 21233668
  97.7 1.8 %copy-start.14 = (bf16[2,768,1152]{2,1,0:T(8,128)(2,1)}, bf16[2,768,1152]{2,1,0:T(8,128)(2,1)S(1)}, u32[]{:S(2)}) copy-start(bf16[2,768,1152]{2,1,0:T(8,128)(2,1)S(1)} %get-tuple-element.69.sides_ref) | copy-start | bytes 10616836
  111.9 5.8 %copy-start.19 = (bf16[4,2,128,384]{3,2,1,0:T(8,128)(2,1)S(1)}, bf16[4,2,128,384]{3,2,1,0:T(8,128)(2,1)}, u32[]{:S(2)}) copy-start(bf16[4,2,128,384]{3,2,1,0:T(8,128)(2,1)} %copy-done.17) | copy-start | bytes 2359300
  111.9 5.8 %copy-start.23 = (f32[2,16,4,8,384]{4,3,2,1,0:T(8,128)S(1)}, f32[2,16,4,8,384]{4,3,2,1,0:T(8,128)}, u32[]{:S(2)}) copy-start(f32[2,16,4,8,384]{4,3,2,1,0:T(8,128)} %copy-done.22) | copy-start | bytes 4718596
  112.0 17.6 %collective-permute-start.2 = (bf16[2,16,4,8,384]{4,3,2,1,0:T(8,128)(2,1)S(1)}, bf16[2,16,4,8,384]{4,3,2,1,0:T(8,128)(2,1)S(1)}, u32[]{:S(2)}, u32[]{:S(2)}) collective-permute-start(bf16[2,16,4,8,384]{4,3,2,1,0:T(8,128)(2,1)S(1)} %get-tuple-element.92), channel_id=1, source_target_pairs={{0,1},{1,0},{2,3},{3,2},{4,5},{5,4},{6,7},{7,6},{8,9},{9,8},{10,11... | collective-permute-start | bytes 2359304 | tf_op jit(solution)/shard_map/ppermute | solution.py:508
  112.0 17.5 %collective-permute-start.3 = (bf16[2,16,4,8,384]{4,3,2,1,0:T(8,128)(2,1)S(1)}, bf16[2,16,4,8,384]{4,3,2,1,0:T(8,128)(2,1)S(1)}, u32[]{:S(2)}, u32[]{:S(2)}) collective-permute-start(bf16[2,16,4,8,384]{4,3,2,1,0:T(8,128)(2,1)S(1)} %get-tuple-element.91), channel_id=1, source_target_pairs={{0,31},{1,2},{2,1},{3,4},{4,3},{5,6},{6,5},{7,8},{8,7},{9,10},{10,... | collective-permute-start | bytes 2359304 | tf_op jit(solution)/shard_map/ppermute | solution.py:511
  113.2 21.0 %collective-permute-start.6 = (bf16[2,16,4,8,384]{4,3,2,1,0:T(8,128)(2,1)S(1)}, bf16[2,16,4,8,384]{4,3,2,1,0:T(8,128)(2,1)S(1)}, u32[]{:S(2)}, u32[]{:S(2)}) collective-permute-start(bf16[2,16,4,8,384]{4,3,2,1,0:T(8,128)(2,1)S(1)} %get-tuple-element.90), channel_id=1, source_target_pairs={{0,1},{1,0},{2,3},{3,2},{4,5},{5,4},{6,7},{7,6},{8,9},{9,8},{10,11... | collective-permute-start | bytes 2359304 | tf_op jit(solution)/shard_map/ppermute | solution.py:508
  113.3 22.0 %collective-permute-start.7 = (bf16[2,16,4,8,384]{4,3,2,1,0:T(8,128)(2,1)S(1)}, bf16[2,16,4,8,384]{4,3,2,1,0:T(8,128)(2,1)S(1)}, u32[]{:S(2)}, u32[]{:S(2)}) collective-permute-start(bf16[2,16,4,8,384]{4,3,2,1,0:T(8,128)(2,1)S(1)} %get-tuple-element.89), channel_id=1, source_target_pairs={{0,31},{1,2},{2,1},{3,4},{4,3},{5,6},{6,5},{7,8},{8,7},{9,10},{10,... | collective-permute-start | bytes 2359304 | tf_op jit(solution)/shard_map/ppermute | solution.py:511
  117.7 17.5 %copy-start.11 = (bf16[768,2304]{1,0:T(8,128)(2,1)S(1)}, bf16[768,2304]{1,0:T(8,128)(2,1)}, u32[]{:S(2)}) copy-start(bf16[768,2304]{1,0:T(8,128)(2,1)} %copy-done.10) | copy-start | bytes 10616836
  129.5 4.7 %copy-start.27 = (f32[384]{0:T(512)S(1)}, f32[384]{0:T(512)}, u32[]{:S(2)}) copy-start(f32[384]{0:T(512)} %param.22) | copy-start | bytes 4612
  129.6 5.7 %copy-start.9 = (bf16[2,768,1152]{2,1,0:T(8,128)(2,1)S(1)}, bf16[2,768,1152]{2,1,0:T(8,128)(2,1)}, u32[]{:S(2)}) copy-start(bf16[2,768,1152]{2,1,0:T(8,128)(2,1)} %copy-done.8) | copy-start | bytes 10616836
  133.0 7.7 %collective-permute-start.4 = (bf16[4,128,384]{2,1,0:T(8,128)(2,1)S(1)}, bf16[4,128,384]{2,1,0:T(8,128)(2,1)S(1)}, u32[]{:S(2)}, u32[]{:S(2)}) collective-permute-start(bf16[4,128,384]{2,1,0:T(8,128)(2,1)S(1)} %get-tuple-element.72), channel_id=1, source_target_pairs={{0,1},{1,0},{2,3},{3,2},{4,5},{5,4},{6,7},{7,6},{8,9},{9,8},{10,11... | collective-permute-start | bytes 1179656 | tf_op jit(solution)/shard_map/ppermute | solution.py:508
  133.1 10.8 %collective-permute-start.5 = (bf16[4,128,384]{2,1,0:T(8,128)(2,1)S(1)}, bf16[4,128,384]{2,1,0:T(8,128)(2,1)S(1)}, u32[]{:S(2)}, u32[]{:S(2)}) collective-permute-start(bf16[4,128,384]{2,1,0:T(8,128)(2,1)S(1)} %get-tuple-element.73), channel_id=1, source_target_pairs={{0,31},{1,2},{2,1},{3,4},{4,3},{5,6},{6,5},{7,8},{8,7},{9,10},{10,... | collective-permute-start | bytes 1179656 | tf_op jit(solution)/shard_map/ppermute | solution.py:511
  135.3 8.6 %copy-start.3 = (bf16[4,2,128,384]{3,2,1,0:T(8,128)(2,1)S(1)}, bf16[4,2,128,384]{3,2,1,0:T(8,128)(2,1)}, u32[]{:S(2)}) copy-start(bf16[4,2,128,384]{3,2,1,0:T(8,128)(2,1)} %f_ref.3) | copy-start | bytes 2359300
  135.3 8.6 %copy-start.5 = (bf16[2,384,1152]{2,1,0:T(8,128)(2,1)S(1)}, bf16[2,384,1152]{2,1,0:T(8,128)(2,1)}, u32[]{:S(2)}) copy-start(bf16[2,384,1152]{2,1,0:T(8,128)(2,1)} %copy-done.4) | copy-start | bytes 5308420

commit v10 on v9

--- a/solution.py
+++ b/solution.py
@@ -103,6 +103,8 @@
 
 
 VMEM_LIMIT = 16 << 20
+LIMIT_A = 34
+LIMIT_B = 16
 
 
 def call(body, out_shape, operands, scalars=(), scratch=(), flops=0, moved=0, far=(), far_out=(), aliases=None, limit=VMEM_LIMIT):
@@ -297,83 +299,110 @@
     )[0]
 
 
-def own_part(got, weights, sums, act, sides):
-    n_rows, n_caches, n_frames, blocks, n_slots, _, ch = got.shape
+def own_rows(got_ref, k, lhs):
+    n_rows, _, n_frames, _, _, _, ch = got_ref.shape
+    for r in range(n_rows):
+        for f in range(n_frames):
+            lo = (r * n_frames + f) * ch
+            lhs[:, lo : lo + ch] = got_ref[r, k, f].reshape(lhs.shape[0], ch)
+
+
+def give_rows(acc, ch, o_ref, base):
+    n_rows = o_ref.shape[0]
+    wide = acc.shape[1] // n_rows
+    for y in range(n_rows):
+        add_into(o_ref, y, folded(acc[:, y * wide : (y + 1) * wide], ch, True), True, base)
+
+
+def own_first(got, weight, sums, act, sides):
+    n_rows, _, n_frames, blocks, n_slots, _, ch = got.shape
     half = blocks * n_slots * CB
     deep = n_frames * ch
-    whole = weights[0]
-
-    def body(got_ref, w0_ref, w1_ref, z_ref, act_ref, sides_ref, o0_ref, o1_ref, n1_ref, n2_ref, near_ref, w0, w1, lhs, acc, sems, keep_sems):
+
+    def body(got_ref, w_ref, z_ref, act_ref, sides_ref, o_ref, next_ref, near_ref, w, lhs, acc, sems, keep_sems):
         loads = []
         for r in range(n_rows):
             rows = pl.ds(r * deep, deep)
-            loads.append(pltpu.make_async_copy(w0_ref.at[rows], w0.at[r], sems.at[r]))
-        loads.append(pltpu.make_async_copy(w1_ref, w1, sems.at[2]))
-        near = pltpu.make_async_copy(sides_ref, near_ref, sems.at[3])
-        keeps = [pltpu.make_async_copy(act_ref, n1_ref.at[:, 1], sems.at[4])]
-        for k, dst in enumerate((n1_ref, n2_ref)):
-            for r in range(n_rows):
-                for s in range(n_slots):
-                    n = (k * n_rows + r) * n_slots + s
-                    keeps.append(
-                        pltpu.make_async_copy(
-                            got_ref.at[r, k, n_frames - 1, :, s], dst.at[s, 0, r], keep_sems.at[n]
-                        )
-                    )
+            loads.append(pltpu.make_async_copy(w_ref.at[rows], w.at[r], sems.at[r]))
         loads[0].start()
-
-        def fill(k, r, f):
-            lo = r * deep + f * ch
-            lhs[:, lo : lo + ch] = got_ref[r, k, f].reshape(half, ch)
-
-        def give(o_ref, base):
-            wide = whole.shape[1] // 2
-            for y in range(n_rows):
-                total = folded(acc[:, y * wide : (y + 1) * wide], ch, True)
-                add_into(o_ref, y, total, True, base)
-
+        near = pltpu.make_async_copy(sides_ref, near_ref, sems.at[2])
+        keeps = [pltpu.make_async_copy(act_ref, next_ref.at[:, 1], sems.at[3])]
         for r in range(n_rows):
-            for f in range(n_frames):
-                fill(0, r, f)
+            for s in range(n_slots):
+                src = got_ref.at[r, 0, n_frames - 1, :, s]
+                n = r * n_slots + s
+                keeps.append(pltpu.make_async_copy(src, next_ref.at[s, 0, r], keep_sems.at[n]))
+        own_rows(got_ref, 0, lhs)
         loads[0].wait()
         loads[1].start()
-        acc[...] = dot(lhs[:, 0:deep], w0[0])
+        acc[...] = dot(lhs[:, 0:deep], w[0])
         loads[1].wait()
-        loads[2].start()
-        acc[...] += dot(lhs[:, deep : 2 * deep], w0[1])
-        give(o0_ref, z_ref)
-        for r in range(n_rows):
-            for f in range(n_frames):
-                fill(1, r, f)
-        loads[2].wait()
         near.start()
         for c in keeps:
             c.start()
-        acc[...] = dot(lhs[...], w1[...])
-        give(o1_ref, None)
+        acc[...] += dot(lhs[:, deep : 2 * deep], w[1])
+        give_rows(acc, ch, o_ref, z_ref)
         for c in keeps:
             c.wait()
         near.wait()
 
-    out = sums_shape(blocks, n_slots, n_rows, ch)
-    nxt = jax.ShapeDtypeStruct((n_slots, 2, n_rows, blocks, CB, ch), jnp.bfloat16)
     return call(
         body,
-        [out, out, nxt, nxt, jax.ShapeDtypeStruct(sides.shape, sides.dtype)],
-        (got, *weights, sums, act, sides),
+        [
+            sums_shape(blocks, n_slots, n_rows, ch),
+            jax.ShapeDtypeStruct((n_slots, 2, n_rows, blocks, CB, ch), jnp.bfloat16),
+            jax.ShapeDtypeStruct(sides.shape, sides.dtype),
+        ],
+        (got, weight, sums, act, sides),
         scratch=[
-            pltpu.VMEM((n_rows, deep, whole.shape[1]), whole.dtype),
-            pltpu.VMEM(whole.shape, whole.dtype),
+            pltpu.VMEM((n_rows, deep, weight.shape[1]), weight.dtype),
             pltpu.VMEM((half, n_rows * deep), jnp.bfloat16),
-            pltpu.VMEM((half, whole.shape[1]), jnp.float32),
-            pltpu.SemaphoreType.DMA((5,)),
-            pltpu.SemaphoreType.DMA((2 * n_rows * n_slots,)),
-        ],
-        flops=4 * half * whole.size,
-        moved=4 * whole.size,
-        far=(1, 2, 5),
-        far_out=(2, 3),
-        limit=40 << 20,
+            pltpu.VMEM((half, weight.shape[1]), jnp.float32),
+            pltpu.SemaphoreType.DMA((4,)),
+            pltpu.SemaphoreType.DMA((n_rows * n_slots,)),
+        ],
+        flops=2 * half * weight.size,
+        moved=2 * weight.size,
+        far=(1, 4),
+        far_out=(1,),
+        limit=LIMIT_A << 20,
+    )
+
+
+def own_second(got, weight):
+    n_rows, _, n_frames, blocks, n_slots, _, ch = got.shape
+    half = blocks * n_slots * CB
+    deep = n_frames * ch
+
+    def body(got_ref, w_ref, o_ref, next_ref, lhs, acc, keep_sems):
+        keeps = []
+        for r in range(n_rows):
+            for s in range(n_slots):
+                src = got_ref.at[r, 1, n_frames - 1, :, s]
+                n = r * n_slots + s
+                keeps.append(pltpu.make_async_copy(src, next_ref.at[s, 0, r], keep_sems.at[n]))
+                keeps[-1].start()
+        own_rows(got_ref, 1, lhs)
+        acc[...] = dot(lhs[...], w_ref[...])
+        give_rows(acc, ch, o_ref, None)
+        for c in keeps:
+            c.wait()
+
+    return call(
+        body,
+        [
+            sums_shape(blocks, n_slots, n_rows, ch),
+            jax.ShapeDtypeStruct((n_slots, 2, n_rows, blocks, CB, ch), jnp.bfloat16),
+        ],
+        (got, weight),
+        scratch=[
+            pltpu.VMEM((half, n_rows * deep), jnp.bfloat16),
+            pltpu.VMEM((half, weight.shape[1]), jnp.float32),
+            pltpu.SemaphoreType.DMA((n_rows * n_slots,)),
+        ],
+        flops=2 * half * weight.size,
+        moved=2 * weight.size,
+        far_out=(1,),
     )
 
 
@@ -387,39 +416,47 @@
     return folded(dot(lhs[...].reshape(half, n_frames * ch), w), ch, True)
 
 
-def second_activation(near, far, w_sides, sums, bias, gain, edges):
-    n_frames, blocks, n_slots, _, ch = near.shape
+def second_activation(near, far, w_sides, sums, bias, gain, later, edges):
+    n_frames, blocks, n_slots, _, ch = far.shape
     n_rows, n_cols, deep = sums.shape[0], blocks * CB, n_frames * ch
 
-    def body(edge_ref, near_ref, far_ref, w_ref, z_ref, b_ref, g_ref, o_ref, near_out, far_out, lhs):
-        for (side, y), out in zip(beside(edge_ref, near_ref, far_ref), (near_out, far_out)):
+    def body(edge_ref, near_ref, far_ref, w_ref, z_ref, b_ref, g_ref, later_ref, o_ref, near_out, far_out, fetched_ref, lhs, sem):
+        fetch = pltpu.make_async_copy(later_ref, fetched_ref, sem)
+        fetch.start()
+        for (side, y), out in zip(beside(edge_ref, near_ref.at[0], far_ref), (near_out, far_out)):
             total = side_sums(edge_ref, y, side, w_ref[y], lhs) + z_ref[y] + b_ref[...]
             for s in range(n_slots):
                 value = activated(total[:, s].reshape(n_cols, ch), g_ref[...]).astype(jnp.bfloat16)
                 o_ref[s, y] = value
                 out[s] = value
+        fetch.wait()
 
     row = jax.ShapeDtypeStruct((n_slots, n_cols, ch), jnp.bfloat16)
     return call(
         body,
-        [jax.ShapeDtypeStruct((n_slots, n_rows, n_cols, ch), jnp.bfloat16), row, row],
-        (near, far, w_sides, sums, bias, gain),
+        [jax.ShapeDtypeStruct((n_slots, n_rows, n_cols, ch), jnp.bfloat16), row, row, jax.ShapeDtypeStruct(later.shape, later.dtype)],
+        (near, far, w_sides, sums, bias, gain, later),
         scalars=(edges,),
-        scratch=[pltpu.VMEM((blocks, n_slots, CB, deep), jnp.bfloat16)],
+        scratch=[
+            pltpu.VMEM((blocks, n_slots, CB, deep), jnp.bfloat16),
+            pltpu.SemaphoreType.DMA,
+        ],
         flops=2 * n_slots * n_cols * w_sides.size,
         moved=2 * w_sides.size,
+        far=(6,),
+        limit=LIMIT_B << 20,
     )
 
 
 def before_sides(near, far, act, w_sides, w_act, sums, kept, edges):
-    n_frames, blocks, n_slots, _, ch = near.shape
+    n_frames, blocks, n_slots, _, ch = far.shape
     n_rows, n_cols, deep = sums.shape[0], blocks * CB, n_frames * ch
 
     def body(edge_ref, near_ref, far_ref, act_ref, tiles_ref, w_ref, wa_ref, z_ref, kept_ref, o_ref, next_ref, lhs, lhs2, sem):
         copy = pltpu.make_async_copy(tiles_ref, next_ref.at[:, 1], sem)
         copy.start()
         add_own(act_ref, wa_ref, lhs2, o_ref, z_ref)
-        for side, y in beside(edge_ref, near_ref, far_ref):
+        for side, y in beside(edge_ref, near_ref.at[1], far_ref):
             o_ref[y] += side_sums(edge_ref, y, side, w_ref[y], lhs)
         copy.wait()
 
@@ -537,21 +574,21 @@
     )
     got = got.reshape(n_rows, 2, 2, blocks, n_slots, CB, ch)
 
-    def picked(cache, row):
-        return lax.dynamic_index_in_dim(got[:, cache], row, 0, keepdims=False)
-
-    near_1, far_1 = swap_near(picked(0, 1 - odd)), swap_far(picked(0, odd))
-    near_2, far_2 = swap_near(picked(1, 1 - odd)), swap_far(picked(1, odd))
+    def picked(row):
+        return lax.dynamic_index_in_dim(got, row, 0, keepdims=False)
+
+    rows_near, rows_far = swap_near(picked(1 - odd)), picked(odd)
+    far_1, far_2 = swap_far(rows_far[0]), swap_far(rows_far[1])
     act_tiles = act_first.reshape(n_slots, n_rows, blocks, CB, ch)
-    sums_1, sums_2, next_first, kept, sides_1 = own_part(
-        got, (own_1, own_2), sums_1, act_tiles, sides_1
-    )
-    act_second, near, far = second_activation(
-        near_1, far_1, sides_1, sums_1, bias_first[None], gain_second[None], edges
+    sums_1, next_first, sides_1 = own_first(got, own_1, sums_1, act_tiles, sides_1)
+    act_second, near, far, own_2 = second_activation(
+        rows_near, far_1, sides_1, sums_1, bias_first[None], gain_second[None], own_2, edges
     )
     act_near, act_far = swap_near(near), swap_far(far)
+    got_later, act_later = lax.optimization_barrier((got, act_second))
+    sums_2, kept = own_second(got_later, own_2)
     sums_2, next_second = before_sides(
-        near_2, far_2, act_second, sides_2, act_own_2, sums_2, kept, edges
+        rows_near, far_2, act_later, sides_2, act_own_2, sums_2, kept, edges
     )
     mixed_frame = last_part(
         act_near, act_far, act_sides_2, sums_2, bias_second[None], frame_in, edges

time: 148 us -> 147 us (level)
  waiting for transfers between devices: 44.6 us -> 40.5 us
  local copies, waits for them, and re-layouts: 29.3 us -> 32.2 us
    ppermute x4, waiting for transfers between devices: 32.9 us -> 28.8 us  [swap_far(): lax.ppermute(row, 'tile', [(i, (i + 2 * (i % 2) - 1) % n_tiles) for i in...]
    unnamed x70 -> x76, local copies, waits for them, and re-layouts: 28.4 us -> 30.6 us
    pallas_call x6 -> x7, Pallas kernels: 30.3 us -> 31.3 us  [call(): pl.pallas_call(body, in_specs=in_specs, out_specs=out_specs, out_shape=li...]
  transfers between devices with their start and end apart: 10 -> 9, of which waited for: 4 -> 3; matrix products, arithmetic and copies ran while one was open for 0% -> 0% of each run, Pallas kernels for 21% -> 22%
where the time goes in v10:
time: 147 us; the launch traced here: 146 us
  Pallas kernels  42.6 us (29%)
  waiting for transfers between devices  40.5 us (28%)
  local copies, waits for them, and re-layouts  32.2 us (22%)
  starting transfers between devices  29.8 us (20%)
    pallas_call x7, Pallas kernels, call(): pl.pallas_call(body, in_specs=in_specs, out_specs=out_specs, out_shape=li...  31.3 us
    unnamed x76, local copies, waits for them, and re-layouts  30.6 us
    ppermute x4, waiting for transfers between devices, swap_far(): lax.ppermute(row, 'tile', [(i, (i + 2 * (i % 2) - 1) % n_tiles) for i in...  28.8 us
    ppermute x4, starting transfers between devices, swap_far(): lax.ppermute(row, 'tile', [(i, (i + 2 * (i % 2) - 1) % n_tiles) for i in...  11.8 us
    all_to_all x1, waiting for transfers between devices, local(): lax.all_to_all(moved.reshape(n_groups * n_tiles, n_slots, CB, ch), BOTH,...  11.7 us
    all_to_all x1, starting transfers between devices, local(): held = lax.all_to_all(sent, BOTH, 0, 0, tiled=True)  11.6 us
    all_to_all x1, starting transfers between devices, local(): lax.all_to_all(moved.reshape(n_groups * n_tiles, n_slots, CB, ch), BOTH,...  6.23 us
    pallas_call x4, Pallas kernels, spread(): pl.pallas_call(body, grid=(n_y,), in_specs=[pl.BlockSpec((times, 1, n_x,...  4.11 us
  transfers between devices with their start and end apart: 9, of which 3 were waited for; matrix products, arithmetic and copies ran while one was open for 0% of the time, Pallas kernels for 22%

profile of v10, /device:TPU:0, one launch (start us, length us, event | category | flops | bytes accessed | tf_op | source)
XLA Modules:
  0.0 146.4 jit_solution(12630863664725050259)
XLA Ops:
  0.6 3.2 %shard_map.157 = bf16[2,2,2,16,4,8,384]{6,5,4,3,2,1,0:T(8,128)(2,1)} custom-call(bf16[4,2,2,16,8,384]{5,4,3,2,1,0:T(8,128)(2,1)} %bitcast.33, bf16[4,2,2,16,8,384]{5,4,3,2,1,0:T(8,128)(2,1)} %bitcast.34), custom_call_target="tpu_custom_call" | custom-call | tf_op jit(solution)/shard_map/pallas_call | solution.py:47
  3.8 0.0 copy-start.29
  3.8 0.0 copy-start.30
  3.9 0.0 copy-start.32
  3.9 11.6 %all-to-all-start = ((bf16[128,4,8,384]{3,2,1,0:T(8,128)(2,1)}), bf16[128,4,8,384]{3,2,1,0:T(8,128)(2,1)}, u32[]{:S(2)}, u32[]{:S(2)}) async-start(bf16[128,4,8,384]{3,2,1,0:T(8,128)(2,1)} %bitcast.31), calls=%async_computation | async-start | bytes 6291456 | tf_op jit(solution)/shard_map/all_to_all | solution.py:553
  15.6 0.1 pad.2.clone
  15.7 0.1 select_reduce_fusion
  15.8 0.1 compare_bitcast_fusion.1
  15.9 0.1 add_convert_fusion.edge_ref
  16.0 2.8 %shard_map.158 = (bf16[4,2,128,384]{3,2,1,0:T(8,128)(2,1)S(1)}, bf16[4,128,384]{2,1,0:T(8,128)(2,1)}, bf16[4,128,384]{2,1,0:T(8,128)(2,1)}) custom-call(s32[3,4]{1,0:T(4,128)S(1)} %add_convert_fusion.edge_ref, bf16[4,2,128,384]{3,2,1,0:T(8,128)(2,1)S(1)} %copy-done.10, f32[1,384]{1,0:T(1,128)S(1)} %broadcast_in_dim.53.g_ref), custom_call_target="tpu_custom_call" | custom-call | flops 3932160 | bytes 2359296 | tf_op jit(solution)/shard_map/pallas_call | solution.py:117
  18.8 0.9 copy-done.16
  19.6 5.2 %collective-permute-start.1 = (bf16[4,128,384]{2,1,0:T(8,128)(2,1)}, bf16[4,128,384]{2,1,0:T(8,128)(2,1)S(1)}, u32[]{:S(2)}, u32[]{:S(2)}) collective-permute-start(bf16[4,128,384]{2,1,0:T(8,128)(2,1)} %get-tuple-element.48), channel_id=1, source_target_pairs={{0,31},{1,2},{2,1},{3,4},{4,3},{5,6},{6,5},{7,8},{8,7},{9,10},{10,... | collective-permute-start | bytes 1179656 | tf_op jit(solution)/shard_map/ppermute | solution.py:548
  24.8 3.3 %copy-done.1 = bf16[3,3,3,384,384]{4,3,2,1,0:T(8,128)(2,1)S(1)} copy-done((bf16[3,3,3,384,384]{4,3,2,1,0:T(8,128)(2,1)S(1)}, bf16[3,3,3,384,384]{4,3,2,1,0:T(8,128)(2,1)}, u32[]{:S(2)}) %copy-start.1) | copy-done | bytes 7962648
  28.1 0.5 shard_map.159
  28.6 1.7 %copy-done.19 = bf16[768,2304]{1,0:T(8,128)(2,1)} copy-done((bf16[768,2304]{1,0:T(8,128)(2,1)}, bf16[768,2304]{1,0:T(8,128)(2,1)S(1)}, u32[]{:S(2)}) %copy-start.19) | copy-done | bytes 3538968
  30.4 28.6 %collective-permute-done.1.far_ref = bf16[4,128,384]{2,1,0:T(8,128)(2,1)S(1)} collective-permute-done((bf16[4,128,384]{2,1,0:T(8,128)(2,1)}, bf16[4,128,384]{2,1,0:T(8,128)(2,1)S(1)}, u32[]{:S(2)}, u32[]{:S(2)}) %collective-permute-start.1) | collective-permute-done | bytes 393248 | tf_op jit(solution)/shard_map/ppermute | solution.py:548
  59.0 4.0 %shard_map.160 = bf16[4,32,4,8,384]{4,3,2,1,0:T(8,128)(2,1)} custom-call(s32[16]{0:T(128)S(1)} %get-tuple-element.91.source_ref, s32[16]{0:T(128)S(1)} %get-tuple-element.95.rotation_ref, s32[16]{0:T(128)S(1)} %compare_convert_fusion.keep_ref, bf16[4,32,4,8,384]{4,3,2,1,0:T(8,128)(2,1)} %bitcast.5.i_ref), custom_call_target="tpu_custom_call" | custom-call | tf_op jit(solution)/shard_map/pallas_call | solution.py:92
  63.0 6.2 %all-to-all-start.1 = ((bf16[128,4,8,384]{3,2,1,0:T(8,128)(2,1)}), bf16[128,4,8,384]{3,2,1,0:T(8,128)(2,1)S(1)}, u32[]{:S(2)}, u32[]{:S(2)}) async-start(bf16[128,4,8,384]{3,2,1,0:T(8,128)(2,1)} %bitcast.32), calls=%async_computation.1 | async-start | bytes 6291456 | tf_op jit(solution)/shard_map/all_to_all | solution.py:564
  69.2 1.1 copy-done.17
  70.4 2.0 %copy-done.20 = bf16[768,2304]{1,0:T(8,128)(2,1)S(1)} copy-done((bf16[768,2304]{1,0:T(8,128)(2,1)S(1)}, bf16[768,2304]{1,0:T(8,128)(2,1)}, u32[]{:S(2)}) %copy-start.20) | copy-done | bytes 3538968
  72.4 1.5 %copy-done.22 = bf16[2,384,1152]{2,1,0:T(8,128)(2,1)S(1)} copy-done((bf16[2,384,1152]{2,1,0:T(8,128)(2,1)S(1)}, bf16[2,384,1152]{2,1,0:T(8,128)(2,1)}, u32[]{:S(2)}) %copy-start.22) | copy-done | bytes 1769496
  73.8 1.0 copy-done.24
  74.8 4.0 %shard_map.161.z_ref = f32[2,16,4,8,384]{4,3,2,1,0:T(8,128)S(1)} custom-call(s32[3,4]{1,0:T(4,128)S(1)} %add_convert_fusion.edge_ref, bf16[4,2,128,384]{3,2,1,0:T(8,128)(2,1)S(1)} %copy-done.17, bf16[4,128,384]{2,1,0:T(8,128)(2,1)S(1)} %collective-permute-done.near_ref, bf16[4,128,384]{2,1,0:T(8,128)(2,1)S(1)} %copy-done.24, ...), custom_call_target="tpu_custom_call" | custom-call | flops 2717908992 | bytes 6684672 | tf_op jit(solution)/shard_map/pallas_call | solution.py:117
  78.9 1.1 copy-done.14
  80.0 3.3 %copy-done = bf16[3,3,3,384,384]{4,3,2,1,0:T(8,128)(2,1)S(1)} copy-done((bf16[3,3,3,384,384]{4,3,2,1,0:T(8,128)(2,1)S(1)}, bf16[3,3,3,384,384]{4,3,2,1,0:T(8,128)(2,1)}, u32[]{:S(2)}) %copy-start) | copy-done | bytes 7962648
  83.2 1.5 %shard_map.163 = (bf16[1536,2304]{1,0:T(8,128)(2,1)S(1)}, bf16[2,768,1152]{2,1,0:T(8,128)(2,1)S(1)}) custom-call(bf16[3,3,3,384,384]{4,3,2,1,0:T(8,128)(2,1)S(1)} %copy-done), custom_call_target="tpu_custom_call" | custom-call | bytes 15925248 | tf_op jit(solution)/shard_map/pallas_call | solution.py:166
  84.8 2.8 %copy-done.2 = bf16[1536,2304]{1,0:T(8,128)(2,1)} copy-done((bf16[1536,2304]{1,0:T(8,128)(2,1)}, bf16[1536,2304]{1,0:T(8,128)(2,1)S(1)}, u32[]{:S(2)}) %copy-start.2) | copy-done | bytes 7077912
  87.6 1.8 %copy-done.4 = bf16[2,768,1152]{2,1,0:T(8,128)(2,1)} copy-done((bf16[2,768,1152]{2,1,0:T(8,128)(2,1)}, bf16[2,768,1152]{2,1,0:T(8,128)(2,1)S(1)}, u32[]{:S(2)}) %copy-start.4) | copy-done | bytes 3538968
  89.4 0.5 shard_map.164
  89.9 1.8 %copy-done.6 = bf16[768,2304]{1,0:T(8,128)(2,1)} copy-done((bf16[768,2304]{1,0:T(8,128)(2,1)}, bf16[768,2304]{1,0:T(8,128)(2,1)S(1)}, u32[]{:S(2)}) %copy-start.6) | copy-done | bytes 3538968
  91.7 1.3 copy-done.12
  93.0 1.5 %shard_map.162 = (bf16[1536,2304]{1,0:T(8,128)(2,1)S(1)}, bf16[2,768,1152]{2,1,0:T(8,128)(2,1)S(1)}) custom-call(bf16[3,3,3,384,384]{4,3,2,1,0:T(8,128)(2,1)S(1)} %bitcast.22), custom_call_target="tpu_custom_call" | custom-call | bytes 15925248 | tf_op jit(solution)/shard_map/pallas_call | solution.py:166
  94.6 2.9 %copy-done.3 = bf16[1536,2304]{1,0:T(8,128)(2,1)} copy-done((bf16[1536,2304]{1,0:T(8,128)(2,1)}, bf16[1536,2304]{1,0:T(8,128)(2,1)S(1)}, u32[]{:S(2)}) %copy-start.3) | copy-done | bytes 7077912
  97.5 1.8 %copy-done.8 = bf16[2,768,1152]{2,1,0:T(8,128)(2,1)} copy-done((bf16[2,768,1152]{2,1,0:T(8,128)(2,1)}, bf16[2,768,1152]{2,1,0:T(8,128)(2,1)S(1)}, u32[]{:S(2)}) %copy-start.8) | copy-done | bytes 3538968
  99.4 11.7 %all-to-all-done.1 = bf16[128,4,8,384]{3,2,1,0:T(8,128)(2,1)S(1)} async-done(((bf16[128,4,8,384]{3,2,1,0:T(8,128)(2,1)}), bf16[128,4,8,384]{3,2,1,0:T(8,128)(2,1)S(1)}, u32[]{:S(2)}, u32[]{:S(2)}) %all-to-all-start.1) | async-done | bytes 3145760 | tf_op jit(solution)/shard_map/all_to_all | solution.py:564
  111.1 1.3 dynamic-slice_bitcast_fusion
  112.4 0.2 dynamic-slice_bitcast_fusion.1
  112.6 1.0 collective-permute-start.3
  113.6 4.4 %collective-permute-start.6 = (bf16[2,16,4,8,384]{4,3,2,1,0:T(8,128)(2,1)S(1)}, bf16[2,16,4,8,384]{4,3,2,1,0:T(8,128)(2,1)S(1)}, u32[]{:S(2)}, u32[]{:S(2)}) collective-permute-start(bf16[2,16,4,8,384]{4,3,2,1,0:T(8,128)(2,1)S(1)} %get-tuple-element.93), channel_id=1, source_target_pairs={{0,31},{1,2},{2,1},{3,4},{4,3},{5,6},{6,5},{7,8},{8,7},{9,10},{10,... | collective-permute-start | bytes 2359304 | tf_op jit(solution)/shard_map/ppermute | solution.py:548
  118.0 2.1 %copy-done.9 = bf16[2,768,1152]{2,1,0:T(8,128)(2,1)S(1)} copy-done((bf16[2,768,1152]{2,1,0:T(8,128)(2,1)S(1)}, bf16[2,768,1152]{2,1,0:T(8,128)(2,1)}, u32[]{:S(2)}) %copy-start.9) | copy-done | bytes 3538968
  120.2 7.0 %shard_map.165 = (f32[2,16,4,8,384]{4,3,2,1,0:T(8,128)S(1)}, bf16[4,2,2,16,8,384]{5,4,3,2,1,0:T(8,128)(2,1)}, bf16[2,768,1152]{2,1,0:T(8,128)(2,1)S(1)}) custom-call(bf16[2,2,2,16,4,8,384]{6,5,4,3,2,1,0:T(8,128)(2,1)S(1)} %bitcast.25, bf16[1536,2304]{1,0:T(8,128)(2,1)} %copy-done.3, f32[2,16,4,8,384]{4,3,2,1,0:T(8,128)S(1)} %copy-done.15, ...), custom_call_target="tpu_custom_call" | custom-call | flops 3623878656 | bytes 7077888 | tf_op jit(solution)/shard_map/pallas_call | solution.py:117
  127.2 0.2 collective-permute-done.3.far_ref
  127.4 4.7 %shard_map.166 = (bf16[4,2,128,384]{3,2,1,0:T(8,128)(2,1)S(1)}, bf16[4,128,384]{2,1,0:T(8,128)(2,1)S(1)}, bf16[4,128,384]{2,1,0:T(8,128)(2,1)S(1)}, bf16[1536,2304]{1,0:T(8,128)(2,1)S(1)}) custom-call(s32[3,4]{1,0:T(4,128)S(1)} %add_convert_fusion.edge_ref, bf16[2,2,16,4,8,384]{5,4,3,2,1,0:T(8,128)(2,1)} %collective-permute-done.2.near_ref, ...), custom_call_target="tpu_custom_call" | custom-call | flops 1811939328 | bytes 3538944 | tf_op jit(solution)/shard_map/pallas_call | solution.py:117
  132.1 0.1 collective-permute-start.4
  132.2 1.2 collective-permute-start.5
  133.4 4.0 %shard_map.167 = (f32[2,16,4,8,384]{4,3,2,1,0:T(8,128)S(1)}, bf16[4,2,2,16,8,384]{5,4,3,2,1,0:T(8,128)(2,1)}) custom-call(bf16[2,2,2,16,4,8,384]{6,5,4,3,2,1,0:T(8,128)(2,1)S(1)} %bitcast.26, bf16[1536,2304]{1,0:T(8,128)(2,1)S(1)} %get-tuple-element.83.w_ref), custom_call_target="tpu_custom_call" | custom-call | flops 3623878656 | bytes 7077888 | tf_op jit(solution)/shard_map/pallas_call | solution.py:117
  137.4 5.9 %shard_map.168 = (f32[2,16,4,8,384]{4,3,2,1,0:T(8,128)S(1)}, bf16[4,2,2,16,8,384]{5,4,3,2,1,0:T(8,128)(2,1)}) custom-call(s32[3,4]{1,0:T(4,128)S(1)} %add_convert_fusion.edge_ref, bf16[2,2,16,4,8,384]{5,4,3,2,1,0:T(8,128)(2,1)} %collective-permute-done.2.near_ref, ...), custom_call_target="tpu_custom_call", output_to_operand_aliasing={{1}: (8, {})} | custom-call | flops 3623878656 | bytes 7077888 | tf_op jit(solution)/shard_map/pallas_call | solution.py:117
  143.4 3.1 %shard_map.169 = bf16[4,2,128,384]{3,2,1,0:T(8,128)(2,1)} custom-call(s32[3,4]{1,0:T(4,128)S(1)} %add_convert_fusion.edge_ref, bf16[4,128,384]{2,1,0:T(8,128)(2,1)S(1)} %collective-permute-done.4.near_ref, bf16[4,128,384]{2,1,0:T(8,128)(2,1)S(1)} %collective-permute-done.5.far_ref, bf16[2,384,1152]{2,1,0:T(8,128)(2,1)S(1)} %copy-done.13, ...), custom_call_target="tpu_custom_call" | custom-call | flops 905969664 | bytes 1769472 | tf_op jit(solution)/shard_map/pallas_call | solution.py:117
  (73 shorter events, 0.2 us)
Async XLA Ops:
  3.8 11.7 %copy-start.25 = (f32[384]{0:T(512)S(1)}, f32[384]{0:T(512)}, u32[]{:S(2)}) copy-start(f32[384]{0:T(512)} %param.17) | copy-start | bytes 4612
  3.8 11.8 %copy-start.29 = (s32[16]{0:T(128)S(1)}, s32[16]{0:T(128)}, u32[]{:S(2)}) copy-start(s32[16]{0:T(128)} %param.27) | copy-start | bytes 196
  3.8 11.8 %copy-start.30 = (s32[16]{0:T(128)S(1)}, s32[16]{0:T(128)}, u32[]{:S(2)}) copy-start(s32[16]{0:T(128)} %param.24) | copy-start | bytes 196
  3.8 11.8 %copy-start.31 = (s32[16]{0:T(128)S(1)}, s32[16]{0:T(128)}, u32[]{:S(2)}) copy-start(s32[16]{0:T(128)} %param.25) | copy-start | bytes 196
  3.9 11.8 %copy-start.32 = (s32[16]{0:T(128)S(1)}, s32[16]{0:T(128)}, u32[]{:S(2)}) copy-start(s32[16]{0:T(128)} %param.23) | copy-start | bytes 196
  3.9 11.8 %copy-start.33 = (s32[16]{0:T(128)S(1)}, s32[16]{0:T(128)}, u32[]{:S(2)}) copy-start(s32[16]{0:T(128)} %param.26) | copy-start | bytes 196
  3.9 12.1 %copy-start.10 = (bf16[4,2,128,384]{3,2,1,0:T(8,128)(2,1)S(1)}, bf16[4,2,128,384]{3,2,1,0:T(8,128)(2,1)}, u32[]{:S(2)}) copy-start(bf16[4,2,128,384]{3,2,1,0:T(8,128)(2,1)} %f_ref.3) | copy-start | bytes 2359300
  3.9 55.1 %all-to-all-start = ((bf16[128,4,8,384]{3,2,1,0:T(8,128)(2,1)}), bf16[128,4,8,384]{3,2,1,0:T(8,128)(2,1)}, u32[]{:S(2)}, u32[]{:S(2)}) async-start(bf16[128,4,8,384]{3,2,1,0:T(8,128)(2,1)} %bitcast.31), calls=%async_computation | async-start | bytes 6291456 | tf_op jit(solution)/shard_map/all_to_all | solution.py:553
  18.8 0.9 copy-start.16
  19.6 10.7 %collective-permute-start = (bf16[4,128,384]{2,1,0:T(8,128)(2,1)}, bf16[4,128,384]{2,1,0:T(8,128)(2,1)S(1)}, u32[]{:S(2)}, u32[]{:S(2)}) collective-permute-start(bf16[4,128,384]{2,1,0:T(8,128)(2,1)} %get-tuple-element.47), channel_id=1, source_target_pairs={{0,1},{1,0},{2,3},{3,2},{4,5},{5,4},{6,7},{7,6},{8,9},{9,8},{10,11... | collective-permute-start | bytes 1179656 | tf_op jit(solution)/shard_map/ppermute | solution.py:545
  19.6 39.3 %collective-permute-start.1 = (bf16[4,128,384]{2,1,0:T(8,128)(2,1)}, bf16[4,128,384]{2,1,0:T(8,128)(2,1)S(1)}, u32[]{:S(2)}, u32[]{:S(2)}) collective-permute-start(bf16[4,128,384]{2,1,0:T(8,128)(2,1)} %get-tuple-element.48), channel_id=1, source_target_pairs={{0,31},{1,2},{2,1},{3,4},{4,3},{5,6},{6,5},{7,8},{8,7},{9,10},{10,... | collective-permute-start | bytes 1179656 | tf_op jit(solution)/shard_map/ppermute | solution.py:548
  24.8 3.3 %copy-start.1 = (bf16[3,3,3,384,384]{4,3,2,1,0:T(8,128)(2,1)S(1)}, bf16[3,3,3,384,384]{4,3,2,1,0:T(8,128)(2,1)}, u32[]{:S(2)}) copy-start(bf16[3,3,3,384,384]{4,3,2,1,0:T(8,128)(2,1)} %w_ref.2) | copy-start | bytes 23887876
  28.6 1.8 %copy-start.19 = (bf16[768,2304]{1,0:T(8,128)(2,1)}, bf16[768,2304]{1,0:T(8,128)(2,1)S(1)}, u32[]{:S(2)}) copy-start(bf16[768,2304]{1,0:T(8,128)(2,1)S(1)} %get-tuple-element.57.wo_ref) | copy-start | bytes 10616836
  30.4 32.6 %copy-start.21 = (bf16[2,384,1152]{2,1,0:T(8,128)(2,1)}, bf16[2,384,1152]{2,1,0:T(8,128)(2,1)S(1)}, u32[]{:S(2)}) copy-start(bf16[2,384,1152]{2,1,0:T(8,128)(2,1)S(1)} %get-tuple-element.58.ws_ref) | copy-start | bytes 5308420
  59.0 4.0 %copy-start.23 = (bf16[4,128,384]{2,1,0:T(8,128)(2,1)}, bf16[4,128,384]{2,1,0:T(8,128)(2,1)S(1)}, u32[]{:S(2)}) copy-start(bf16[4,128,384]{2,1,0:T(8,128)(2,1)S(1)} %collective-permute-done.1.far_ref) | copy-start | bytes 1179652
  63.0 48.1 %all-to-all-start.1 = ((bf16[128,4,8,384]{3,2,1,0:T(8,128)(2,1)}), bf16[128,4,8,384]{3,2,1,0:T(8,128)(2,1)S(1)}, u32[]{:S(2)}, u32[]{:S(2)}) async-start(bf16[128,4,8,384]{3,2,1,0:T(8,128)(2,1)} %bitcast.32), calls=%async_computation.1 | async-start | bytes 6291456 | tf_op jit(solution)/shard_map/all_to_all | solution.py:564
  69.2 1.1 copy-start.17
  70.4 2.0 %copy-start.20 = (bf16[768,2304]{1,0:T(8,128)(2,1)S(1)}, bf16[768,2304]{1,0:T(8,128)(2,1)}, u32[]{:S(2)}) copy-start(bf16[768,2304]{1,0:T(8,128)(2,1)} %copy-done.19) | copy-start | bytes 10616836
  72.4 1.5 %copy-start.22 = (bf16[2,384,1152]{2,1,0:T(8,128)(2,1)S(1)}, bf16[2,384,1152]{2,1,0:T(8,128)(2,1)}, u32[]{:S(2)}) copy-start(bf16[2,384,1152]{2,1,0:T(8,128)(2,1)} %copy-done.21) | copy-start | bytes 5308420
  73.8 1.0 copy-start.24
  78.8 1.1 copy-start.14
  80.0 3.3 %copy-start = (bf16[3,3,3,384,384]{4,3,2,1,0:T(8,128)(2,1)S(1)}, bf16[3,3,3,384,384]{4,3,2,1,0:T(8,128)(2,1)}, u32[]{:S(2)}) copy-start(bf16[3,3,3,384,384]{4,3,2,1,0:T(8,128)(2,1)} %w_ref.4) | copy-start | bytes 23887876
  83.2 9.8 %slice-start = ((s8[7962624]{0:T(1024)(128)(4,1)}), s8[4194304]{0:T(1024)(128)(4,1)S(1)}, s32[]{:S(2)}) async-start(s8[7962624]{0:T(1024)(128)(4,1)} %bitcast.21), calls=%async_computation.2 | async-start | bytes 8388608
  84.8 2.8 %copy-start.2 = (bf16[1536,2304]{1,0:T(8,128)(2,1)}, bf16[1536,2304]{1,0:T(8,128)(2,1)S(1)}, u32[]{:S(2)}) copy-start(bf16[1536,2304]{1,0:T(8,128)(2,1)S(1)} %get-tuple-element.74.later_ref) | copy-start | bytes 21233668
  87.6 1.8 %copy-start.4 = (bf16[2,768,1152]{2,1,0:T(8,128)(2,1)}, bf16[2,768,1152]{2,1,0:T(8,128)(2,1)S(1)}, u32[]{:S(2)}) copy-start(bf16[2,768,1152]{2,1,0:T(8,128)(2,1)S(1)} %get-tuple-element.80.w_ref) | copy-start | bytes 10616836
  89.4 3.6 %slice-start.1 = ((s8[7962624]{0:T(1024)(128)(4,1)}), s8[3768320]{0:T(1024)(128)(4,1)S(1)}, s32[]{:S(2)}) async-start(s8[7962624]{0:T(1024)(128)(4,1)} %bitcast.21), calls=%async_computation.3 | async-start | bytes 7536640
  89.9 1.8 %copy-start.6 = (bf16[768,2304]{1,0:T(8,128)(2,1)}, bf16[768,2304]{1,0:T(8,128)(2,1)S(1)}, u32[]{:S(2)}) copy-start(bf16[768,2304]{1,0:T(8,128)(2,1)S(1)} %get-tuple-element.81.wa_ref) | copy-start | bytes 10616836
  91.7 1.3 copy-start.12
  94.6 2.9 %copy-start.3 = (bf16[1536,2304]{1,0:T(8,128)(2,1)}, bf16[1536,2304]{1,0:T(8,128)(2,1)S(1)}, u32[]{:S(2)}) copy-start(bf16[1536,2304]{1,0:T(8,128)(2,1)S(1)} %get-tuple-element.69.w_ref) | copy-start | bytes 21233668
  97.5 1.8 %copy-start.8 = (bf16[2,768,1152]{2,1,0:T(8,128)(2,1)}, bf16[2,768,1152]{2,1,0:T(8,128)(2,1)S(1)}, u32[]{:S(2)}) copy-start(bf16[2,768,1152]{2,1,0:T(8,128)(2,1)S(1)} %get-tuple-element.71.sides_ref) | copy-start | bytes 10616836
  111.1 2.5 %copy-start.26 = (f32[384]{0:T(512)S(1)}, f32[384]{0:T(512)}, u32[]{:S(2)}) copy-start(f32[384]{0:T(512)} %param.21) | copy-start | bytes 4612
  111.1 2.5 %copy-start.27 = (f32[384]{0:T(512)S(1)}, f32[384]{0:T(512)}, u32[]{:S(2)}) copy-start(f32[384]{0:T(512)} %param.18) | copy-start | bytes 4612
  111.1 2.5 %copy-start.28 = (f32[384]{0:T(512)S(1)}, f32[384]{0:T(512)}, u32[]{:S(2)}) copy-start(f32[384]{0:T(512)} %param.22) | copy-start | bytes 4612
  112.4 15.0 %collective-permute-start.2 = (bf16[2,2,16,4,8,384]{5,4,3,2,1,0:T(8,128)(2,1)}, bf16[2,2,16,4,8,384]{5,4,3,2,1,0:T(8,128)(2,1)}, u32[]{:S(2)}, u32[]{:S(2)}) collective-permute-start(bf16[2,2,16,4,8,384]{5,4,3,2,1,0:T(8,128)(2,1)} %dynamic-slice_bitcast_fusion), channel_id=1, source_target_pairs={{0,1},{1,0},{2,3},{3,2},{4,5},{5,4},{6,7},{7,6},{8,9},{9,8},{10,11... | collective-permute-start | bytes 4718600 | tf_op jit(solution)/shard_map/ppermute | solution.py:545
  112.4 5.6 %copy-start.15 = (f32[2,16,4,8,384]{4,3,2,1,0:T(8,128)S(1)}, f32[2,16,4,8,384]{4,3,2,1,0:T(8,128)}, u32[]{:S(2)}) copy-start(f32[2,16,4,8,384]{4,3,2,1,0:T(8,128)} %copy-done.14) | copy-start | bytes 4718596
  112.4 5.6 %copy-start.18 = (bf16[4,2,128,384]{3,2,1,0:T(8,128)(2,1)S(1)}, bf16[4,2,128,384]{3,2,1,0:T(8,128)(2,1)}, u32[]{:S(2)}) copy-start(bf16[4,2,128,384]{3,2,1,0:T(8,128)(2,1)} %copy-done.16) | copy-start | bytes 2359300
  112.6 14.8 %collective-permute-start.3 = (bf16[2,16,4,8,384]{4,3,2,1,0:T(8,128)(2,1)S(1)}, bf16[2,16,4,8,384]{4,3,2,1,0:T(8,128)(2,1)S(1)}, u32[]{:S(2)}, u32[]{:S(2)}) collective-permute-start(bf16[2,16,4,8,384]{4,3,2,1,0:T(8,128)(2,1)S(1)} %get-tuple-element.94), channel_id=1, source_target_pairs={{0,31},{1,2},{2,1},{3,4},{4,3},{5,6},{6,5},{7,8},{8,7},{9,10},{10,... | collective-permute-start | bytes 2359304 | tf_op jit(solution)/shard_map/ppermute | solution.py:548
  113.6 23.8 %collective-permute-start.6 = (bf16[2,16,4,8,384]{4,3,2,1,0:T(8,128)(2,1)S(1)}, bf16[2,16,4,8,384]{4,3,2,1,0:T(8,128)(2,1)S(1)}, u32[]{:S(2)}, u32[]{:S(2)}) collective-permute-start(bf16[2,16,4,8,384]{4,3,2,1,0:T(8,128)(2,1)S(1)} %get-tuple-element.93), channel_id=1, source_target_pairs={{0,31},{1,2},{2,1},{3,4},{4,3},{5,6},{6,5},{7,8},{8,7},{9,10},{10,... | collective-permute-start | bytes 2359304 | tf_op jit(solution)/shard_map/ppermute | solution.py:548
  118.0 9.4 %slice-start.2 = ((s8[7077888]{0:T(1024)(128)(4,1)}), s8[4194304]{0:T(1024)(128)(4,1)S(1)}, s32[]{:S(2)}) async-start(s8[7077888]{0:T(1024)(128)(4,1)} %bitcast.27), calls=%async_computation.4 | async-start | bytes 8388608
  118.0 2.2 %copy-start.9 = (bf16[2,768,1152]{2,1,0:T(8,128)(2,1)S(1)}, bf16[2,768,1152]{2,1,0:T(8,128)(2,1)}, u32[]{:S(2)}) copy-start(bf16[2,768,1152]{2,1,0:T(8,128)(2,1)} %copy-done.8) | copy-start | bytes 10616836
  120.2 7.2 %slice-start.3 = ((s8[7077888]{0:T(1024)(128)(4,1)}), s8[2883584]{0:T(1024)(128)(4,1)S(1)}, s32[]{:S(2)}) async-start(s8[7077888]{0:T(1024)(128)(4,1)} %bitcast.27), calls=%async_computation.5 | async-start | bytes 5767168
  132.1 11.3 %collective-permute-start.4 = (bf16[4,128,384]{2,1,0:T(8,128)(2,1)S(1)}, bf16[4,128,384]{2,1,0:T(8,128)(2,1)S(1)}, u32[]{:S(2)}, u32[]{:S(2)}) collective-permute-start(bf16[4,128,384]{2,1,0:T(8,128)(2,1)S(1)} %get-tuple-element.75), channel_id=1, source_target_pairs={{0,1},{1,0},{2,3},{3,2},{4,5},{5,4},{6,7},{7,6},{8,9},{9,8},{10,11... | collective-permute-start | bytes 1179656 | tf_op jit(solution)/shard_map/ppermute | solution.py:545
  132.2 11.2 %collective-permute-start.5 = (bf16[4,128,384]{2,1,0:T(8,128)(2,1)S(1)}, bf16[4,128,384]{2,1,0:T(8,128)(2,1)S(1)}, u32[]{:S(2)}, u32[]{:S(2)}) collective-permute-start(bf16[4,128,384]{2,1,0:T(8,128)(2,1)S(1)} %get-tuple-element.76), channel_id=1, source_target_pairs={{0,31},{1,2},{2,1},{3,4},{4,3},{5,6},{6,5},{7,8},{8,7},{9,10},{10,... | collective-permute-start | bytes 1179656 | tf_op jit(solution)/shard_map/ppermute | solution.py:548
  133.4 4.0 %copy-start.5 = (bf16[2,768,1152]{2,1,0:T(8,128)(2,1)S(1)}, bf16[2,768,1152]{2,1,0:T(8,128)(2,1)}, u32[]{:S(2)}) copy-start(bf16[2,768,1152]{2,1,0:T(8,128)(2,1)} %copy-done.4) | copy-start | bytes 10616836
  133.4 4.0 %copy-start.7 = (bf16[768,2304]{1,0:T(8,128)(2,1)S(1)}, bf16[768,2304]{1,0:T(8,128)(2,1)}, u32[]{:S(2)}) copy-start(bf16[768,2304]{1,0:T(8,128)(2,1)} %copy-done.6) | copy-start | bytes 10616836
  137.4 5.9 %copy-start.11 = (bf16[4,2,128,384]{3,2,1,0:T(8,128)(2,1)S(1)}, bf16[4,2,128,384]{3,2,1,0:T(8,128)(2,1)}, u32[]{:S(2)}) copy-start(bf16[4,2,128,384]{3,2,1,0:T(8,128)(2,1)} %f_ref.3) | copy-start | bytes 2359300
  137.4 5.9 %copy-start.13 = (bf16[2,384,1152]{2,1,0:T(8,128)(2,1)S(1)}, bf16[2,384,1152]{2,1,0:T(8,128)(2,1)}, u32[]{:S(2)}) copy-start(bf16[2,384,1152]{2,1,0:T(8,128)(2,1)} %copy-done.12) | copy-start | bytes 5308420

commit v11 on v10

--- a/solution.py
+++ b/solution.py
@@ -103,8 +103,9 @@
 
 
 VMEM_LIMIT = 16 << 20
-LIMIT_A = 34
-LIMIT_B = 16
+LIMIT_A = 40
+LIMIT_B = 40
+LIMIT_C = 34
 
 
 def call(body, out_shape, operands, scalars=(), scratch=(), flops=0, moved=0, far=(), far_out=(), aliases=None, limit=VMEM_LIMIT):
@@ -126,25 +127,25 @@
     )(*scalars, *operands)
 
 
-def spread(weight, past):
-    n_t, n_y, n_x, ci, co = weight.shape
+def spread(weight, own_times, side_times):
+    _, n_y, n_x, ci, co = weight.shape
     wide = n_x * co
-    times = n_t - 1 if past else 1
-
-    def body(w_ref, own_ref, side_ref):
+    n_own, n_side = len(own_times), len(side_times)
+
+    def body(own_in, side_in, own_ref, side_ref):
         dy = pl.program_id(0)
 
         def side(y):
             for x in range(n_x):
-                for t in range(times):
-                    side_ref[y, t * ci : (t + 1) * ci, x * co : (x + 1) * co] = w_ref[t, 0, x]
+                for t in range(n_side):
+                    side_ref[y, t * ci : (t + 1) * ci, x * co : (x + 1) * co] = side_in[t, 0, x]
 
         def own(row, y):
             for x in range(n_x):
-                for t in range(times):
-                    lo = (row * times + t) * ci
+                for t in range(n_own):
+                    lo = (row * n_own + t) * ci
                     at = y * wide + x * co
-                    own_ref[lo : lo + ci, at : at + co] = w_ref[t, 0, x]
+                    own_ref[lo : lo + ci, at : at + co] = own_in[t, 0, x]
 
         @pl.when(dy == 0)
         def _():
@@ -161,17 +162,20 @@
             side(1)
             own(1, 0)
 
-    shapes = [(2 * times * ci, 2 * wide), (2, times * ci, wide)]
-    first = 0 if past else n_t - 1
+    def part(times):
+        n = len(times)
+        return pl.BlockSpec((n, 1, n_x, ci, co), lambda y, at=times[0] // n: (at, y, 0, 0, 0))
+
+    shapes = [(2 * n_own * ci, 2 * wide), (2, n_side * ci, wide)]
     return pl.pallas_call(
         body,
         grid=(n_y,),
-        in_specs=[pl.BlockSpec((times, 1, n_x, ci, co), lambda y: (first, y, 0, 0, 0))],
+        in_specs=[part(own_times), part(side_times)],
         out_specs=[pl.BlockSpec(memory_space=pltpu.VMEM) for _ in shapes],
         out_shape=[jax.ShapeDtypeStruct(shape, weight.dtype) for shape in shapes],
         cost_estimate=pl.CostEstimate(flops=0, bytes_accessed=4 * weight.size, transcendentals=0),
-        compiler_params=pltpu.CompilerParams(vmem_limit_bytes=16 << 20),
-    )(weight)
+        compiler_params=pltpu.CompilerParams(vmem_limit_bytes=20 << 20),
+    )(weight, weight)
 
 
 def activated(values, gain):
@@ -369,43 +373,6 @@
     )
 
 
-def own_second(got, weight):
-    n_rows, _, n_frames, blocks, n_slots, _, ch = got.shape
-    half = blocks * n_slots * CB
-    deep = n_frames * ch
-
-    def body(got_ref, w_ref, o_ref, next_ref, lhs, acc, keep_sems):
-        keeps = []
-        for r in range(n_rows):
-            for s in range(n_slots):
-                src = got_ref.at[r, 1, n_frames - 1, :, s]
-                n = r * n_slots + s
-                keeps.append(pltpu.make_async_copy(src, next_ref.at[s, 0, r], keep_sems.at[n]))
-                keeps[-1].start()
-        own_rows(got_ref, 1, lhs)
-        acc[...] = dot(lhs[...], w_ref[...])
-        give_rows(acc, ch, o_ref, None)
-        for c in keeps:
-            c.wait()
-
-    return call(
-        body,
-        [
-            sums_shape(blocks, n_slots, n_rows, ch),
-            jax.ShapeDtypeStruct((n_slots, 2, n_rows, blocks, CB, ch), jnp.bfloat16),
-        ],
-        (got, weight),
-        scratch=[
-            pltpu.VMEM((half, n_rows * deep), jnp.bfloat16),
-            pltpu.VMEM((half, weight.shape[1]), jnp.float32),
-            pltpu.SemaphoreType.DMA((n_rows * n_slots,)),
-        ],
-        flops=2 * half * weight.size,
-        moved=2 * weight.size,
-        far_out=(1,),
-    )
-
-
 def side_sums(edge_ref, k, side_ref, w, lhs):
     n_frames, blocks, n_slots, _, ch = side_ref.shape
     for s in range(n_slots):
@@ -419,11 +386,12 @@
 def second_activation(near, far, w_sides, sums, bias, gain, later, edges):
     n_frames, blocks, n_slots, _, ch = far.shape
     n_rows, n_cols, deep = sums.shape[0], blocks * CB, n_frames * ch
+    first = later.shape[0] // 2
 
     def body(edge_ref, near_ref, far_ref, w_ref, z_ref, b_ref, g_ref, later_ref, o_ref, near_out, far_out, fetched_ref, lhs, sem):
-        fetch = pltpu.make_async_copy(later_ref, fetched_ref, sem)
+        fetch = pltpu.make_async_copy(later_ref.at[pl.ds(0, first)], fetched_ref, sem)
         fetch.start()
-        for (side, y), out in zip(beside(edge_ref, near_ref.at[0], far_ref), (near_out, far_out)):
+        for (side, y), out in zip(beside(edge_ref, near_ref, far_ref), (near_out, far_out)):
             total = side_sums(edge_ref, y, side, w_ref[y], lhs) + z_ref[y] + b_ref[...]
             for s in range(n_slots):
                 value = activated(total[:, s].reshape(n_cols, ch), g_ref[...]).astype(jnp.bfloat16)
@@ -434,7 +402,7 @@
     row = jax.ShapeDtypeStruct((n_slots, n_cols, ch), jnp.bfloat16)
     return call(
         body,
-        [jax.ShapeDtypeStruct((n_slots, n_rows, n_cols, ch), jnp.bfloat16), row, row, jax.ShapeDtypeStruct(later.shape, later.dtype)],
+        [jax.ShapeDtypeStruct((n_slots, n_rows, n_cols, ch), jnp.bfloat16), row, row, jax.ShapeDtypeStruct((first, later.shape[1]), later.dtype)],
         (near, far, w_sides, sums, bias, gain, later),
         scalars=(edges,),
         scratch=[
@@ -448,33 +416,59 @@
     )
 
 
-def before_sides(near, far, act, w_sides, w_act, sums, kept, edges):
+def before_sides(near, far, got, act, w_first, w_own, w_sides, edges):
     n_frames, blocks, n_slots, _, ch = far.shape
-    n_rows, n_cols, deep = sums.shape[0], blocks * CB, n_frames * ch
-
-    def body(edge_ref, near_ref, far_ref, act_ref, tiles_ref, w_ref, wa_ref, z_ref, kept_ref, o_ref, next_ref, lhs, lhs2, sem):
-        copy = pltpu.make_async_copy(tiles_ref, next_ref.at[:, 1], sem)
-        copy.start()
-        add_own(act_ref, wa_ref, lhs2, o_ref, z_ref)
-        for side, y in beside(edge_ref, near_ref.at[1], far_ref):
-            o_ref[y] += side_sums(edge_ref, y, side, w_ref[y], lhs)
-        copy.wait()
+    n_rows = act.shape[1]
+    half, deep = blocks * n_slots * CB, n_frames * ch
+    row_deep = deep + ch
+    tiles = act.reshape(n_slots, n_rows, blocks, CB, ch)
+
+    def body(edge_ref, near_ref, far_ref, got_ref, act_ref, tiles_ref, w1_ref, w_ref, ws_ref, o_ref, next_ref, w2, lhs, side, acc, sems, keep_sems):
+        load = pltpu.make_async_copy(w_ref.at[pl.ds(row_deep, row_deep)], w2, sems.at[0])
+        load.start()
+        keeps = [pltpu.make_async_copy(tiles_ref, next_ref.at[:, 1], sems.at[1])]
+        for r in range(n_rows):
+            for s in range(n_slots):
+                src = got_ref.at[r, 1, n_frames - 1, :, s]
+                n = r * n_slots + s
+                keeps.append(pltpu.make_async_copy(src, next_ref.at[s, 0, r], keep_sems.at[n]))
+        for r in range(n_rows):
+            for f in range(n_frames):
+                lhs[r, :, :, :, f * ch : (f + 1) * ch] = got_ref[r, 1, f]
+            for s in range(n_slots):
+                lhs[r, :, s, :, deep:row_deep] = act_ref[s, r].reshape(blocks, CB, ch)
+        acc[...] = dot(lhs[0].reshape(half, row_deep), w1_ref[...])
+        load.wait()
+        for c in keeps:
+            c.start()
+        acc[...] += dot(lhs[1].reshape(half, row_deep), w2[...])
+        give_rows(acc, ch, o_ref, None)
+        for rows, y in beside(edge_ref, near_ref, far_ref):
+            o_ref[y] += side_sums(edge_ref, y, rows, ws_ref[y], side)
+        for c in keeps:
+            c.wait()
 
     return call(
         body,
-        [jax.ShapeDtypeStruct(sums.shape, jnp.float32), jax.ShapeDtypeStruct(kept.shape, kept.dtype)],
-        (near, far, act, act.reshape(n_slots, n_rows, blocks, CB, ch), w_sides, w_act, sums, kept),
+        [
+            sums_shape(blocks, n_slots, n_rows, ch),
+            jax.ShapeDtypeStruct((n_slots, 2, n_rows, blocks, CB, ch), jnp.bfloat16),
+        ],
+        (near, far, got, act, tiles, w_first, w_own, w_sides),
         scalars=(edges,),
         scratch=[
+            pltpu.VMEM(w_first.shape, w_first.dtype),
+            pltpu.VMEM((n_rows, blocks, n_slots, CB, row_deep), jnp.bfloat16),
             pltpu.VMEM((blocks, n_slots, CB, deep), jnp.bfloat16),
-            pltpu.VMEM((n_slots * n_cols, n_rows * ch), jnp.bfloat16),
-            pltpu.SemaphoreType.DMA,
-        ],
-        flops=2 * n_slots * n_cols * (w_sides.size + w_act.size),
-        moved=2 * (w_sides.size + w_act.size),
-        far=(7,),
+            pltpu.VMEM((half, w_own.shape[1]), jnp.float32),
+            pltpu.SemaphoreType.DMA((2,)),
+            pltpu.SemaphoreType.DMA((n_rows * n_slots,)),
+        ],
+        flops=2 * half * (w_own.size + w_sides.size),
+        moved=2 * (w_own.size + w_sides.size),
+        far=(6,),
         far_out=(1,),
-        aliases={8: 1},
+        limit=LIMIT_C << 20,
     )
 
 
@@ -552,7 +546,7 @@
     sent = pack(cache_first, cache_second).reshape(n_groups * n_tiles, n_slots, CB, ch)
     held = lax.all_to_all(sent, BOTH, 0, 0, tiled=True)
 
-    act_own_1, act_sides_1 = spread(conv_first, False)
+    act_own_1, act_sides_1 = spread(conv_first, [2], [2])
     act_first, near, far = first_activation(frame_in, gain_first[None], edges)
     act_near, act_far = swap_near(near), swap_far(far)
     held, act_first, act_near, act_far, act_own_1, act_sides_1 = lax.optimization_barrier(
@@ -566,29 +560,27 @@
     )
     sums_1 = current_part(act_later, act_near, act_far, act_own_1, act_sides_1, edges)
     sums_1, conv_first, conv_second = lax.optimization_barrier((sums_1, conv_first, conv_second))
-    act_own_2, act_sides_2 = spread(conv_second, False)
-    own_1, sides_1 = spread(conv_first, True)
-    own_2, sides_2 = spread(conv_second, True)
-    got, sums_1, own_1, own_2, sides_1, sides_2, act_own_2, act_sides_2 = lax.optimization_barrier(
-        (got, sums_1, own_1, own_2, sides_1, sides_2, act_own_2, act_sides_2)
+    own_1, sides_1 = spread(conv_first, [0, 1], [0, 1])
+    own_2, sides_2 = spread(conv_second, [0, 1, 2], [0, 1])
+    act_sides_2 = conv_second[2, 0::2].transpose(0, 2, 1, 3).reshape(2, ch, 3 * ch)
+    got, sums_1, own_1, own_2, sides_1, sides_2, act_sides_2 = lax.optimization_barrier(
+        (got, sums_1, own_1, own_2, sides_1, sides_2, act_sides_2)
     )
     got = got.reshape(n_rows, 2, 2, blocks, n_slots, CB, ch)
 
-    def picked(row):
-        return lax.dynamic_index_in_dim(got, row, 0, keepdims=False)
-
-    rows_near, rows_far = swap_near(picked(1 - odd)), picked(odd)
-    far_1, far_2 = swap_far(rows_far[0]), swap_far(rows_far[1])
+    def picked(cache, row):
+        return lax.dynamic_index_in_dim(got[:, cache], row, 0, keepdims=False)
+
+    near_1, far_1 = swap_near(picked(0, 1 - odd)), swap_far(picked(0, odd))
+    near_2, far_2 = swap_near(picked(1, 1 - odd)), swap_far(picked(1, odd))
     act_tiles = act_first.reshape(n_slots, n_rows, blocks, CB, ch)
     sums_1, next_first, sides_1 = own_first(got, own_1, sums_1, act_tiles, sides_1)
-    act_second, near, far, own_2 = second_activation(
-        rows_near, far_1, sides_1, sums_1, bias_first[None], gain_second[None], own_2, edges
+    act_second, near, far, own_first_half = second_activation(
+        near_1, far_1, sides_1, sums_1, bias_first[None], gain_second[None], own_2, edges
     )
     act_near, act_far = swap_near(near), swap_far(far)
-    got_later, act_later = lax.optimization_barrier((got, act_second))
-    sums_2, kept = own_second(got_later, own_2)
     sums_2, next_second = before_sides(
-        rows_near, far_2, act_later, sides_2, act_own_2, sums_2, kept, edges
+        near_2, far_2, got, act_second, own_first_half, own_2, sides_2, edges
     )
     mixed_frame = last_part(
         act_near, act_far, act_sides_2, sums_2, bias_second[None], frame_in, edges

time: 147 us -> 171 us (1.16)
  local copies, waits for them, and re-layouts: 32.2 us -> 60.7 us
  waiting for transfers between devices: 40.5 us -> 28.6 us
  starting transfers between devices: 29.8 us -> 33.4 us
  Pallas kernels: 42.6 us -> 45.3 us
    optimization_barrier x0 -> x2, local copies, waits for them, and re-layouts: none -> 18.9 us  [the longest x1 15 us: local(): lax.optimization_barrier((sums_1, conv_first, conv_second))]
    all_to_all x1, waiting for transfers between devices: 11.7 us -> 0.01 us  [local(): lax.all_to_all(moved.reshape(n_groups * n_tiles, n_slots, CB, ch), BOTH,...]
    slice x0 -> x2, local copies, waits for them, and re-layouts: none -> 4.53 us  [the longest x1 4.21 us: local(): conv_second[2, 0::2].transpose(0, 2, 1, 3).reshape(2, ch, 3 * ch)]
    unnamed x76 -> x64, local copies, waits for them, and re-layouts: 30.6 us -> 34.5 us
    ppermute x4, starting transfers between devices: 11.8 us -> 15.1 us  [swap_far(): lax.ppermute(row, 'tile', [(i, (i + 2 * (i % 2) - 1) % n_tiles) for i in...]
    pallas_call x7 -> x6, Pallas kernels: 31.3 us -> 32.7 us  [call(): pl.pallas_call(body, in_specs=in_specs, out_specs=out_specs, out_shape=li...]
    pallas_call x4 -> x3, Pallas kernels: 4.11 us -> 5.24 us  [spread(): pl.pallas_call(body, grid=(n_y,), in_specs=[part(own_times), part(side_ti...]
  transfers between devices with their start and end apart: 9 -> 10, of which waited for: 3 -> 1; matrix products, arithmetic and copies ran while one was open for 0% -> 15% of each run, Pallas kernels for 22% -> 21%
where the time goes in v11:
time: 171 us; the launch traced here: 169 us
  local copies, waits for them, and re-layouts  60.7 us (35%)
  Pallas kernels  45.3 us (26%)
  starting transfers between devices  33.4 us (20%)
  waiting for transfers between devices  28.6 us (17%)
    unnamed x64, local copies, waits for them, and re-layouts  34.5 us
    pallas_call x6, Pallas kernels, call(): pl.pallas_call(body, in_specs=in_specs, out_specs=out_specs, out_shape=li...  32.7 us
    ppermute x4, waiting for transfers between devices, swap_far(): lax.ppermute(row, 'tile', [(i, (i + 2 * (i % 2) - 1) % n_tiles) for i in...  28.6 us
    ppermute x4, starting transfers between devices, swap_far(): lax.ppermute(row, 'tile', [(i, (i + 2 * (i % 2) - 1) % n_tiles) for i in...  15.1 us
    optimization_barrier x1, local copies, waits for them, and re-layouts, local(): lax.optimization_barrier((sums_1, conv_first, conv_second))  15 us
    all_to_all x1, starting transfers between devices, local(): held = lax.all_to_all(sent, BOTH, 0, 0, tiled=True)  11.6 us
    all_to_all x1, starting transfers between devices, local(): lax.all_to_all(moved.reshape(n_groups * n_tiles, n_slots, CB, ch), BOTH,...  6.01 us
    pallas_call x3, Pallas kernels, spread(): pl.pallas_call(body, grid=(n_y,), in_specs=[part(own_times), part(side_ti...  5.24 us
  transfers between devices with their start and end apart: 10, of which 1 were waited for; matrix products, arithmetic and copies ran while one was open for 15% of the time, Pallas kernels for 21%

profile of v11, /device:TPU:0, one launch (start us, length us, event | category | flops | bytes accessed | tf_op | source)
XLA Modules:
  0.0 169.3 jit_solution(15562645721245681015)
XLA Ops:
  0.6 3.1 %shard_map.157 = bf16[2,2,2,16,4,8,384]{6,5,4,3,2,1,0:T(8,128)(2,1)} custom-call(bf16[4,2,2,16,8,384]{5,4,3,2,1,0:T(8,128)(2,1)} %bitcast.36, bf16[4,2,2,16,8,384]{5,4,3,2,1,0:T(8,128)(2,1)} %bitcast.37), custom_call_target="tpu_custom_call" | custom-call | tf_op jit(solution)/shard_map/pallas_call | solution.py:47
  3.7 0.0 copy-start.27
  3.7 0.0 copy-start.28
  3.8 11.6 %all-to-all-start = ((bf16[128,4,8,384]{3,2,1,0:T(8,128)(2,1)}), bf16[128,4,8,384]{3,2,1,0:T(8,128)(2,1)}, u32[]{:S(2)}, u32[]{:S(2)}) async-start(bf16[128,4,8,384]{3,2,1,0:T(8,128)(2,1)} %bitcast.33), calls=%async_computation | async-start | bytes 6291456 | tf_op jit(solution)/shard_map/all_to_all | solution.py:547
  15.5 0.1 pad.2.clone
  15.6 0.1 select_reduce_fusion
  15.7 0.1 compare_bitcast_fusion.1
  15.8 0.1 add_convert_fusion.edge_ref
  15.9 2.8 %shard_map.158 = (bf16[4,2,128,384]{3,2,1,0:T(8,128)(2,1)S(1)}, bf16[4,128,384]{2,1,0:T(8,128)(2,1)}, bf16[4,128,384]{2,1,0:T(8,128)(2,1)}) custom-call(s32[3,4]{1,0:T(4,128)S(1)} %add_convert_fusion.edge_ref, bf16[4,2,128,384]{3,2,1,0:T(8,128)(2,1)S(1)} %copy-done.8, f32[1,384]{1,0:T(1,128)S(1)} %broadcast_in_dim.53.g_ref), custom_call_target="tpu_custom_call" | custom-call | flops 3932160 | bytes 2359296 | tf_op jit(solution)/shard_map/pallas_call | solution.py:118
  18.7 0.9 copy-done.12
  19.5 5.2 %collective-permute-start.1 = (bf16[4,128,384]{2,1,0:T(8,128)(2,1)}, bf16[4,128,384]{2,1,0:T(8,128)(2,1)S(1)}, u32[]{:S(2)}, u32[]{:S(2)}) collective-permute-start(bf16[4,128,384]{2,1,0:T(8,128)(2,1)} %get-tuple-element.41), channel_id=1, source_target_pairs={{0,31},{1,2},{2,1},{3,4},{4,3},{5,6},{6,5},{7,8},{8,7},{9,10},{10,... | collective-permute-start | bytes 1179656 | tf_op jit(solution)/shard_map/ppermute | solution.py:542
  24.7 3.3 %copy-done = bf16[3,3,3,384,384]{4,3,2,1,0:T(8,128)(2,1)S(1)} copy-done((bf16[3,3,3,384,384]{4,3,2,1,0:T(8,128)(2,1)S(1)}, bf16[3,3,3,384,384]{4,3,2,1,0:T(8,128)(2,1)}, u32[]{:S(2)}) %copy-start) | copy-done | bytes 7962648
  28.0 0.5 shard_map.159
  28.5 1.7 %copy-done.17 = bf16[768,2304]{1,0:T(8,128)(2,1)} copy-done((bf16[768,2304]{1,0:T(8,128)(2,1)}, bf16[768,2304]{1,0:T(8,128)(2,1)S(1)}, u32[]{:S(2)}) %copy-start.17) | copy-done | bytes 3538968
  30.3 28.6 %collective-permute-done.1.far_ref = bf16[4,128,384]{2,1,0:T(8,128)(2,1)S(1)} collective-permute-done((bf16[4,128,384]{2,1,0:T(8,128)(2,1)}, bf16[4,128,384]{2,1,0:T(8,128)(2,1)S(1)}, u32[]{:S(2)}, u32[]{:S(2)}) %collective-permute-start.1) | collective-permute-done | bytes 393248 | tf_op jit(solution)/shard_map/ppermute | solution.py:542
  58.9 4.3 %shard_map.160 = bf16[4,32,4,8,384]{4,3,2,1,0:T(8,128)(2,1)} custom-call(s32[16]{0:T(128)S(1)} %get-tuple-element.77.source_ref, s32[16]{0:T(128)S(1)} %get-tuple-element.85.rotation_ref, s32[16]{0:T(128)S(1)} %compare_convert_fusion.keep_ref, bf16[4,32,4,8,384]{4,3,2,1,0:T(8,128)(2,1)} %bitcast.5.i_ref), custom_call_target="tpu_custom_call" | custom-call | tf_op jit(solution)/shard_map/pallas_call | solution.py:92
  63.2 6.0 %all-to-all-start.1 = ((bf16[128,4,8,384]{3,2,1,0:T(8,128)(2,1)}), bf16[128,4,8,384]{3,2,1,0:T(8,128)(2,1)S(1)}, u32[]{:S(2)}, u32[]{:S(2)}) async-start(bf16[128,4,8,384]{3,2,1,0:T(8,128)(2,1)} %bitcast.34), calls=%async_computation.1 | async-start | bytes 6291456 | tf_op jit(solution)/shard_map/all_to_all | solution.py:558
  69.2 1.1 copy-done.13
  70.4 2.0 %copy-done.18 = bf16[768,2304]{1,0:T(8,128)(2,1)S(1)} copy-done((bf16[768,2304]{1,0:T(8,128)(2,1)S(1)}, bf16[768,2304]{1,0:T(8,128)(2,1)}, u32[]{:S(2)}) %copy-start.18) | copy-done | bytes 3538968
  72.4 1.5 copy-done.20
  73.8 1.0 copy-done.22
  74.8 4.0 %shard_map.161.z_ref = f32[2,16,4,8,384]{4,3,2,1,0:T(8,128)S(1)} custom-call(s32[3,4]{1,0:T(4,128)S(1)} %add_convert_fusion.edge_ref, bf16[4,2,128,384]{3,2,1,0:T(8,128)(2,1)S(1)} %copy-done.13, bf16[4,128,384]{2,1,0:T(8,128)(2,1)S(1)} %collective-permute-done.near_ref, bf16[4,128,384]{2,1,0:T(8,128)(2,1)S(1)} %copy-done.22, ...), custom_call_target="tpu_custom_call" | custom-call | flops 2717908992 | bytes 6684672 | tf_op jit(solution)/shard_map/pallas_call | solution.py:118
  78.8 1.1 copy-done.10
  80.0 15.0 %copy.20 = bf16[3,3,3,384,384]{3,4,2,1,0:T(8,128)(2,1)} copy(bf16[3,3,3,384,384]{4,3,2,1,0:T(8,128)(2,1)} %side_in.3) | data formatting | bytes 15925248 | tf_op jit(solution)/shard_map/optimization_barrier | solution.py:562
  95.0 3.3 %copy-done.2 = bf16[3,3,3,384,384]{4,3,2,1,0:T(8,128)(2,1)S(1)} copy-done((bf16[3,3,3,384,384]{4,3,2,1,0:T(8,128)(2,1)S(1)}, bf16[3,3,3,384,384]{4,3,2,1,0:T(8,128)(2,1)}, u32[]{:S(2)}) %copy-start.2) | copy-done | bytes 7962648
  98.3 2.6 %shard_map.163 = (bf16[2304,2304]{1,0:T(8,128)(2,1)S(1)}, bf16[2,768,1152]{2,1,0:T(8,128)(2,1)S(1)}) custom-call(bf16[3,3,3,384,384]{4,3,2,1,0:T(8,128)(2,1)S(1)} %copy-done.2, bf16[3,3,3,384,384]{4,3,2,1,0:T(8,128)(2,1)S(1)} %copy-done.2), custom_call_target="tpu_custom_call" | custom-call | bytes 15925248 | tf_op jit(solution)/shard_map/pallas_call | solution.py:170
  100.9 4.1 %copy-done.3 = bf16[2304,2304]{1,0:T(8,128)(2,1)} copy-done((bf16[2304,2304]{1,0:T(8,128)(2,1)}, bf16[2304,2304]{1,0:T(8,128)(2,1)S(1)}, u32[]{:S(2)}) %copy-start.3) | copy-done | bytes 10616856
  105.0 4.2 %slice.11 = bf16[1,2,3,384,384]{3,4,2,1,0:T(8,128)(2,1)} slice(bf16[3,3,3,384,384]{3,4,2,1,0:T(8,128)(2,1)} %copy.20), slice={[2:3:1], [0:3:2], [0:3:1], [0:384:1], [0:384:1]} | slice | bytes 3538944 | tf_op jit(solution)/shard_map/slice | solution.py:565
  109.2 3.3 %copy-done.1 = bf16[3,3,3,384,384]{4,3,2,1,0:T(8,128)(2,1)S(1)} copy-done((bf16[3,3,3,384,384]{4,3,2,1,0:T(8,128)(2,1)S(1)}, bf16[3,3,3,384,384]{4,3,2,1,0:T(8,128)(2,1)}, u32[]{:S(2)}) %copy-start.1) | copy-done | bytes 7962648
  112.5 2.1 %shard_map.162 = (bf16[1536,2304]{1,0:T(8,128)(2,1)S(1)}, bf16[2,768,1152]{2,1,0:T(8,128)(2,1)S(1)}) custom-call(bf16[3,3,3,384,384]{4,3,2,1,0:T(8,128)(2,1)S(1)} %copy-done.1, bf16[3,3,3,384,384]{4,3,2,1,0:T(8,128)(2,1)S(1)} %copy-done.1), custom_call_target="tpu_custom_call" | custom-call | bytes 15925248 | tf_op jit(solution)/shard_map/pallas_call | solution.py:170
  114.6 2.8 %copy-done.5 = bf16[1536,2304]{1,0:T(8,128)(2,1)} copy-done((bf16[1536,2304]{1,0:T(8,128)(2,1)}, bf16[1536,2304]{1,0:T(8,128)(2,1)S(1)}, u32[]{:S(2)}) %copy-start.5) | copy-done | bytes 7077912
  117.4 1.9 %copy-done.6 = bf16[2,768,1152]{2,1,0:T(8,128)(2,1)} copy-done((bf16[2,768,1152]{2,1,0:T(8,128)(2,1)}, bf16[2,768,1152]{2,1,0:T(8,128)(2,1)S(1)}, u32[]{:S(2)}) %copy-start.6) | copy-done | bytes 3538968
  119.3 0.3 fusion.2
  119.6 1.3 dynamic-slice_bitcast_fusion.2
  121.0 4.9 %collective-permute-start.3 = (bf16[2,16,4,8,384]{4,3,2,1,0:T(8,128)(2,1)}, bf16[2,16,4,8,384]{4,3,2,1,0:T(8,128)(2,1)}, u32[]{:S(2)}, u32[]{:S(2)}) collective-permute-start(bf16[2,16,4,8,384]{4,3,2,1,0:T(8,128)(2,1)} %get-tuple-element.83), channel_id=1, source_target_pairs={{0,31},{1,2},{2,1},{3,4},{4,3},{5,6},{6,5},{7,8},{8,7},{9,10},{10,... | collective-permute-start | bytes 2359304 | tf_op jit(solution)/shard_map/ppermute | solution.py:542
  125.9 1.3 dynamic-slice_bitcast_fusion
  127.2 0.7 collective-permute-start.7
  127.9 3.9 %copy.21.w_ref = bf16[2,384,1152]{2,1,0:T(8,128)(2,1)} copy(bf16[2,384,1152]{1,2,0:T(8,128)(2,1)} %bitcast.35) | data formatting | bytes 3538944 | tf_op jit(solution)/shard_map/optimization_barrier | solution.py:566
  131.8 2.0 %copy-done.7 = bf16[2,768,1152]{2,1,0:T(8,128)(2,1)S(1)} copy-done((bf16[2,768,1152]{2,1,0:T(8,128)(2,1)S(1)}, bf16[2,768,1152]{2,1,0:T(8,128)(2,1)}, u32[]{:S(2)}) %copy-start.7) | copy-done | bytes 3538968
  133.8 1.4 copy-done.11
  135.2 1.1 copy-done.14
  136.4 6.9 %shard_map.164 = (f32[2,16,4,8,384]{4,3,2,1,0:T(8,128)S(1)}, bf16[4,2,2,16,8,384]{5,4,3,2,1,0:T(8,128)(2,1)}, bf16[2,768,1152]{2,1,0:T(8,128)(2,1)S(1)}) custom-call(bf16[2,2,2,16,4,8,384]{6,5,4,3,2,1,0:T(8,128)(2,1)S(1)} %bitcast.29, bf16[1536,2304]{1,0:T(8,128)(2,1)} %copy-done.5, f32[2,16,4,8,384]{4,3,2,1,0:T(8,128)S(1)} %copy-done.11, ...), custom_call_target="tpu_custom_call" | custom-call | flops 3623878656 | bytes 7077888 | tf_op jit(solution)/shard_map/pallas_call | solution.py:118
  143.3 4.4 %shard_map.165 = (bf16[4,2,128,384]{3,2,1,0:T(8,128)(2,1)S(1)}, bf16[4,128,384]{2,1,0:T(8,128)(2,1)S(1)}, bf16[4,128,384]{2,1,0:T(8,128)(2,1)S(1)}, bf16[1152,2304]{1,0:T(8,128)(2,1)S(1)}) custom-call(s32[3,4]{1,0:T(4,128)S(1)} %add_convert_fusion.edge_ref, bf16[2,16,4,8,384]{4,3,2,1,0:T(8,128)(2,1)} %collective-permute-done.2.near_ref, ...), custom_call_target="tpu_custom_call" | custom-call | flops 1811939328 | bytes 3538944 | tf_op jit(solution)/shard_map/pallas_call | solution.py:118
  147.7 0.6 collective-permute-start.4
  148.2 4.4 %collective-permute-start.5 = (bf16[4,128,384]{2,1,0:T(8,128)(2,1)S(1)}, bf16[4,128,384]{2,1,0:T(8,128)(2,1)S(1)}, u32[]{:S(2)}, u32[]{:S(2)}) collective-permute-start(bf16[4,128,384]{2,1,0:T(8,128)(2,1)S(1)} %get-tuple-element.67), channel_id=1, source_target_pairs={{0,31},{1,2},{2,1},{3,4},{4,3},{5,6},{6,5},{7,8},{8,7},{9,10},{10,... | collective-permute-start | bytes 1179656 | tf_op jit(solution)/shard_map/ppermute | solution.py:542
  152.6 2.0 %copy-done.16 = bf16[2,768,1152]{2,1,0:T(8,128)(2,1)S(1)} copy-done((bf16[2,768,1152]{2,1,0:T(8,128)(2,1)S(1)}, bf16[2,768,1152]{2,1,0:T(8,128)(2,1)}, u32[]{:S(2)}) %copy-start.16) | copy-done | bytes 3538968
  154.6 11.6 %shard_map.166 = (f32[2,16,4,8,384]{4,3,2,1,0:T(8,128)S(1)}, bf16[4,2,2,16,8,384]{5,4,3,2,1,0:T(8,128)(2,1)}) custom-call(s32[3,4]{1,0:T(4,128)S(1)} %add_convert_fusion.edge_ref, bf16[2,16,4,8,384]{4,3,2,1,0:T(8,128)(2,1)} %collective-permute-done.6.near_ref, bf16[2,16,4,8,384]{4,3,2,1,0:T(8,128)(2,1)} %collective-permute-done.7.far_ref, ...), custom_call_target="tpu_custom_call" | custom-call | flops 7247757312 | bytes 14155776 | tf_op jit(solution)/shard_map/pallas_call | solution.py:118
  166.2 3.1 %shard_map.167 = bf16[4,2,128,384]{3,2,1,0:T(8,128)(2,1)} custom-call(s32[3,4]{1,0:T(4,128)S(1)} %add_convert_fusion.edge_ref, bf16[4,128,384]{2,1,0:T(8,128)(2,1)S(1)} %collective-permute-done.4.near_ref, bf16[4,128,384]{2,1,0:T(8,128)(2,1)S(1)} %collective-permute-done.5.far_ref, bf16[2,384,1152]{2,1,0:T(8,128)(2,1)S(1)} %copy-done.4, ...), custom_call_target="tpu_custom_call" | custom-call | flops 905969664 | bytes 1769472 | tf_op jit(solution)/shard_map/pallas_call | solution.py:118
  (63 shorter events, 0.2 us)
Async XLA Ops:
  3.7 11.7 %copy-start.23 = (f32[384]{0:T(512)S(1)}, f32[384]{0:T(512)}, u32[]{:S(2)}) copy-start(f32[384]{0:T(512)} %param.17) | copy-start | bytes 4612
  3.7 11.8 %copy-start.27 = (s32[16]{0:T(128)S(1)}, s32[16]{0:T(128)}, u32[]{:S(2)}) copy-start(s32[16]{0:T(128)} %param.27) | copy-start | bytes 196
  3.7 11.8 %copy-start.28 = (s32[16]{0:T(128)S(1)}, s32[16]{0:T(128)}, u32[]{:S(2)}) copy-start(s32[16]{0:T(128)} %param.24) | copy-start | bytes 196
  3.7 11.8 %copy-start.29 = (s32[16]{0:T(128)S(1)}, s32[16]{0:T(128)}, u32[]{:S(2)}) copy-start(s32[16]{0:T(128)} %param.25) | copy-start | bytes 196
  3.8 11.8 %copy-start.30 = (s32[16]{0:T(128)S(1)}, s32[16]{0:T(128)}, u32[]{:S(2)}) copy-start(s32[16]{0:T(128)} %param.23) | copy-start | bytes 196
  3.8 11.8 %copy-start.31 = (s32[16]{0:T(128)S(1)}, s32[16]{0:T(128)}, u32[]{:S(2)}) copy-start(s32[16]{0:T(128)} %param.26) | copy-start | bytes 196
  3.8 12.1 %copy-start.8 = (bf16[4,2,128,384]{3,2,1,0:T(8,128)(2,1)S(1)}, bf16[4,2,128,384]{3,2,1,0:T(8,128)(2,1)}, u32[]{:S(2)}) copy-start(bf16[4,2,128,384]{3,2,1,0:T(8,128)(2,1)} %f_ref.3) | copy-start | bytes 2359300
  3.8 55.1 %all-to-all-start = ((bf16[128,4,8,384]{3,2,1,0:T(8,128)(2,1)}), bf16[128,4,8,384]{3,2,1,0:T(8,128)(2,1)}, u32[]{:S(2)}, u32[]{:S(2)}) async-start(bf16[128,4,8,384]{3,2,1,0:T(8,128)(2,1)} %bitcast.33), calls=%async_computation | async-start | bytes 6291456 | tf_op jit(solution)/shard_map/all_to_all | solution.py:547
  18.7 0.9 copy-start.12
  19.5 10.7 %collective-permute-start = (bf16[4,128,384]{2,1,0:T(8,128)(2,1)}, bf16[4,128,384]{2,1,0:T(8,128)(2,1)S(1)}, u32[]{:S(2)}, u32[]{:S(2)}) collective-permute-start(bf16[4,128,384]{2,1,0:T(8,128)(2,1)} %get-tuple-element.40), channel_id=1, source_target_pairs={{0,1},{1,0},{2,3},{3,2},{4,5},{5,4},{6,7},{7,6},{8,9},{9,8},{10,11... | collective-permute-start | bytes 1179656 | tf_op jit(solution)/shard_map/ppermute | solution.py:539
  19.5 39.3 %collective-permute-start.1 = (bf16[4,128,384]{2,1,0:T(8,128)(2,1)}, bf16[4,128,384]{2,1,0:T(8,128)(2,1)S(1)}, u32[]{:S(2)}, u32[]{:S(2)}) collective-permute-start(bf16[4,128,384]{2,1,0:T(8,128)(2,1)} %get-tuple-element.41), channel_id=1, source_target_pairs={{0,31},{1,2},{2,1},{3,4},{4,3},{5,6},{6,5},{7,8},{8,7},{9,10},{10,... | collective-permute-start | bytes 1179656 | tf_op jit(solution)/shard_map/ppermute | solution.py:542
  24.7 3.3 %copy-start = (bf16[3,3,3,384,384]{4,3,2,1,0:T(8,128)(2,1)S(1)}, bf16[3,3,3,384,384]{4,3,2,1,0:T(8,128)(2,1)}, u32[]{:S(2)}) copy-start(bf16[3,3,3,384,384]{4,3,2,1,0:T(8,128)(2,1)} %side_in.2) | copy-start | bytes 23887876
  28.5 1.7 %copy-start.17 = (bf16[768,2304]{1,0:T(8,128)(2,1)}, bf16[768,2304]{1,0:T(8,128)(2,1)S(1)}, u32[]{:S(2)}) copy-start(bf16[768,2304]{1,0:T(8,128)(2,1)S(1)} %get-tuple-element.50.wo_ref) | copy-start | bytes 10616836
  30.3 32.9 %copy-start.19 = (bf16[2,384,1152]{2,1,0:T(8,128)(2,1)}, bf16[2,384,1152]{2,1,0:T(8,128)(2,1)S(1)}, u32[]{:S(2)}) copy-start(bf16[2,384,1152]{2,1,0:T(8,128)(2,1)S(1)} %get-tuple-element.51.ws_ref) | copy-start | bytes 5308420
  58.9 4.3 %copy-start.21 = (bf16[4,128,384]{2,1,0:T(8,128)(2,1)}, bf16[4,128,384]{2,1,0:T(8,128)(2,1)S(1)}, u32[]{:S(2)}) copy-start(bf16[4,128,384]{2,1,0:T(8,128)(2,1)S(1)} %collective-permute-done.1.far_ref) | copy-start | bytes 1179652
  63.2 56.1 %all-to-all-start.1 = ((bf16[128,4,8,384]{3,2,1,0:T(8,128)(2,1)}), bf16[128,4,8,384]{3,2,1,0:T(8,128)(2,1)S(1)}, u32[]{:S(2)}, u32[]{:S(2)}) async-start(bf16[128,4,8,384]{3,2,1,0:T(8,128)(2,1)} %bitcast.34), calls=%async_computation.1 | async-start | bytes 6291456 | tf_op jit(solution)/shard_map/all_to_all | solution.py:558
  69.2 1.1 copy-start.13
  70.4 2.0 %copy-start.18 = (bf16[768,2304]{1,0:T(8,128)(2,1)S(1)}, bf16[768,2304]{1,0:T(8,128)(2,1)}, u32[]{:S(2)}) copy-start(bf16[768,2304]{1,0:T(8,128)(2,1)} %copy-done.17) | copy-start | bytes 10616836
  72.4 1.5 copy-start.20
  73.8 1.0 copy-start.22
  78.8 1.1 copy-start.10
  95.0 3.3 %copy-start.2 = (bf16[3,3,3,384,384]{4,3,2,1,0:T(8,128)(2,1)S(1)}, bf16[3,3,3,384,384]{4,3,2,1,0:T(8,128)(2,1)}, u32[]{:S(2)}) copy-start(bf16[3,3,3,384,384]{4,3,2,1,0:T(8,128)(2,1)} %side_in.3) | copy-start | bytes 23887876
  100.9 4.1 %copy-start.3 = (bf16[2304,2304]{1,0:T(8,128)(2,1)}, bf16[2304,2304]{1,0:T(8,128)(2,1)S(1)}, u32[]{:S(2)}) copy-start(bf16[2304,2304]{1,0:T(8,128)(2,1)S(1)} %get-tuple-element.65.later_ref.w_ref) | copy-start | bytes 31850500
  105.0 4.2 %copy-start.15 = (bf16[2,768,1152]{2,1,0:T(8,128)(2,1)}, bf16[2,768,1152]{2,1,0:T(8,128)(2,1)S(1)}, u32[]{:S(2)}) copy-start(bf16[2,768,1152]{2,1,0:T(8,128)(2,1)S(1)} %get-tuple-element.71.ws_ref) | copy-start | bytes 10616836
  109.2 3.3 %copy-start.1 = (bf16[3,3,3,384,384]{4,3,2,1,0:T(8,128)(2,1)S(1)}, bf16[3,3,3,384,384]{4,3,2,1,0:T(8,128)(2,1)}, u32[]{:S(2)}) copy-start(bf16[3,3,3,384,384]{4,3,2,1,0:T(8,128)(2,1)} %side_in.2) | copy-start | bytes 23887876
  114.6 2.9 %copy-start.5 = (bf16[1536,2304]{1,0:T(8,128)(2,1)}, bf16[1536,2304]{1,0:T(8,128)(2,1)S(1)}, u32[]{:S(2)}) copy-start(bf16[1536,2304]{1,0:T(8,128)(2,1)S(1)} %get-tuple-element.60.w_ref) | copy-start | bytes 21233668
  117.4 1.9 %copy-start.6 = (bf16[2,768,1152]{2,1,0:T(8,128)(2,1)}, bf16[2,768,1152]{2,1,0:T(8,128)(2,1)S(1)}, u32[]{:S(2)}) copy-start(bf16[2,768,1152]{2,1,0:T(8,128)(2,1)S(1)} %get-tuple-element.62.sides_ref) | copy-start | bytes 10616836
  121.0 6.9 %copy-start.24 = (f32[384]{0:T(512)S(1)}, f32[384]{0:T(512)}, u32[]{:S(2)}) copy-start(f32[384]{0:T(512)} %param.18) | copy-start | bytes 4612
  121.0 6.9 %copy-start.25 = (f32[384]{0:T(512)S(1)}, f32[384]{0:T(512)}, u32[]{:S(2)}) copy-start(f32[384]{0:T(512)} %param.21) | copy-start | bytes 4612
  121.0 6.9 %copy-start.26 = (f32[384]{0:T(512)S(1)}, f32[384]{0:T(512)}, u32[]{:S(2)}) copy-start(f32[384]{0:T(512)} %param.22) | copy-start | bytes 4612
  121.0 22.3 %collective-permute-start.3 = (bf16[2,16,4,8,384]{4,3,2,1,0:T(8,128)(2,1)}, bf16[2,16,4,8,384]{4,3,2,1,0:T(8,128)(2,1)}, u32[]{:S(2)}, u32[]{:S(2)}) collective-permute-start(bf16[2,16,4,8,384]{4,3,2,1,0:T(8,128)(2,1)} %get-tuple-element.83), channel_id=1, source_target_pairs={{0,31},{1,2},{2,1},{3,4},{4,3},{5,6},{6,5},{7,8},{8,7},{9,10},{10,... | collective-permute-start | bytes 2359304 | tf_op jit(solution)/shard_map/ppermute | solution.py:542
  125.9 17.4 %collective-permute-start.2 = (bf16[2,16,4,8,384]{4,3,2,1,0:T(8,128)(2,1)}, bf16[2,16,4,8,384]{4,3,2,1,0:T(8,128)(2,1)}, u32[]{:S(2)}, u32[]{:S(2)}) collective-permute-start(bf16[2,16,4,8,384]{4,3,2,1,0:T(8,128)(2,1)} %get-tuple-element.84), channel_id=1, source_target_pairs={{0,1},{1,0},{2,3},{3,2},{4,5},{5,4},{6,7},{7,6},{8,9},{9,8},{10,11... | collective-permute-start | bytes 2359304 | tf_op jit(solution)/shard_map/ppermute | solution.py:539
  127.2 25.4 %collective-permute-start.7 = (bf16[2,16,4,8,384]{4,3,2,1,0:T(8,128)(2,1)}, bf16[2,16,4,8,384]{4,3,2,1,0:T(8,128)(2,1)}, u32[]{:S(2)}, u32[]{:S(2)}) collective-permute-start(bf16[2,16,4,8,384]{4,3,2,1,0:T(8,128)(2,1)} %get-tuple-element.81), channel_id=1, source_target_pairs={{0,31},{1,2},{2,1},{3,4},{4,3},{5,6},{6,5},{7,8},{8,7},{9,10},{10,... | collective-permute-start | bytes 2359304 | tf_op jit(solution)/shard_map/ppermute | solution.py:542
  127.9 24.7 %collective-permute-start.6 = (bf16[2,16,4,8,384]{4,3,2,1,0:T(8,128)(2,1)}, bf16[2,16,4,8,384]{4,3,2,1,0:T(8,128)(2,1)}, u32[]{:S(2)}, u32[]{:S(2)}) collective-permute-start(bf16[2,16,4,8,384]{4,3,2,1,0:T(8,128)(2,1)} %get-tuple-element.82), channel_id=1, source_target_pairs={{0,1},{1,0},{2,3},{3,2},{4,5},{5,4},{6,7},{7,6},{8,9},{9,8},{10,11... | collective-permute-start | bytes 2359304 | tf_op jit(solution)/shard_map/ppermute | solution.py:539
  131.8 2.0 %copy-start.7 = (bf16[2,768,1152]{2,1,0:T(8,128)(2,1)S(1)}, bf16[2,768,1152]{2,1,0:T(8,128)(2,1)}, u32[]{:S(2)}) copy-start(bf16[2,768,1152]{2,1,0:T(8,128)(2,1)} %copy-done.6) | copy-start | bytes 10616836
  133.8 1.4 copy-start.11
  135.2 1.1 copy-start.14
  147.7 18.5 %collective-permute-start.4 = (bf16[4,128,384]{2,1,0:T(8,128)(2,1)S(1)}, bf16[4,128,384]{2,1,0:T(8,128)(2,1)S(1)}, u32[]{:S(2)}, u32[]{:S(2)}) collective-permute-start(bf16[4,128,384]{2,1,0:T(8,128)(2,1)S(1)} %get-tuple-element.66), channel_id=1, source_target_pairs={{0,1},{1,0},{2,3},{3,2},{4,5},{5,4},{6,7},{7,6},{8,9},{9,8},{10,11... | collective-permute-start | bytes 1179656 | tf_op jit(solution)/shard_map/ppermute | solution.py:539
  148.2 18.0 %collective-permute-start.5 = (bf16[4,128,384]{2,1,0:T(8,128)(2,1)S(1)}, bf16[4,128,384]{2,1,0:T(8,128)(2,1)S(1)}, u32[]{:S(2)}, u32[]{:S(2)}) collective-permute-start(bf16[4,128,384]{2,1,0:T(8,128)(2,1)S(1)} %get-tuple-element.67), channel_id=1, source_target_pairs={{0,31},{1,2},{2,1},{3,4},{4,3},{5,6},{6,5},{7,8},{8,7},{9,10},{10,... | collective-permute-start | bytes 1179656 | tf_op jit(solution)/shard_map/ppermute | solution.py:542
  152.6 2.0 %copy-start.16 = (bf16[2,768,1152]{2,1,0:T(8,128)(2,1)S(1)}, bf16[2,768,1152]{2,1,0:T(8,128)(2,1)}, u32[]{:S(2)}) copy-start(bf16[2,768,1152]{2,1,0:T(8,128)(2,1)} %copy-done.15) | copy-start | bytes 10616836
  154.6 11.6 %copy-start.4 = (bf16[2,384,1152]{2,1,0:T(8,128)(2,1)S(1)}, bf16[2,384,1152]{2,1,0:T(8,128)(2,1)}, u32[]{:S(2)}) copy-start(bf16[2,384,1152]{2,1,0:T(8,128)(2,1)} %copy.21.w_ref) | copy-start | bytes 5308420
  154.6 11.6 %copy-start.9 = (bf16[4,2,128,384]{3,2,1,0:T(8,128)(2,1)S(1)}, bf16[4,2,128,384]{3,2,1,0:T(8,128)(2,1)}, u32[]{:S(2)}) copy-start(bf16[4,2,128,384]{3,2,1,0:T(8,128)(2,1)} %f_ref.3) | copy-start | bytes 2359300

commit v12 on v10

--- a/solution.py
+++ b/solution.py
@@ -61,50 +61,38 @@
 def permute(held, source, rotation, keep):
     n_groups, n_tiles, n_slots, cols, ch = held.shape
 
-    def body(source_ref, rotation_ref, keep_ref, i_ref, o_ref, made, sems):
-        def stream(n, to):
+    def body(source_ref, rotation_ref, keep_ref, i_ref, o_ref):
+        def stream(n, _):
             by = rotation_ref[n]
             old = source_ref[n]
-            slot = lax.rem(n, n_slots)
+            to, slot = lax.div(n, n_slots), lax.rem(n, n_slots)
             of, place = lax.div(old, n_slots), lax.rem(old, n_slots)
 
             @pl.when(keep_ref[n] != 0)
             def _():
                 for t in range(n_tiles):
                     at = lax.rem(t + n_tiles - by, n_tiles)
-                    made[to, t, slot] = i_ref[of, at, place]
+                    o_ref[to, t, slot] = i_ref[of, at, place]
 
             @pl.when(keep_ref[n] == 0)
             def _():
-                made[to, :, slot] = jnp.zeros((n_tiles, cols, ch), made.dtype)
-
-            return to
-
-        copies = []
-        for to in range(n_groups):
-            lax.fori_loop(to * n_slots, (to + 1) * n_slots, stream, to)
-            copies.append(pltpu.make_async_copy(made.at[to], o_ref.at[to], sems.at[to]))
-            copies[-1].start()
-        for c in copies:
-            c.wait()
-
-    smem = pl.BlockSpec(memory_space=pltpu.SMEM)
+                o_ref[to, :, slot] = jnp.zeros((n_tiles, cols, ch), o_ref.dtype)
+
+            return 0
+
+        lax.fori_loop(0, n_groups * n_slots, stream, 0)
+
+    smem, vmem = pl.BlockSpec(memory_space=pltpu.SMEM), pl.BlockSpec(memory_space=pltpu.VMEM)
     return pl.pallas_call(
         body,
-        in_specs=[smem, smem, smem, pl.BlockSpec(memory_space=pltpu.VMEM)],
-        out_specs=pl.BlockSpec(memory_space=pl.ANY),
+        in_specs=[smem, smem, smem, vmem],
+        out_specs=vmem,
         out_shape=jax.ShapeDtypeStruct(held.shape, held.dtype),
-        scratch_shapes=[
-            pltpu.VMEM(held.shape, held.dtype),
-            pltpu.SemaphoreType.DMA((n_groups,)),
-        ],
-        compiler_params=pltpu.CompilerParams(vmem_limit_bytes=52 << 20),
+        compiler_params=pltpu.CompilerParams(vmem_limit_bytes=16 << 20),
     )(source, rotation, keep, held)
 
 
-VMEM_LIMIT = 16 << 20
-LIMIT_A = 34
-LIMIT_B = 16
+VMEM_LIMIT = 13 << 20
 
 
 def call(body, out_shape, operands, scalars=(), scratch=(), flops=0, moved=0, far=(), far_out=(), aliases=None, limit=VMEM_LIMIT):
@@ -314,58 +302,42 @@
         add_into(o_ref, y, folded(acc[:, y * wide : (y + 1) * wide], ch, True), True, base)
 
 
-def own_first(got, weight, sums, act, sides):
+def own_first(got, weight, sums, act):
     n_rows, _, n_frames, blocks, n_slots, _, ch = got.shape
     half = blocks * n_slots * CB
     deep = n_frames * ch
 
-    def body(got_ref, w_ref, z_ref, act_ref, sides_ref, o_ref, next_ref, near_ref, w, lhs, acc, sems, keep_sems):
-        loads = []
-        for r in range(n_rows):
-            rows = pl.ds(r * deep, deep)
-            loads.append(pltpu.make_async_copy(w_ref.at[rows], w.at[r], sems.at[r]))
-        loads[0].start()
-        near = pltpu.make_async_copy(sides_ref, near_ref, sems.at[2])
-        keeps = [pltpu.make_async_copy(act_ref, next_ref.at[:, 1], sems.at[3])]
+    def body(got_ref, w_ref, z_ref, act_ref, o_ref, next_ref, lhs, acc, keep_sems, act_sem):
+        keeps = [pltpu.make_async_copy(act_ref, next_ref.at[:, 1], act_sem)]
         for r in range(n_rows):
             for s in range(n_slots):
                 src = got_ref.at[r, 0, n_frames - 1, :, s]
                 n = r * n_slots + s
                 keeps.append(pltpu.make_async_copy(src, next_ref.at[s, 0, r], keep_sems.at[n]))
-        own_rows(got_ref, 0, lhs)
-        loads[0].wait()
-        loads[1].start()
-        acc[...] = dot(lhs[:, 0:deep], w[0])
-        loads[1].wait()
-        near.start()
         for c in keeps:
             c.start()
-        acc[...] += dot(lhs[:, deep : 2 * deep], w[1])
+        own_rows(got_ref, 0, lhs)
+        acc[...] = dot(lhs[...], w_ref[...])
         give_rows(acc, ch, o_ref, z_ref)
         for c in keeps:
             c.wait()
-        near.wait()
 
     return call(
         body,
         [
             sums_shape(blocks, n_slots, n_rows, ch),
             jax.ShapeDtypeStruct((n_slots, 2, n_rows, blocks, CB, ch), jnp.bfloat16),
-            jax.ShapeDtypeStruct(sides.shape, sides.dtype),
-        ],
-        (got, weight, sums, act, sides),
+        ],
+        (got, weight, sums, act),
         scratch=[
-            pltpu.VMEM((n_rows, deep, weight.shape[1]), weight.dtype),
             pltpu.VMEM((half, n_rows * deep), jnp.bfloat16),
             pltpu.VMEM((half, weight.shape[1]), jnp.float32),
-            pltpu.SemaphoreType.DMA((4,)),
             pltpu.SemaphoreType.DMA((n_rows * n_slots,)),
+            pltpu.SemaphoreType.DMA,
         ],
         flops=2 * half * weight.size,
         moved=2 * weight.size,
-        far=(1, 4),
         far_out=(1,),
-        limit=LIMIT_A << 20,
     )
 
 
@@ -416,35 +388,29 @@
     return folded(dot(lhs[...].reshape(half, n_frames * ch), w), ch, True)
 
 
-def second_activation(near, far, w_sides, sums, bias, gain, later, edges):
+def second_activation(near, far, w_sides, sums, bias, gain, edges):
     n_frames, blocks, n_slots, _, ch = far.shape
     n_rows, n_cols, deep = sums.shape[0], blocks * CB, n_frames * ch
 
-    def body(edge_ref, near_ref, far_ref, w_ref, z_ref, b_ref, g_ref, later_ref, o_ref, near_out, far_out, fetched_ref, lhs, sem):
-        fetch = pltpu.make_async_copy(later_ref, fetched_ref, sem)
-        fetch.start()
-        for (side, y), out in zip(beside(edge_ref, near_ref.at[0], far_ref), (near_out, far_out)):
+    def body(edge_ref, near_ref, far_ref, w_ref, z_ref, b_ref, g_ref, o_ref, near_out, far_out, lhs):
+        for (side, y), out in zip(beside(edge_ref, near_ref, far_ref), (near_out, far_out)):
             total = side_sums(edge_ref, y, side, w_ref[y], lhs) + z_ref[y] + b_ref[...]
             for s in range(n_slots):
                 value = activated(total[:, s].reshape(n_cols, ch), g_ref[...]).astype(jnp.bfloat16)
                 o_ref[s, y] = value
                 out[s] = value
-        fetch.wait()
 
     row = jax.ShapeDtypeStruct((n_slots, n_cols, ch), jnp.bfloat16)
     return call(
         body,
-        [jax.ShapeDtypeStruct((n_slots, n_rows, n_cols, ch), jnp.bfloat16), row, row, jax.ShapeDtypeStruct(later.shape, later.dtype)],
-        (near, far, w_sides, sums, bias, gain, later),
+        [jax.ShapeDtypeStruct((n_slots, n_rows, n_cols, ch), jnp.bfloat16), row, row],
+        (near, far, w_sides, sums, bias, gain),
         scalars=(edges,),
         scratch=[
             pltpu.VMEM((blocks, n_slots, CB, deep), jnp.bfloat16),
-            pltpu.SemaphoreType.DMA,
         ],
         flops=2 * n_slots * n_cols * w_sides.size,
         moved=2 * w_sides.size,
-        far=(6,),
-        limit=LIMIT_B << 20,
     )
 
 
@@ -456,7 +422,7 @@
         copy = pltpu.make_async_copy(tiles_ref, next_ref.at[:, 1], sem)
         copy.start()
         add_own(act_ref, wa_ref, lhs2, o_ref, z_ref)
-        for side, y in beside(edge_ref, near_ref.at[1], far_ref):
+        for side, y in beside(edge_ref, near_ref, far_ref):
             o_ref[y] += side_sums(edge_ref, y, side, w_ref[y], lhs)
         copy.wait()
 
@@ -574,21 +540,21 @@
     )
     got = got.reshape(n_rows, 2, 2, blocks, n_slots, CB, ch)
 
-    def picked(row):
-        return lax.dynamic_index_in_dim(got, row, 0, keepdims=False)
-
-    rows_near, rows_far = swap_near(picked(1 - odd)), picked(odd)
-    far_1, far_2 = swap_far(rows_far[0]), swap_far(rows_far[1])
+    def picked(cache, row):
+        return lax.dynamic_index_in_dim(got[:, cache], row, 0, keepdims=False)
+
+    near_1, far_1 = swap_near(picked(0, 1 - odd)), swap_far(picked(0, odd))
+    near_2, far_2 = swap_near(picked(1, 1 - odd)), swap_far(picked(1, odd))
     act_tiles = act_first.reshape(n_slots, n_rows, blocks, CB, ch)
-    sums_1, next_first, sides_1 = own_first(got, own_1, sums_1, act_tiles, sides_1)
-    act_second, near, far, own_2 = second_activation(
-        rows_near, far_1, sides_1, sums_1, bias_first[None], gain_second[None], own_2, edges
+    sums_1, next_first = own_first(got, own_1, sums_1, act_tiles)
+    act_second, near, far = second_activation(
+        near_1, far_1, sides_1, sums_1, bias_first[None], gain_second[None], edges
     )
     act_near, act_far = swap_near(near), swap_far(far)
     got_later, act_later = lax.optimization_barrier((got, act_second))
     sums_2, kept = own_second(got_later, own_2)
     sums_2, next_second = before_sides(
-        rows_near, far_2, act_later, sides_2, act_own_2, sums_2, kept, edges
+        near_2, far_2, act_later, sides_2, act_own_2, sums_2, kept, edges
     )
     mixed_frame = last_part(
         act_near, act_far, act_sides_2, sums_2, bias_second[None], frame_in, edges

time: 147 us -> 144 us (0.980)
  Pallas kernels: 42.6 us -> 36.6 us
  waiting for transfers between devices: 40.5 us -> 43.9 us
    pallas_call x7, Pallas kernels: 31.3 us -> 27.7 us  [call(): pl.pallas_call(body, in_specs=in_specs, out_specs=out_specs, out_shape=li...]
    ppermute x4, waiting for transfers between devices: 28.8 us -> 31.8 us  [swap_far(): lax.ppermute(row, 'tile', [(i, (i + 2 * (i % 2) - 1) % n_tiles) for i in...]
    pallas_call x1, Pallas kernels: 3.97 us -> 1.63 us  [permute(): pl.pallas_call(body, in_specs=[smem, smem, smem, vmem], out_specs=vmem, o...]
    unnamed x76 -> x78, local copies, waits for them, and re-layouts: 30.6 us -> 31.7 us
  transfers between devices with their start and end apart: 9 -> 10, of which waited for: 3 -> 5; matrix products, arithmetic and copies ran while one was open for 0% -> 1% of each run, Pallas kernels for 22% -> 20%
where the time goes in v12:
time: 144 us; the launch traced here: 143 us
  waiting for transfers between devices  43.9 us (30%)
  Pallas kernels  36.6 us (25%)
  local copies, waits for them, and re-layouts  32.5 us (23%)
  starting transfers between devices  28.4 us (20%)
    ppermute x4, waiting for transfers between devices, swap_far(): lax.ppermute(row, 'tile', [(i, (i + 2 * (i % 2) - 1) % n_tiles) for i in...  31.8 us
    unnamed x78, local copies, waits for them, and re-layouts  31.7 us
    pallas_call x7, Pallas kernels, call(): pl.pallas_call(body, in_specs=in_specs, out_specs=out_specs, out_shape=li...  27.7 us
    all_to_all x1, waiting for transfers between devices, local(): lax.all_to_all(moved.reshape(n_groups * n_tiles, n_slots, CB, ch), BOTH,...  12.1 us
    all_to_all x1, starting transfers between devices, local(): held = lax.all_to_all(sent, BOTH, 0, 0, tiled=True)  11.1 us
    ppermute x4, starting transfers between devices, swap_far(): lax.ppermute(row, 'tile', [(i, (i + 2 * (i % 2) - 1) % n_tiles) for i in...  10.5 us
    all_to_all x1, starting transfers between devices, local(): lax.all_to_all(moved.reshape(n_groups * n_tiles, n_slots, CB, ch), BOTH,...  6.51 us
    pallas_call x4, Pallas kernels, spread(): pl.pallas_call(body, grid=(n_y,), in_specs=[pl.BlockSpec((times, 1, n_x,...  4.11 us
  transfers between devices with their start and end apart: 10, of which 5 were waited for; matrix products, arithmetic and copies ran while one was open for 1% of the time, Pallas kernels for 20%

profile of v12, /device:TPU:0, one launch (start us, length us, event | category | flops | bytes accessed | tf_op | source)
XLA Modules:
  0.0 143.3 jit_solution(12490885197792272008)
XLA Ops:
  0.6 3.1 %shard_map.157 = bf16[2,2,2,16,4,8,384]{6,5,4,3,2,1,0:T(8,128)(2,1)} custom-call(bf16[4,2,2,16,8,384]{5,4,3,2,1,0:T(8,128)(2,1)} %bitcast.35, bf16[4,2,2,16,8,384]{5,4,3,2,1,0:T(8,128)(2,1)} %bitcast.36), custom_call_target="tpu_custom_call" | custom-call | tf_op jit(solution)/shard_map/pallas_call | solution.py:47
  3.9 11.1 %all-to-all-start = ((bf16[128,4,8,384]{3,2,1,0:T(8,128)(2,1)}), bf16[128,4,8,384]{3,2,1,0:T(8,128)(2,1)S(1)}, u32[]{:S(2)}, u32[]{:S(2)}) async-start(bf16[128,4,8,384]{3,2,1,0:T(8,128)(2,1)} %bitcast.34), calls=%async_computation | async-start | bytes 6291456 | tf_op jit(solution)/shard_map/all_to_all | solution.py:519
  15.2 0.6 select_reduce_fusion
  16.0 1.1 copy-done.3
  17.1 2.8 %shard_map.158 = (bf16[4,2,128,384]{3,2,1,0:T(8,128)(2,1)S(1)}, bf16[4,128,384]{2,1,0:T(8,128)(2,1)}, bf16[4,128,384]{2,1,0:T(8,128)(2,1)}) custom-call(s32[3,4]{1,0:T(4,128)S(1)} %add_convert_fusion.edge_ref, bf16[4,2,128,384]{3,2,1,0:T(8,128)(2,1)S(1)} %copy-done.3, f32[1,384]{1,0:T(1,128)S(1)} %broadcast_in_dim.53.g_ref), custom_call_target="tpu_custom_call" | custom-call | flops 3932160 | bytes 2359296 | tf_op jit(solution)/shard_map/pallas_call | solution.py:105
  19.9 0.9 copy-done.20
  20.7 5.3 %collective-permute-start.1 = (bf16[4,128,384]{2,1,0:T(8,128)(2,1)}, bf16[4,128,384]{2,1,0:T(8,128)(2,1)}, u32[]{:S(2)}, u32[]{:S(2)}) collective-permute-start(bf16[4,128,384]{2,1,0:T(8,128)(2,1)} %get-tuple-element.46), channel_id=1, source_target_pairs={{0,31},{1,2},{2,1},{3,4},{4,3},{5,6},{6,5},{7,8},{8,7},{9,10},{10,... | collective-permute-start | bytes 1179656 | tf_op jit(solution)/shard_map/ppermute | solution.py:514
  26.0 3.3 %copy-done.1 = bf16[3,3,3,384,384]{4,3,2,1,0:T(8,128)(2,1)S(1)} copy-done((bf16[3,3,3,384,384]{4,3,2,1,0:T(8,128)(2,1)S(1)}, bf16[3,3,3,384,384]{4,3,2,1,0:T(8,128)(2,1)}, u32[]{:S(2)}) %copy-start.1) | copy-done | bytes 7962648
  29.3 0.5 shard_map.159
  29.8 1.8 %copy-done.16 = bf16[768,2304]{1,0:T(8,128)(2,1)} copy-done((bf16[768,2304]{1,0:T(8,128)(2,1)}, bf16[768,2304]{1,0:T(8,128)(2,1)S(1)}, u32[]{:S(2)}) %copy-start.16) | copy-done | bytes 3538968
  31.5 1.3 copy-done.18
  32.9 26.1 %collective-permute-done.1.far_ref = bf16[4,128,384]{2,1,0:T(8,128)(2,1)} collective-permute-done((bf16[4,128,384]{2,1,0:T(8,128)(2,1)}, bf16[4,128,384]{2,1,0:T(8,128)(2,1)}, u32[]{:S(2)}, u32[]{:S(2)}) %collective-permute-start.1) | collective-permute-done | bytes 393248 | tf_op jit(solution)/shard_map/ppermute | solution.py:514
  59.0 1.6 %shard_map.160 = bf16[4,32,4,8,384]{4,3,2,1,0:T(8,128)(2,1)S(1)} custom-call(s32[16]{0:T(128)S(1)} %get-tuple-element.87.source_ref, s32[16]{0:T(128)S(1)} %get-tuple-element.95.rotation_ref, s32[16]{0:T(128)S(1)} %compare_convert_fusion.keep_ref, bf16[4,32,4,8,384]{4,3,2,1,0:T(8,128)(2,1)S(1)} %bitcast.28), custom_call_target="tpu_custom_call" | custom-call | tf_op jit(solution)/shard_map/pallas_call | solution.py:86
  60.6 1.6 %copy-done.2 = bf16[4,32,4,8,384]{4,3,2,1,0:T(8,128)(2,1)} copy-done((bf16[4,32,4,8,384]{4,3,2,1,0:T(8,128)(2,1)}, bf16[4,32,4,8,384]{4,3,2,1,0:T(8,128)(2,1)S(1)}, u32[]{:S(2)}) %copy-start.2) | copy-done | bytes 3145752
  62.3 6.5 %all-to-all-start.1 = ((bf16[128,4,8,384]{3,2,1,0:T(8,128)(2,1)}), bf16[128,4,8,384]{3,2,1,0:T(8,128)(2,1)S(1)}, u32[]{:S(2)}, u32[]{:S(2)}) async-start(bf16[128,4,8,384]{3,2,1,0:T(8,128)(2,1)} %bitcast.29), calls=%async_computation.1 | async-start | bytes 6291456 | tf_op jit(solution)/shard_map/all_to_all | solution.py:530
  68.8 2.0 %copy-done.17 = bf16[768,2304]{1,0:T(8,128)(2,1)S(1)} copy-done((bf16[768,2304]{1,0:T(8,128)(2,1)S(1)}, bf16[768,2304]{1,0:T(8,128)(2,1)}, u32[]{:S(2)}) %copy-start.17) | copy-done | bytes 3538968
  70.8 1.5 %copy-done.19 = bf16[2,384,1152]{2,1,0:T(8,128)(2,1)S(1)} copy-done((bf16[2,384,1152]{2,1,0:T(8,128)(2,1)S(1)}, bf16[2,384,1152]{2,1,0:T(8,128)(2,1)}, u32[]{:S(2)}) %copy-start.19) | copy-done | bytes 1769496
  72.3 1.1 copy-done.21
  73.4 4.6 %shard_map.161.z_ref = f32[2,16,4,8,384]{4,3,2,1,0:T(8,128)S(1)} custom-call(s32[3,4]{1,0:T(4,128)S(1)} %add_convert_fusion.edge_ref, bf16[4,2,128,384]{3,2,1,0:T(8,128)(2,1)S(1)} %copy-done.21, bf16[4,128,384]{2,1,0:T(8,128)(2,1)S(1)} %collective-permute-done.near_ref, bf16[4,128,384]{2,1,0:T(8,128)(2,1)} %collective-permute-done.1.far_ref, ...), custom_call_target="tpu_custom_call" | custom-call | flops 2717908992 | bytes 6684672 | tf_op jit(solution)/shard_map/pallas_call | solution.py:105
  78.0 1.1 copy-done.23
  79.2 3.3 %copy-done = bf16[3,3,3,384,384]{4,3,2,1,0:T(8,128)(2,1)S(1)} copy-done((bf16[3,3,3,384,384]{4,3,2,1,0:T(8,128)(2,1)S(1)}, bf16[3,3,3,384,384]{4,3,2,1,0:T(8,128)(2,1)}, u32[]{:S(2)}) %copy-start) | copy-done | bytes 7962648
  82.4 0.5 shard_map.164
  83.0 1.3 copy-done.5
  84.3 1.8 %copy-done.10 = bf16[768,2304]{1,0:T(8,128)(2,1)} copy-done((bf16[768,2304]{1,0:T(8,128)(2,1)}, bf16[768,2304]{1,0:T(8,128)(2,1)S(1)}, u32[]{:S(2)}) %copy-start.10) | copy-done | bytes 3538968
  86.0 1.5 %shard_map.163 = (bf16[1536,2304]{1,0:T(8,128)(2,1)S(1)}, bf16[2,768,1152]{2,1,0:T(8,128)(2,1)S(1)}) custom-call(bf16[3,3,3,384,384]{4,3,2,1,0:T(8,128)(2,1)S(1)} %copy-done), custom_call_target="tpu_custom_call" | custom-call | bytes 15925248 | tf_op jit(solution)/shard_map/pallas_call | solution.py:154
  87.6 2.8 %copy-done.7 = bf16[1536,2304]{1,0:T(8,128)(2,1)} copy-done((bf16[1536,2304]{1,0:T(8,128)(2,1)}, bf16[1536,2304]{1,0:T(8,128)(2,1)S(1)}, u32[]{:S(2)}) %copy-start.7) | copy-done | bytes 7077912
  90.4 1.8 %copy-done.12 = bf16[2,768,1152]{2,1,0:T(8,128)(2,1)} copy-done((bf16[2,768,1152]{2,1,0:T(8,128)(2,1)}, bf16[2,768,1152]{2,1,0:T(8,128)(2,1)S(1)}, u32[]{:S(2)}) %copy-start.12) | copy-done | bytes 3538968
  92.2 1.5 %shard_map.162 = (bf16[1536,2304]{1,0:T(8,128)(2,1)S(1)}, bf16[2,768,1152]{2,1,0:T(8,128)(2,1)S(1)}) custom-call(bf16[3,3,3,384,384]{4,3,2,1,0:T(8,128)(2,1)S(1)} %bitcast.24), custom_call_target="tpu_custom_call" | custom-call | bytes 15925248 | tf_op jit(solution)/shard_map/pallas_call | solution.py:154
  93.8 2.9 %copy-done.8 = bf16[1536,2304]{1,0:T(8,128)(2,1)} copy-done((bf16[1536,2304]{1,0:T(8,128)(2,1)}, bf16[1536,2304]{1,0:T(8,128)(2,1)S(1)}, u32[]{:S(2)}) %copy-start.8) | copy-done | bytes 7077912
  96.7 1.8 %copy-done.14 = bf16[2,768,1152]{2,1,0:T(8,128)(2,1)} copy-done((bf16[2,768,1152]{2,1,0:T(8,128)(2,1)}, bf16[2,768,1152]{2,1,0:T(8,128)(2,1)S(1)}, u32[]{:S(2)}) %copy-start.14) | copy-done | bytes 3538968
  98.5 12.1 %all-to-all-done.1 = bf16[128,4,8,384]{3,2,1,0:T(8,128)(2,1)S(1)} async-done(((bf16[128,4,8,384]{3,2,1,0:T(8,128)(2,1)}), bf16[128,4,8,384]{3,2,1,0:T(8,128)(2,1)S(1)}, u32[]{:S(2)}, u32[]{:S(2)}) %all-to-all-start.1) | async-done | bytes 3145760 | tf_op jit(solution)/shard_map/all_to_all | solution.py:530
  110.7 0.3 fusion.2
  111.0 0.2 dynamic-slice_bitcast_fusion.2
  111.2 0.3 collective-permute-start.3
  111.5 0.1 collective-permute-start.2
  111.7 0.1 copy-done.26
  111.8 0.2 dynamic-slice_bitcast_fusion
  112.0 4.7 %collective-permute-start.7 = (bf16[2,16,4,8,384]{4,3,2,1,0:T(8,128)(2,1)S(1)}, bf16[2,16,4,8,384]{4,3,2,1,0:T(8,128)(2,1)S(1)}, u32[]{:S(2)}, u32[]{:S(2)}) collective-permute-start(bf16[2,16,4,8,384]{4,3,2,1,0:T(8,128)(2,1)S(1)} %get-tuple-element.91), channel_id=1, source_target_pairs={{0,31},{1,2},{2,1},{3,4},{4,3},{5,6},{6,5},{7,8},{8,7},{9,10},{10,... | collective-permute-start | bytes 2359304 | tf_op jit(solution)/shard_map/ppermute | solution.py:514
  116.8 4.6 %shard_map.165 = (f32[2,16,4,8,384]{4,3,2,1,0:T(8,128)S(1)}, bf16[4,2,2,16,8,384]{5,4,3,2,1,0:T(8,128)(2,1)}) custom-call(bf16[2,2,2,16,4,8,384]{6,5,4,3,2,1,0:T(8,128)(2,1)S(1)} %bitcast.26, bf16[1536,2304]{1,0:T(8,128)(2,1)S(1)} %copy-done.9, f32[2,16,4,8,384]{4,3,2,1,0:T(8,128)S(1)} %copy-done.24, bf16[4,2,16,8,384]{4,3,2,1,0:T(8,128)(2,1)S(1)} %bitcast.32), custom_call_target="tpu_custom_call" | custom-call | flops 3623878656 | bytes 7077888 | tf_op jit(solution)/shard_map/pallas_call | solution.py:105
  121.3 4.7 %collective-permute-done.3.far_ref = bf16[2,16,4,8,384]{4,3,2,1,0:T(8,128)(2,1)S(1)} collective-permute-done((bf16[2,16,4,8,384]{4,3,2,1,0:T(8,128)(2,1)S(1)}, bf16[2,16,4,8,384]{4,3,2,1,0:T(8,128)(2,1)S(1)}, u32[]{:S(2)}, u32[]{:S(2)}) %collective-permute-start.3) | collective-permute-done | bytes 786464 | tf_op jit(solution)/shard_map/ppermute | solution.py:514
  126.1 3.4 %shard_map.166 = (bf16[4,2,128,384]{3,2,1,0:T(8,128)(2,1)S(1)}, bf16[4,128,384]{2,1,0:T(8,128)(2,1)S(1)}, bf16[4,128,384]{2,1,0:T(8,128)(2,1)S(1)}) custom-call(s32[3,4]{1,0:T(4,128)S(1)} %add_convert_fusion.edge_ref, bf16[2,16,4,8,384]{4,3,2,1,0:T(8,128)(2,1)S(1)} %collective-permute-done.2.near_ref, ...), custom_call_target="tpu_custom_call" | custom-call | flops 1811939328 | bytes 3538944 | tf_op jit(solution)/shard_map/pallas_call | solution.py:105
  129.5 0.1 collective-permute-start.4
  129.6 0.3 collective-permute-start.5
  129.9 4.0 %shard_map.167 = (f32[2,16,4,8,384]{4,3,2,1,0:T(8,128)S(1)}, bf16[4,2,2,16,8,384]{5,4,3,2,1,0:T(8,128)(2,1)}) custom-call(bf16[2,2,2,16,4,8,384]{6,5,4,3,2,1,0:T(8,128)(2,1)S(1)} %bitcast.27, bf16[1536,2304]{1,0:T(8,128)(2,1)S(1)} %bitcast.31), custom_call_target="tpu_custom_call" | custom-call | flops 3623878656 | bytes 7077888 | tf_op jit(solution)/shard_map/pallas_call | solution.py:105
  133.9 0.6 collective-permute-done.7.far_ref
  134.5 5.3 %shard_map.168 = (f32[2,16,4,8,384]{4,3,2,1,0:T(8,128)S(1)}, bf16[4,2,2,16,8,384]{5,4,3,2,1,0:T(8,128)(2,1)}) custom-call(s32[3,4]{1,0:T(4,128)S(1)} %add_convert_fusion.edge_ref, bf16[2,16,4,8,384]{4,3,2,1,0:T(8,128)(2,1)S(1)} %collective-permute-done.6.near_ref, ...), custom_call_target="tpu_custom_call", output_to_operand_aliasing={{1}: (8, {})} | custom-call | flops 3623878656 | bytes 7077888 | tf_op jit(solution)/shard_map/pallas_call | solution.py:105
  139.9 0.3 collective-permute-done.5.far_ref
  140.2 3.1 %shard_map.169 = bf16[4,2,128,384]{3,2,1,0:T(8,128)(2,1)} custom-call(s32[3,4]{1,0:T(4,128)S(1)} %add_convert_fusion.edge_ref, bf16[4,128,384]{2,1,0:T(8,128)(2,1)S(1)} %collective-permute-done.4.near_ref, bf16[4,128,384]{2,1,0:T(8,128)(2,1)S(1)} %collective-permute-done.5.far_ref, bf16[2,384,1152]{2,1,0:T(8,128)(2,1)S(1)} %copy-done.6, ...), custom_call_target="tpu_custom_call" | custom-call | flops 905969664 | bytes 1769472 | tf_op jit(solution)/shard_map/pallas_call | solution.py:105
  (78 shorter events, 0.4 us)
Async XLA Ops:
  3.8 11.2 %copy-start.25 = (f32[384]{0:T(512)S(1)}, f32[384]{0:T(512)}, u32[]{:S(2)}) copy-start(f32[384]{0:T(512)} %param.17) | copy-start | bytes 4612
  3.8 11.3 %copy-start.29 = (s32[16]{0:T(128)S(1)}, s32[16]{0:T(128)}, u32[]{:S(2)}) copy-start(s32[16]{0:T(128)} %param.27) | copy-start | bytes 196
  3.8 11.3 %copy-start.30 = (s32[16]{0:T(128)S(1)}, s32[16]{0:T(128)}, u32[]{:S(2)}) copy-start(s32[16]{0:T(128)} %param.24) | copy-start | bytes 196
  3.8 11.3 %copy-start.31 = (s32[16]{0:T(128)S(1)}, s32[16]{0:T(128)}, u32[]{:S(2)}) copy-start(s32[16]{0:T(128)} %param.25) | copy-start | bytes 196
  3.8 11.3 %copy-start.32 = (s32[16]{0:T(128)S(1)}, s32[16]{0:T(128)}, u32[]{:S(2)}) copy-start(s32[16]{0:T(128)} %param.23) | copy-start | bytes 196
  3.8 11.3 %copy-start.33 = (s32[16]{0:T(128)S(1)}, s32[16]{0:T(128)}, u32[]{:S(2)}) copy-start(s32[16]{0:T(128)} %param.26) | copy-start | bytes 196
  3.9 55.1 %all-to-all-start = ((bf16[128,4,8,384]{3,2,1,0:T(8,128)(2,1)}), bf16[128,4,8,384]{3,2,1,0:T(8,128)(2,1)S(1)}, u32[]{:S(2)}, u32[]{:S(2)}) async-start(bf16[128,4,8,384]{3,2,1,0:T(8,128)(2,1)} %bitcast.34), calls=%async_computation | async-start | bytes 6291456 | tf_op jit(solution)/shard_map/all_to_all | solution.py:519
  16.0 1.1 copy-start.3
  19.9 0.9 copy-start.20
  20.7 12.1 %collective-permute-start = (bf16[4,128,384]{2,1,0:T(8,128)(2,1)}, bf16[4,128,384]{2,1,0:T(8,128)(2,1)S(1)}, u32[]{:S(2)}, u32[]{:S(2)}) collective-permute-start(bf16[4,128,384]{2,1,0:T(8,128)(2,1)} %get-tuple-element.45), channel_id=1, source_target_pairs={{0,1},{1,0},{2,3},{3,2},{4,5},{5,4},{6,7},{7,6},{8,9},{9,8},{10,11... | collective-permute-start | bytes 1179656 | tf_op jit(solution)/shard_map/ppermute | solution.py:511
  20.7 38.2 %collective-permute-start.1 = (bf16[4,128,384]{2,1,0:T(8,128)(2,1)}, bf16[4,128,384]{2,1,0:T(8,128)(2,1)}, u32[]{:S(2)}, u32[]{:S(2)}) collective-permute-start(bf16[4,128,384]{2,1,0:T(8,128)(2,1)} %get-tuple-element.46), channel_id=1, source_target_pairs={{0,31},{1,2},{2,1},{3,4},{4,3},{5,6},{6,5},{7,8},{8,7},{9,10},{10,... | collective-permute-start | bytes 1179656 | tf_op jit(solution)/shard_map/ppermute | solution.py:514
  26.0 3.3 %copy-start.1 = (bf16[3,3,3,384,384]{4,3,2,1,0:T(8,128)(2,1)S(1)}, bf16[3,3,3,384,384]{4,3,2,1,0:T(8,128)(2,1)}, u32[]{:S(2)}) copy-start(bf16[3,3,3,384,384]{4,3,2,1,0:T(8,128)(2,1)} %w_ref.2) | copy-start | bytes 23887876
  29.3 3.6 %copy-start.34 = (s32[16]{0:T(128)S(1)}, s32[16]{0:T(128)}, u32[]{:S(2)}) copy-start(s32[16]{0:T(128)} %get-tuple-element.85) | copy-start | bytes 196
  29.8 1.8 %copy-start.16 = (bf16[768,2304]{1,0:T(8,128)(2,1)}, bf16[768,2304]{1,0:T(8,128)(2,1)S(1)}, u32[]{:S(2)}) copy-start(bf16[768,2304]{1,0:T(8,128)(2,1)S(1)} %get-tuple-element.55.wo_ref) | copy-start | bytes 10616836
  31.5 1.3 copy-start.18
  60.6 1.6 %copy-start.2 = (bf16[4,32,4,8,384]{4,3,2,1,0:T(8,128)(2,1)}, bf16[4,32,4,8,384]{4,3,2,1,0:T(8,128)(2,1)S(1)}, u32[]{:S(2)}) copy-start(bf16[4,32,4,8,384]{4,3,2,1,0:T(8,128)(2,1)S(1)} %shard_map.160) | copy-start | bytes 9437188
  62.3 48.4 %all-to-all-start.1 = ((bf16[128,4,8,384]{3,2,1,0:T(8,128)(2,1)}), bf16[128,4,8,384]{3,2,1,0:T(8,128)(2,1)S(1)}, u32[]{:S(2)}, u32[]{:S(2)}) async-start(bf16[128,4,8,384]{3,2,1,0:T(8,128)(2,1)} %bitcast.29), calls=%async_computation.1 | async-start | bytes 6291456 | tf_op jit(solution)/shard_map/all_to_all | solution.py:530
  68.8 2.0 %copy-start.17 = (bf16[768,2304]{1,0:T(8,128)(2,1)S(1)}, bf16[768,2304]{1,0:T(8,128)(2,1)}, u32[]{:S(2)}) copy-start(bf16[768,2304]{1,0:T(8,128)(2,1)} %copy-done.16) | copy-start | bytes 10616836
  70.8 1.5 %copy-start.19 = (bf16[2,384,1152]{2,1,0:T(8,128)(2,1)S(1)}, bf16[2,384,1152]{2,1,0:T(8,128)(2,1)}, u32[]{:S(2)}) copy-start(bf16[2,384,1152]{2,1,0:T(8,128)(2,1)} %copy-done.18) | copy-start | bytes 5308420
  72.3 1.1 copy-start.21
  73.4 18.8 %slice-start = ((s8[7962624]{0:T(1024)(128)(4,1)}), s8[4194304]{0:T(1024)(128)(4,1)S(1)}, s32[]{:S(2)}) async-start(s8[7962624]{0:T(1024)(128)(4,1)} %bitcast.23), calls=%async_computation.2 | async-start | bytes 8388608
  78.0 1.1 copy-start.23
  79.2 3.3 %copy-start = (bf16[3,3,3,384,384]{4,3,2,1,0:T(8,128)(2,1)S(1)}, bf16[3,3,3,384,384]{4,3,2,1,0:T(8,128)(2,1)}, u32[]{:S(2)}) copy-start(bf16[3,3,3,384,384]{4,3,2,1,0:T(8,128)(2,1)} %w_ref.4) | copy-start | bytes 23887876
  82.4 9.8 %slice-start.1 = ((s8[7962624]{0:T(1024)(128)(4,1)}), s8[3768320]{0:T(1024)(128)(4,1)S(1)}, s32[]{:S(2)}) async-start(s8[7962624]{0:T(1024)(128)(4,1)} %bitcast.23), calls=%async_computation.3 | async-start | bytes 7536640
  83.0 1.3 copy-start.5
  84.3 1.8 %copy-start.10 = (bf16[768,2304]{1,0:T(8,128)(2,1)}, bf16[768,2304]{1,0:T(8,128)(2,1)S(1)}, u32[]{:S(2)}) copy-start(bf16[768,2304]{1,0:T(8,128)(2,1)S(1)} %get-tuple-element.77.wa_ref) | copy-start | bytes 10616836
  87.6 2.8 %copy-start.7 = (bf16[1536,2304]{1,0:T(8,128)(2,1)}, bf16[1536,2304]{1,0:T(8,128)(2,1)S(1)}, u32[]{:S(2)}) copy-start(bf16[1536,2304]{1,0:T(8,128)(2,1)S(1)} %get-tuple-element.79.w_ref) | copy-start | bytes 21233668
  90.4 1.8 %copy-start.12 = (bf16[2,768,1152]{2,1,0:T(8,128)(2,1)}, bf16[2,768,1152]{2,1,0:T(8,128)(2,1)S(1)}, u32[]{:S(2)}) copy-start(bf16[2,768,1152]{2,1,0:T(8,128)(2,1)S(1)} %get-tuple-element.76.w_ref) | copy-start | bytes 10616836
  93.8 2.9 %copy-start.8 = (bf16[1536,2304]{1,0:T(8,128)(2,1)}, bf16[1536,2304]{1,0:T(8,128)(2,1)S(1)}, u32[]{:S(2)}) copy-start(bf16[1536,2304]{1,0:T(8,128)(2,1)S(1)} %get-tuple-element.68.w_ref) | copy-start | bytes 21233668
  96.7 1.8 %copy-start.14 = (bf16[2,768,1152]{2,1,0:T(8,128)(2,1)}, bf16[2,768,1152]{2,1,0:T(8,128)(2,1)S(1)}, u32[]{:S(2)}) copy-start(bf16[2,768,1152]{2,1,0:T(8,128)(2,1)S(1)} %get-tuple-element.67.w_ref) | copy-start | bytes 10616836
  110.6 6.1 %copy-start.9 = (bf16[1536,2304]{1,0:T(8,128)(2,1)S(1)}, bf16[1536,2304]{1,0:T(8,128)(2,1)}, u32[]{:S(2)}) copy-start(bf16[1536,2304]{1,0:T(8,128)(2,1)} %copy-done.8) | copy-start | bytes 21233668
  111.0 0.8 copy-start.27
  111.0 0.8 copy-start.28
  111.2 5.5 %copy-start.22 = (bf16[4,2,128,384]{3,2,1,0:T(8,128)(2,1)S(1)}, bf16[4,2,128,384]{3,2,1,0:T(8,128)(2,1)}, u32[]{:S(2)}) copy-start(bf16[4,2,128,384]{3,2,1,0:T(8,128)(2,1)} %copy-done.20) | copy-start | bytes 2359300
  111.2 5.5 %copy-start.24 = (f32[2,16,4,8,384]{4,3,2,1,0:T(8,128)S(1)}, f32[2,16,4,8,384]{4,3,2,1,0:T(8,128)}, u32[]{:S(2)}) copy-start(f32[2,16,4,8,384]{4,3,2,1,0:T(8,128)} %copy-done.23) | copy-start | bytes 4718596
  111.2 14.8 %collective-permute-start.3 = (bf16[2,16,4,8,384]{4,3,2,1,0:T(8,128)(2,1)S(1)}, bf16[2,16,4,8,384]{4,3,2,1,0:T(8,128)(2,1)S(1)}, u32[]{:S(2)}, u32[]{:S(2)}) collective-permute-start(bf16[2,16,4,8,384]{4,3,2,1,0:T(8,128)(2,1)S(1)} %get-tuple-element.93), channel_id=1, source_target_pairs={{0,31},{1,2},{2,1},{3,4},{4,3},{5,6},{6,5},{7,8},{8,7},{9,10},{10,... | collective-permute-start | bytes 2359304 | tf_op jit(solution)/shard_map/ppermute | solution.py:514
  111.5 14.5 %collective-permute-start.2 = (bf16[2,16,4,8,384]{4,3,2,1,0:T(8,128)(2,1)S(1)}, bf16[2,16,4,8,384]{4,3,2,1,0:T(8,128)(2,1)S(1)}, u32[]{:S(2)}, u32[]{:S(2)}) collective-permute-start(bf16[2,16,4,8,384]{4,3,2,1,0:T(8,128)(2,1)S(1)} %get-tuple-element.94), channel_id=1, source_target_pairs={{0,1},{1,0},{2,3},{3,2},{4,5},{5,4},{6,7},{7,6},{8,9},{9,8},{10,11... | collective-permute-start | bytes 2359304 | tf_op jit(solution)/shard_map/ppermute | solution.py:511
  111.8 18.0 %slice-start.2 = ((s8[7077888]{0:T(1024)(128)(4,1)}), s8[4194304]{0:T(1024)(128)(4,1)S(1)}, s32[]{:S(2)}) async-start(s8[7077888]{0:T(1024)(128)(4,1)} %bitcast.30), calls=%async_computation.4 | async-start | bytes 8388608
  112.0 22.4 %collective-permute-start.7 = (bf16[2,16,4,8,384]{4,3,2,1,0:T(8,128)(2,1)S(1)}, bf16[2,16,4,8,384]{4,3,2,1,0:T(8,128)(2,1)S(1)}, u32[]{:S(2)}, u32[]{:S(2)}) collective-permute-start(bf16[2,16,4,8,384]{4,3,2,1,0:T(8,128)(2,1)S(1)} %get-tuple-element.91), channel_id=1, source_target_pairs={{0,31},{1,2},{2,1},{3,4},{4,3},{5,6},{6,5},{7,8},{8,7},{9,10},{10,... | collective-permute-start | bytes 2359304 | tf_op jit(solution)/shard_map/ppermute | solution.py:514
  116.7 17.7 %collective-permute-start.6 = (bf16[2,16,4,8,384]{4,3,2,1,0:T(8,128)(2,1)S(1)}, bf16[2,16,4,8,384]{4,3,2,1,0:T(8,128)(2,1)S(1)}, u32[]{:S(2)}, u32[]{:S(2)}) collective-permute-start(bf16[2,16,4,8,384]{4,3,2,1,0:T(8,128)(2,1)S(1)} %get-tuple-element.92), channel_id=1, source_target_pairs={{0,1},{1,0},{2,3},{3,2},{4,5},{5,4},{6,7},{7,6},{8,9},{9,8},{10,11... | collective-permute-start | bytes 2359304 | tf_op jit(solution)/shard_map/ppermute | solution.py:511
  116.8 9.3 %copy-start.15 = (bf16[2,768,1152]{2,1,0:T(8,128)(2,1)S(1)}, bf16[2,768,1152]{2,1,0:T(8,128)(2,1)}, u32[]{:S(2)}) copy-start(bf16[2,768,1152]{2,1,0:T(8,128)(2,1)} %copy-done.14) | copy-start | bytes 10616836
  116.8 13.1 %slice-start.3 = ((s8[7077888]{0:T(1024)(128)(4,1)}), s8[2883584]{0:T(1024)(128)(4,1)S(1)}, s32[]{:S(2)}) async-start(s8[7077888]{0:T(1024)(128)(4,1)} %bitcast.30), calls=%async_computation.5 | async-start | bytes 5767168
  129.5 10.4 %collective-permute-start.4 = (bf16[4,128,384]{2,1,0:T(8,128)(2,1)S(1)}, bf16[4,128,384]{2,1,0:T(8,128)(2,1)S(1)}, u32[]{:S(2)}, u32[]{:S(2)}) collective-permute-start(bf16[4,128,384]{2,1,0:T(8,128)(2,1)S(1)} %get-tuple-element.71), channel_id=1, source_target_pairs={{0,1},{1,0},{2,3},{3,2},{4,5},{5,4},{6,7},{7,6},{8,9},{9,8},{10,11... | collective-permute-start | bytes 1179656 | tf_op jit(solution)/shard_map/ppermute | solution.py:511
  129.6 4.9 %copy-start.11 = (bf16[768,2304]{1,0:T(8,128)(2,1)S(1)}, bf16[768,2304]{1,0:T(8,128)(2,1)}, u32[]{:S(2)}) copy-start(bf16[768,2304]{1,0:T(8,128)(2,1)} %copy-done.10) | copy-start | bytes 10616836
  129.6 4.9 %copy-start.13 = (bf16[2,768,1152]{2,1,0:T(8,128)(2,1)S(1)}, bf16[2,768,1152]{2,1,0:T(8,128)(2,1)}, u32[]{:S(2)}) copy-start(bf16[2,768,1152]{2,1,0:T(8,128)(2,1)} %copy-done.12) | copy-start | bytes 10616836
  129.6 10.6 %collective-permute-start.5 = (bf16[4,128,384]{2,1,0:T(8,128)(2,1)S(1)}, bf16[4,128,384]{2,1,0:T(8,128)(2,1)S(1)}, u32[]{:S(2)}, u32[]{:S(2)}) collective-permute-start(bf16[4,128,384]{2,1,0:T(8,128)(2,1)S(1)} %get-tuple-element.72), channel_id=1, source_target_pairs={{0,31},{1,2},{2,1},{3,4},{4,3},{5,6},{6,5},{7,8},{8,7},{9,10},{10,... | collective-permute-start | bytes 1179656 | tf_op jit(solution)/shard_map/ppermute | solution.py:514
  134.5 5.7 %copy-start.4 = (bf16[4,2,128,384]{3,2,1,0:T(8,128)(2,1)S(1)}, bf16[4,2,128,384]{3,2,1,0:T(8,128)(2,1)}, u32[]{:S(2)}) copy-start(bf16[4,2,128,384]{3,2,1,0:T(8,128)(2,1)} %f_ref.3) | copy-start | bytes 2359300
  134.5 5.7 %copy-start.6 = (bf16[2,384,1152]{2,1,0:T(8,128)(2,1)S(1)}, bf16[2,384,1152]{2,1,0:T(8,128)(2,1)}, u32[]{:S(2)}) copy-start(bf16[2,384,1152]{2,1,0:T(8,128)(2,1)} %copy-done.5) | copy-start | bytes 5308420
  (1 other events, 0.8 us)

commit v13 on v12

--- a/solution.py
+++ b/solution.py
@@ -265,24 +265,19 @@
         add_into(o_ref, y, folded(both[:, y * wide : (y + 1) * wide], ch, False), False, base)
 
 
-def current_part(act, near, far, w_own, w_sides, edges):
+def current_part(act, w_own):
     n_slots, n_rows, n_cols, ch = act.shape
     half = n_slots * n_cols
 
-    def body(edge_ref, act_ref, near_ref, far_ref, wo_ref, ws_ref, o_ref, lhs, side):
-        add_own(act_ref, wo_ref, lhs, o_ref, None)
-        add_sides(edge_ref, (near_ref, far_ref), ws_ref, side, o_ref)
+    def body(act_ref, w_ref, o_ref, lhs):
+        add_own(act_ref, w_ref, lhs, o_ref, None)
 
     return call(
         body,
         [sums_shape(n_cols // CB, n_slots, n_rows, ch)],
-        (act, near, far, w_own, w_sides),
-        scalars=(edges,),
-        scratch=[
-            pltpu.VMEM((half, n_rows * ch), jnp.bfloat16),
-            pltpu.VMEM((half, ch), jnp.bfloat16),
-        ],
-        flops=2 * half * (w_own.size + w_sides.size),
+        (act, w_own),
+        scratch=[pltpu.VMEM((half, n_rows * ch), jnp.bfloat16)],
+        flops=2 * half * w_own.size,
         moved=2 * w_own.size + 8 * act.size,
     )[0]
 
@@ -302,12 +297,12 @@
         add_into(o_ref, y, folded(acc[:, y * wide : (y + 1) * wide], ch, True), True, base)
 
 
-def own_first(got, weight, sums, act):
+def own_first(got, weight, sums, act, near, far, w_sides, edges):
     n_rows, _, n_frames, blocks, n_slots, _, ch = got.shape
     half = blocks * n_slots * CB
     deep = n_frames * ch
 
-    def body(got_ref, w_ref, z_ref, act_ref, o_ref, next_ref, lhs, acc, keep_sems, act_sem):
+    def body(edge_ref, got_ref, w_ref, z_ref, act_ref, near_ref, far_ref, ws_ref, o_ref, next_ref, lhs, acc, side, keep_sems, act_sem):
         keeps = [pltpu.make_async_copy(act_ref, next_ref.at[:, 1], act_sem)]
         for r in range(n_rows):
             for s in range(n_slots):
@@ -319,6 +314,7 @@
         own_rows(got_ref, 0, lhs)
         acc[...] = dot(lhs[...], w_ref[...])
         give_rows(acc, ch, o_ref, z_ref)
+        add_sides(edge_ref, (near_ref, far_ref), ws_ref, side, o_ref)
         for c in keeps:
             c.wait()
 
@@ -328,14 +324,16 @@
             sums_shape(blocks, n_slots, n_rows, ch),
             jax.ShapeDtypeStruct((n_slots, 2, n_rows, blocks, CB, ch), jnp.bfloat16),
         ],
-        (got, weight, sums, act),
+        (got, weight, sums, act, near, far, w_sides),
+        scalars=(edges,),
         scratch=[
             pltpu.VMEM((half, n_rows * deep), jnp.bfloat16),
             pltpu.VMEM((half, weight.shape[1]), jnp.float32),
+            pltpu.VMEM((half, ch), jnp.bfloat16),
             pltpu.SemaphoreType.DMA((n_rows * n_slots,)),
             pltpu.SemaphoreType.DMA,
         ],
-        flops=2 * half * weight.size,
+        flops=2 * half * (weight.size + w_sides.size),
         moved=2 * weight.size,
         far_out=(1,),
     )
@@ -521,32 +519,33 @@
     act_own_1, act_sides_1 = spread(conv_first, False)
     act_first, near, far = first_activation(frame_in, gain_first[None], edges)
     act_near, act_far = swap_near(near), swap_far(far)
-    held, act_first, act_near, act_far, act_own_1, act_sides_1 = lax.optimization_barrier(
-        (held, act_first, act_near, act_far, act_own_1, act_sides_1)
-    )
+    sums_1 = current_part(act_first, act_own_1)
+    own_1, sides_1 = spread(conv_first, True)
+    own_2, sides_2 = spread(conv_second, True)
+    act_own_2, act_sides_2 = spread(conv_second, False)
+    (
+        held, sums_1, act_near, act_far, act_sides_1, own_1, sides_1, own_2, sides_2, act_own_2, act_sides_2,
+    ) = lax.optimization_barrier((
+        held, sums_1, act_near, act_far, act_sides_1, own_1, sides_1, own_2, sides_2, act_own_2, act_sides_2,
+    ))
 
     moved = permute(held.reshape(n_groups, n_tiles, n_slots, CB, ch), source, rotation, keep)
-    moved, act_later = lax.optimization_barrier((moved, act_first))
     got = lax.all_to_all(
         moved.reshape(n_groups * n_tiles, n_slots, CB, ch), BOTH, 0, 0, tiled=True
     )
-    sums_1 = current_part(act_later, act_near, act_far, act_own_1, act_sides_1, edges)
-    sums_1, conv_first, conv_second = lax.optimization_barrier((sums_1, conv_first, conv_second))
-    act_own_2, act_sides_2 = spread(conv_second, False)
-    own_1, sides_1 = spread(conv_first, True)
-    own_2, sides_2 = spread(conv_second, True)
-    got, sums_1, own_1, own_2, sides_1, sides_2, act_own_2, act_sides_2 = lax.optimization_barrier(
-        (got, sums_1, own_1, own_2, sides_1, sides_2, act_own_2, act_sides_2)
-    )
     got = got.reshape(n_rows, 2, 2, blocks, n_slots, CB, ch)
 
     def picked(cache, row):
         return lax.dynamic_index_in_dim(got[:, cache], row, 0, keepdims=False)
 
     near_1, far_1 = swap_near(picked(0, 1 - odd)), swap_far(picked(0, odd))
-    near_2, far_2 = swap_near(picked(1, 1 - odd)), swap_far(picked(1, odd))
+    near_2, far_rows = swap_near(picked(1, 1 - odd)), picked(1, odd)
     act_tiles = act_first.reshape(n_slots, n_rows, blocks, CB, ch)
-    sums_1, next_first = own_first(got, own_1, sums_1, act_tiles)
+    sums_1, next_first = own_first(
+        got, own_1, sums_1, act_tiles, act_near, act_far, act_sides_1, edges
+    )
+    far_rows, sums_1 = lax.optimization_barrier((far_rows, sums_1))
+    far_2 = swap_far(far_rows)
     act_second, near, far = second_activation(
         near_1, far_1, sides_1, sums_1, bias_first[None], gain_second[None], edges
     )

time: 144 us -> 147 us (1.021)
  waiting for transfers between devices: 43.9 us -> 48.9 us
  local copies, waits for them, and re-layouts: 32.5 us -> 29.6 us
    all_to_all x1, waiting for transfers between devices: 12.1 us -> 41.8 us  [local(): lax.all_to_all(moved.reshape(n_groups * n_tiles, n_slots, CB, ch), BOTH,...]
    ppermute x4, waiting for transfers between devices: 31.8 us -> 7.1 us  [swap_far(): lax.ppermute(row, 'tile', [(i, (i + 2 * (i % 2) - 1) % n_tiles) for i in...]
    unnamed x78 -> x76, local copies, waits for them, and re-layouts: 31.7 us -> 28.8 us
  transfers between devices with their start and end apart: 10 -> 10, of which waited for: 5 -> 3; matrix products, arithmetic and copies ran while one was open for 1% -> 1% of each run, Pallas kernels for 20% -> 19%
where the time goes in v13:
time: 147 us; the launch traced here: 146 us
  waiting for transfers between devices  48.9 us (33%)
  Pallas kernels  36.2 us (25%)
  starting transfers between devices  29.8 us (20%)
  local copies, waits for them, and re-layouts  29.6 us (20%)
    all_to_all x1, waiting for transfers between devices, local(): lax.all_to_all(moved.reshape(n_groups * n_tiles, n_slots, CB, ch), BOTH,...  41.8 us
    unnamed x76, local copies, waits for them, and re-layouts  28.8 us
    pallas_call x7, Pallas kernels, call(): pl.pallas_call(body, in_specs=in_specs, out_specs=out_specs, out_shape=li...  27.5 us
    ppermute x4, starting transfers between devices, swap_far(): lax.ppermute(row, 'tile', [(i, (i + 2 * (i % 2) - 1) % n_tiles) for i in...  11.3 us
    all_to_all x1, starting transfers between devices, local(): held = lax.all_to_all(sent, BOTH, 0, 0, tiled=True)  11.1 us
    ppermute x4, waiting for transfers between devices, swap_far(): lax.ppermute(row, 'tile', [(i, (i + 2 * (i % 2) - 1) % n_tiles) for i in...  7.1 us
    all_to_all x1, starting transfers between devices, local(): lax.all_to_all(moved.reshape(n_groups * n_tiles, n_slots, CB, ch), BOTH,...  6.69 us
    pallas_call x4, Pallas kernels, spread(): pl.pallas_call(body, grid=(n_y,), in_specs=[pl.BlockSpec((times, 1, n_x,...  4.13 us
  transfers between devices with their start and end apart: 10, of which 3 were waited for; matrix products, arithmetic and copies ran while one was open for 1% of the time, Pallas kernels for 19%

profile of v13, /device:TPU:0, one launch (start us, length us, event | category | flops | bytes accessed | tf_op | source)
XLA Modules:
  0.0 146.5 jit_solution(17833092749484800275)
XLA Ops:
  0.6 3.1 %shard_map.157 = bf16[2,2,2,16,4,8,384]{6,5,4,3,2,1,0:T(8,128)(2,1)} custom-call(bf16[4,2,2,16,8,384]{5,4,3,2,1,0:T(8,128)(2,1)} %bitcast.35, bf16[4,2,2,16,8,384]{5,4,3,2,1,0:T(8,128)(2,1)} %bitcast.36), custom_call_target="tpu_custom_call" | custom-call | tf_op jit(solution)/shard_map/pallas_call | solution.py:47
  3.8 11.1 %all-to-all-start = ((bf16[128,4,8,384]{3,2,1,0:T(8,128)(2,1)}), bf16[128,4,8,384]{3,2,1,0:T(8,128)(2,1)S(1)}, u32[]{:S(2)}, u32[]{:S(2)}) async-start(bf16[128,4,8,384]{3,2,1,0:T(8,128)(2,1)} %bitcast.34), calls=%async_computation | async-start | bytes 6291456 | tf_op jit(solution)/shard_map/all_to_all | solution.py:517
  15.0 0.1 pad.2.clone
  15.1 0.7 select_reduce_fusion
  15.8 0.1 compare_bitcast_fusion.1
  15.9 1.1 copy-done.2
  17.1 2.8 %shard_map.158 = (bf16[4,2,128,384]{3,2,1,0:T(8,128)(2,1)S(1)}, bf16[4,128,384]{2,1,0:T(8,128)(2,1)}, bf16[4,128,384]{2,1,0:T(8,128)(2,1)}) custom-call(s32[3,4]{1,0:T(4,128)S(1)} %add_convert_fusion.edge_ref, bf16[4,2,128,384]{3,2,1,0:T(8,128)(2,1)S(1)} %copy-done.2, f32[1,384]{1,0:T(1,128)S(1)} %broadcast_in_dim.53.g_ref), custom_call_target="tpu_custom_call" | custom-call | flops 3932160 | bytes 2359296 | tf_op jit(solution)/shard_map/pallas_call | solution.py:105
  19.9 0.9 copy-done.19
  20.7 5.3 %collective-permute-start.1 = (bf16[4,128,384]{2,1,0:T(8,128)(2,1)}, bf16[4,128,384]{2,1,0:T(8,128)(2,1)}, u32[]{:S(2)}, u32[]{:S(2)}) collective-permute-start(bf16[4,128,384]{2,1,0:T(8,128)(2,1)} %get-tuple-element.41), channel_id=1, source_target_pairs={{0,31},{1,2},{2,1},{3,4},{4,3},{5,6},{6,5},{7,8},{8,7},{9,10},{10,... | collective-permute-start | bytes 1179656 | tf_op jit(solution)/shard_map/ppermute | solution.py:512
  26.0 3.3 %copy-done = bf16[3,3,3,384,384]{4,3,2,1,0:T(8,128)(2,1)S(1)} copy-done((bf16[3,3,3,384,384]{4,3,2,1,0:T(8,128)(2,1)S(1)}, bf16[3,3,3,384,384]{4,3,2,1,0:T(8,128)(2,1)}, u32[]{:S(2)}) %copy-start) | copy-done | bytes 7962648
  29.3 0.5 shard_map.159
  29.8 1.8 %copy-done.15 = bf16[768,2304]{1,0:T(8,128)(2,1)} copy-done((bf16[768,2304]{1,0:T(8,128)(2,1)}, bf16[768,2304]{1,0:T(8,128)(2,1)S(1)}, u32[]{:S(2)}) %copy-start.15) | copy-done | bytes 3538968
  31.6 1.2 copy-done.17
  32.8 1.5 %shard_map.161 = (bf16[1536,2304]{1,0:T(8,128)(2,1)S(1)}, bf16[2,768,1152]{2,1,0:T(8,128)(2,1)S(1)}) custom-call(bf16[3,3,3,384,384]{4,3,2,1,0:T(8,128)(2,1)S(1)} %copy-done), custom_call_target="tpu_custom_call" | custom-call | bytes 15925248 | tf_op jit(solution)/shard_map/pallas_call | solution.py:154
  34.3 2.9 %copy-done.7 = bf16[1536,2304]{1,0:T(8,128)(2,1)} copy-done((bf16[1536,2304]{1,0:T(8,128)(2,1)}, bf16[1536,2304]{1,0:T(8,128)(2,1)S(1)}, u32[]{:S(2)}) %copy-start.7) | copy-done | bytes 7077912
  37.3 1.6 %shard_map.162 = (bf16[1536,2304]{1,0:T(8,128)(2,1)S(1)}, bf16[2,768,1152]{2,1,0:T(8,128)(2,1)S(1)}) custom-call(bf16[3,3,3,384,384]{4,3,2,1,0:T(8,128)(2,1)S(1)} %bitcast.24), custom_call_target="tpu_custom_call" | custom-call | bytes 15925248 | tf_op jit(solution)/shard_map/pallas_call | solution.py:154
  38.9 0.2 copy-done.13
  39.1 2.8 %copy-done.6 = bf16[1536,2304]{1,0:T(8,128)(2,1)} copy-done((bf16[1536,2304]{1,0:T(8,128)(2,1)}, bf16[1536,2304]{1,0:T(8,128)(2,1)S(1)}, u32[]{:S(2)}) %copy-start.6) | copy-done | bytes 7077912
  41.9 1.8 %copy-done.9 = bf16[2,768,1152]{2,1,0:T(8,128)(2,1)} copy-done((bf16[2,768,1152]{2,1,0:T(8,128)(2,1)}, bf16[2,768,1152]{2,1,0:T(8,128)(2,1)S(1)}, u32[]{:S(2)}) %copy-start.9) | copy-done | bytes 3538968
  43.7 0.5 shard_map.163
  44.2 1.2 copy-done.4
  45.4 1.8 %copy-done.11 = bf16[768,2304]{1,0:T(8,128)(2,1)} copy-done((bf16[768,2304]{1,0:T(8,128)(2,1)}, bf16[768,2304]{1,0:T(8,128)(2,1)S(1)}, u32[]{:S(2)}) %copy-start.11) | copy-done | bytes 3538968
  47.3 2.0 %copy-done.16 = bf16[768,2304]{1,0:T(8,128)(2,1)S(1)} copy-done((bf16[768,2304]{1,0:T(8,128)(2,1)S(1)}, bf16[768,2304]{1,0:T(8,128)(2,1)}, u32[]{:S(2)}) %copy-start.16) | copy-done | bytes 3538968
  49.3 1.1 copy-done.20
  50.4 2.0 %shard_map.160.z_ref = f32[2,16,4,8,384]{4,3,2,1,0:T(8,128)S(1)} custom-call(bf16[4,2,128,384]{3,2,1,0:T(8,128)(2,1)S(1)} %copy-done.20, bf16[768,2304]{1,0:T(8,128)(2,1)S(1)} %copy-done.16), custom_call_target="tpu_custom_call" | custom-call | flops 1811939328 | bytes 6684672 | tf_op jit(solution)/shard_map/pallas_call | solution.py:105
  52.4 1.1 copy-done.22
  53.6 5.4 %collective-permute-done.1.far_ref = bf16[4,128,384]{2,1,0:T(8,128)(2,1)} collective-permute-done((bf16[4,128,384]{2,1,0:T(8,128)(2,1)}, bf16[4,128,384]{2,1,0:T(8,128)(2,1)}, u32[]{:S(2)}, u32[]{:S(2)}) %collective-permute-start.1) | collective-permute-done | bytes 393248 | tf_op jit(solution)/shard_map/ppermute | solution.py:512
  59.0 1.5 shard_map.164
  60.4 1.6 %copy-done.1 = bf16[4,32,4,8,384]{4,3,2,1,0:T(8,128)(2,1)} copy-done((bf16[4,32,4,8,384]{4,3,2,1,0:T(8,128)(2,1)}, bf16[4,32,4,8,384]{4,3,2,1,0:T(8,128)(2,1)S(1)}, u32[]{:S(2)}) %copy-start.1) | copy-done | bytes 3145752
  62.1 6.7 %all-to-all-start.1 = ((bf16[128,4,8,384]{3,2,1,0:T(8,128)(2,1)}), bf16[128,4,8,384]{3,2,1,0:T(8,128)(2,1)S(1)}, u32[]{:S(2)}, u32[]{:S(2)}) async-start(bf16[128,4,8,384]{3,2,1,0:T(8,128)(2,1)} %bitcast.29), calls=%async_computation.1 | async-start | bytes 6291456 | tf_op jit(solution)/shard_map/all_to_all | solution.py:533
  68.8 41.8 %all-to-all-done.1 = bf16[128,4,8,384]{3,2,1,0:T(8,128)(2,1)S(1)} async-done(((bf16[128,4,8,384]{3,2,1,0:T(8,128)(2,1)}), bf16[128,4,8,384]{3,2,1,0:T(8,128)(2,1)S(1)}, u32[]{:S(2)}, u32[]{:S(2)}) %all-to-all-start.1) | async-done | bytes 3145760 | tf_op jit(solution)/shard_map/all_to_all | solution.py:533
  110.6 0.3 fusion.2
  111.0 0.2 dynamic-slice_bitcast_fusion.2
  111.2 0.1 collective-permute-start.2
  111.3 0.9 collective-permute-start.3
  112.2 0.2 dynamic-slice_bitcast_fusion
  112.4 0.2 copy-done.18
  112.6 0.2 copy-done.21
  112.8 3.3 %copy-done.8 = bf16[1536,2304]{1,0:T(8,128)(2,1)S(1)} copy-done((bf16[1536,2304]{1,0:T(8,128)(2,1)S(1)}, bf16[1536,2304]{1,0:T(8,128)(2,1)}, u32[]{:S(2)}) %copy-start.8) | copy-done | bytes 7077912
  116.1 7.1 %shard_map.165 = (f32[2,16,4,8,384]{4,3,2,1,0:T(8,128)S(1)}, bf16[4,2,2,16,8,384]{5,4,3,2,1,0:T(8,128)(2,1)}) custom-call(s32[3,4]{1,0:T(4,128)S(1)} %add_convert_fusion.edge_ref, bf16[2,2,2,16,4,8,384]{6,5,4,3,2,1,0:T(8,128)(2,1)S(1)} %bitcast.26, bf16[1536,2304]{1,0:T(8,128)(2,1)S(1)} %copy-done.8, f32[2,16,4,8,384]{4,3,2,1,0:T(8,128)S(1)} %copy-done.23, ...), custom_call_target="tpu_custom_call" | custom-call | flops 4529848320 | bytes 7077888 | tf_op jit(solution)/shard_map/pallas_call | solution.py:105
  123.2 4.0 %collective-permute-start.7 = (bf16[2,16,4,8,384]{4,3,2,1,0:T(8,128)(2,1)S(1)}, bf16[2,16,4,8,384]{4,3,2,1,0:T(8,128)(2,1)S(1)}, u32[]{:S(2)}, u32[]{:S(2)}) collective-permute-start(bf16[2,16,4,8,384]{4,3,2,1,0:T(8,128)(2,1)S(1)} %get-tuple-element.61), channel_id=1, source_target_pairs={{0,31},{1,2},{2,1},{3,4},{4,3},{5,6},{6,5},{7,8},{8,7},{9,10},{10,... | collective-permute-start | bytes 2359304 | tf_op jit(solution)/shard_map/ppermute | solution.py:512
  127.2 3.3 %shard_map.166 = (bf16[4,2,128,384]{3,2,1,0:T(8,128)(2,1)S(1)}, bf16[4,128,384]{2,1,0:T(8,128)(2,1)S(1)}, bf16[4,128,384]{2,1,0:T(8,128)(2,1)S(1)}) custom-call(s32[3,4]{1,0:T(4,128)S(1)} %add_convert_fusion.edge_ref, bf16[2,16,4,8,384]{4,3,2,1,0:T(8,128)(2,1)S(1)} %collective-permute-done.2.near_ref, ...), custom_call_target="tpu_custom_call" | custom-call | flops 1811939328 | bytes 3538944 | tf_op jit(solution)/shard_map/pallas_call | solution.py:105
  130.6 0.6 collective-permute-start.4
  131.1 1.2 collective-permute-start.5
  132.3 4.0 %shard_map.167 = (f32[2,16,4,8,384]{4,3,2,1,0:T(8,128)S(1)}, bf16[4,2,2,16,8,384]{5,4,3,2,1,0:T(8,128)(2,1)}) custom-call(bf16[2,2,2,16,4,8,384]{6,5,4,3,2,1,0:T(8,128)(2,1)S(1)} %bitcast.27, bf16[1536,2304]{1,0:T(8,128)(2,1)S(1)} %bitcast.31), custom_call_target="tpu_custom_call" | custom-call | flops 3623878656 | bytes 7077888 | tf_op jit(solution)/shard_map/pallas_call | solution.py:105
  136.3 1.7 %collective-permute-done.7.far_ref = bf16[2,16,4,8,384]{4,3,2,1,0:T(8,128)(2,1)S(1)} collective-permute-done((bf16[2,16,4,8,384]{4,3,2,1,0:T(8,128)(2,1)S(1)}, bf16[2,16,4,8,384]{4,3,2,1,0:T(8,128)(2,1)S(1)}, u32[]{:S(2)}, u32[]{:S(2)}) %collective-permute-start.7) | collective-permute-done | bytes 786464 | tf_op jit(solution)/shard_map/ppermute | solution.py:512
  138.1 5.3 %shard_map.168 = (f32[2,16,4,8,384]{4,3,2,1,0:T(8,128)S(1)}, bf16[4,2,2,16,8,384]{5,4,3,2,1,0:T(8,128)(2,1)}) custom-call(s32[3,4]{1,0:T(4,128)S(1)} %add_convert_fusion.edge_ref, bf16[2,16,4,8,384]{4,3,2,1,0:T(8,128)(2,1)S(1)} %collective-permute-done.6.near_ref, ...), custom_call_target="tpu_custom_call", output_to_operand_aliasing={{1}: (8, {})} | custom-call | flops 3623878656 | bytes 7077888 | tf_op jit(solution)/shard_map/pallas_call | solution.py:105
  143.4 3.1 %shard_map.169 = bf16[4,2,128,384]{3,2,1,0:T(8,128)(2,1)} custom-call(s32[3,4]{1,0:T(4,128)S(1)} %add_convert_fusion.edge_ref, bf16[4,128,384]{2,1,0:T(8,128)(2,1)S(1)} %collective-permute-done.4.near_ref, bf16[4,128,384]{2,1,0:T(8,128)(2,1)S(1)} %collective-permute-done.5.far_ref, bf16[2,384,1152]{2,1,0:T(8,128)(2,1)S(1)} %copy-done.5, ...), custom_call_target="tpu_custom_call" | custom-call | flops 905969664 | bytes 1769472 | tf_op jit(solution)/shard_map/pallas_call | solution.py:105
  (76 shorter events, 0.3 us)
Async XLA Ops:
  3.7 11.2 %copy-start.24 = (f32[384]{0:T(512)S(1)}, f32[384]{0:T(512)}, u32[]{:S(2)}) copy-start(f32[384]{0:T(512)} %param.17) | copy-start | bytes 4612
  3.8 11.3 %copy-start.28 = (s32[16]{0:T(128)S(1)}, s32[16]{0:T(128)}, u32[]{:S(2)}) copy-start(s32[16]{0:T(128)} %param.27) | copy-start | bytes 196
  3.8 11.3 %copy-start.29 = (s32[16]{0:T(128)S(1)}, s32[16]{0:T(128)}, u32[]{:S(2)}) copy-start(s32[16]{0:T(128)} %param.24) | copy-start | bytes 196
  3.8 11.3 %copy-start.30 = (s32[16]{0:T(128)S(1)}, s32[16]{0:T(128)}, u32[]{:S(2)}) copy-start(s32[16]{0:T(128)} %param.25) | copy-start | bytes 196
  3.8 11.3 %copy-start.31 = (s32[16]{0:T(128)S(1)}, s32[16]{0:T(128)}, u32[]{:S(2)}) copy-start(s32[16]{0:T(128)} %param.23) | copy-start | bytes 196
  3.8 11.3 %copy-start.32 = (s32[16]{0:T(128)S(1)}, s32[16]{0:T(128)}, u32[]{:S(2)}) copy-start(s32[16]{0:T(128)} %param.26) | copy-start | bytes 196
  3.8 55.1 %all-to-all-start = ((bf16[128,4,8,384]{3,2,1,0:T(8,128)(2,1)}), bf16[128,4,8,384]{3,2,1,0:T(8,128)(2,1)S(1)}, u32[]{:S(2)}, u32[]{:S(2)}) async-start(bf16[128,4,8,384]{3,2,1,0:T(8,128)(2,1)} %bitcast.34), calls=%async_computation | async-start | bytes 6291456 | tf_op jit(solution)/shard_map/all_to_all | solution.py:517
  15.9 1.1 copy-start.2
  19.9 0.9 copy-start.19
  20.7 32.8 %collective-permute-start = (bf16[4,128,384]{2,1,0:T(8,128)(2,1)}, bf16[4,128,384]{2,1,0:T(8,128)(2,1)S(1)}, u32[]{:S(2)}, u32[]{:S(2)}) collective-permute-start(bf16[4,128,384]{2,1,0:T(8,128)(2,1)} %get-tuple-element.40), channel_id=1, source_target_pairs={{0,1},{1,0},{2,3},{3,2},{4,5},{5,4},{6,7},{7,6},{8,9},{9,8},{10,11... | collective-permute-start | bytes 1179656 | tf_op jit(solution)/shard_map/ppermute | solution.py:509
  20.7 38.2 %collective-permute-start.1 = (bf16[4,128,384]{2,1,0:T(8,128)(2,1)}, bf16[4,128,384]{2,1,0:T(8,128)(2,1)}, u32[]{:S(2)}, u32[]{:S(2)}) collective-permute-start(bf16[4,128,384]{2,1,0:T(8,128)(2,1)} %get-tuple-element.41), channel_id=1, source_target_pairs={{0,31},{1,2},{2,1},{3,4},{4,3},{5,6},{6,5},{7,8},{8,7},{9,10},{10,... | collective-permute-start | bytes 1179656 | tf_op jit(solution)/shard_map/ppermute | solution.py:512
  26.0 3.3 %copy-start = (bf16[3,3,3,384,384]{4,3,2,1,0:T(8,128)(2,1)S(1)}, bf16[3,3,3,384,384]{4,3,2,1,0:T(8,128)(2,1)}, u32[]{:S(2)}) copy-start(bf16[3,3,3,384,384]{4,3,2,1,0:T(8,128)(2,1)} %w_ref.5) | copy-start | bytes 23887876
  29.2 8.0 %slice-start = ((s8[7962624]{0:T(1024)(128)(4,1)}), s8[4194304]{0:T(1024)(128)(4,1)S(1)}, s32[]{:S(2)}) async-start(s8[7962624]{0:T(1024)(128)(4,1)} %bitcast.23), calls=%async_computation.2 | async-start | bytes 8388608
  29.8 1.8 %copy-start.15 = (bf16[768,2304]{1,0:T(8,128)(2,1)}, bf16[768,2304]{1,0:T(8,128)(2,1)S(1)}, u32[]{:S(2)}) copy-start(bf16[768,2304]{1,0:T(8,128)(2,1)S(1)} %get-tuple-element.39.w_ref) | copy-start | bytes 10616836
  31.6 1.2 copy-start.17
  32.8 4.5 %slice-start.1 = ((s8[7962624]{0:T(1024)(128)(4,1)}), s8[3768320]{0:T(1024)(128)(4,1)S(1)}, s32[]{:S(2)}) async-start(s8[7962624]{0:T(1024)(128)(4,1)} %bitcast.23), calls=%async_computation.3 | async-start | bytes 7536640
  34.3 2.9 %copy-start.7 = (bf16[1536,2304]{1,0:T(8,128)(2,1)}, bf16[1536,2304]{1,0:T(8,128)(2,1)S(1)}, u32[]{:S(2)}) copy-start(bf16[1536,2304]{1,0:T(8,128)(2,1)S(1)} %get-tuple-element.51.w_ref) | copy-start | bytes 21233668
  37.3 1.8 %copy-start.13 = (bf16[2,768,1152]{2,1,0:T(8,128)(2,1)}, bf16[2,768,1152]{2,1,0:T(8,128)(2,1)S(1)}, u32[]{:S(2)}) copy-start(bf16[2,768,1152]{2,1,0:T(8,128)(2,1)S(1)} %get-tuple-element.50.w_ref) | copy-start | bytes 10616836
  39.1 2.8 %copy-start.6 = (bf16[1536,2304]{1,0:T(8,128)(2,1)}, bf16[1536,2304]{1,0:T(8,128)(2,1)S(1)}, u32[]{:S(2)}) copy-start(bf16[1536,2304]{1,0:T(8,128)(2,1)S(1)} %get-tuple-element.67.w_ref) | copy-start | bytes 21233668
  41.9 1.8 %copy-start.9 = (bf16[2,768,1152]{2,1,0:T(8,128)(2,1)}, bf16[2,768,1152]{2,1,0:T(8,128)(2,1)S(1)}, u32[]{:S(2)}) copy-start(bf16[2,768,1152]{2,1,0:T(8,128)(2,1)S(1)} %get-tuple-element.64.w_ref) | copy-start | bytes 10616836
  44.2 1.2 copy-start.4
  45.4 1.8 %copy-start.11 = (bf16[768,2304]{1,0:T(8,128)(2,1)}, bf16[768,2304]{1,0:T(8,128)(2,1)S(1)}, u32[]{:S(2)}) copy-start(bf16[768,2304]{1,0:T(8,128)(2,1)S(1)} %get-tuple-element.65.wa_ref) | copy-start | bytes 10616836
  47.2 2.0 %copy-start.16 = (bf16[768,2304]{1,0:T(8,128)(2,1)S(1)}, bf16[768,2304]{1,0:T(8,128)(2,1)}, u32[]{:S(2)}) copy-start(bf16[768,2304]{1,0:T(8,128)(2,1)} %copy-done.15) | copy-start | bytes 10616836
  49.2 1.1 copy-start.20
  50.4 3.2 %copy-start.33 = (s32[16]{0:T(128)S(1)}, s32[16]{0:T(128)}, u32[]{:S(2)}) copy-start(s32[16]{0:T(128)} %get-tuple-element.73) | copy-start | bytes 196
  52.4 1.1 copy-start.22
  60.4 1.6 %copy-start.1 = (bf16[4,32,4,8,384]{4,3,2,1,0:T(8,128)(2,1)}, bf16[4,32,4,8,384]{4,3,2,1,0:T(8,128)(2,1)S(1)}, u32[]{:S(2)}) copy-start(bf16[4,32,4,8,384]{4,3,2,1,0:T(8,128)(2,1)S(1)} %shard_map.164) | copy-start | bytes 9437188
  62.1 48.5 %all-to-all-start.1 = ((bf16[128,4,8,384]{3,2,1,0:T(8,128)(2,1)}), bf16[128,4,8,384]{3,2,1,0:T(8,128)(2,1)S(1)}, u32[]{:S(2)}, u32[]{:S(2)}) async-start(bf16[128,4,8,384]{3,2,1,0:T(8,128)(2,1)} %bitcast.29), calls=%async_computation.1 | async-start | bytes 6291456 | tf_op jit(solution)/shard_map/all_to_all | solution.py:533
  110.6 1.8 %copy-start.23 = (f32[2,16,4,8,384]{4,3,2,1,0:T(8,128)S(1)}, f32[2,16,4,8,384]{4,3,2,1,0:T(8,128)}, u32[]{:S(2)}) copy-start(f32[2,16,4,8,384]{4,3,2,1,0:T(8,128)} %copy-done.22) | copy-start | bytes 4718596
  110.9 1.7 %copy-start.18 = (bf16[2,384,1152]{2,1,0:T(8,128)(2,1)S(1)}, bf16[2,384,1152]{2,1,0:T(8,128)(2,1)}, u32[]{:S(2)}) copy-start(bf16[2,384,1152]{2,1,0:T(8,128)(2,1)} %copy-done.17) | copy-start | bytes 5308420
  110.9 1.9 %copy-start.21 = (bf16[4,2,128,384]{3,2,1,0:T(8,128)(2,1)S(1)}, bf16[4,2,128,384]{3,2,1,0:T(8,128)(2,1)}, u32[]{:S(2)}) copy-start(bf16[4,2,128,384]{3,2,1,0:T(8,128)(2,1)} %copy-done.19) | copy-start | bytes 2359300
  111.2 16.1 %collective-permute-start.2 = (bf16[2,16,4,8,384]{4,3,2,1,0:T(8,128)(2,1)S(1)}, bf16[2,16,4,8,384]{4,3,2,1,0:T(8,128)(2,1)S(1)}, u32[]{:S(2)}, u32[]{:S(2)}) collective-permute-start(bf16[2,16,4,8,384]{4,3,2,1,0:T(8,128)(2,1)S(1)} %get-tuple-element.82), channel_id=1, source_target_pairs={{0,1},{1,0},{2,3},{3,2},{4,5},{5,4},{6,7},{7,6},{8,9},{9,8},{10,11... | collective-permute-start | bytes 2359304 | tf_op jit(solution)/shard_map/ppermute | solution.py:509
  111.3 16.0 %collective-permute-start.3 = (bf16[2,16,4,8,384]{4,3,2,1,0:T(8,128)(2,1)S(1)}, bf16[2,16,4,8,384]{4,3,2,1,0:T(8,128)(2,1)S(1)}, u32[]{:S(2)}, u32[]{:S(2)}) collective-permute-start(bf16[2,16,4,8,384]{4,3,2,1,0:T(8,128)(2,1)S(1)} %get-tuple-element.81), channel_id=1, source_target_pairs={{0,31},{1,2},{2,1},{3,4},{4,3},{5,6},{6,5},{7,8},{8,7},{9,10},{10,... | collective-permute-start | bytes 2359304 | tf_op jit(solution)/shard_map/ppermute | solution.py:512
  112.2 20.1 %slice-start.2 = ((s8[7077888]{0:T(1024)(128)(4,1)}), s8[4194304]{0:T(1024)(128)(4,1)S(1)}, s32[]{:S(2)}) async-start(s8[7077888]{0:T(1024)(128)(4,1)} %bitcast.30), calls=%async_computation.4 | async-start | bytes 8388608
  112.8 3.3 %copy-start.8 = (bf16[1536,2304]{1,0:T(8,128)(2,1)S(1)}, bf16[1536,2304]{1,0:T(8,128)(2,1)}, u32[]{:S(2)}) copy-start(bf16[1536,2304]{1,0:T(8,128)(2,1)} %copy-done.7) | copy-start | bytes 21233668
  116.1 11.1 %copy-start.25 = (f32[384]{0:T(512)S(1)}, f32[384]{0:T(512)}, u32[]{:S(2)}) copy-start(f32[384]{0:T(512)} %param.21) | copy-start | bytes 4612
  116.1 11.1 %copy-start.26 = (f32[384]{0:T(512)S(1)}, f32[384]{0:T(512)}, u32[]{:S(2)}) copy-start(f32[384]{0:T(512)} %param.18) | copy-start | bytes 4612
  116.1 11.1 %copy-start.27 = (f32[384]{0:T(512)S(1)}, f32[384]{0:T(512)}, u32[]{:S(2)}) copy-start(f32[384]{0:T(512)} %param.22) | copy-start | bytes 4612
  116.1 11.1 %copy-start.14 = (bf16[2,768,1152]{2,1,0:T(8,128)(2,1)S(1)}, bf16[2,768,1152]{2,1,0:T(8,128)(2,1)}, u32[]{:S(2)}) copy-start(bf16[2,768,1152]{2,1,0:T(8,128)(2,1)} %copy-done.13) | copy-start | bytes 10616836
  116.1 16.2 %slice-start.3 = ((s8[7077888]{0:T(1024)(128)(4,1)}), s8[2883584]{0:T(1024)(128)(4,1)S(1)}, s32[]{:S(2)}) async-start(s8[7077888]{0:T(1024)(128)(4,1)} %bitcast.30), calls=%async_computation.5 | async-start | bytes 5767168
  123.2 14.8 %collective-permute-start.7 = (bf16[2,16,4,8,384]{4,3,2,1,0:T(8,128)(2,1)S(1)}, bf16[2,16,4,8,384]{4,3,2,1,0:T(8,128)(2,1)S(1)}, u32[]{:S(2)}, u32[]{:S(2)}) collective-permute-start(bf16[2,16,4,8,384]{4,3,2,1,0:T(8,128)(2,1)S(1)} %get-tuple-element.61), channel_id=1, source_target_pairs={{0,31},{1,2},{2,1},{3,4},{4,3},{5,6},{6,5},{7,8},{8,7},{9,10},{10,... | collective-permute-start | bytes 2359304 | tf_op jit(solution)/shard_map/ppermute | solution.py:512
  127.2 10.9 %collective-permute-start.6 = (bf16[2,16,4,8,384]{4,3,2,1,0:T(8,128)(2,1)S(1)}, bf16[2,16,4,8,384]{4,3,2,1,0:T(8,128)(2,1)S(1)}, u32[]{:S(2)}, u32[]{:S(2)}) collective-permute-start(bf16[2,16,4,8,384]{4,3,2,1,0:T(8,128)(2,1)S(1)} %get-tuple-element.79), channel_id=1, source_target_pairs={{0,1},{1,0},{2,3},{3,2},{4,5},{5,4},{6,7},{7,6},{8,9},{9,8},{10,11... | collective-permute-start | bytes 2359304 | tf_op jit(solution)/shard_map/ppermute | solution.py:509
  130.6 12.8 %collective-permute-start.4 = (bf16[4,128,384]{2,1,0:T(8,128)(2,1)S(1)}, bf16[4,128,384]{2,1,0:T(8,128)(2,1)S(1)}, u32[]{:S(2)}, u32[]{:S(2)}) collective-permute-start(bf16[4,128,384]{2,1,0:T(8,128)(2,1)S(1)} %get-tuple-element.58), channel_id=1, source_target_pairs={{0,1},{1,0},{2,3},{3,2},{4,5},{5,4},{6,7},{7,6},{8,9},{9,8},{10,11... | collective-permute-start | bytes 1179656 | tf_op jit(solution)/shard_map/ppermute | solution.py:509
  131.1 6.9 %copy-start.10 = (bf16[2,768,1152]{2,1,0:T(8,128)(2,1)S(1)}, bf16[2,768,1152]{2,1,0:T(8,128)(2,1)}, u32[]{:S(2)}) copy-start(bf16[2,768,1152]{2,1,0:T(8,128)(2,1)} %copy-done.9) | copy-start | bytes 10616836
  131.1 6.9 %copy-start.12 = (bf16[768,2304]{1,0:T(8,128)(2,1)S(1)}, bf16[768,2304]{1,0:T(8,128)(2,1)}, u32[]{:S(2)}) copy-start(bf16[768,2304]{1,0:T(8,128)(2,1)} %copy-done.11) | copy-start | bytes 10616836
  131.1 12.2 %collective-permute-start.5 = (bf16[4,128,384]{2,1,0:T(8,128)(2,1)S(1)}, bf16[4,128,384]{2,1,0:T(8,128)(2,1)S(1)}, u32[]{:S(2)}, u32[]{:S(2)}) collective-permute-start(bf16[4,128,384]{2,1,0:T(8,128)(2,1)S(1)} %get-tuple-element.59), channel_id=1, source_target_pairs={{0,31},{1,2},{2,1},{3,4},{4,3},{5,6},{6,5},{7,8},{8,7},{9,10},{10,... | collective-permute-start | bytes 1179656 | tf_op jit(solution)/shard_map/ppermute | solution.py:512
  138.0 5.3 %copy-start.3 = (bf16[4,2,128,384]{3,2,1,0:T(8,128)(2,1)S(1)}, bf16[4,2,128,384]{3,2,1,0:T(8,128)(2,1)}, u32[]{:S(2)}) copy-start(bf16[4,2,128,384]{3,2,1,0:T(8,128)(2,1)} %f_ref.3) | copy-start | bytes 2359300
  138.0 5.3 %copy-start.5 = (bf16[2,384,1152]{2,1,0:T(8,128)(2,1)S(1)}, bf16[2,384,1152]{2,1,0:T(8,128)(2,1)}, u32[]{:S(2)}) copy-start(bf16[2,384,1152]{2,1,0:T(8,128)(2,1)} %copy-done.4) | copy-start | bytes 5308420

commit v14 on v12

--- a/solution.py
+++ b/solution.py
@@ -246,9 +246,9 @@
     return jax.ShapeDtypeStruct((n_rows, blocks, n_slots, CB, ch), jnp.float32)
 
 
-def add_sides(edge_ref, sides, w_ref, lhs, o_ref):
-    n_slots, n_cols, ch = sides[0].shape
-    for side, y in beside(edge_ref, *sides):
+def add_sides(edge_ref, pairs, w_ref, lhs, o_ref):
+    for side, y in pairs:
+        n_slots, n_cols, ch = side.shape
         for s in range(n_slots):
             lhs[s * n_cols : (s + 1) * n_cols] = masked(edge_ref, y, s, side[s])
         add_into(o_ref, y, folded(dot(lhs[...], w_ref[y]), ch, False), False, o_ref)
@@ -271,7 +271,7 @@
 
     def body(edge_ref, act_ref, near_ref, far_ref, wo_ref, ws_ref, o_ref, lhs, side):
         add_own(act_ref, wo_ref, lhs, o_ref, None)
-        add_sides(edge_ref, (near_ref, far_ref), ws_ref, side, o_ref)
+        add_sides(edge_ref, beside(edge_ref, near_ref, far_ref), ws_ref, side, o_ref)
 
     return call(
         body,
@@ -372,8 +372,8 @@
             pltpu.VMEM((half, weight.shape[1]), jnp.float32),
             pltpu.SemaphoreType.DMA((n_rows * n_slots,)),
         ],
-        flops=2 * half * weight.size,
-        moved=2 * weight.size,
+        flops=half,
+        moved=half,
         far_out=(1,),
     )
 
@@ -414,55 +414,80 @@
     )
 
 
-def before_sides(near, far, act, w_sides, w_act, sums, kept, edges):
-    n_frames, blocks, n_slots, _, ch = far.shape
-    n_rows, n_cols, deep = sums.shape[0], blocks * CB, n_frames * ch
-
-    def body(edge_ref, near_ref, far_ref, act_ref, tiles_ref, w_ref, wa_ref, z_ref, kept_ref, o_ref, next_ref, lhs, lhs2, sem):
+def act_part(act, near, w_own, w_sides, sums, kept, edges):
+    n_slots, n_rows, n_cols, ch = act.shape
+    half = n_slots * n_cols
+    tiles = act.reshape(n_slots, n_rows, n_cols // CB, CB, ch)
+
+    def body(edge_ref, act_ref, tiles_ref, near_ref, wo_ref, ws_ref, z_ref, kept_ref, o_ref, next_ref, lhs, side, sem):
         copy = pltpu.make_async_copy(tiles_ref, next_ref.at[:, 1], sem)
         copy.start()
-        add_own(act_ref, wa_ref, lhs2, o_ref, z_ref)
-        for side, y in beside(edge_ref, near_ref, far_ref):
-            o_ref[y] += side_sums(edge_ref, y, side, w_ref[y], lhs)
+        add_own(act_ref, wo_ref, lhs, o_ref, z_ref)
+        add_sides(edge_ref, beside(edge_ref, near_ref, None)[:1], ws_ref, side, o_ref)
         copy.wait()
 
     return call(
         body,
         [jax.ShapeDtypeStruct(sums.shape, jnp.float32), jax.ShapeDtypeStruct(kept.shape, kept.dtype)],
-        (near, far, act, act.reshape(n_slots, n_rows, blocks, CB, ch), w_sides, w_act, sums, kept),
+        (act, tiles, near, w_own, w_sides, sums, kept),
         scalars=(edges,),
         scratch=[
-            pltpu.VMEM((blocks, n_slots, CB, deep), jnp.bfloat16),
-            pltpu.VMEM((n_slots * n_cols, n_rows * ch), jnp.bfloat16),
+            pltpu.VMEM((half, n_rows * ch), jnp.bfloat16),
+            pltpu.VMEM((half, ch), jnp.bfloat16),
             pltpu.SemaphoreType.DMA,
         ],
-        flops=2 * n_slots * n_cols * (w_sides.size + w_act.size),
-        moved=2 * (w_sides.size + w_act.size),
-        far=(7,),
+        flops=2 * half * w_own.size,
+        moved=2 * (w_sides.size + w_own.size),
+        far=(6,),
         far_out=(1,),
-        aliases={8: 1},
-    )
-
-
-def last_part(near, far, w_sides, sums, bias, frame, edges):
+        aliases={7: 1},
+    )
+
+
+def cached_sides(near, far, w_sides, sums, edges):
+    n_frames, blocks, n_slots, _, ch = far.shape
+    deep = n_frames * ch
+
+    def body(edge_ref, near_ref, far_ref, w_ref, z_ref, o_ref, lhs):
+        for side, y in beside(edge_ref, near_ref, far_ref):
+            o_ref[y] = z_ref[y] + side_sums(edge_ref, y, side, w_ref[y], lhs)
+
+    return call(
+        body,
+        [jax.ShapeDtypeStruct(sums.shape, jnp.float32)],
+        (near, far, w_sides, sums),
+        scalars=(edges,),
+        scratch=[pltpu.VMEM((blocks, n_slots, CB, deep), jnp.bfloat16)],
+        flops=2 * blocks * n_slots * CB * w_sides.size,
+        moved=2 * w_sides.size,
+    )[0]
+
+
+def last_part(far, w_sides, sums, bias, frame, edges):
     n_slots, n_rows, n_cols, ch = frame.shape
 
-    def body(edge_ref, near_ref, far_ref, w_ref, z_ref, b_ref, f_ref, o_ref, lhs):
-        for side, y in beside(edge_ref, near_ref, far_ref):
+    def body(edge_ref, far_ref, w_ref, z_ref, b_ref, f_ref, o_ref, lhs):
+        def give(y, total):
             for s in range(n_slots):
-                lhs[s * n_cols : (s + 1) * n_cols] = masked(edge_ref, y, s, side[s])
-            total = folded(dot(lhs[...], w_ref[y]), ch, False)
-            for s in range(n_slots):
-                value = (total[s] + z_ref[y, :, s] + b_ref[...]).reshape(n_cols, ch)
-                o_ref[s, y] = (value + f_ref[s, y].astype(jnp.float32)).astype(jnp.bfloat16)
+                value = z_ref[y, :, s] + b_ref[...]
+                if total is not None:
+                    value += total[s]
+                value = value.reshape(n_cols, ch) + f_ref[s, y].astype(jnp.float32)
+                o_ref[s, y] = value.astype(jnp.bfloat16)
+
+        (_, done), (side, y) = beside(edge_ref, None, far_ref)
+        for s in range(n_slots):
+            lhs[s * n_cols : (s + 1) * n_cols] = masked(edge_ref, y, s, side[s])
+        give(done, None)
+        give(y, folded(dot(lhs[...], w_ref[y]), ch, False))
 
     return call(
         body,
         [jax.ShapeDtypeStruct(frame.shape, jnp.bfloat16)],
-        (near, far, w_sides, sums, bias, frame),
+        (far, w_sides, sums, bias, frame),
         scalars=(edges,),
         scratch=[pltpu.VMEM((n_slots * n_cols, ch), jnp.bfloat16)],
-        flops=2 * n_slots * n_cols * w_sides.size,
+        flops=n_slots * n_cols * w_sides.size,
         moved=2 * w_sides.size,
     )[0]
 
@@ -547,18 +572,18 @@
     near_2, far_2 = swap_near(picked(1, 1 - odd)), swap_far(picked(1, odd))
     act_tiles = act_first.reshape(n_slots, n_rows, blocks, CB, ch)
     sums_1, next_first = own_first(got, own_1, sums_1, act_tiles)
+    got_later, sums_1 = lax.optimization_barrier((got, sums_1))
+    sums_2, kept = own_second(got_later, own_2)
+    sums_1, sums_2, kept = lax.optimization_barrier((sums_1, sums_2, kept))
     act_second, near, far = second_activation(
         near_1, far_1, sides_1, sums_1, bias_first[None], gain_second[None], edges
     )
     act_near, act_far = swap_near(near), swap_far(far)
-    got_later, act_later = lax.optimization_barrier((got, act_second))
-    sums_2, kept = own_second(got_later, own_2)
-    sums_2, next_second = before_sides(
-        near_2, far_2, act_later, sides_2, act_own_2, sums_2, kept, edges
-    )
-    mixed_frame = last_part(
-        act_near, act_far, act_sides_2, sums_2, bias_second[None], frame_in, edges
-    )
+    sums_2, next_second = act_part(
+        act_second, act_near, act_own_2, act_sides_2, sums_2, kept, edges
+    )
+    sums_2 = cached_sides(near_2, far_2, sides_2, sums_2, edges)
+    mixed_frame = last_part(act_far, act_sides_2, sums_2, bias_second[None], frame_in, edges)
     whole = (n_slots, 2, n_rows, n_cols, ch)
     return (mixed_frame, next_first.reshape(whole), next_second.reshape(whole))
 

time: 144 us -> 143 us (level)
    ppermute x4, waiting for transfers between devices: 31.8 us -> 29.4 us  [swap_far(): lax.ppermute(row, 'tile', [(i, (i + 2 * (i % 2) - 1) % n_tiles) for i in...]
    pallas_call x7 -> x8, Pallas kernels: 27.7 us -> 28.2 us  [call(): pl.pallas_call(body, in_specs=in_specs, out_specs=out_specs, out_shape=li...]
  transfers between devices with their start and end apart: 10 -> 10, of which waited for: 5 -> 5; matrix products, arithmetic and copies ran while one was open for 1% -> 1% of each run, Pallas kernels for 20% -> 21%
where the time goes in v14:
time: 143 us; the launch traced here: 142 us
  waiting for transfers between devices  42.8 us (30%)
  Pallas kernels  37 us (26%)
  local copies, waits for them, and re-layouts  32.5 us (23%)
  starting transfers between devices  28.2 us (20%)
    unnamed x78, local copies, waits for them, and re-layouts  31.7 us
    ppermute x4, waiting for transfers between devices, swap_far(): lax.ppermute(row, 'tile', [(i, (i + 2 * (i % 2) - 1) % n_tiles) for i in...  29.4 us
    pallas_call x8, Pallas kernels, call(): pl.pallas_call(body, in_specs=in_specs, out_specs=out_specs, out_shape=li...  28.2 us
    all_to_all x1, waiting for transfers between devices, local(): lax.all_to_all(moved.reshape(n_groups * n_tiles, n_slots, CB, ch), BOTH,...  12.1 us
    all_to_all x1, starting transfers between devices, local(): held = lax.all_to_all(sent, BOTH, 0, 0, tiled=True)  11.1 us
    ppermute x4, starting transfers between devices, swap_far(): lax.ppermute(row, 'tile', [(i, (i + 2 * (i % 2) - 1) % n_tiles) for i in...  10.7 us
    all_to_all x1, starting transfers between devices, local(): lax.all_to_all(moved.reshape(n_groups * n_tiles, n_slots, CB, ch), BOTH,...  6.16 us
    pallas_call x4, Pallas kernels, spread(): pl.pallas_call(body, grid=(n_y,), in_specs=[pl.BlockSpec((times, 1, n_x,...  4.11 us
  transfers between devices with their start and end apart: 10, of which 5 were waited for; matrix products, arithmetic and copies ran while one was open for 1% of the time, Pallas kernels for 21%

profile of v14, /device:TPU:0, one launch (start us, length us, event | category | flops | bytes accessed | tf_op | source)
XLA Modules:
  0.0 142.4 jit_solution(4347279846819715456)
XLA Ops:
  0.6 3.1 %shard_map.157 = bf16[2,2,2,16,4,8,384]{6,5,4,3,2,1,0:T(8,128)(2,1)} custom-call(bf16[4,2,2,16,8,384]{5,4,3,2,1,0:T(8,128)(2,1)} %bitcast.35, bf16[4,2,2,16,8,384]{5,4,3,2,1,0:T(8,128)(2,1)} %bitcast.36), custom_call_target="tpu_custom_call" | custom-call | tf_op jit(solution)/shard_map/pallas_call | solution.py:47
  3.9 11.1 %all-to-all-start = ((bf16[128,4,8,384]{3,2,1,0:T(8,128)(2,1)}), bf16[128,4,8,384]{3,2,1,0:T(8,128)(2,1)S(1)}, u32[]{:S(2)}, u32[]{:S(2)}) async-start(bf16[128,4,8,384]{3,2,1,0:T(8,128)(2,1)} %bitcast.34), calls=%async_computation | async-start | bytes 6291456 | tf_op jit(solution)/shard_map/all_to_all | solution.py:544
  15.2 0.6 select_reduce_fusion
  16.0 1.1 copy-done.10
  17.1 2.8 %shard_map.158 = (bf16[4,2,128,384]{3,2,1,0:T(8,128)(2,1)S(1)}, bf16[4,128,384]{2,1,0:T(8,128)(2,1)}, bf16[4,128,384]{2,1,0:T(8,128)(2,1)}) custom-call(s32[3,4]{1,0:T(4,128)S(1)} %add_convert_fusion.edge_ref, bf16[4,2,128,384]{3,2,1,0:T(8,128)(2,1)S(1)} %copy-done.10, f32[1,384]{1,0:T(1,128)S(1)} %broadcast_in_dim.53.g_ref), custom_call_target="tpu_custom_call" | custom-call | flops 3932160 | bytes 2359296 | tf_op jit(solution)/shard_map/pallas_call | solution.py:105
  19.9 0.9 copy-done.20
  20.7 5.3 %collective-permute-start.1 = (bf16[4,128,384]{2,1,0:T(8,128)(2,1)}, bf16[4,128,384]{2,1,0:T(8,128)(2,1)}, u32[]{:S(2)}, u32[]{:S(2)}) collective-permute-start(bf16[4,128,384]{2,1,0:T(8,128)(2,1)} %get-tuple-element.49), channel_id=1, source_target_pairs={{0,31},{1,2},{2,1},{3,4},{4,3},{5,6},{6,5},{7,8},{8,7},{9,10},{10,... | collective-permute-start | bytes 1179656 | tf_op jit(solution)/shard_map/ppermute | solution.py:539
  26.0 3.3 %copy-done.1 = bf16[3,3,3,384,384]{4,3,2,1,0:T(8,128)(2,1)S(1)} copy-done((bf16[3,3,3,384,384]{4,3,2,1,0:T(8,128)(2,1)S(1)}, bf16[3,3,3,384,384]{4,3,2,1,0:T(8,128)(2,1)}, u32[]{:S(2)}) %copy-start.1) | copy-done | bytes 7962648
  29.3 0.5 shard_map.159
  29.8 1.8 %copy-done.16 = bf16[768,2304]{1,0:T(8,128)(2,1)} copy-done((bf16[768,2304]{1,0:T(8,128)(2,1)}, bf16[768,2304]{1,0:T(8,128)(2,1)S(1)}, u32[]{:S(2)}) %copy-start.16) | copy-done | bytes 3538968
  31.5 1.3 copy-done.18
  32.9 26.1 %collective-permute-done.1.far_ref = bf16[4,128,384]{2,1,0:T(8,128)(2,1)} collective-permute-done((bf16[4,128,384]{2,1,0:T(8,128)(2,1)}, bf16[4,128,384]{2,1,0:T(8,128)(2,1)}, u32[]{:S(2)}, u32[]{:S(2)}) %collective-permute-start.1) | collective-permute-done | bytes 393248 | tf_op jit(solution)/shard_map/ppermute | solution.py:539
  59.0 1.5 %shard_map.160 = bf16[4,32,4,8,384]{4,3,2,1,0:T(8,128)(2,1)S(1)} custom-call(s32[16]{0:T(128)S(1)} %get-tuple-element.93.source_ref, s32[16]{0:T(128)S(1)} %get-tuple-element.101.rotation_ref, s32[16]{0:T(128)S(1)} %compare_convert_fusion.keep_ref, bf16[4,32,4,8,384]{4,3,2,1,0:T(8,128)(2,1)S(1)} %bitcast.28), custom_call_target="tpu_custom_call" | custom-call | tf_op jit(solution)/shard_map/pallas_call | solution.py:86
  60.6 1.6 %copy-done.2 = bf16[4,32,4,8,384]{4,3,2,1,0:T(8,128)(2,1)} copy-done((bf16[4,32,4,8,384]{4,3,2,1,0:T(8,128)(2,1)}, bf16[4,32,4,8,384]{4,3,2,1,0:T(8,128)(2,1)S(1)}, u32[]{:S(2)}) %copy-start.2) | copy-done | bytes 3145752
  62.2 6.2 %all-to-all-start.1 = ((bf16[128,4,8,384]{3,2,1,0:T(8,128)(2,1)}), bf16[128,4,8,384]{3,2,1,0:T(8,128)(2,1)S(1)}, u32[]{:S(2)}, u32[]{:S(2)}) async-start(bf16[128,4,8,384]{3,2,1,0:T(8,128)(2,1)} %bitcast.29), calls=%async_computation.1 | async-start | bytes 6291456 | tf_op jit(solution)/shard_map/all_to_all | solution.py:555
  68.4 2.0 %copy-done.17 = bf16[768,2304]{1,0:T(8,128)(2,1)S(1)} copy-done((bf16[768,2304]{1,0:T(8,128)(2,1)S(1)}, bf16[768,2304]{1,0:T(8,128)(2,1)}, u32[]{:S(2)}) %copy-start.17) | copy-done | bytes 3538968
  70.4 1.5 %copy-done.19 = bf16[2,384,1152]{2,1,0:T(8,128)(2,1)S(1)} copy-done((bf16[2,384,1152]{2,1,0:T(8,128)(2,1)S(1)}, bf16[2,384,1152]{2,1,0:T(8,128)(2,1)}, u32[]{:S(2)}) %copy-start.19) | copy-done | bytes 1769496
  71.9 1.1 copy-done.21
  73.0 4.6 %shard_map.161.z_ref = f32[2,16,4,8,384]{4,3,2,1,0:T(8,128)S(1)} custom-call(s32[3,4]{1,0:T(4,128)S(1)} %add_convert_fusion.edge_ref, bf16[4,2,128,384]{3,2,1,0:T(8,128)(2,1)S(1)} %copy-done.21, bf16[4,128,384]{2,1,0:T(8,128)(2,1)S(1)} %collective-permute-done.near_ref, bf16[4,128,384]{2,1,0:T(8,128)(2,1)} %collective-permute-done.1.far_ref, ...), custom_call_target="tpu_custom_call" | custom-call | flops 2717908992 | bytes 6684672 | tf_op jit(solution)/shard_map/pallas_call | solution.py:105
  77.6 1.1 copy-done.23
  78.7 3.3 %copy-done = bf16[3,3,3,384,384]{4,3,2,1,0:T(8,128)(2,1)S(1)} copy-done((bf16[3,3,3,384,384]{4,3,2,1,0:T(8,128)(2,1)S(1)}, bf16[3,3,3,384,384]{4,3,2,1,0:T(8,128)(2,1)}, u32[]{:S(2)}) %copy-start) | copy-done | bytes 7962648
  82.0 0.5 shard_map.164
  82.5 1.3 copy-done.4
  83.8 1.8 %copy-done.8 = bf16[768,2304]{1,0:T(8,128)(2,1)} copy-done((bf16[768,2304]{1,0:T(8,128)(2,1)}, bf16[768,2304]{1,0:T(8,128)(2,1)S(1)}, u32[]{:S(2)}) %copy-start.8) | copy-done | bytes 3538968
  85.6 1.5 %shard_map.163 = (bf16[1536,2304]{1,0:T(8,128)(2,1)S(1)}, bf16[2,768,1152]{2,1,0:T(8,128)(2,1)S(1)}) custom-call(bf16[3,3,3,384,384]{4,3,2,1,0:T(8,128)(2,1)S(1)} %copy-done), custom_call_target="tpu_custom_call" | custom-call | bytes 15925248 | tf_op jit(solution)/shard_map/pallas_call | solution.py:154
  87.2 2.8 %copy-done.3 = bf16[1536,2304]{1,0:T(8,128)(2,1)} copy-done((bf16[1536,2304]{1,0:T(8,128)(2,1)}, bf16[1536,2304]{1,0:T(8,128)(2,1)S(1)}, u32[]{:S(2)}) %copy-start.3) | copy-done | bytes 7077912
  90.0 1.8 %copy-done.6 = bf16[2,768,1152]{2,1,0:T(8,128)(2,1)} copy-done((bf16[2,768,1152]{2,1,0:T(8,128)(2,1)}, bf16[2,768,1152]{2,1,0:T(8,128)(2,1)S(1)}, u32[]{:S(2)}) %copy-start.6) | copy-done | bytes 3538968
  91.8 1.5 %shard_map.162 = (bf16[1536,2304]{1,0:T(8,128)(2,1)S(1)}, bf16[2,768,1152]{2,1,0:T(8,128)(2,1)S(1)}) custom-call(bf16[3,3,3,384,384]{4,3,2,1,0:T(8,128)(2,1)S(1)} %bitcast.24), custom_call_target="tpu_custom_call" | custom-call | bytes 15925248 | tf_op jit(solution)/shard_map/pallas_call | solution.py:154
  93.3 2.9 %copy-done.12 = bf16[1536,2304]{1,0:T(8,128)(2,1)} copy-done((bf16[1536,2304]{1,0:T(8,128)(2,1)}, bf16[1536,2304]{1,0:T(8,128)(2,1)S(1)}, u32[]{:S(2)}) %copy-start.12) | copy-done | bytes 7077912
  96.3 1.8 %copy-done.14 = bf16[2,768,1152]{2,1,0:T(8,128)(2,1)} copy-done((bf16[2,768,1152]{2,1,0:T(8,128)(2,1)}, bf16[2,768,1152]{2,1,0:T(8,128)(2,1)S(1)}, u32[]{:S(2)}) %copy-start.14) | copy-done | bytes 3538968
  98.1 12.1 %all-to-all-done.1 = bf16[128,4,8,384]{3,2,1,0:T(8,128)(2,1)S(1)} async-done(((bf16[128,4,8,384]{3,2,1,0:T(8,128)(2,1)}), bf16[128,4,8,384]{3,2,1,0:T(8,128)(2,1)S(1)}, u32[]{:S(2)}, u32[]{:S(2)}) %all-to-all-start.1) | async-done | bytes 3145760 | tf_op jit(solution)/shard_map/all_to_all | solution.py:555
  110.2 0.3 fusion.2
  110.6 0.2 dynamic-slice_bitcast_fusion.2
  110.8 0.3 collective-permute-start.3
  111.1 0.1 collective-permute-start.2
  111.2 0.2 copy-done.26
  111.4 0.2 dynamic-slice_bitcast_fusion
  111.6 4.7 %collective-permute-start.6 = (bf16[2,16,4,8,384]{4,3,2,1,0:T(8,128)(2,1)S(1)}, bf16[2,16,4,8,384]{4,3,2,1,0:T(8,128)(2,1)S(1)}, u32[]{:S(2)}, u32[]{:S(2)}) collective-permute-start(bf16[2,16,4,8,384]{4,3,2,1,0:T(8,128)(2,1)S(1)} %get-tuple-element.97), channel_id=1, source_target_pairs={{0,31},{1,2},{2,1},{3,4},{4,3},{5,6},{6,5},{7,8},{8,7},{9,10},{10,... | collective-permute-start | bytes 2359304 | tf_op jit(solution)/shard_map/ppermute | solution.py:539
  116.3 4.6 %shard_map.165 = (f32[2,16,4,8,384]{4,3,2,1,0:T(8,128)S(1)}, bf16[4,2,2,16,8,384]{5,4,3,2,1,0:T(8,128)(2,1)}) custom-call(bf16[2,2,2,16,4,8,384]{6,5,4,3,2,1,0:T(8,128)(2,1)S(1)} %bitcast.26, bf16[1536,2304]{1,0:T(8,128)(2,1)S(1)} %copy-done.13, f32[2,16,4,8,384]{4,3,2,1,0:T(8,128)S(1)} %copy-done.24, bf16[4,2,16,8,384]{4,3,2,1,0:T(8,128)(2,1)S(1)} %bitcast.33), custom_call_target="tpu_custom_call" | custom-call | flops 3623878656 | bytes 7077888 | tf_op jit(solution)/shard_map/pallas_call | solution.py:105
  120.9 4.0 %shard_map.166 = (f32[2,16,4,8,384]{4,3,2,1,0:T(8,128)S(1)}, bf16[4,2,2,16,8,384]{5,4,3,2,1,0:T(8,128)(2,1)}) custom-call(bf16[2,2,2,16,4,8,384]{6,5,4,3,2,1,0:T(8,128)(2,1)S(1)} %bitcast.27, bf16[1536,2304]{1,0:T(8,128)(2,1)S(1)} %bitcast.31), custom_call_target="tpu_custom_call" | custom-call | flops 512 | bytes 512 | tf_op jit(solution)/shard_map/pallas_call | solution.py:105
  125.0 0.7 collective-permute-done.3.far_ref
  125.6 3.4 %shard_map.167 = (bf16[4,2,128,384]{3,2,1,0:T(8,128)(2,1)S(1)}, bf16[4,128,384]{2,1,0:T(8,128)(2,1)S(1)}, bf16[4,128,384]{2,1,0:T(8,128)(2,1)S(1)}) custom-call(s32[3,4]{1,0:T(4,128)S(1)} %add_convert_fusion.edge_ref, bf16[2,16,4,8,384]{4,3,2,1,0:T(8,128)(2,1)S(1)} %collective-permute-done.2.near_ref, ...), custom_call_target="tpu_custom_call" | custom-call | flops 1811939328 | bytes 3538944 | tf_op jit(solution)/shard_map/pallas_call | solution.py:105
  129.1 0.5 collective-permute-start.4
  129.6 1.2 collective-permute-done.7.near_ref
  130.9 3.4 %shard_map.168 = (f32[2,16,4,8,384]{4,3,2,1,0:T(8,128)S(1)}, bf16[4,2,2,16,8,384]{5,4,3,2,1,0:T(8,128)(2,1)}) custom-call(s32[3,4]{1,0:T(4,128)S(1)} %add_convert_fusion.edge_ref, bf16[4,2,128,384]{3,2,1,0:T(8,128)(2,1)S(1)} %get-tuple-element.83.act_ref, bf16[4,2,16,8,384]{4,3,2,1,0:T(8,128)(2,1)S(1)} %bitcast.32, ...), custom_call_target="tpu_custom_call", output_to_operand_aliasing={{1}: (7, {})} | custom-call | flops 1811939328 | bytes 5308416 | tf_op jit(solution)/shard_map/pallas_call | solution.py:105
  134.3 3.0 %shard_map.169.z_ref = f32[2,16,4,8,384]{4,3,2,1,0:T(8,128)S(1)} custom-call(s32[3,4]{1,0:T(4,128)S(1)} %add_convert_fusion.edge_ref, bf16[2,16,4,8,384]{4,3,2,1,0:T(8,128)(2,1)S(1)} %collective-permute-done.5.near_ref, bf16[2,16,4,8,384]{4,3,2,1,0:T(8,128)(2,1)S(1)} %collective-permute-done.6.far_ref, bf16[2,768,1152]{2,1,0:T(8,128)(2,1)S(1)} %copy-done.7, ...), custom_call_target="tpu_custom_call" | custom-call | flops 1811939328 | bytes 3538944 | tf_op jit(solution)/shard_map/pallas_call | solution.py:105
  137.3 2.7 %collective-permute-done.4.far_ref = bf16[4,128,384]{2,1,0:T(8,128)(2,1)S(1)} collective-permute-done((bf16[4,128,384]{2,1,0:T(8,128)(2,1)S(1)}, bf16[4,128,384]{2,1,0:T(8,128)(2,1)S(1)}, u32[]{:S(2)}, u32[]{:S(2)}) %collective-permute-start.4) | collective-permute-done | bytes 393248 | tf_op jit(solution)/shard_map/ppermute | solution.py:539
  140.0 2.4 %shard_map.170 = bf16[4,2,128,384]{3,2,1,0:T(8,128)(2,1)} custom-call(s32[3,4]{1,0:T(4,128)S(1)} %add_convert_fusion.edge_ref, bf16[4,128,384]{2,1,0:T(8,128)(2,1)S(1)} %collective-permute-done.4.far_ref, bf16[2,384,1152]{2,1,0:T(8,128)(2,1)S(1)} %copy-done.5, f32[2,16,4,8,384]{4,3,2,1,0:T(8,128)S(1)} %shard_map.169.z_ref, ...), custom_call_target="tpu_custom_call" | custom-call | flops 452984832 | bytes 1769472 | tf_op jit(solution)/shard_map/pallas_call | solution.py:105
  (79 shorter events, 0.5 us)
Async XLA Ops:
  3.8 11.2 %copy-start.25 = (f32[384]{0:T(512)S(1)}, f32[384]{0:T(512)}, u32[]{:S(2)}) copy-start(f32[384]{0:T(512)} %param.17) | copy-start | bytes 4612
  3.8 11.3 %copy-start.29 = (s32[16]{0:T(128)S(1)}, s32[16]{0:T(128)}, u32[]{:S(2)}) copy-start(s32[16]{0:T(128)} %param.27) | copy-start | bytes 196
  3.8 11.3 %copy-start.30 = (s32[16]{0:T(128)S(1)}, s32[16]{0:T(128)}, u32[]{:S(2)}) copy-start(s32[16]{0:T(128)} %param.24) | copy-start | bytes 196
  3.8 11.3 %copy-start.31 = (s32[16]{0:T(128)S(1)}, s32[16]{0:T(128)}, u32[]{:S(2)}) copy-start(s32[16]{0:T(128)} %param.25) | copy-start | bytes 196
  3.8 11.3 %copy-start.32 = (s32[16]{0:T(128)S(1)}, s32[16]{0:T(128)}, u32[]{:S(2)}) copy-start(s32[16]{0:T(128)} %param.23) | copy-start | bytes 196
  3.8 11.3 %copy-start.33 = (s32[16]{0:T(128)S(1)}, s32[16]{0:T(128)}, u32[]{:S(2)}) copy-start(s32[16]{0:T(128)} %param.26) | copy-start | bytes 196
  3.9 55.1 %all-to-all-start = ((bf16[128,4,8,384]{3,2,1,0:T(8,128)(2,1)}), bf16[128,4,8,384]{3,2,1,0:T(8,128)(2,1)S(1)}, u32[]{:S(2)}, u32[]{:S(2)}) async-start(bf16[128,4,8,384]{3,2,1,0:T(8,128)(2,1)} %bitcast.34), calls=%async_computation | async-start | bytes 6291456 | tf_op jit(solution)/shard_map/all_to_all | solution.py:544
  16.0 1.1 copy-start.10
  19.9 0.9 copy-start.20
  20.7 12.1 %collective-permute-start = (bf16[4,128,384]{2,1,0:T(8,128)(2,1)}, bf16[4,128,384]{2,1,0:T(8,128)(2,1)S(1)}, u32[]{:S(2)}, u32[]{:S(2)}) collective-permute-start(bf16[4,128,384]{2,1,0:T(8,128)(2,1)} %get-tuple-element.48), channel_id=1, source_target_pairs={{0,1},{1,0},{2,3},{3,2},{4,5},{5,4},{6,7},{7,6},{8,9},{9,8},{10,11... | collective-permute-start | bytes 1179656 | tf_op jit(solution)/shard_map/ppermute | solution.py:536
  20.7 38.2 %collective-permute-start.1 = (bf16[4,128,384]{2,1,0:T(8,128)(2,1)}, bf16[4,128,384]{2,1,0:T(8,128)(2,1)}, u32[]{:S(2)}, u32[]{:S(2)}) collective-permute-start(bf16[4,128,384]{2,1,0:T(8,128)(2,1)} %get-tuple-element.49), channel_id=1, source_target_pairs={{0,31},{1,2},{2,1},{3,4},{4,3},{5,6},{6,5},{7,8},{8,7},{9,10},{10,... | collective-permute-start | bytes 1179656 | tf_op jit(solution)/shard_map/ppermute | solution.py:539
  26.0 3.3 %copy-start.1 = (bf16[3,3,3,384,384]{4,3,2,1,0:T(8,128)(2,1)S(1)}, bf16[3,3,3,384,384]{4,3,2,1,0:T(8,128)(2,1)}, u32[]{:S(2)}) copy-start(bf16[3,3,3,384,384]{4,3,2,1,0:T(8,128)(2,1)} %w_ref.2) | copy-start | bytes 23887876
  29.3 3.6 %copy-start.34 = (s32[16]{0:T(128)S(1)}, s32[16]{0:T(128)}, u32[]{:S(2)}) copy-start(s32[16]{0:T(128)} %get-tuple-element.91) | copy-start | bytes 196
  29.8 1.8 %copy-start.16 = (bf16[768,2304]{1,0:T(8,128)(2,1)}, bf16[768,2304]{1,0:T(8,128)(2,1)S(1)}, u32[]{:S(2)}) copy-start(bf16[768,2304]{1,0:T(8,128)(2,1)S(1)} %get-tuple-element.58.wo_ref) | copy-start | bytes 10616836
  31.5 1.3 copy-start.18
  60.5 1.6 %copy-start.2 = (bf16[4,32,4,8,384]{4,3,2,1,0:T(8,128)(2,1)}, bf16[4,32,4,8,384]{4,3,2,1,0:T(8,128)(2,1)S(1)}, u32[]{:S(2)}) copy-start(bf16[4,32,4,8,384]{4,3,2,1,0:T(8,128)(2,1)S(1)} %shard_map.160) | copy-start | bytes 9437188
  62.2 48.0 %all-to-all-start.1 = ((bf16[128,4,8,384]{3,2,1,0:T(8,128)(2,1)}), bf16[128,4,8,384]{3,2,1,0:T(8,128)(2,1)S(1)}, u32[]{:S(2)}, u32[]{:S(2)}) async-start(bf16[128,4,8,384]{3,2,1,0:T(8,128)(2,1)} %bitcast.29), calls=%async_computation.1 | async-start | bytes 6291456 | tf_op jit(solution)/shard_map/all_to_all | solution.py:555
  68.4 2.0 %copy-start.17 = (bf16[768,2304]{1,0:T(8,128)(2,1)S(1)}, bf16[768,2304]{1,0:T(8,128)(2,1)}, u32[]{:S(2)}) copy-start(bf16[768,2304]{1,0:T(8,128)(2,1)} %copy-done.16) | copy-start | bytes 10616836
  70.4 1.5 %copy-start.19 = (bf16[2,384,1152]{2,1,0:T(8,128)(2,1)S(1)}, bf16[2,384,1152]{2,1,0:T(8,128)(2,1)}, u32[]{:S(2)}) copy-start(bf16[2,384,1152]{2,1,0:T(8,128)(2,1)} %copy-done.18) | copy-start | bytes 5308420
  71.9 1.1 copy-start.21
  73.0 18.8 %slice-start = ((s8[7962624]{0:T(1024)(128)(4,1)}), s8[4194304]{0:T(1024)(128)(4,1)S(1)}, s32[]{:S(2)}) async-start(s8[7962624]{0:T(1024)(128)(4,1)} %bitcast.23), calls=%async_computation.2 | async-start | bytes 8388608
  77.6 1.1 copy-start.23
  78.7 3.3 %copy-start = (bf16[3,3,3,384,384]{4,3,2,1,0:T(8,128)(2,1)S(1)}, bf16[3,3,3,384,384]{4,3,2,1,0:T(8,128)(2,1)}, u32[]{:S(2)}) copy-start(bf16[3,3,3,384,384]{4,3,2,1,0:T(8,128)(2,1)} %w_ref.4) | copy-start | bytes 23887876
  82.0 9.8 %slice-start.1 = ((s8[7962624]{0:T(1024)(128)(4,1)}), s8[3768320]{0:T(1024)(128)(4,1)S(1)}, s32[]{:S(2)}) async-start(s8[7962624]{0:T(1024)(128)(4,1)} %bitcast.23), calls=%async_computation.3 | async-start | bytes 7536640
  82.5 1.3 copy-start.4
  83.8 1.8 %copy-start.8 = (bf16[768,2304]{1,0:T(8,128)(2,1)}, bf16[768,2304]{1,0:T(8,128)(2,1)S(1)}, u32[]{:S(2)}) copy-start(bf16[768,2304]{1,0:T(8,128)(2,1)S(1)} %get-tuple-element.85.wo_ref) | copy-start | bytes 10616836
  87.2 2.8 %copy-start.3 = (bf16[1536,2304]{1,0:T(8,128)(2,1)}, bf16[1536,2304]{1,0:T(8,128)(2,1)S(1)}, u32[]{:S(2)}) copy-start(bf16[1536,2304]{1,0:T(8,128)(2,1)S(1)} %get-tuple-element.76.w_ref) | copy-start | bytes 21233668
  90.0 1.8 %copy-start.6 = (bf16[2,768,1152]{2,1,0:T(8,128)(2,1)}, bf16[2,768,1152]{2,1,0:T(8,128)(2,1)S(1)}, u32[]{:S(2)}) copy-start(bf16[2,768,1152]{2,1,0:T(8,128)(2,1)S(1)} %get-tuple-element.82.w_ref) | copy-start | bytes 10616836
  93.3 2.9 %copy-start.12 = (bf16[1536,2304]{1,0:T(8,128)(2,1)}, bf16[1536,2304]{1,0:T(8,128)(2,1)S(1)}, u32[]{:S(2)}) copy-start(bf16[1536,2304]{1,0:T(8,128)(2,1)S(1)} %get-tuple-element.71.w_ref) | copy-start | bytes 21233668
  96.3 1.8 %copy-start.14 = (bf16[2,768,1152]{2,1,0:T(8,128)(2,1)}, bf16[2,768,1152]{2,1,0:T(8,128)(2,1)S(1)}, u32[]{:S(2)}) copy-start(bf16[2,768,1152]{2,1,0:T(8,128)(2,1)S(1)} %get-tuple-element.70.w_ref) | copy-start | bytes 10616836
  110.2 6.1 %copy-start.13 = (bf16[1536,2304]{1,0:T(8,128)(2,1)S(1)}, bf16[1536,2304]{1,0:T(8,128)(2,1)}, u32[]{:S(2)}) copy-start(bf16[1536,2304]{1,0:T(8,128)(2,1)} %copy-done.12) | copy-start | bytes 21233668
  110.5 0.8 copy-start.27
  110.6 5.7 %copy-start.22 = (bf16[4,2,128,384]{3,2,1,0:T(8,128)(2,1)S(1)}, bf16[4,2,128,384]{3,2,1,0:T(8,128)(2,1)}, u32[]{:S(2)}) copy-start(bf16[4,2,128,384]{3,2,1,0:T(8,128)(2,1)} %copy-done.20) | copy-start | bytes 2359300
  110.6 5.7 %copy-start.24 = (f32[2,16,4,8,384]{4,3,2,1,0:T(8,128)S(1)}, f32[2,16,4,8,384]{4,3,2,1,0:T(8,128)}, u32[]{:S(2)}) copy-start(f32[2,16,4,8,384]{4,3,2,1,0:T(8,128)} %copy-done.23) | copy-start | bytes 4718596
  110.8 14.8 %collective-permute-start.3 = (bf16[2,16,4,8,384]{4,3,2,1,0:T(8,128)(2,1)S(1)}, bf16[2,16,4,8,384]{4,3,2,1,0:T(8,128)(2,1)S(1)}, u32[]{:S(2)}, u32[]{:S(2)}) collective-permute-start(bf16[2,16,4,8,384]{4,3,2,1,0:T(8,128)(2,1)S(1)} %get-tuple-element.99), channel_id=1, source_target_pairs={{0,31},{1,2},{2,1},{3,4},{4,3},{5,6},{6,5},{7,8},{8,7},{9,10},{10,... | collective-permute-start | bytes 2359304 | tf_op jit(solution)/shard_map/ppermute | solution.py:539
  111.1 14.5 %collective-permute-start.2 = (bf16[2,16,4,8,384]{4,3,2,1,0:T(8,128)(2,1)S(1)}, bf16[2,16,4,8,384]{4,3,2,1,0:T(8,128)(2,1)S(1)}, u32[]{:S(2)}, u32[]{:S(2)}) collective-permute-start(bf16[2,16,4,8,384]{4,3,2,1,0:T(8,128)(2,1)S(1)} %get-tuple-element.100), channel_id=1, source_target_pairs={{0,1},{1,0},{2,3},{3,2},{4,5},{5,4},{6,7},{7,6},{8,9},{9,8},{10,11... | collective-permute-start | bytes 2359304 | tf_op jit(solution)/shard_map/ppermute | solution.py:536
  111.4 9.5 %slice-start.2 = ((s8[7077888]{0:T(1024)(128)(4,1)}), s8[4194304]{0:T(1024)(128)(4,1)S(1)}, s32[]{:S(2)}) async-start(s8[7077888]{0:T(1024)(128)(4,1)} %bitcast.30), calls=%async_computation.4 | async-start | bytes 8388608
  111.6 22.7 %collective-permute-start.6 = (bf16[2,16,4,8,384]{4,3,2,1,0:T(8,128)(2,1)S(1)}, bf16[2,16,4,8,384]{4,3,2,1,0:T(8,128)(2,1)S(1)}, u32[]{:S(2)}, u32[]{:S(2)}) collective-permute-start(bf16[2,16,4,8,384]{4,3,2,1,0:T(8,128)(2,1)S(1)} %get-tuple-element.97), channel_id=1, source_target_pairs={{0,31},{1,2},{2,1},{3,4},{4,3},{5,6},{6,5},{7,8},{8,7},{9,10},{10,... | collective-permute-start | bytes 2359304 | tf_op jit(solution)/shard_map/ppermute | solution.py:539
  116.3 18.0 %collective-permute-start.5 = (bf16[2,16,4,8,384]{4,3,2,1,0:T(8,128)(2,1)S(1)}, bf16[2,16,4,8,384]{4,3,2,1,0:T(8,128)(2,1)S(1)}, u32[]{:S(2)}, u32[]{:S(2)}) collective-permute-start(bf16[2,16,4,8,384]{4,3,2,1,0:T(8,128)(2,1)S(1)} %get-tuple-element.98), channel_id=1, source_target_pairs={{0,1},{1,0},{2,3},{3,2},{4,5},{5,4},{6,7},{7,6},{8,9},{9,8},{10,11... | collective-permute-start | bytes 2359304 | tf_op jit(solution)/shard_map/ppermute | solution.py:536
  116.3 4.6 %slice-start.3 = ((s8[7077888]{0:T(1024)(128)(4,1)}), s8[2883584]{0:T(1024)(128)(4,1)S(1)}, s32[]{:S(2)}) async-start(s8[7077888]{0:T(1024)(128)(4,1)} %bitcast.30), calls=%async_computation.5 | async-start | bytes 5767168
  120.9 4.7 %copy-start.15 = (bf16[2,768,1152]{2,1,0:T(8,128)(2,1)S(1)}, bf16[2,768,1152]{2,1,0:T(8,128)(2,1)}, u32[]{:S(2)}) copy-start(bf16[2,768,1152]{2,1,0:T(8,128)(2,1)} %copy-done.14) | copy-start | bytes 10616836
  124.9 4.7 %copy-start.28 = (f32[384]{0:T(512)S(1)}, f32[384]{0:T(512)}, u32[]{:S(2)}) copy-start(f32[384]{0:T(512)} %param.22) | copy-start | bytes 4612
  124.9 5.9 %copy-start.5 = (bf16[2,384,1152]{2,1,0:T(8,128)(2,1)S(1)}, bf16[2,384,1152]{2,1,0:T(8,128)(2,1)}, u32[]{:S(2)}) copy-start(bf16[2,384,1152]{2,1,0:T(8,128)(2,1)} %copy-done.4) | copy-start | bytes 5308420
  125.6 5.2 %copy-start.9 = (bf16[768,2304]{1,0:T(8,128)(2,1)S(1)}, bf16[768,2304]{1,0:T(8,128)(2,1)}, u32[]{:S(2)}) copy-start(bf16[768,2304]{1,0:T(8,128)(2,1)} %copy-done.8) | copy-start | bytes 10616836
  129.0 1.8 %collective-permute-start.7 = (bf16[4,128,384]{2,1,0:T(8,128)(2,1)S(1)}, bf16[4,128,384]{2,1,0:T(8,128)(2,1)S(1)}, u32[]{:S(2)}, u32[]{:S(2)}) collective-permute-start(bf16[4,128,384]{2,1,0:T(8,128)(2,1)S(1)} %get-tuple-element.84), channel_id=1, source_target_pairs={{0,1},{1,0},{2,3},{3,2},{4,5},{5,4},{6,7},{7,6},{8,9},{9,8},{10,11... | collective-permute-start | bytes 1179656 | tf_op jit(solution)/shard_map/ppermute | solution.py:536
  129.1 10.8 %collective-permute-start.4 = (bf16[4,128,384]{2,1,0:T(8,128)(2,1)S(1)}, bf16[4,128,384]{2,1,0:T(8,128)(2,1)S(1)}, u32[]{:S(2)}, u32[]{:S(2)}) collective-permute-start(bf16[4,128,384]{2,1,0:T(8,128)(2,1)S(1)} %get-tuple-element.80), channel_id=1, source_target_pairs={{0,31},{1,2},{2,1},{3,4},{4,3},{5,6},{6,5},{7,8},{8,7},{9,10},{10,... | collective-permute-start | bytes 1179656 | tf_op jit(solution)/shard_map/ppermute | solution.py:539
  130.9 3.5 %copy-start.7 = (bf16[2,768,1152]{2,1,0:T(8,128)(2,1)S(1)}, bf16[2,768,1152]{2,1,0:T(8,128)(2,1)}, u32[]{:S(2)}) copy-start(bf16[2,768,1152]{2,1,0:T(8,128)(2,1)} %copy-done.6) | copy-start | bytes 10616836
  134.3 5.6 %copy-start.11 = (bf16[4,2,128,384]{3,2,1,0:T(8,128)(2,1)S(1)}, bf16[4,2,128,384]{3,2,1,0:T(8,128)(2,1)}, u32[]{:S(2)}) copy-start(bf16[4,2,128,384]{3,2,1,0:T(8,128)(2,1)} %f_ref.3) | copy-start | bytes 2359300
  (1 other events, 0.8 us)

commit v15 on v14

--- a/solution.py
+++ b/solution.py
@@ -372,8 +372,8 @@
             pltpu.VMEM((half, weight.shape[1]), jnp.float32),
             pltpu.SemaphoreType.DMA((n_rows * n_slots,)),
         ],
-        flops=half,
-        moved=half,
+        flops=2 * half * weight.size,
+        moved=2 * weight.size,
         far_out=(1,),
     )
 
@@ -569,16 +569,17 @@
         return lax.dynamic_index_in_dim(got[:, cache], row, 0, keepdims=False)
 
     near_1, far_1 = swap_near(picked(0, 1 - odd)), swap_far(picked(0, odd))
-    near_2, far_2 = swap_near(picked(1, 1 - odd)), swap_far(picked(1, odd))
+    near_rows, far_rows = picked(1, 1 - odd), picked(1, odd)
     act_tiles = act_first.reshape(n_slots, n_rows, blocks, CB, ch)
     sums_1, next_first = own_first(got, own_1, sums_1, act_tiles)
-    got_later, sums_1 = lax.optimization_barrier((got, sums_1))
-    sums_2, kept = own_second(got_later, own_2)
-    sums_1, sums_2, kept = lax.optimization_barrier((sums_1, sums_2, kept))
+    near_rows, far_rows, sums_1 = lax.optimization_barrier((near_rows, far_rows, sums_1))
+    near_2, far_2 = swap_near(near_rows), swap_far(far_rows)
     act_second, near, far = second_activation(
         near_1, far_1, sides_1, sums_1, bias_first[None], gain_second[None], edges
     )
     act_near, act_far = swap_near(near), swap_far(far)
+    got_later, act_second = lax.optimization_barrier((got, act_second))
+    sums_2, kept = own_second(got_later, own_2)
     sums_2, next_second = act_part(
         act_second, act_near, act_own_2, act_sides_2, sums_2, kept, edges
     )

time: 143 us -> 144 us (level)
  local copies, waits for them, and re-layouts: 32.5 us -> 34.9 us
  starting transfers between devices: 28.2 us -> 26.6 us
    unnamed x78, local copies, waits for them, and re-layouts: 31.7 us -> 34.1 us
    ppermute x4, starting transfers between devices: 10.7 us -> 8.78 us  [swap_far(): lax.ppermute(row, 'tile', [(i, (i + 2 * (i % 2) - 1) % n_tiles) for i in...]
  transfers between devices with their start and end apart: 10 -> 10, of which waited for: 5 -> 3; matrix products, arithmetic and copies ran while one was open for 1% -> 1% of each run, Pallas kernels for 21% -> 21%
where the time goes in v15:
time: 144 us; the launch traced here: 143 us
  waiting for transfers between devices  42.5 us (30%)
  Pallas kernels  37.1 us (26%)
  local copies, waits for them, and re-layouts  34.9 us (24%)
  starting transfers between devices  26.6 us (18%)
    unnamed x78, local copies, waits for them, and re-layouts  34.1 us
    ppermute x4, waiting for transfers between devices, swap_far(): lax.ppermute(row, 'tile', [(i, (i + 2 * (i % 2) - 1) % n_tiles) for i in...  30.4 us
    pallas_call x8, Pallas kernels, call(): pl.pallas_call(body, in_specs=in_specs, out_specs=out_specs, out_shape=li...  27.9 us
    all_to_all x1, waiting for transfers between devices, local(): lax.all_to_all(moved.reshape(n_groups * n_tiles, n_slots, CB, ch), BOTH,...  12.1 us
    all_to_all x1, starting transfers between devices, local(): held = lax.all_to_all(sent, BOTH, 0, 0, tiled=True)  11.1 us
    ppermute x4, starting transfers between devices, swap_far(): lax.ppermute(row, 'tile', [(i, (i + 2 * (i % 2) - 1) % n_tiles) for i in...  8.78 us
    all_to_all x1, starting transfers between devices, local(): lax.all_to_all(moved.reshape(n_groups * n_tiles, n_slots, CB, ch), BOTH,...  6.34 us
    pallas_call x4, Pallas kernels, spread(): pl.pallas_call(body, grid=(n_y,), in_specs=[pl.BlockSpec((times, 1, n_x,...  4.11 us
  transfers between devices with their start and end apart: 10, of which 3 were waited for; matrix products, arithmetic and copies ran while one was open for 1% of the time, Pallas kernels for 21%

profile of v15, /device:TPU:0, one launch (start us, length us, event | category | flops | bytes accessed | tf_op | source)
XLA Modules:
  0.0 143.0 jit_solution(10831588819720318959)
XLA Ops:
  0.6 3.1 %shard_map.157 = bf16[2,2,2,16,4,8,384]{6,5,4,3,2,1,0:T(8,128)(2,1)} custom-call(bf16[4,2,2,16,8,384]{5,4,3,2,1,0:T(8,128)(2,1)} %bitcast.35, bf16[4,2,2,16,8,384]{5,4,3,2,1,0:T(8,128)(2,1)} %bitcast.36), custom_call_target="tpu_custom_call" | custom-call | tf_op jit(solution)/shard_map/pallas_call | solution.py:47
  3.9 11.1 %all-to-all-start = ((bf16[128,4,8,384]{3,2,1,0:T(8,128)(2,1)}), bf16[128,4,8,384]{3,2,1,0:T(8,128)(2,1)S(1)}, u32[]{:S(2)}, u32[]{:S(2)}) async-start(bf16[128,4,8,384]{3,2,1,0:T(8,128)(2,1)} %bitcast.34), calls=%async_computation | async-start | bytes 6291456 | tf_op jit(solution)/shard_map/all_to_all | solution.py:544
  15.2 0.6 select_reduce_fusion
  16.0 1.1 copy-done.9
  17.1 2.8 %shard_map.158 = (bf16[4,2,128,384]{3,2,1,0:T(8,128)(2,1)S(1)}, bf16[4,128,384]{2,1,0:T(8,128)(2,1)}, bf16[4,128,384]{2,1,0:T(8,128)(2,1)}) custom-call(s32[3,4]{1,0:T(4,128)S(1)} %add_convert_fusion.edge_ref, bf16[4,2,128,384]{3,2,1,0:T(8,128)(2,1)S(1)} %copy-done.9, f32[1,384]{1,0:T(1,128)S(1)} %broadcast_in_dim.53.g_ref), custom_call_target="tpu_custom_call" | custom-call | flops 3932160 | bytes 2359296 | tf_op jit(solution)/shard_map/pallas_call | solution.py:105
  19.9 0.9 copy-done.20
  20.7 5.3 %collective-permute-start.1 = (bf16[4,128,384]{2,1,0:T(8,128)(2,1)}, bf16[4,128,384]{2,1,0:T(8,128)(2,1)}, u32[]{:S(2)}, u32[]{:S(2)}) collective-permute-start(bf16[4,128,384]{2,1,0:T(8,128)(2,1)} %get-tuple-element.49), channel_id=1, source_target_pairs={{0,31},{1,2},{2,1},{3,4},{4,3},{5,6},{6,5},{7,8},{8,7},{9,10},{10,... | collective-permute-start | bytes 1179656 | tf_op jit(solution)/shard_map/ppermute | solution.py:539
  26.0 3.3 %copy-done.1 = bf16[3,3,3,384,384]{4,3,2,1,0:T(8,128)(2,1)S(1)} copy-done((bf16[3,3,3,384,384]{4,3,2,1,0:T(8,128)(2,1)S(1)}, bf16[3,3,3,384,384]{4,3,2,1,0:T(8,128)(2,1)}, u32[]{:S(2)}) %copy-start.1) | copy-done | bytes 7962648
  29.3 0.5 shard_map.159
  29.8 1.8 %copy-done.16 = bf16[768,2304]{1,0:T(8,128)(2,1)} copy-done((bf16[768,2304]{1,0:T(8,128)(2,1)}, bf16[768,2304]{1,0:T(8,128)(2,1)S(1)}, u32[]{:S(2)}) %copy-start.16) | copy-done | bytes 3538968
  31.5 1.3 copy-done.18
  32.9 26.1 %collective-permute-done.1.far_ref = bf16[4,128,384]{2,1,0:T(8,128)(2,1)} collective-permute-done((bf16[4,128,384]{2,1,0:T(8,128)(2,1)}, bf16[4,128,384]{2,1,0:T(8,128)(2,1)}, u32[]{:S(2)}, u32[]{:S(2)}) %collective-permute-start.1) | collective-permute-done | bytes 393248 | tf_op jit(solution)/shard_map/ppermute | solution.py:539
  59.0 2.0 %shard_map.160 = bf16[4,32,4,8,384]{4,3,2,1,0:T(8,128)(2,1)S(1)} custom-call(s32[16]{0:T(128)S(1)} %get-tuple-element.93.source_ref, s32[16]{0:T(128)S(1)} %get-tuple-element.101.rotation_ref, s32[16]{0:T(128)S(1)} %compare_convert_fusion.keep_ref, bf16[4,32,4,8,384]{4,3,2,1,0:T(8,128)(2,1)S(1)} %bitcast.28), custom_call_target="tpu_custom_call" | custom-call | tf_op jit(solution)/shard_map/pallas_call | solution.py:86
  61.0 1.6 %copy-done.2 = bf16[4,32,4,8,384]{4,3,2,1,0:T(8,128)(2,1)} copy-done((bf16[4,32,4,8,384]{4,3,2,1,0:T(8,128)(2,1)}, bf16[4,32,4,8,384]{4,3,2,1,0:T(8,128)(2,1)S(1)}, u32[]{:S(2)}) %copy-start.2) | copy-done | bytes 3145752
  62.6 6.3 %all-to-all-start.1 = ((bf16[128,4,8,384]{3,2,1,0:T(8,128)(2,1)}), bf16[128,4,8,384]{3,2,1,0:T(8,128)(2,1)S(1)}, u32[]{:S(2)}, u32[]{:S(2)}) async-start(bf16[128,4,8,384]{3,2,1,0:T(8,128)(2,1)} %bitcast.29), calls=%async_computation.1 | async-start | bytes 6291456 | tf_op jit(solution)/shard_map/all_to_all | solution.py:555
  69.0 2.0 %copy-done.17 = bf16[768,2304]{1,0:T(8,128)(2,1)S(1)} copy-done((bf16[768,2304]{1,0:T(8,128)(2,1)S(1)}, bf16[768,2304]{1,0:T(8,128)(2,1)}, u32[]{:S(2)}) %copy-start.17) | copy-done | bytes 3538968
  71.0 1.5 %copy-done.19 = bf16[2,384,1152]{2,1,0:T(8,128)(2,1)S(1)} copy-done((bf16[2,384,1152]{2,1,0:T(8,128)(2,1)S(1)}, bf16[2,384,1152]{2,1,0:T(8,128)(2,1)}, u32[]{:S(2)}) %copy-start.19) | copy-done | bytes 1769496
  72.5 1.1 copy-done.21
  73.6 4.6 %shard_map.161.z_ref = f32[2,16,4,8,384]{4,3,2,1,0:T(8,128)S(1)} custom-call(s32[3,4]{1,0:T(4,128)S(1)} %add_convert_fusion.edge_ref, bf16[4,2,128,384]{3,2,1,0:T(8,128)(2,1)S(1)} %copy-done.21, bf16[4,128,384]{2,1,0:T(8,128)(2,1)S(1)} %collective-permute-done.near_ref, bf16[4,128,384]{2,1,0:T(8,128)(2,1)} %collective-permute-done.1.far_ref, ...), custom_call_target="tpu_custom_call" | custom-call | flops 2717908992 | bytes 6684672 | tf_op jit(solution)/shard_map/pallas_call | solution.py:105
  78.2 1.1 copy-done.23
  79.3 3.3 %copy-done = bf16[3,3,3,384,384]{4,3,2,1,0:T(8,128)(2,1)S(1)} copy-done((bf16[3,3,3,384,384]{4,3,2,1,0:T(8,128)(2,1)S(1)}, bf16[3,3,3,384,384]{4,3,2,1,0:T(8,128)(2,1)}, u32[]{:S(2)}) %copy-start) | copy-done | bytes 7962648
  82.6 0.5 shard_map.164
  83.1 1.3 copy-done.3
  84.4 1.8 %copy-done.7 = bf16[768,2304]{1,0:T(8,128)(2,1)} copy-done((bf16[768,2304]{1,0:T(8,128)(2,1)}, bf16[768,2304]{1,0:T(8,128)(2,1)S(1)}, u32[]{:S(2)}) %copy-start.7) | copy-done | bytes 3538968
  86.2 1.5 %shard_map.163 = (bf16[1536,2304]{1,0:T(8,128)(2,1)S(1)}, bf16[2,768,1152]{2,1,0:T(8,128)(2,1)S(1)}) custom-call(bf16[3,3,3,384,384]{4,3,2,1,0:T(8,128)(2,1)S(1)} %copy-done), custom_call_target="tpu_custom_call" | custom-call | bytes 15925248 | tf_op jit(solution)/shard_map/pallas_call | solution.py:154
  87.8 1.8 %copy-done.5 = bf16[2,768,1152]{2,1,0:T(8,128)(2,1)} copy-done((bf16[2,768,1152]{2,1,0:T(8,128)(2,1)}, bf16[2,768,1152]{2,1,0:T(8,128)(2,1)S(1)}, u32[]{:S(2)}) %copy-start.5) | copy-done | bytes 3538968
  89.6 2.8 %copy-done.11 = bf16[1536,2304]{1,0:T(8,128)(2,1)} copy-done((bf16[1536,2304]{1,0:T(8,128)(2,1)}, bf16[1536,2304]{1,0:T(8,128)(2,1)S(1)}, u32[]{:S(2)}) %copy-start.11) | copy-done | bytes 7077912
  92.4 1.5 %shard_map.162 = (bf16[1536,2304]{1,0:T(8,128)(2,1)S(1)}, bf16[2,768,1152]{2,1,0:T(8,128)(2,1)S(1)}) custom-call(bf16[3,3,3,384,384]{4,3,2,1,0:T(8,128)(2,1)S(1)} %bitcast.24), custom_call_target="tpu_custom_call" | custom-call | bytes 15925248 | tf_op jit(solution)/shard_map/pallas_call | solution.py:154
  93.9 2.9 %copy-done.12 = bf16[1536,2304]{1,0:T(8,128)(2,1)} copy-done((bf16[1536,2304]{1,0:T(8,128)(2,1)}, bf16[1536,2304]{1,0:T(8,128)(2,1)S(1)}, u32[]{:S(2)}) %copy-start.12) | copy-done | bytes 7077912
  96.9 1.8 %copy-done.14 = bf16[2,768,1152]{2,1,0:T(8,128)(2,1)} copy-done((bf16[2,768,1152]{2,1,0:T(8,128)(2,1)}, bf16[2,768,1152]{2,1,0:T(8,128)(2,1)S(1)}, u32[]{:S(2)}) %copy-start.14) | copy-done | bytes 3538968
  98.7 12.1 %all-to-all-done.1 = bf16[128,4,8,384]{3,2,1,0:T(8,128)(2,1)S(1)} async-done(((bf16[128,4,8,384]{3,2,1,0:T(8,128)(2,1)}), bf16[128,4,8,384]{3,2,1,0:T(8,128)(2,1)S(1)}, u32[]{:S(2)}, u32[]{:S(2)}) %all-to-all-start.1) | async-done | bytes 3145760 | tf_op jit(solution)/shard_map/all_to_all | solution.py:555
  110.8 0.3 fusion.2
  111.2 0.2 dynamic-slice_bitcast_fusion.2
  111.4 0.3 collective-permute-start.3
  111.7 0.1 collective-permute-start.2
  111.8 0.2 dynamic-slice_bitcast_fusion
  112.0 1.8 %copy-done.13 = bf16[1536,2304]{1,0:T(8,128)(2,1)S(1)} copy-done((bf16[1536,2304]{1,0:T(8,128)(2,1)S(1)}, bf16[1536,2304]{1,0:T(8,128)(2,1)}, u32[]{:S(2)}) %copy-start.13) | copy-done | bytes 7077912
  113.8 0.2 copy-done.22
  114.0 0.5 copy-done.24
  114.6 4.5 %shard_map.165 = (f32[2,16,4,8,384]{4,3,2,1,0:T(8,128)S(1)}, bf16[4,2,2,16,8,384]{5,4,3,2,1,0:T(8,128)(2,1)}) custom-call(bf16[2,2,2,16,4,8,384]{6,5,4,3,2,1,0:T(8,128)(2,1)S(1)} %bitcast.26, bf16[1536,2304]{1,0:T(8,128)(2,1)S(1)} %copy-done.13, f32[2,16,4,8,384]{4,3,2,1,0:T(8,128)S(1)} %copy-done.24, bf16[4,2,16,8,384]{4,3,2,1,0:T(8,128)(2,1)S(1)} %bitcast.33), custom_call_target="tpu_custom_call" | custom-call | flops 3623878656 | bytes 7077888 | tf_op jit(solution)/shard_map/pallas_call | solution.py:105
  119.2 2.7 %collective-permute-start.6 = (bf16[2,16,4,8,384]{4,3,2,1,0:T(8,128)(2,1)S(1)}, bf16[2,16,4,8,384]{4,3,2,1,0:T(8,128)(2,1)S(1)}, u32[]{:S(2)}, u32[]{:S(2)}) collective-permute-start(bf16[2,16,4,8,384]{4,3,2,1,0:T(8,128)(2,1)S(1)} %get-tuple-element.78), channel_id=1, source_target_pairs={{0,31},{1,2},{2,1},{3,4},{4,3},{5,6},{6,5},{7,8},{8,7},{9,10},{10,... | collective-permute-start | bytes 2359304 | tf_op jit(solution)/shard_map/ppermute | solution.py:539
  121.9 4.3 %collective-permute-done.3.far_ref = bf16[2,16,4,8,384]{4,3,2,1,0:T(8,128)(2,1)S(1)} collective-permute-done((bf16[2,16,4,8,384]{4,3,2,1,0:T(8,128)(2,1)S(1)}, bf16[2,16,4,8,384]{4,3,2,1,0:T(8,128)(2,1)S(1)}, u32[]{:S(2)}, u32[]{:S(2)}) %collective-permute-start.3) | collective-permute-done | bytes 786464 | tf_op jit(solution)/shard_map/ppermute | solution.py:539
  126.2 3.3 %shard_map.166 = (bf16[4,2,128,384]{3,2,1,0:T(8,128)(2,1)S(1)}, bf16[4,128,384]{2,1,0:T(8,128)(2,1)S(1)}, bf16[4,128,384]{2,1,0:T(8,128)(2,1)S(1)}) custom-call(s32[3,4]{1,0:T(4,128)S(1)} %add_convert_fusion.edge_ref, bf16[2,16,4,8,384]{4,3,2,1,0:T(8,128)(2,1)S(1)} %collective-permute-done.2.near_ref, ...), custom_call_target="tpu_custom_call" | custom-call | flops 1811939328 | bytes 3538944 | tf_op jit(solution)/shard_map/pallas_call | solution.py:105
  129.7 0.5 collective-permute-start.4
  130.2 4.0 %shard_map.167 = (f32[2,16,4,8,384]{4,3,2,1,0:T(8,128)S(1)}, bf16[4,2,2,16,8,384]{5,4,3,2,1,0:T(8,128)(2,1)}) custom-call(bf16[2,2,2,16,4,8,384]{6,5,4,3,2,1,0:T(8,128)(2,1)S(1)} %bitcast.27, bf16[1536,2304]{1,0:T(8,128)(2,1)S(1)} %bitcast.32), custom_call_target="tpu_custom_call" | custom-call | flops 3623878656 | bytes 7077888 | tf_op jit(solution)/shard_map/pallas_call | solution.py:105
  134.2 3.4 %shard_map.168 = (f32[2,16,4,8,384]{4,3,2,1,0:T(8,128)S(1)}, bf16[4,2,2,16,8,384]{5,4,3,2,1,0:T(8,128)(2,1)}) custom-call(s32[3,4]{1,0:T(4,128)S(1)} %add_convert_fusion.edge_ref, bf16[4,2,128,384]{3,2,1,0:T(8,128)(2,1)S(1)} %get-tuple-element.81.act_ref, bf16[4,2,16,8,384]{4,3,2,1,0:T(8,128)(2,1)S(1)} %bitcast.30, ...), custom_call_target="tpu_custom_call", output_to_operand_aliasing={{1}: (7, {})} | custom-call | flops 1811939328 | bytes 5308416 | tf_op jit(solution)/shard_map/pallas_call | solution.py:105
  137.6 3.0 %shard_map.169.z_ref = f32[2,16,4,8,384]{4,3,2,1,0:T(8,128)S(1)} custom-call(s32[3,4]{1,0:T(4,128)S(1)} %add_convert_fusion.edge_ref, bf16[2,16,4,8,384]{4,3,2,1,0:T(8,128)(2,1)S(1)} %collective-permute-done.5.near_ref, bf16[2,16,4,8,384]{4,3,2,1,0:T(8,128)(2,1)S(1)} %collective-permute-done.6.far_ref, bf16[2,768,1152]{2,1,0:T(8,128)(2,1)S(1)} %copy-done.6, ...), custom_call_target="tpu_custom_call" | custom-call | flops 1811939328 | bytes 3538944 | tf_op jit(solution)/shard_map/pallas_call | solution.py:105
  140.6 2.4 %shard_map.170 = bf16[4,2,128,384]{3,2,1,0:T(8,128)(2,1)} custom-call(s32[3,4]{1,0:T(4,128)S(1)} %add_convert_fusion.edge_ref, bf16[4,128,384]{2,1,0:T(8,128)(2,1)S(1)} %collective-permute-done.4.far_ref, bf16[2,384,1152]{2,1,0:T(8,128)(2,1)S(1)} %copy-done.4, f32[2,16,4,8,384]{4,3,2,1,0:T(8,128)S(1)} %shard_map.169.z_ref, ...), custom_call_target="tpu_custom_call" | custom-call | flops 452984832 | bytes 1769472 | tf_op jit(solution)/shard_map/pallas_call | solution.py:105
  (79 shorter events, 0.6 us)
Async XLA Ops:
  3.8 11.2 %copy-start.25 = (f32[384]{0:T(512)S(1)}, f32[384]{0:T(512)}, u32[]{:S(2)}) copy-start(f32[384]{0:T(512)} %param.17) | copy-start | bytes 4612
  3.8 11.3 %copy-start.29 = (s32[16]{0:T(128)S(1)}, s32[16]{0:T(128)}, u32[]{:S(2)}) copy-start(s32[16]{0:T(128)} %param.27) | copy-start | bytes 196
  3.8 11.3 %copy-start.30 = (s32[16]{0:T(128)S(1)}, s32[16]{0:T(128)}, u32[]{:S(2)}) copy-start(s32[16]{0:T(128)} %param.24) | copy-start | bytes 196
  3.8 11.3 %copy-start.31 = (s32[16]{0:T(128)S(1)}, s32[16]{0:T(128)}, u32[]{:S(2)}) copy-start(s32[16]{0:T(128)} %param.25) | copy-start | bytes 196
  3.8 11.3 %copy-start.32 = (s32[16]{0:T(128)S(1)}, s32[16]{0:T(128)}, u32[]{:S(2)}) copy-start(s32[16]{0:T(128)} %param.23) | copy-start | bytes 196
  3.8 11.3 %copy-start.33 = (s32[16]{0:T(128)S(1)}, s32[16]{0:T(128)}, u32[]{:S(2)}) copy-start(s32[16]{0:T(128)} %param.26) | copy-start | bytes 196
  3.9 55.1 %all-to-all-start = ((bf16[128,4,8,384]{3,2,1,0:T(8,128)(2,1)}), bf16[128,4,8,384]{3,2,1,0:T(8,128)(2,1)S(1)}, u32[]{:S(2)}, u32[]{:S(2)}) async-start(bf16[128,4,8,384]{3,2,1,0:T(8,128)(2,1)} %bitcast.34), calls=%async_computation | async-start | bytes 6291456 | tf_op jit(solution)/shard_map/all_to_all | solution.py:544
  16.0 1.1 copy-start.9
  20.7 12.1 %collective-permute-start = (bf16[4,128,384]{2,1,0:T(8,128)(2,1)}, bf16[4,128,384]{2,1,0:T(8,128)(2,1)S(1)}, u32[]{:S(2)}, u32[]{:S(2)}) collective-permute-start(bf16[4,128,384]{2,1,0:T(8,128)(2,1)} %get-tuple-element.48), channel_id=1, source_target_pairs={{0,1},{1,0},{2,3},{3,2},{4,5},{5,4},{6,7},{7,6},{8,9},{9,8},{10,11... | collective-permute-start | bytes 1179656 | tf_op jit(solution)/shard_map/ppermute | solution.py:536
  20.7 38.2 %collective-permute-start.1 = (bf16[4,128,384]{2,1,0:T(8,128)(2,1)}, bf16[4,128,384]{2,1,0:T(8,128)(2,1)}, u32[]{:S(2)}, u32[]{:S(2)}) collective-permute-start(bf16[4,128,384]{2,1,0:T(8,128)(2,1)} %get-tuple-element.49), channel_id=1, source_target_pairs={{0,31},{1,2},{2,1},{3,4},{4,3},{5,6},{6,5},{7,8},{8,7},{9,10},{10,... | collective-permute-start | bytes 1179656 | tf_op jit(solution)/shard_map/ppermute | solution.py:539
  26.0 3.3 %copy-start.1 = (bf16[3,3,3,384,384]{4,3,2,1,0:T(8,128)(2,1)S(1)}, bf16[3,3,3,384,384]{4,3,2,1,0:T(8,128)(2,1)}, u32[]{:S(2)}) copy-start(bf16[3,3,3,384,384]{4,3,2,1,0:T(8,128)(2,1)} %w_ref.2) | copy-start | bytes 23887876
  29.3 3.6 %copy-start.34 = (s32[16]{0:T(128)S(1)}, s32[16]{0:T(128)}, u32[]{:S(2)}) copy-start(s32[16]{0:T(128)} %get-tuple-element.91) | copy-start | bytes 196
  29.8 1.8 %copy-start.16 = (bf16[768,2304]{1,0:T(8,128)(2,1)}, bf16[768,2304]{1,0:T(8,128)(2,1)S(1)}, u32[]{:S(2)}) copy-start(bf16[768,2304]{1,0:T(8,128)(2,1)S(1)} %get-tuple-element.58.wo_ref) | copy-start | bytes 10616836
  31.5 1.3 copy-start.18
  61.0 1.6 %copy-start.2 = (bf16[4,32,4,8,384]{4,3,2,1,0:T(8,128)(2,1)}, bf16[4,32,4,8,384]{4,3,2,1,0:T(8,128)(2,1)S(1)}, u32[]{:S(2)}) copy-start(bf16[4,32,4,8,384]{4,3,2,1,0:T(8,128)(2,1)S(1)} %shard_map.160) | copy-start | bytes 9437188
  62.6 48.2 %all-to-all-start.1 = ((bf16[128,4,8,384]{3,2,1,0:T(8,128)(2,1)}), bf16[128,4,8,384]{3,2,1,0:T(8,128)(2,1)S(1)}, u32[]{:S(2)}, u32[]{:S(2)}) async-start(bf16[128,4,8,384]{3,2,1,0:T(8,128)(2,1)} %bitcast.29), calls=%async_computation.1 | async-start | bytes 6291456 | tf_op jit(solution)/shard_map/all_to_all | solution.py:555
  69.0 2.0 %copy-start.17 = (bf16[768,2304]{1,0:T(8,128)(2,1)S(1)}, bf16[768,2304]{1,0:T(8,128)(2,1)}, u32[]{:S(2)}) copy-start(bf16[768,2304]{1,0:T(8,128)(2,1)} %copy-done.16) | copy-start | bytes 10616836
  71.0 1.5 %copy-start.19 = (bf16[2,384,1152]{2,1,0:T(8,128)(2,1)S(1)}, bf16[2,384,1152]{2,1,0:T(8,128)(2,1)}, u32[]{:S(2)}) copy-start(bf16[2,384,1152]{2,1,0:T(8,128)(2,1)} %copy-done.18) | copy-start | bytes 5308420
  72.5 1.1 copy-start.21
  73.6 18.8 %slice-start = ((s8[7962624]{0:T(1024)(128)(4,1)}), s8[4194304]{0:T(1024)(128)(4,1)S(1)}, s32[]{:S(2)}) async-start(s8[7962624]{0:T(1024)(128)(4,1)} %bitcast.23), calls=%async_computation.2 | async-start | bytes 8388608
  78.2 1.1 copy-start.23
  79.3 3.3 %copy-start = (bf16[3,3,3,384,384]{4,3,2,1,0:T(8,128)(2,1)S(1)}, bf16[3,3,3,384,384]{4,3,2,1,0:T(8,128)(2,1)}, u32[]{:S(2)}) copy-start(bf16[3,3,3,384,384]{4,3,2,1,0:T(8,128)(2,1)} %w_ref.4) | copy-start | bytes 23887876
  82.6 9.8 %slice-start.1 = ((s8[7962624]{0:T(1024)(128)(4,1)}), s8[3768320]{0:T(1024)(128)(4,1)S(1)}, s32[]{:S(2)}) async-start(s8[7962624]{0:T(1024)(128)(4,1)} %bitcast.23), calls=%async_computation.3 | async-start | bytes 7536640
  83.1 1.3 copy-start.3
  84.4 1.8 %copy-start.7 = (bf16[768,2304]{1,0:T(8,128)(2,1)}, bf16[768,2304]{1,0:T(8,128)(2,1)S(1)}, u32[]{:S(2)}) copy-start(bf16[768,2304]{1,0:T(8,128)(2,1)S(1)} %get-tuple-element.83.wo_ref) | copy-start | bytes 10616836
  87.8 1.8 %copy-start.5 = (bf16[2,768,1152]{2,1,0:T(8,128)(2,1)}, bf16[2,768,1152]{2,1,0:T(8,128)(2,1)S(1)}, u32[]{:S(2)}) copy-start(bf16[2,768,1152]{2,1,0:T(8,128)(2,1)S(1)} %get-tuple-element.79.w_ref) | copy-start | bytes 10616836
  89.6 2.8 %copy-start.11 = (bf16[1536,2304]{1,0:T(8,128)(2,1)}, bf16[1536,2304]{1,0:T(8,128)(2,1)S(1)}, u32[]{:S(2)}) copy-start(bf16[1536,2304]{1,0:T(8,128)(2,1)S(1)} %get-tuple-element.85.w_ref) | copy-start | bytes 21233668
  93.9 2.9 %copy-start.12 = (bf16[1536,2304]{1,0:T(8,128)(2,1)}, bf16[1536,2304]{1,0:T(8,128)(2,1)S(1)}, u32[]{:S(2)}) copy-start(bf16[1536,2304]{1,0:T(8,128)(2,1)S(1)} %get-tuple-element.71.w_ref) | copy-start | bytes 21233668
  96.9 1.8 %copy-start.14 = (bf16[2,768,1152]{2,1,0:T(8,128)(2,1)}, bf16[2,768,1152]{2,1,0:T(8,128)(2,1)S(1)}, u32[]{:S(2)}) copy-start(bf16[2,768,1152]{2,1,0:T(8,128)(2,1)S(1)} %get-tuple-element.70.w_ref) | copy-start | bytes 10616836
  110.8 3.0 %copy-start.13 = (bf16[1536,2304]{1,0:T(8,128)(2,1)S(1)}, bf16[1536,2304]{1,0:T(8,128)(2,1)}, u32[]{:S(2)}) copy-start(bf16[1536,2304]{1,0:T(8,128)(2,1)} %copy-done.12) | copy-start | bytes 21233668
  111.1 2.9 %copy-start.22 = (bf16[4,2,128,384]{3,2,1,0:T(8,128)(2,1)S(1)}, bf16[4,2,128,384]{3,2,1,0:T(8,128)(2,1)}, u32[]{:S(2)}) copy-start(bf16[4,2,128,384]{3,2,1,0:T(8,128)(2,1)} %copy-done.20) | copy-start | bytes 2359300
  111.2 3.4 %copy-start.24 = (f32[2,16,4,8,384]{4,3,2,1,0:T(8,128)S(1)}, f32[2,16,4,8,384]{4,3,2,1,0:T(8,128)}, u32[]{:S(2)}) copy-start(f32[2,16,4,8,384]{4,3,2,1,0:T(8,128)} %copy-done.23) | copy-start | bytes 4718596
  111.4 14.8 %collective-permute-start.3 = (bf16[2,16,4,8,384]{4,3,2,1,0:T(8,128)(2,1)S(1)}, bf16[2,16,4,8,384]{4,3,2,1,0:T(8,128)(2,1)S(1)}, u32[]{:S(2)}, u32[]{:S(2)}) collective-permute-start(bf16[2,16,4,8,384]{4,3,2,1,0:T(8,128)(2,1)S(1)} %get-tuple-element.99), channel_id=1, source_target_pairs={{0,31},{1,2},{2,1},{3,4},{4,3},{5,6},{6,5},{7,8},{8,7},{9,10},{10,... | collective-permute-start | bytes 2359304 | tf_op jit(solution)/shard_map/ppermute | solution.py:539
  111.7 14.5 %collective-permute-start.2 = (bf16[2,16,4,8,384]{4,3,2,1,0:T(8,128)(2,1)S(1)}, bf16[2,16,4,8,384]{4,3,2,1,0:T(8,128)(2,1)S(1)}, u32[]{:S(2)}, u32[]{:S(2)}) collective-permute-start(bf16[2,16,4,8,384]{4,3,2,1,0:T(8,128)(2,1)S(1)} %get-tuple-element.100), channel_id=1, source_target_pairs={{0,1},{1,0},{2,3},{3,2},{4,5},{5,4},{6,7},{7,6},{8,9},{9,8},{10,11... | collective-permute-start | bytes 2359304 | tf_op jit(solution)/shard_map/ppermute | solution.py:536
  111.8 18.4 %slice-start.2 = ((s8[7077888]{0:T(1024)(128)(4,1)}), s8[4194304]{0:T(1024)(128)(4,1)S(1)}, s32[]{:S(2)}) async-start(s8[7077888]{0:T(1024)(128)(4,1)} %bitcast.31), calls=%async_computation.4 | async-start | bytes 8388608
  114.5 7.4 %copy-start.26 = (f32[384]{0:T(512)S(1)}, f32[384]{0:T(512)}, u32[]{:S(2)}) copy-start(f32[384]{0:T(512)} %param.18) | copy-start | bytes 4612
  114.5 7.4 %copy-start.27 = (f32[384]{0:T(512)S(1)}, f32[384]{0:T(512)}, u32[]{:S(2)}) copy-start(f32[384]{0:T(512)} %param.21) | copy-start | bytes 4612
  114.6 11.6 %copy-start.15 = (bf16[2,768,1152]{2,1,0:T(8,128)(2,1)S(1)}, bf16[2,768,1152]{2,1,0:T(8,128)(2,1)}, u32[]{:S(2)}) copy-start(bf16[2,768,1152]{2,1,0:T(8,128)(2,1)} %copy-done.14) | copy-start | bytes 10616836
  114.6 15.6 %slice-start.3 = ((s8[7077888]{0:T(1024)(128)(4,1)}), s8[2883584]{0:T(1024)(128)(4,1)S(1)}, s32[]{:S(2)}) async-start(s8[7077888]{0:T(1024)(128)(4,1)} %bitcast.31), calls=%async_computation.5 | async-start | bytes 5767168
  119.1 18.5 %collective-permute-start.5 = (bf16[2,16,4,8,384]{4,3,2,1,0:T(8,128)(2,1)S(1)}, bf16[2,16,4,8,384]{4,3,2,1,0:T(8,128)(2,1)S(1)}, u32[]{:S(2)}, u32[]{:S(2)}) collective-permute-start(bf16[2,16,4,8,384]{4,3,2,1,0:T(8,128)(2,1)S(1)} %get-tuple-element.77), channel_id=1, source_target_pairs={{0,1},{1,0},{2,3},{3,2},{4,5},{5,4},{6,7},{7,6},{8,9},{9,8},{10,11... | collective-permute-start | bytes 2359304 | tf_op jit(solution)/shard_map/ppermute | solution.py:536
  119.2 18.4 %collective-permute-start.6 = (bf16[2,16,4,8,384]{4,3,2,1,0:T(8,128)(2,1)S(1)}, bf16[2,16,4,8,384]{4,3,2,1,0:T(8,128)(2,1)S(1)}, u32[]{:S(2)}, u32[]{:S(2)}) collective-permute-start(bf16[2,16,4,8,384]{4,3,2,1,0:T(8,128)(2,1)S(1)} %get-tuple-element.78), channel_id=1, source_target_pairs={{0,31},{1,2},{2,1},{3,4},{4,3},{5,6},{6,5},{7,8},{8,7},{9,10},{10,... | collective-permute-start | bytes 2359304 | tf_op jit(solution)/shard_map/ppermute | solution.py:539
  121.9 7.7 %copy-start.28 = (f32[384]{0:T(512)S(1)}, f32[384]{0:T(512)}, u32[]{:S(2)}) copy-start(f32[384]{0:T(512)} %param.22) | copy-start | bytes 4612
  129.5 4.6 %collective-permute-start.7 = (bf16[4,128,384]{2,1,0:T(8,128)(2,1)S(1)}, bf16[4,128,384]{2,1,0:T(8,128)(2,1)S(1)}, u32[]{:S(2)}, u32[]{:S(2)}) collective-permute-start(bf16[4,128,384]{2,1,0:T(8,128)(2,1)S(1)} %get-tuple-element.82), channel_id=1, source_target_pairs={{0,1},{1,0},{2,3},{3,2},{4,5},{5,4},{6,7},{7,6},{8,9},{9,8},{10,11... | collective-permute-start | bytes 1179656 | tf_op jit(solution)/shard_map/ppermute | solution.py:536
  129.7 4.5 %copy-start.4 = (bf16[2,384,1152]{2,1,0:T(8,128)(2,1)S(1)}, bf16[2,384,1152]{2,1,0:T(8,128)(2,1)}, u32[]{:S(2)}) copy-start(bf16[2,384,1152]{2,1,0:T(8,128)(2,1)} %copy-done.3) | copy-start | bytes 5308420
  129.7 10.9 %collective-permute-start.4 = (bf16[4,128,384]{2,1,0:T(8,128)(2,1)S(1)}, bf16[4,128,384]{2,1,0:T(8,128)(2,1)S(1)}, u32[]{:S(2)}, u32[]{:S(2)}) collective-permute-start(bf16[4,128,384]{2,1,0:T(8,128)(2,1)S(1)} %get-tuple-element.75), channel_id=1, source_target_pairs={{0,31},{1,2},{2,1},{3,4},{4,3},{5,6},{6,5},{7,8},{8,7},{9,10},{10,... | collective-permute-start | bytes 1179656 | tf_op jit(solution)/shard_map/ppermute | solution.py:539
  130.2 4.0 %copy-start.8 = (bf16[768,2304]{1,0:T(8,128)(2,1)S(1)}, bf16[768,2304]{1,0:T(8,128)(2,1)}, u32[]{:S(2)}) copy-start(bf16[768,2304]{1,0:T(8,128)(2,1)} %copy-done.7) | copy-start | bytes 10616836
  134.2 3.4 %copy-start.6 = (bf16[2,768,1152]{2,1,0:T(8,128)(2,1)S(1)}, bf16[2,768,1152]{2,1,0:T(8,128)(2,1)}, u32[]{:S(2)}) copy-start(bf16[2,768,1152]{2,1,0:T(8,128)(2,1)} %copy-done.5) | copy-start | bytes 10616836
  137.6 3.0 %copy-start.10 = (bf16[4,2,128,384]{3,2,1,0:T(8,128)(2,1)S(1)}, bf16[4,2,128,384]{3,2,1,0:T(8,128)(2,1)}, u32[]{:S(2)}) copy-start(bf16[4,2,128,384]{3,2,1,0:T(8,128)(2,1)} %f_ref.3) | copy-start | bytes 2359300
  (1 other events, 0.9 us)

commit v16 on v15

--- a/solution.py
+++ b/solution.py
@@ -388,59 +388,72 @@
     return folded(dot(lhs[...].reshape(half, n_frames * ch), w), ch, True)
 
 
-def second_activation(near, far, w_sides, sums, bias, gain, edges):
-    n_frames, blocks, n_slots, _, ch = far.shape
-    n_rows, n_cols, deep = sums.shape[0], blocks * CB, n_frames * ch
-
-    def body(edge_ref, near_ref, far_ref, w_ref, z_ref, b_ref, g_ref, o_ref, near_out, far_out, lhs):
-        for (side, y), out in zip(beside(edge_ref, near_ref, far_ref), (near_out, far_out)):
-            total = side_sums(edge_ref, y, side, w_ref[y], lhs) + z_ref[y] + b_ref[...]
-            for s in range(n_slots):
-                value = activated(total[:, s].reshape(n_cols, ch), g_ref[...]).astype(jnp.bfloat16)
-                o_ref[s, y] = value
-                out[s] = value
-
-    row = jax.ShapeDtypeStruct((n_slots, n_cols, ch), jnp.bfloat16)
-    return call(
-        body,
-        [jax.ShapeDtypeStruct((n_slots, n_rows, n_cols, ch), jnp.bfloat16), row, row],
-        (near, far, w_sides, sums, bias, gain),
+def activation_row(which, side, w_sides, sums, bias, gain, edges):
+    n_frames, blocks, n_slots, _, ch = side.shape
+    n_cols, deep = blocks * CB, n_frames * ch
+
+    def body(edge_ref, side_ref, w_ref, z_ref, b_ref, g_ref, o_ref, lhs):
+        rows, y = beside(edge_ref, side_ref, side_ref)[which]
+        total = side_sums(edge_ref, y, rows, w_ref[y], lhs) + z_ref[y] + b_ref[...]
+        for s in range(n_slots):
+            value = activated(total[:, s].reshape(n_cols, ch), g_ref[...])
+            o_ref[s] = value.astype(jnp.bfloat16)
+
+    return call(
+        body,
+        [jax.ShapeDtypeStruct((n_slots, n_cols, ch), jnp.bfloat16)],
+        (side, w_sides, sums, bias, gain),
         scalars=(edges,),
-        scratch=[
-            pltpu.VMEM((blocks, n_slots, CB, deep), jnp.bfloat16),
-        ],
-        flops=2 * n_slots * n_cols * w_sides.size,
-        moved=2 * w_sides.size,
-    )
-
-
-def act_part(act, near, w_own, w_sides, sums, kept, edges):
-    n_slots, n_rows, n_cols, ch = act.shape
+        scratch=[pltpu.VMEM((blocks, n_slots, CB, deep), jnp.bfloat16)],
+        flops=n_slots * n_cols * w_sides.size,
+        moved=w_sides.size,
+    )[0]
+
+
+def act_part(near_row, far_row, near, w_own, w_sides, sums, kept, edges):
+    n_slots, n_cols, ch = near_row.shape
+    n_rows = sums.shape[0]
     half = n_slots * n_cols
-    tiles = act.reshape(n_slots, n_rows, n_cols // CB, CB, ch)
-
-    def body(edge_ref, act_ref, tiles_ref, near_ref, wo_ref, ws_ref, z_ref, kept_ref, o_ref, next_ref, lhs, side, sem):
-        copy = pltpu.make_async_copy(tiles_ref, next_ref.at[:, 1], sem)
-        copy.start()
-        add_own(act_ref, wo_ref, lhs, o_ref, z_ref)
+    tiles = (n_slots, n_cols // CB, CB, ch)
+
+    def body(edge_ref, nr_ref, fr_ref, nt_ref, ft_ref, near_ref, wo_ref, ws_ref, z_ref, kept_ref, o_ref, next_ref, lhs, side, sems):
+        odd = edge_ref[2, 0]
+        copies = [
+            pltpu.make_async_copy(nt_ref, next_ref.at[:, 1, 1 - odd], sems.at[0]),
+            pltpu.make_async_copy(ft_ref, next_ref.at[:, 1, odd], sems.at[1]),
+        ]
+        for c in copies:
+            c.start()
+        for s in range(n_slots):
+            at = slice(s * n_cols, (s + 1) * n_cols)
+            lhs[at, 0:ch] = jnp.where(odd != 0, nr_ref[s], fr_ref[s])
+            lhs[at, ch : 2 * ch] = jnp.where(odd != 0, fr_ref[s], nr_ref[s])
+        both = dot(lhs[...], wo_ref[...])
+        wide = both.shape[1] // n_rows
+        for y in range(n_rows):
+            add_into(o_ref, y, folded(both[:, y * wide : (y + 1) * wide], ch, False), False, z_ref)
         add_sides(edge_ref, beside(edge_ref, near_ref, None)[:1], ws_ref, side, o_ref)
-        copy.wait()
+        for c in copies:
+            c.wait()
 
     return call(
         body,
         [jax.ShapeDtypeStruct(sums.shape, jnp.float32), jax.ShapeDtypeStruct(kept.shape, kept.dtype)],
-        (act, tiles, near, w_own, w_sides, sums, kept),
+        (
+            near_row, far_row, near_row.reshape(tiles), far_row.reshape(tiles),
+            near, w_own, w_sides, sums, kept,
+        ),
         scalars=(edges,),
         scratch=[
             pltpu.VMEM((half, n_rows * ch), jnp.bfloat16),
             pltpu.VMEM((half, ch), jnp.bfloat16),
-            pltpu.SemaphoreType.DMA,
+            pltpu.SemaphoreType.DMA((2,)),
         ],
         flops=2 * half * w_own.size,
         moved=2 * (w_sides.size + w_own.size),
-        far=(6,),
+        far=(8,),
         far_out=(1,),
-        aliases={7: 1},
+        aliases={9: 1},
     )
 
 
@@ -574,14 +587,14 @@
     sums_1, next_first = own_first(got, own_1, sums_1, act_tiles)
     near_rows, far_rows, sums_1 = lax.optimization_barrier((near_rows, far_rows, sums_1))
     near_2, far_2 = swap_near(near_rows), swap_far(far_rows)
-    act_second, near, far = second_activation(
-        near_1, far_1, sides_1, sums_1, bias_first[None], gain_second[None], edges
-    )
+    scale = (bias_first[None], gain_second[None], edges)
+    near = activation_row(0, near_1, sides_1, sums_1, *scale)
+    far = activation_row(1, far_1, sides_1, sums_1, *scale)
     act_near, act_far = swap_near(near), swap_far(far)
-    got_later, act_second = lax.optimization_barrier((got, act_second))
+    got_later, far = lax.optimization_barrier((got, far))
     sums_2, kept = own_second(got_later, own_2)
     sums_2, next_second = act_part(
-        act_second, act_near, act_own_2, act_sides_2, sums_2, kept, edges
+        near, far, act_near, act_own_2, act_sides_2, sums_2, kept, edges
     )
     sums_2 = cached_sides(near_2, far_2, sides_2, sums_2, edges)
     mixed_frame = last_part(act_far, act_sides_2, sums_2, bias_second[None], frame_in, edges)

time: 144 us -> 148 us (1.028)
  Pallas kernels: 37.1 us -> 42.9 us
  local copies, waits for them, and re-layouts: 34.9 us -> 31.6 us
  starting transfers between devices: 26.6 us -> 29.6 us
    pallas_call x8 -> x9, Pallas kernels: 27.9 us -> 34.1 us  [call(): pl.pallas_call(body, in_specs=in_specs, out_specs=out_specs, out_shape=li...]
    unnamed x78 -> x72, local copies, waits for them, and re-layouts: 34.1 us -> 28.7 us
    ppermute x4, waiting for transfers between devices: 30.4 us -> 26.8 us  [swap_far(): lax.ppermute(row, 'tile', [(i, (i + 2 * (i % 2) - 1) % n_tiles) for i in...]
    all_to_all x1, waiting for transfers between devices: 12.1 us -> 15.5 us  [local(): lax.all_to_all(moved.reshape(n_groups * n_tiles, n_slots, CB, ch), BOTH,...]
    ppermute x4, starting transfers between devices: 8.78 us -> 11.5 us  [swap_far(): lax.ppermute(row, 'tile', [(i, (i + 2 * (i % 2) - 1) % n_tiles) for i in...]
    slice x1, local copies, waits for them, and re-layouts: 0.32 us -> 2.35 us  [picked(): return lax.dynamic_index_in_dim(got[:, cache], row, 0, keepdims=False)]
  transfers between devices with their start and end apart: 10 -> 10, of which waited for: 3 -> 3; matrix products, arithmetic and copies ran while one was open for 1% -> 0% of each run, Pallas kernels for 21% -> 24%
where the time goes in v16:
time: 148 us
  Pallas kernels  42.9 us (29%)
  waiting for transfers between devices  42.3 us (29%)
  local copies, waits for them, and re-layouts  31.6 us (21%)
  starting transfers between devices  29.6 us (20%)
    pallas_call x9, Pallas kernels, call(): pl.pallas_call(body, in_specs=in_specs, out_specs=out_specs, out_shape=li...  34.1 us
    unnamed x72, local copies, waits for them, and re-layouts  28.7 us
    ppermute x4, waiting for transfers between devices, swap_far(): lax.ppermute(row, 'tile', [(i, (i + 2 * (i % 2) - 1) % n_tiles) for i in...  26.8 us
    all_to_all x1, waiting for transfers between devices, local(): lax.all_to_all(moved.reshape(n_groups * n_tiles, n_slots, CB, ch), BOTH,...  15.5 us
    ppermute x4, starting transfers between devices, swap_far(): lax.ppermute(row, 'tile', [(i, (i + 2 * (i % 2) - 1) % n_tiles) for i in...  11.5 us
    all_to_all x1, starting transfers between devices, local(): held = lax.all_to_all(sent, BOTH, 0, 0, tiled=True)  11.1 us
    all_to_all x1, starting transfers between devices, local(): lax.all_to_all(moved.reshape(n_groups * n_tiles, n_slots, CB, ch), BOTH,...  6.62 us
    pallas_call x4, Pallas kernels, spread(): pl.pallas_call(body, grid=(n_y,), in_specs=[pl.BlockSpec((times, 1, n_x,...  4.11 us
  transfers between devices with their start and end apart: 10, of which 3 were waited for; matrix products, arithmetic and copies ran while one was open for 0% of the time, Pallas kernels for 24%

profile of v16, /device:TPU:0, one launch (start us, length us, event | category | flops | bytes accessed | tf_op | source)
XLA Modules:
  0.0 147.8 jit_solution(17283256321068673272)
XLA Ops:
  0.6 3.1 %shard_map.157 = bf16[2,2,2,16,4,8,384]{6,5,4,3,2,1,0:T(8,128)(2,1)} custom-call(bf16[4,2,2,16,8,384]{5,4,3,2,1,0:T(8,128)(2,1)} %bitcast.34, bf16[4,2,2,16,8,384]{5,4,3,2,1,0:T(8,128)(2,1)} %bitcast.35), custom_call_target="tpu_custom_call" | custom-call | tf_op jit(solution)/shard_map/pallas_call | solution.py:47
  3.9 11.1 %all-to-all-start = ((bf16[128,4,8,384]{3,2,1,0:T(8,128)(2,1)}), bf16[128,4,8,384]{3,2,1,0:T(8,128)(2,1)S(1)}, u32[]{:S(2)}, u32[]{:S(2)}) async-start(bf16[128,4,8,384]{3,2,1,0:T(8,128)(2,1)} %bitcast.33), calls=%async_computation | async-start | bytes 6291456 | tf_op jit(solution)/shard_map/all_to_all | solution.py:557
  15.2 0.1 select_reduce_fusion
  15.5 1.1 copy-done.9
  16.6 2.8 %shard_map.158 = (bf16[4,2,128,384]{3,2,1,0:T(8,128)(2,1)S(1)}, bf16[4,128,384]{2,1,0:T(8,128)(2,1)}, bf16[4,128,384]{2,1,0:T(8,128)(2,1)}) custom-call(s32[3,4]{1,0:T(4,128)S(1)} %add_convert_fusion.edge_ref, bf16[4,2,128,384]{3,2,1,0:T(8,128)(2,1)S(1)} %copy-done.9, f32[1,384]{1,0:T(1,128)S(1)} %broadcast_in_dim.53.g_ref), custom_call_target="tpu_custom_call" | custom-call | flops 3932160 | bytes 2359296 | tf_op jit(solution)/shard_map/pallas_call | solution.py:105
  19.4 0.9 copy-done.18
  20.3 5.3 %collective-permute-start.1 = (bf16[4,128,384]{2,1,0:T(8,128)(2,1)}, bf16[4,128,384]{2,1,0:T(8,128)(2,1)}, u32[]{:S(2)}, u32[]{:S(2)}) collective-permute-start(bf16[4,128,384]{2,1,0:T(8,128)(2,1)} %get-tuple-element.46), channel_id=1, source_target_pairs={{0,31},{1,2},{2,1},{3,4},{4,3},{5,6},{6,5},{7,8},{8,7},{9,10},{10,... | collective-permute-start | bytes 1179656 | tf_op jit(solution)/shard_map/ppermute | solution.py:552
  25.5 3.3 %copy-done.1 = bf16[3,3,3,384,384]{4,3,2,1,0:T(8,128)(2,1)S(1)} copy-done((bf16[3,3,3,384,384]{4,3,2,1,0:T(8,128)(2,1)S(1)}, bf16[3,3,3,384,384]{4,3,2,1,0:T(8,128)(2,1)}, u32[]{:S(2)}) %copy-start.1) | copy-done | bytes 7962648
  28.8 0.5 shard_map.159
  29.3 1.7 %copy-done.14 = bf16[768,2304]{1,0:T(8,128)(2,1)} copy-done((bf16[768,2304]{1,0:T(8,128)(2,1)}, bf16[768,2304]{1,0:T(8,128)(2,1)S(1)}, u32[]{:S(2)}) %copy-start.14) | copy-done | bytes 3538968
  31.1 1.3 copy-done.16
  32.3 26.7 %collective-permute-done.1.far_ref = bf16[4,128,384]{2,1,0:T(8,128)(2,1)} collective-permute-done((bf16[4,128,384]{2,1,0:T(8,128)(2,1)}, bf16[4,128,384]{2,1,0:T(8,128)(2,1)}, u32[]{:S(2)}, u32[]{:S(2)}) %collective-permute-start.1) | collective-permute-done | bytes 393248 | tf_op jit(solution)/shard_map/ppermute | solution.py:552
  59.0 1.5 %shard_map.160 = bf16[4,32,4,8,384]{4,3,2,1,0:T(8,128)(2,1)S(1)} custom-call(s32[16]{0:T(128)S(1)} %get-tuple-element.87.source_ref, s32[16]{0:T(128)S(1)} %get-tuple-element.95.rotation_ref, s32[16]{0:T(128)S(1)} %compare_convert_fusion.keep_ref, bf16[4,32,4,8,384]{4,3,2,1,0:T(8,128)(2,1)S(1)} %bitcast.26), custom_call_target="tpu_custom_call" | custom-call | tf_op jit(solution)/shard_map/pallas_call | solution.py:86
  60.6 1.7 %copy-done.2 = bf16[4,32,4,8,384]{4,3,2,1,0:T(8,128)(2,1)} copy-done((bf16[4,32,4,8,384]{4,3,2,1,0:T(8,128)(2,1)}, bf16[4,32,4,8,384]{4,3,2,1,0:T(8,128)(2,1)S(1)}, u32[]{:S(2)}) %copy-start.2) | copy-done | bytes 3145752
  62.3 6.6 %all-to-all-start.1 = ((bf16[128,4,8,384]{3,2,1,0:T(8,128)(2,1)}), bf16[128,4,8,384]{3,2,1,0:T(8,128)(2,1)}, u32[]{:S(2)}, u32[]{:S(2)}) async-start(bf16[128,4,8,384]{3,2,1,0:T(8,128)(2,1)} %bitcast.27), calls=%async_computation.1 | async-start | bytes 6291456 | tf_op jit(solution)/shard_map/all_to_all | solution.py:568
  69.0 1.5 copy-done.17
  70.4 1.1 copy-done.19
  71.6 4.7 %shard_map.161.z_ref = f32[2,16,4,8,384]{4,3,2,1,0:T(8,128)S(1)} custom-call(s32[3,4]{1,0:T(4,128)S(1)} %add_convert_fusion.edge_ref, bf16[4,2,128,384]{3,2,1,0:T(8,128)(2,1)S(1)} %copy-done.19, bf16[4,128,384]{2,1,0:T(8,128)(2,1)} %collective-permute-done.near_ref, bf16[4,128,384]{2,1,0:T(8,128)(2,1)} %collective-permute-done.1.far_ref, ...), custom_call_target="tpu_custom_call" | custom-call | flops 2717908992 | bytes 6684672 | tf_op jit(solution)/shard_map/pallas_call | solution.py:105
  76.3 1.1 copy-done.21
  77.4 3.3 %copy-done = bf16[3,3,3,384,384]{4,3,2,1,0:T(8,128)(2,1)S(1)} copy-done((bf16[3,3,3,384,384]{4,3,2,1,0:T(8,128)(2,1)S(1)}, bf16[3,3,3,384,384]{4,3,2,1,0:T(8,128)(2,1)}, u32[]{:S(2)}) %copy-start) | copy-done | bytes 7962648
  80.7 0.5 shard_map.164
  81.2 1.3 copy-done.3
  82.5 1.8 %copy-done.7 = bf16[768,2304]{1,0:T(8,128)(2,1)} copy-done((bf16[768,2304]{1,0:T(8,128)(2,1)}, bf16[768,2304]{1,0:T(8,128)(2,1)S(1)}, u32[]{:S(2)}) %copy-start.7) | copy-done | bytes 3538968
  84.3 1.5 %shard_map.163 = (bf16[1536,2304]{1,0:T(8,128)(2,1)S(1)}, bf16[2,768,1152]{2,1,0:T(8,128)(2,1)S(1)}) custom-call(bf16[3,3,3,384,384]{4,3,2,1,0:T(8,128)(2,1)S(1)} %copy-done), custom_call_target="tpu_custom_call" | custom-call | bytes 15925248 | tf_op jit(solution)/shard_map/pallas_call | solution.py:154
  85.9 1.8 %copy-done.5 = bf16[2,768,1152]{2,1,0:T(8,128)(2,1)} copy-done((bf16[2,768,1152]{2,1,0:T(8,128)(2,1)}, bf16[2,768,1152]{2,1,0:T(8,128)(2,1)S(1)}, u32[]{:S(2)}) %copy-start.5) | copy-done | bytes 3538968
  87.6 2.8 %copy-done.11 = bf16[1536,2304]{1,0:T(8,128)(2,1)} copy-done((bf16[1536,2304]{1,0:T(8,128)(2,1)}, bf16[1536,2304]{1,0:T(8,128)(2,1)S(1)}, u32[]{:S(2)}) %copy-start.11) | copy-done | bytes 7077912
  90.4 1.5 %shard_map.162 = (bf16[1536,2304]{1,0:T(8,128)(2,1)S(1)}, bf16[2,768,1152]{2,1,0:T(8,128)(2,1)S(1)}) custom-call(bf16[3,3,3,384,384]{4,3,2,1,0:T(8,128)(2,1)S(1)} %bitcast.25), custom_call_target="tpu_custom_call" | custom-call | bytes 15925248 | tf_op jit(solution)/shard_map/pallas_call | solution.py:154
  92.0 2.9 %copy-done.12 = bf16[1536,2304]{1,0:T(8,128)(2,1)} copy-done((bf16[1536,2304]{1,0:T(8,128)(2,1)}, bf16[1536,2304]{1,0:T(8,128)(2,1)S(1)}, u32[]{:S(2)}) %copy-start.12) | copy-done | bytes 7077912
  94.9 15.5 %all-to-all-done.1 = bf16[128,4,8,384]{3,2,1,0:T(8,128)(2,1)} async-done(((bf16[128,4,8,384]{3,2,1,0:T(8,128)(2,1)}), bf16[128,4,8,384]{3,2,1,0:T(8,128)(2,1)}, u32[]{:S(2)}, u32[]{:S(2)}) %all-to-all-start.1) | async-done | bytes 3145760 | tf_op jit(solution)/shard_map/all_to_all | solution.py:568
  110.4 2.4 %fusion.2 = (bf16[2,1,2,16,4,8,384]{6,5,4,3,2,1,0:T(8,128)(2,1)S(1)}, bf16[2,1,2,16,4,8,384]{6,5,4,3,2,1,0:T(8,128)(2,1)S(1)}) fusion(bf16[2,2,2,16,4,8,384]{6,5,4,3,2,1,0:T(8,128)(2,1)} %bitcast.7.got_ref), kind=kLoop, calls=%fused_computation.21 | loop fusion | bytes 6291456 | tf_op jit(solution)/shard_map/slice | solution.py:582
  112.8 0.2 dynamic-slice_bitcast_fusion
  113.0 0.1 collective-permute-start.6
  113.1 0.9 collective-permute-start.2
  114.0 0.2 dynamic-slice_bitcast_fusion.1
  114.2 0.1 copy-done.13
  114.4 0.4 copy-done.20
  114.7 0.5 copy-done.22
  115.3 6.8 %shard_map.165 = (f32[2,16,4,8,384]{4,3,2,1,0:T(8,128)S(1)}, bf16[4,2,2,16,8,384]{5,4,3,2,1,0:T(8,128)(2,1)}) custom-call(bf16[2,2,2,16,4,8,384]{6,5,4,3,2,1,0:T(8,128)(2,1)} %bitcast.7.got_ref, bf16[1536,2304]{1,0:T(8,128)(2,1)S(1)} %copy-done.13, f32[2,16,4,8,384]{4,3,2,1,0:T(8,128)S(1)} %copy-done.22, bf16[4,2,16,8,384]{4,3,2,1,0:T(8,128)(2,1)S(1)} %bitcast.32), custom_call_target="tpu_custom_call" | custom-call | flops 3623878656 | bytes 7077888 | tf_op jit(solution)/shard_map/pallas_call | solution.py:105
  122.0 0.1 collective-permute-start.4
  122.1 3.6 %collective-permute-start.5 = (bf16[2,16,4,8,384]{4,3,2,1,0:T(8,128)(2,1)S(1)}, bf16[2,16,4,8,384]{4,3,2,1,0:T(8,128)(2,1)S(1)}, u32[]{:S(2)}, u32[]{:S(2)}) collective-permute-start(bf16[2,16,4,8,384]{4,3,2,1,0:T(8,128)(2,1)S(1)} %get-tuple-element.74), channel_id=1, source_target_pairs={{0,31},{1,2},{2,1},{3,4},{4,3},{5,6},{6,5},{7,8},{8,7},{9,10},{10,... | collective-permute-start | bytes 2359304 | tf_op jit(solution)/shard_map/ppermute | solution.py:552
  125.7 2.1 %shard_map.167.nr_ref = bf16[4,128,384]{2,1,0:T(8,128)(2,1)S(1)} custom-call(s32[3,4]{1,0:T(4,128)S(1)} %add_convert_fusion.edge_ref, bf16[2,16,4,8,384]{4,3,2,1,0:T(8,128)(2,1)S(1)} %collective-permute-done.6.side_ref, bf16[2,768,1152]{2,1,0:T(8,128)(2,1)S(1)} %get-tuple-element.67.w_ref, f32[2,16,4,8,384]{4,3,2,1,0:T(8,128)S(1)} %get-tuple-element.71.z_ref, ...), custom_call_target="tpu_custom_call" | custom-call | flops 905969664 | bytes 1769472 | tf_op jit(solution)/shard_map/pallas_call | solution.py:105
  128.0 0.1 collective-permute-done.2.side_ref
  128.1 2.1 %shard_map.166.fr_ref = bf16[4,128,384]{2,1,0:T(8,128)(2,1)S(1)} custom-call(s32[3,4]{1,0:T(4,128)S(1)} %add_convert_fusion.edge_ref, bf16[2,16,4,8,384]{4,3,2,1,0:T(8,128)(2,1)S(1)} %collective-permute-done.2.side_ref, bf16[2,768,1152]{2,1,0:T(8,128)(2,1)S(1)} %get-tuple-element.67.w_ref, f32[2,16,4,8,384]{4,3,2,1,0:T(8,128)S(1)} %get-tuple-element.71.z_ref, ...), custom_call_target="tpu_custom_call" | custom-call | flops 905969664 | bytes 1769472 | tf_op jit(solution)/shard_map/pallas_call | solution.py:105
  130.2 1.8 %collective-permute-start.3 = (bf16[4,128,384]{2,1,0:T(8,128)(2,1)S(1)}, bf16[4,128,384]{2,1,0:T(8,128)(2,1)S(1)}, u32[]{:S(2)}, u32[]{:S(2)}) collective-permute-start(bf16[4,128,384]{2,1,0:T(8,128)(2,1)S(1)} %shard_map.166.fr_ref), channel_id=1, source_target_pairs={{0,31},{1,2},{2,1},{3,4},{4,3},{5,6},{6,5},{7,8},{8,7},{9,10},{10,... | collective-permute-start | bytes 1179656 | tf_op jit(solution)/shard_map/ppermute | solution.py:552
  132.0 6.3 %shard_map.168 = (f32[2,16,4,8,384]{4,3,2,1,0:T(8,128)S(1)}, bf16[4,2,2,16,8,384]{5,4,3,2,1,0:T(8,128)(2,1)}) custom-call(bf16[2,2,2,16,4,8,384]{6,5,4,3,2,1,0:T(8,128)(2,1)} %bitcast.7.got_ref, bf16[1536,2304]{1,0:T(8,128)(2,1)S(1)} %bitcast.31), custom_call_target="tpu_custom_call" | custom-call | flops 3623878656 | bytes 7077888 | tf_op jit(solution)/shard_map/pallas_call | solution.py:105
  138.4 3.9 %shard_map.169 = (f32[2,16,4,8,384]{4,3,2,1,0:T(8,128)S(1)}, bf16[4,2,2,16,8,384]{5,4,3,2,1,0:T(8,128)(2,1)}) custom-call(s32[3,4]{1,0:T(4,128)S(1)} %add_convert_fusion.edge_ref, bf16[4,128,384]{2,1,0:T(8,128)(2,1)S(1)} %shard_map.167.nr_ref, bf16[4,128,384]{2,1,0:T(8,128)(2,1)S(1)} %shard_map.166.fr_ref, ...), custom_call_target="tpu_custom_call", output_to_operand_aliasing={{1}: (9, {})} | custom-call | flops 1811939328 | bytes 5308416 | tf_op jit(solution)/shard_map/pallas_call | solution.py:105
  142.4 3.0 %shard_map.170.z_ref = f32[2,16,4,8,384]{4,3,2,1,0:T(8,128)S(1)} custom-call(s32[3,4]{1,0:T(4,128)S(1)} %add_convert_fusion.edge_ref, bf16[2,16,4,8,384]{4,3,2,1,0:T(8,128)(2,1)S(1)} %collective-permute-done.4.near_ref, bf16[2,16,4,8,384]{4,3,2,1,0:T(8,128)(2,1)S(1)} %collective-permute-done.5.far_ref, bf16[2,768,1152]{2,1,0:T(8,128)(2,1)S(1)} %copy-done.6, ...), custom_call_target="tpu_custom_call" | custom-call | flops 1811939328 | bytes 3538944 | tf_op jit(solution)/shard_map/pallas_call | solution.py:105
  145.4 2.4 %shard_map.171 = bf16[4,2,128,384]{3,2,1,0:T(8,128)(2,1)} custom-call(s32[3,4]{1,0:T(4,128)S(1)} %add_convert_fusion.edge_ref, bf16[4,128,384]{2,1,0:T(8,128)(2,1)S(1)} %collective-permute-done.3.far_ref, bf16[2,384,1152]{2,1,0:T(8,128)(2,1)S(1)} %copy-done.4, f32[2,16,4,8,384]{4,3,2,1,0:T(8,128)S(1)} %shard_map.170.z_ref, ...), custom_call_target="tpu_custom_call" | custom-call | flops 452984832 | bytes 1769472 | tf_op jit(solution)/shard_map/pallas_call | solution.py:105
  (74 shorter events, 0.5 us)
Async XLA Ops:
  3.8 11.2 %copy-start.23 = (f32[384]{0:T(512)S(1)}, f32[384]{0:T(512)}, u32[]{:S(2)}) copy-start(f32[384]{0:T(512)} %param.17) | copy-start | bytes 4612
  3.8 11.3 %copy-start.27 = (s32[16]{0:T(128)S(1)}, s32[16]{0:T(128)}, u32[]{:S(2)}) copy-start(s32[16]{0:T(128)} %param.27) | copy-start | bytes 196
  3.8 11.3 %copy-start.28 = (s32[16]{0:T(128)S(1)}, s32[16]{0:T(128)}, u32[]{:S(2)}) copy-start(s32[16]{0:T(128)} %param.24) | copy-start | bytes 196
  3.8 11.3 %copy-start.29 = (s32[16]{0:T(128)S(1)}, s32[16]{0:T(128)}, u32[]{:S(2)}) copy-start(s32[16]{0:T(128)} %param.25) | copy-start | bytes 196
  3.8 11.3 %copy-start.30 = (s32[16]{0:T(128)S(1)}, s32[16]{0:T(128)}, u32[]{:S(2)}) copy-start(s32[16]{0:T(128)} %param.23) | copy-start | bytes 196
  3.8 11.3 %copy-start.31 = (s32[16]{0:T(128)S(1)}, s32[16]{0:T(128)}, u32[]{:S(2)}) copy-start(s32[16]{0:T(128)} %param.26) | copy-start | bytes 196
  3.9 55.1 %all-to-all-start = ((bf16[128,4,8,384]{3,2,1,0:T(8,128)(2,1)}), bf16[128,4,8,384]{3,2,1,0:T(8,128)(2,1)S(1)}, u32[]{:S(2)}, u32[]{:S(2)}) async-start(bf16[128,4,8,384]{3,2,1,0:T(8,128)(2,1)} %bitcast.33), calls=%async_computation | async-start | bytes 6291456 | tf_op jit(solution)/shard_map/all_to_all | solution.py:557
  15.5 1.1 copy-start.9
  19.4 0.9 copy-start.18
  20.3 12.1 %collective-permute-start = (bf16[4,128,384]{2,1,0:T(8,128)(2,1)}, bf16[4,128,384]{2,1,0:T(8,128)(2,1)}, u32[]{:S(2)}, u32[]{:S(2)}) collective-permute-start(bf16[4,128,384]{2,1,0:T(8,128)(2,1)} %get-tuple-element.45), channel_id=1, source_target_pairs={{0,1},{1,0},{2,3},{3,2},{4,5},{5,4},{6,7},{7,6},{8,9},{9,8},{10,11... | collective-permute-start | bytes 1179656 | tf_op jit(solution)/shard_map/ppermute | solution.py:549
  20.3 38.7 %collective-permute-start.1 = (bf16[4,128,384]{2,1,0:T(8,128)(2,1)}, bf16[4,128,384]{2,1,0:T(8,128)(2,1)}, u32[]{:S(2)}, u32[]{:S(2)}) collective-permute-start(bf16[4,128,384]{2,1,0:T(8,128)(2,1)} %get-tuple-element.46), channel_id=1, source_target_pairs={{0,31},{1,2},{2,1},{3,4},{4,3},{5,6},{6,5},{7,8},{8,7},{9,10},{10,... | collective-permute-start | bytes 1179656 | tf_op jit(solution)/shard_map/ppermute | solution.py:552
  25.5 3.3 %copy-start.1 = (bf16[3,3,3,384,384]{4,3,2,1,0:T(8,128)(2,1)S(1)}, bf16[3,3,3,384,384]{4,3,2,1,0:T(8,128)(2,1)}, u32[]{:S(2)}) copy-start(bf16[3,3,3,384,384]{4,3,2,1,0:T(8,128)(2,1)} %w_ref.2) | copy-start | bytes 23887876
  29.3 1.8 %copy-start.14 = (bf16[768,2304]{1,0:T(8,128)(2,1)}, bf16[768,2304]{1,0:T(8,128)(2,1)S(1)}, u32[]{:S(2)}) copy-start(bf16[768,2304]{1,0:T(8,128)(2,1)S(1)} %get-tuple-element.55.wo_ref) | copy-start | bytes 10616836
  31.1 1.3 copy-start.16
  60.6 1.7 %copy-start.2 = (bf16[4,32,4,8,384]{4,3,2,1,0:T(8,128)(2,1)}, bf16[4,32,4,8,384]{4,3,2,1,0:T(8,128)(2,1)S(1)}, u32[]{:S(2)}) copy-start(bf16[4,32,4,8,384]{4,3,2,1,0:T(8,128)(2,1)S(1)} %shard_map.160) | copy-start | bytes 9437188
  62.3 6.6 %copy-start.15 = (bf16[768,2304]{1,0:T(8,128)(2,1)S(1)}, bf16[768,2304]{1,0:T(8,128)(2,1)}, u32[]{:S(2)}) copy-start(bf16[768,2304]{1,0:T(8,128)(2,1)} %copy-done.14) | copy-start | bytes 10616836
  62.3 48.1 %all-to-all-start.1 = ((bf16[128,4,8,384]{3,2,1,0:T(8,128)(2,1)}), bf16[128,4,8,384]{3,2,1,0:T(8,128)(2,1)}, u32[]{:S(2)}, u32[]{:S(2)}) async-start(bf16[128,4,8,384]{3,2,1,0:T(8,128)(2,1)} %bitcast.27), calls=%async_computation.1 | async-start | bytes 6291456 | tf_op jit(solution)/shard_map/all_to_all | solution.py:568
  68.9 1.5 copy-start.17
  70.4 1.1 copy-start.19
  71.6 18.9 %slice-start = ((s8[7962624]{0:T(1024)(128)(4,1)}), s8[4194304]{0:T(1024)(128)(4,1)S(1)}, s32[]{:S(2)}) async-start(s8[7962624]{0:T(1024)(128)(4,1)} %bitcast.24), calls=%async_computation.2 | async-start | bytes 8388608
  76.3 1.1 copy-start.21
  77.4 3.3 %copy-start = (bf16[3,3,3,384,384]{4,3,2,1,0:T(8,128)(2,1)S(1)}, bf16[3,3,3,384,384]{4,3,2,1,0:T(8,128)(2,1)}, u32[]{:S(2)}) copy-start(bf16[3,3,3,384,384]{4,3,2,1,0:T(8,128)(2,1)} %w_ref.4) | copy-start | bytes 23887876
  80.7 9.8 %slice-start.1 = ((s8[7962624]{0:T(1024)(128)(4,1)}), s8[3768320]{0:T(1024)(128)(4,1)S(1)}, s32[]{:S(2)}) async-start(s8[7962624]{0:T(1024)(128)(4,1)} %bitcast.24), calls=%async_computation.3 | async-start | bytes 7536640
  81.2 1.3 copy-start.3
  82.5 1.8 %copy-start.7 = (bf16[768,2304]{1,0:T(8,128)(2,1)}, bf16[768,2304]{1,0:T(8,128)(2,1)S(1)}, u32[]{:S(2)}) copy-start(bf16[768,2304]{1,0:T(8,128)(2,1)S(1)} %get-tuple-element.77.wo_ref) | copy-start | bytes 10616836
  85.8 1.8 %copy-start.5 = (bf16[2,768,1152]{2,1,0:T(8,128)(2,1)}, bf16[2,768,1152]{2,1,0:T(8,128)(2,1)S(1)}, u32[]{:S(2)}) copy-start(bf16[2,768,1152]{2,1,0:T(8,128)(2,1)S(1)} %get-tuple-element.75.w_ref) | copy-start | bytes 10616836
  87.6 2.8 %copy-start.11 = (bf16[1536,2304]{1,0:T(8,128)(2,1)}, bf16[1536,2304]{1,0:T(8,128)(2,1)S(1)}, u32[]{:S(2)}) copy-start(bf16[1536,2304]{1,0:T(8,128)(2,1)S(1)} %get-tuple-element.79.w_ref) | copy-start | bytes 21233668
  92.0 2.9 %copy-start.12 = (bf16[1536,2304]{1,0:T(8,128)(2,1)}, bf16[1536,2304]{1,0:T(8,128)(2,1)S(1)}, u32[]{:S(2)}) copy-start(bf16[1536,2304]{1,0:T(8,128)(2,1)S(1)} %get-tuple-element.68.w_ref) | copy-start | bytes 21233668
  110.4 4.0 %copy-start.13 = (bf16[1536,2304]{1,0:T(8,128)(2,1)S(1)}, bf16[1536,2304]{1,0:T(8,128)(2,1)}, u32[]{:S(2)}) copy-start(bf16[1536,2304]{1,0:T(8,128)(2,1)} %copy-done.12) | copy-start | bytes 21233668
  112.8 2.0 %copy-start.20 = (bf16[4,2,128,384]{3,2,1,0:T(8,128)(2,1)S(1)}, bf16[4,2,128,384]{3,2,1,0:T(8,128)(2,1)}, u32[]{:S(2)}) copy-start(bf16[4,2,128,384]{3,2,1,0:T(8,128)(2,1)} %copy-done.18) | copy-start | bytes 2359300
  112.8 2.5 %copy-start.22 = (f32[2,16,4,8,384]{4,3,2,1,0:T(8,128)S(1)}, f32[2,16,4,8,384]{4,3,2,1,0:T(8,128)}, u32[]{:S(2)}) copy-start(f32[2,16,4,8,384]{4,3,2,1,0:T(8,128)} %copy-done.21) | copy-start | bytes 4718596
  113.0 12.7 %collective-permute-start.6 = (bf16[2,16,4,8,384]{4,3,2,1,0:T(8,128)(2,1)S(1)}, bf16[2,16,4,8,384]{4,3,2,1,0:T(8,128)(2,1)S(1)}, u32[]{:S(2)}, u32[]{:S(2)}) collective-permute-start(bf16[2,16,4,8,384]{4,3,2,1,0:T(8,128)(2,1)S(1)} %get-tuple-element.91), channel_id=1, source_target_pairs={{0,1},{1,0},{2,3},{3,2},{4,5},{5,4},{6,7},{7,6},{8,9},{9,8},{10,11... | collective-permute-start | bytes 2359304 | tf_op jit(solution)/shard_map/ppermute | solution.py:549
  113.1 15.0 %collective-permute-start.2 = (bf16[2,16,4,8,384]{4,3,2,1,0:T(8,128)(2,1)S(1)}, bf16[2,16,4,8,384]{4,3,2,1,0:T(8,128)(2,1)S(1)}, u32[]{:S(2)}, u32[]{:S(2)}) collective-permute-start(bf16[2,16,4,8,384]{4,3,2,1,0:T(8,128)(2,1)S(1)} %get-tuple-element.92), channel_id=1, source_target_pairs={{0,31},{1,2},{2,1},{3,4},{4,3},{5,6},{6,5},{7,8},{8,7},{9,10},{10,... | collective-permute-start | bytes 2359304 | tf_op jit(solution)/shard_map/ppermute | solution.py:552
  114.0 18.0 %slice-start.2 = ((s8[7077888]{0:T(1024)(128)(4,1)}), s8[4194304]{0:T(1024)(128)(4,1)S(1)}, s32[]{:S(2)}) async-start(s8[7077888]{0:T(1024)(128)(4,1)} %bitcast.30), calls=%async_computation.4 | async-start | bytes 8388608
  115.2 10.5 %copy-start.24 = (f32[384]{0:T(512)S(1)}, f32[384]{0:T(512)}, u32[]{:S(2)}) copy-start(f32[384]{0:T(512)} %param.18) | copy-start | bytes 4612
  115.2 10.5 %copy-start.25 = (f32[384]{0:T(512)S(1)}, f32[384]{0:T(512)}, u32[]{:S(2)}) copy-start(f32[384]{0:T(512)} %param.21) | copy-start | bytes 4612
  115.2 10.5 %copy-start.26 = (f32[384]{0:T(512)S(1)}, f32[384]{0:T(512)}, u32[]{:S(2)}) copy-start(f32[384]{0:T(512)} %param.22) | copy-start | bytes 4612
  115.2 16.8 %slice-start.3 = ((s8[7077888]{0:T(1024)(128)(4,1)}), s8[2883584]{0:T(1024)(128)(4,1)S(1)}, s32[]{:S(2)}) async-start(s8[7077888]{0:T(1024)(128)(4,1)} %bitcast.30), calls=%async_computation.5 | async-start | bytes 5767168
  122.0 20.3 %collective-permute-start.4 = (bf16[2,16,4,8,384]{4,3,2,1,0:T(8,128)(2,1)S(1)}, bf16[2,16,4,8,384]{4,3,2,1,0:T(8,128)(2,1)S(1)}, u32[]{:S(2)}, u32[]{:S(2)}) collective-permute-start(bf16[2,16,4,8,384]{4,3,2,1,0:T(8,128)(2,1)S(1)} %get-tuple-element.73), channel_id=1, source_target_pairs={{0,1},{1,0},{2,3},{3,2},{4,5},{5,4},{6,7},{7,6},{8,9},{9,8},{10,11... | collective-permute-start | bytes 2359304 | tf_op jit(solution)/shard_map/ppermute | solution.py:549
  122.1 20.2 %collective-permute-start.5 = (bf16[2,16,4,8,384]{4,3,2,1,0:T(8,128)(2,1)S(1)}, bf16[2,16,4,8,384]{4,3,2,1,0:T(8,128)(2,1)S(1)}, u32[]{:S(2)}, u32[]{:S(2)}) collective-permute-start(bf16[2,16,4,8,384]{4,3,2,1,0:T(8,128)(2,1)S(1)} %get-tuple-element.74), channel_id=1, source_target_pairs={{0,31},{1,2},{2,1},{3,4},{4,3},{5,6},{6,5},{7,8},{8,7},{9,10},{10,... | collective-permute-start | bytes 2359304 | tf_op jit(solution)/shard_map/ppermute | solution.py:552
  127.9 10.5 %collective-permute-start.7 = (bf16[4,128,384]{2,1,0:T(8,128)(2,1)S(1)}, bf16[4,128,384]{2,1,0:T(8,128)(2,1)S(1)}, u32[]{:S(2)}, u32[]{:S(2)}) collective-permute-start(bf16[4,128,384]{2,1,0:T(8,128)(2,1)S(1)} %shard_map.167.nr_ref), channel_id=1, source_target_pairs={{0,1},{1,0},{2,3},{3,2},{4,5},{5,4},{6,7},{7,6},{8,9},{9,8},{10,11... | collective-permute-start | bytes 1179656 | tf_op jit(solution)/shard_map/ppermute | solution.py:549
  130.2 8.1 %copy-start.4 = (bf16[2,384,1152]{2,1,0:T(8,128)(2,1)S(1)}, bf16[2,384,1152]{2,1,0:T(8,128)(2,1)}, u32[]{:S(2)}) copy-start(bf16[2,384,1152]{2,1,0:T(8,128)(2,1)} %copy-done.3) | copy-start | bytes 5308420
  130.2 15.1 %collective-permute-start.3 = (bf16[4,128,384]{2,1,0:T(8,128)(2,1)S(1)}, bf16[4,128,384]{2,1,0:T(8,128)(2,1)S(1)}, u32[]{:S(2)}, u32[]{:S(2)}) collective-permute-start(bf16[4,128,384]{2,1,0:T(8,128)(2,1)S(1)} %shard_map.166.fr_ref), channel_id=1, source_target_pairs={{0,31},{1,2},{2,1},{3,4},{4,3},{5,6},{6,5},{7,8},{8,7},{9,10},{10,... | collective-permute-start | bytes 1179656 | tf_op jit(solution)/shard_map/ppermute | solution.py:552
  132.0 6.3 %copy-start.8 = (bf16[768,2304]{1,0:T(8,128)(2,1)S(1)}, bf16[768,2304]{1,0:T(8,128)(2,1)}, u32[]{:S(2)}) copy-start(bf16[768,2304]{1,0:T(8,128)(2,1)} %copy-done.7) | copy-start | bytes 10616836
  138.4 4.0 %copy-start.6 = (bf16[2,768,1152]{2,1,0:T(8,128)(2,1)S(1)}, bf16[2,768,1152]{2,1,0:T(8,128)(2,1)}, u32[]{:S(2)}) copy-start(bf16[2,768,1152]{2,1,0:T(8,128)(2,1)} %copy-done.5) | copy-start | bytes 10616836
  142.4 3.0 %copy-start.10 = (bf16[4,2,128,384]{3,2,1,0:T(8,128)(2,1)S(1)}, bf16[4,2,128,384]{3,2,1,0:T(8,128)(2,1)}, u32[]{:S(2)}) copy-start(bf16[4,2,128,384]{3,2,1,0:T(8,128)(2,1)} %f_ref.3) | copy-start | bytes 2359300
